TPU v7x, 32 devices: a whole 2x2x4 slice. The times are simulated.
32 devices in a mesh: snap: 4 (over y, x), dom: 8 (over z, core).
Axes of the slice: x: 2, y: 2, z: 4, core: 2. Of those that a mesh axis runs over, the one named last changes fastest.
Arguments:
- readings: bfloat16 [4, 2, 4096], P('snap', None, 'dom'), may hold values from -6 to 6
- previous: bfloat16 [4, 64, 4096], P('snap', None, 'dom'), may hold values from -3 to 3
- upstream: bfloat16 [4, 64, 4096], P('snap', None, 'dom'), may hold values from -6 to 6
- gate_weight: bfloat16 [128, 330], replicated, may hold values from -0.3125 to 0.3125
- gate_bias: float32 [128], replicated, may hold values from -4 to 4
- cand_weight: bfloat16 [64, 330], replicated, may hold values from -0.3125 to 0.3125
- cand_bias: float32 [64], replicated, may hold values from -3 to 3
- neighbours: int32 [4, 4096], P(None, 'dom'), may hold values from 0 to 543, as said below
- edge_weight: float32 [4, 4096], P(None, 'dom'), may hold values from 0.1 to 1
- send_rows: int32 [8, 32], P('dom'), may hold values from 0 to 511, as said below
Outputs:
- state_grad: bfloat16 [4, 64, 4096], P('snap', None, 'dom')
- gate_weight_grad: float32 [128, 330], replicated
- gate_bias_grad: float32 [128], replicated
- cand_weight_grad: float32 [64, 330], replicated
- cand_bias_grad: float32 [64], replicated
Inputs may be any that keep to these rules, and one draw needn't show every extreme that they name: Value v of neighbours[d, i] below 512 is a row of segment i's own partition; v = 512 + q * 4 + s names slot s of what partition q sends to segment i's partition. Row d = 0 names each row of a partition exactly once, and in every partition every value from 512 to 543 appears. `send_rows`: row q holds rows of partition q; slots p * 4 to p * 4 + 3 are those sent to partition p; rows may repeat.
All inputs are finite; a program needn't handle non-finite values.
Results may differ from a plain program's by a relative error of at most 0.006.
Values may be sent and summed in bfloat16 or wider, within the bound.
No kernel may reach another device: no remote copies, remote signals or barrier semaphores. Data moves between devices by JAX's collectives and lax.ppermute only.
A program may use at most 64 MiB of HBM per device.

v0:
```python
import functools
import math

import jax
import jax.numpy as jnp
from jax import lax
from jax.experimental import pallas as pl
from jax.experimental.pallas import tpu as pltpu
from jax.sharding import PartitionSpec as P

F32 = jnp.float32
BF16 = jnp.bfloat16
LANES = 128


def nn(a, b):
    return lax.dot_general(a, b, (((1,), (0,)), ((), ())), preferred_element_type=F32)


def nt(a, b):
    return lax.dot_general(a, b, (((1,), (1,)), ((), ())), preferred_element_type=F32)


def tn(a, b):
    return lax.dot_general(a, b, (((0,), (0,)), ((), ())), preferred_element_type=F32)


def iota(shape, axis):
    return lax.broadcasted_iota(jnp.int32, shape, axis)


def column(row):
    k = row.shape[1]
    spread = jnp.broadcast_to(row.astype(F32), (k, k))
    return jnp.sum(jnp.where(iota((k, k), 0) == iota((k, k), 1), spread, 0.0), axis=1, keepdims=True)


def run(kernel, name, outs, *args, scratch=(), flops=20_000_000):
    whole = pl.BlockSpec(memory_space=pltpu.VMEM)
    return pl.pallas_call(
        kernel,
        name=name,
        out_shape=[jax.ShapeDtypeStruct(shape, kind) for shape, kind in outs],
        in_specs=[whole] * len(args),
        out_specs=[whole] * len(outs),
        scratch_shapes=list(scratch),
        compiler_params=pltpu.CompilerParams(vmem_limit_bytes=24 * 1024 * 1024),
        cost_estimate=pl.CostEstimate(flops=flops, bytes_accessed=2_000_000, transcendentals=0),
    )(*args)


def prep_kernel(cap, nb, w, rows, readings, previous, e, s, b, pay):
    degree, n = nb.shape
    nh = s.shape[0]
    hid = previous.shape[1]
    fin = readings.shape[1]
    step = 32
    for at in range(0, n + nh, step):
        node = iota((step, n), 0) + at
        total = jnp.zeros((step, n), F32)
        for d in range(degree):
            total = total + jnp.where(node == nb[d : d + 1, :], w[d : d + 1, :], 0.0)
        e[at : at + step, :] = total.astype(BF16)
    sent = column(rows[...]).astype(jnp.int32)
    s[...] = jnp.where(iota((nh, n), 1) == sent, 1.0, 0.0).astype(BF16)
    b[:hid, :] = previous[0]
    rest = b.shape[0] - hid
    row = iota((rest, n), 0)
    tail = jnp.where(row == fin, 1.0, 0.0)
    for f in range(fin):
        tail = jnp.where(row == f, readings[0, f : f + 1, :].astype(F32), tail)
    b[hid:, :] = tail.astype(BF16)
    base = b[...]
    chans = base.shape[0]
    bound = nt(s[...], base)
    halo = nt(e[n:, :], base)
    for p in range(nh // cap):
        pay[p, :, :chans] = bound[p * cap : (p + 1) * cap, :]
        pay[p, :, LANES : LANES + chans] = halo[p * cap : (p + 1) * cap, :]


def order_matrix(shape, chans, hid, fin, block):
    k = iota(shape, 0)
    col = iota(shape, 1)
    m = lax.div(col, jnp.int32(block))
    c = col - m * block
    source = jnp.where(c < hid, m * chans + fin + c, jnp.where(c < hid + fin, m * chans + c - hid, -1))
    return jnp.where(k == source, 1.0, 0.0).astype(BF16)


def mid_a_kernel(hid, fin, orders, e, b, gw, cw, fa, ra, gw_o, cw_o):
    n = e.shape[1]
    a = e[:n, :]
    base = b[...]
    fa[...] = nt(base, a)
    ra[...] = nn(base, a)
    block = base.shape[0]
    order = order_matrix((gw.shape[1], orders * block), hid + fin, hid, fin, block)
    gw_o[...] = nn(gw[...], order).astype(BF16)
    cw_o[...] = nn(cw[...], order).astype(BF16)


def post_a_kernel(one, cap, recv, e, s, fa, ra, f1, r1, ro, ri, pay, flat):
    n = e.shape[1]
    nh = s.shape[0]
    chans = fa.shape[0]
    for p in range(nh // cap):
        flat[p * cap : (p + 1) * cap, :] = recv[p]
    h = e[n:, :]
    sel = s[...]
    seen = flat[:, :chans].astype(BF16)
    back = flat[:, LANES : LANES + chans]
    back_degree = flat[:, LANES + one : LANES + one + 1]
    out_degree = fa[one : one + 1, :] + jnp.sum(sel.astype(F32) * back_degree, axis=0, keepdims=True)
    pulled = ra[...] + tn(seen, h)
    inv_o = 1.0 / out_degree
    inv_i = 1.0 / pulled[one : one + 1, :]
    ro[...] = inv_o
    ri[...] = inv_i
    first_out = ((fa[...] + tn(back.astype(BF16), sel)) * inv_o).astype(BF16)
    first_in = (pulled * inv_i).astype(BF16)
    f1[...] = first_out
    r1[...] = first_in
    bound = nt(sel, first_in)
    halo = nt(h, first_out)
    hi, ho = scaled(h, inv_i), scaled(h, inv_o)
    si, so = scaled(sel, inv_i), scaled(sel, inv_o)
    coefs = (nt(sel, hi), nt(h, so), nt(sel, ho), nt(h, si))
    for p in range(nh // cap):
        at = slice(p * cap, (p + 1) * cap)
        pay[p, :, :chans] = bound[at, :]
        pay[p, :, LANES : LANES + chans] = halo[at, :]
        for k, coef in enumerate(coefs):
            pay[p, :, 2 * LANES + k * nh : 2 * LANES + (k + 1) * nh] = coef[at, :]


def scaled(rows, factor):
    return (rows.astype(F32) * factor).astype(BF16)


def mid_b_kernel(e, s, f1, r1, ro, ri, f2l, r2l, kc, ke, ka):
    n = e.shape[1]
    a = e[:n, :]
    h = e[n:, :]
    sel = s[...]
    nh = sel.shape[0]
    chans = f1.shape[0]
    inv_o, inv_i = ro[...], ri[...]
    outs = nt(jnp.concatenate([f1[...], scaled(sel, inv_o), scaled(sel, inv_i)], axis=0), a)
    ins = nn(jnp.concatenate([r1[...], scaled(h, inv_i), scaled(h, inv_o)], axis=0), a)
    f2l[...] = outs[:chans]
    r2l[...] = ins[:chans]
    kc[:nh, :] = ins[chans : chans + nh].astype(BF16)
    kc[nh:, :] = h
    ke[:nh, :] = outs[chans : chans + nh].astype(BF16)
    ke[nh:, :] = sel
    ka[:nh, :] = (2.0 * ins[chans + nh :]).astype(BF16)
    ka[nh : 2 * nh, :] = h
    ka[2 * nh : 3 * nh, :] = (2.0 * outs[chans + nh :]).astype(BF16)
    ka[3 * nh :, :] = sel


def send(pay, cap, left, right, left_two, right_two):
    nh = left.shape[0]
    rows = jnp.concatenate([left, right], axis=1)
    rows_two = jnp.concatenate([left_two, right_two], axis=1)
    both = jnp.concatenate([rows, rows_two], axis=0).astype(BF16)
    k = iota((2 * nh, 2 * nh), 0)
    part = lax.div(k, jnp.int32(2 * cap))
    spot = k - part * (2 * cap)
    source = jnp.where(spot < cap, part * cap + spot, nh + part * cap + spot - cap)
    mine = nn(jnp.where(iota((2 * nh, 2 * nh), 1) == source, 1.0, 0.0).astype(BF16), both)
    for p in range(nh // cap):
        own = mine[p * 2 * cap : (p + 1) * 2 * cap, :]
        pay[p] = jnp.concatenate([rows, own], axis=0).astype(BF16)


def post_b_kernel(cap, one, recv, e, s, b, f1, r1, f2l, r2l, ro, ri, gw, gb, states, reset, update, y, f1l, r1l, pay, flat):
    n = e.shape[1]
    nh = s.shape[0]
    hid = y.shape[0]
    chans = b.shape[0]
    for p in range(nh // cap):
        flat[p * cap : (p + 1) * cap, :] = recv[p, :, : 2 * LANES]
    a = e[:n, :]
    h = e[n:, :]
    sel = s[...]
    inv_o, inv_i = ro[...], ri[...]
    base = b[...].astype(F32)
    seen = flat[:, :chans].astype(BF16)
    back = flat[:, LANES : LANES + chans].astype(BF16)
    f2 = 2.0 * (f2l[...] + tn(back, sel)) * inv_o - base
    r2 = 2.0 * (r2l[...] + tn(seen, h)) * inv_i - base
    states[:chans, :] = b[...]
    states[chans : 2 * chans, :] = f1[...]
    states[2 * chans : 3 * chans, :] = f2.astype(BF16)
    states[3 * chans : 4 * chans, :] = r1[...]
    states[4 * chans :, :] = r2.astype(BF16)
    gates = jax.nn.sigmoid(nn(gw[...], states[...]) + column(gb[...]))
    reset[...] = gates[:hid]
    update[...] = gates[hid:]
    now = (gates[:hid] * base[:hid]).astype(BF16)
    y[...] = now
    local_out = nt(now, a) * inv_o
    local_in = nn(now, a) * inv_i
    f1l[...] = local_out
    r1l[...] = local_in
    bound = nt(sel, jnp.concatenate([now, local_in.astype(BF16)], axis=0))
    halo = nt(h, jnp.concatenate([now, local_out.astype(BF16)], axis=0))
    send(pay, cap, bound[:, :hid], halo[:, :hid], bound[:, hid:], halo[:, hid:])


def gather_matrix(coef, out, nd, cap, per, first, factor):
    nh = nd * cap
    width = nd * per
    k = iota((nh, width), 0)
    col = iota((nh, width), 1)
    r = lax.div(col, jnp.int32(per))
    u = col - r * per
    p = lax.div(u, jnp.int32(cap))
    spot = u - p * cap
    here = lax.div(k, jnp.int32(cap))
    slot = k - here * cap
    inside = u < nh
    place = jnp.where((k == r * cap + spot) & inside, 1.0, 0.0).astype(BF16)
    keep = (here == p) & inside
    for i in range(2):
        wide = nn(coef[:, (first + i) * nh : (first + i + 1) * nh].astype(BF16), place)
        own = (r == here) & (u == nh + cap + slot)
        out[(i + 1) * nh : (i + 2) * nh, :] = jnp.where(keep, factor * wide, jnp.where(own, 1.0, 0.0)).astype(BF16)
    out[:nh, :] = jnp.where((r == here) & (u == nh + slot), 1.0, 0.0).astype(BF16)


def mid_c_kernel(nd, cap, per, fused, recv, e, f1l, r1l, f2l, r2l, *rest):
    n = e.shape[1]
    a = e[:n, :]
    f2l[...] = nt(f1l[...].astype(BF16), a)
    r2l[...] = nn(r1l[...].astype(BF16), a)
    if fused:
        gd, ga, flat = rest
        for p in range(nd):
            flat[p * cap : (p + 1) * cap, :] = recv[p, :, 2 * LANES :]
        gather_matrix(flat, gd, nd, cap, per, 0, 1.0)
        gather_matrix(flat, ga, nd, cap, per, 2, 2.0)


def arrived(fused, hid, nh, g, recv):
    if fused:
        halo = nn(g[...], recv[...].reshape(recv.shape[0] * recv.shape[1], recv.shape[2]))
        two = halo[nh : 2 * nh, :hid], halo[2 * nh :, hid:]
    else:
        halo = recv[...]
        two = halo[nh:, :hid], halo[nh:, hid:]
    one = halo[:nh]
    return one[:, :hid], one[:, hid:], two[0], two[1]


def back_and_send(cap, hid, g, a, h, sel, inv_o, inv_i, z1, z2, pay):
    g0, g1, g2, g3, g4 = (g[m * hid : (m + 1) * hid, :].astype(BF16).astype(F32) for m in range(5))
    y1 = (g2 * inv_o).astype(BF16)
    y2 = (g4 * inv_i).astype(BF16)
    now1 = ((g1 + 2.0 * nn(y1, a)) * inv_o).astype(BF16)
    now2 = ((g3 + 2.0 * nt(y2, a)) * inv_i).astype(BF16)
    z1[...] = now1
    z2[...] = now2
    bound = nt(sel, jnp.concatenate([y1, now1], axis=0))
    halo = nt(h, jnp.concatenate([y2, now2], axis=0))
    send(pay, cap, bound[:, :hid], halo[:, :hid], bound[:, hid:], halo[:, hid:])
    return g0 - g2 - g4


def hidden_weights(w, hid, block, orders):
    return jnp.concatenate([w[:, m * block : m * block + hid] for m in range(orders)], axis=1)


def post_c_kernel(fused, cap, orders, g, recv, e, s, kc, ke, y, f1l, r1l, f2l, r2l, ro, ri, states, cw, cb, upstream, update,
                  mixed, cand_grad, gate_update, z1, z2, direct, pay):
    n = e.shape[1]
    nh = s.shape[0]
    hid = y.shape[0]
    block = states.shape[0] // orders
    a = e[:n, :]
    h = e[n:, :]
    sel = s[...]
    inv_o, inv_i = ro[...], ri[...]
    c1, e1, c2, e2 = arrived(fused, hid, nh, g, recv)
    base = y[...].astype(F32)
    c1, e1 = c1.astype(BF16), e1.astype(BF16)
    cc = jnp.concatenate([c1, c2.astype(BF16)], axis=0)
    ee = jnp.concatenate([e1, e2.astype(BF16)], axis=0)
    f1 = f1l[...] + tn(e1, sel) * inv_o
    f2 = 2.0 * (f2l[...] + tn(ee, ke[...])) * inv_o - base
    r1 = r1l[...] + tn(c1, h) * inv_i
    r2 = 2.0 * (r2l[...] + tn(cc, kc[...])) * inv_i - base
    for m, value in enumerate((y[...], f1, f2, r1, r2)):
        mixed[m * block : m * block + hid, :] = value.astype(BF16)
        mixed[m * block + hid : (m + 1) * block, :] = states[m * block + hid : (m + 1) * block, :]
    weights = cw[...]
    cand = jnp.tanh(nn(weights, mixed[...]) + column(cb[...]))
    up = upstream[0].astype(F32)
    gate = update[...]
    grad = (up * (1.0 - gate) * (1.0 - cand * cand)).astype(BF16)
    cand_grad[...] = grad
    held = states[:hid, :].astype(F32)
    gate_update[...] = (up * (held - cand) * gate * (1.0 - gate)).astype(BF16)
    back = tn(hidden_weights(weights, hid, block, orders), grad)
    direct[...] = back_and_send(cap, hid, back, a, h, sel, inv_o, inv_i, z1, z2, pay)


def weight_part(grad, features, orders, chans, hid, fin):
    block = features.shape[0] // orders
    width = -(-(orders * chans + 1) // LANES) * LANES
    shape = (width, orders * block)
    k = iota(shape, 0)
    col = iota(shape, 1)
    m = lax.div(col, jnp.int32(block))
    c = col - m * block
    source = jnp.where(c < hid, m * chans + fin + c, jnp.where(c < hid + fin, m * chans + c - hid, -1))
    source = jnp.where(col == hid + fin, orders * chans, source)
    order = jnp.where(k == source, 1.0, 0.0).astype(BF16)
    return nt(nt(grad, features).astype(BF16), order)


def mid_d_kernel(orders, fin, e, z1, z2, direct, cand_grad, mixed, gate_update, states, base, part):
    n = e.shape[1]
    a = e[:n, :]
    hid = z1.shape[0]
    base[...] = direct[...] + nn(z1[...], a) + nt(z2[...], a)
    part[:hid, :] = weight_part(gate_update[...], states[...], orders, hid + fin, hid, fin).astype(BF16)
    part[hid:, :] = weight_part(cand_grad[...], mixed[...], orders, hid + fin, hid, fin).astype(BF16)


def add_halo(fused, g, recv, ka, base):
    hid = base.shape[0]
    nh = ka.shape[0] // 4
    c1, e1, c2, e2 = arrived(fused, hid, nh, g, recv)
    return base[...] + tn(jnp.concatenate([c1, c2, e1, e2], axis=0).astype(BF16), ka[...])


def post_d_kernel(fused, cap, orders, g, recv, e, s, ka, base, ro, ri, states, gw, upstream, reset, update, gate_update,
                  gate_reset, z1, z2, direct, pay):
    n = e.shape[1]
    hid = base.shape[0]
    block = states.shape[0] // orders
    scaled_grad = add_halo(fused, g, recv, ka, base)
    held = states[:hid, :].astype(F32)
    gate = reset[...]
    grad = (scaled_grad * held * gate * (1.0 - gate)).astype(BF16)
    gate_reset[...] = grad
    weights = hidden_weights(gw[...], hid, block, orders)
    back = tn(weights, jnp.concatenate([grad, gate_update[...]], axis=0))
    rest = back_and_send(cap, hid, back, e[:n, :], e[n:, :], s[...], ro[...], ri[...], z1, z2, pay)
    direct[...] = rest + upstream[0].astype(F32) * update[...] + scaled_grad * gate


def mid_e_kernel(orders, fin, rows, e, z1, z2, direct, gate_reset, states, part, base, grads):
    n = e.shape[1]
    a = e[:n, :]
    hid = z1.shape[0]
    base[...] = direct[...] + nn(z1[...], a) + nt(z2[...], a)
    first = weight_part(gate_reset[...], states[...], orders, hid + fin, hid, fin)
    both = jnp.concatenate([first, part[...].astype(F32)], axis=0)
    for k in range(grads.shape[0]):
        if k * rows < both.shape[0]:
            grads[k] = both[k * rows : (k + 1) * rows, :].astype(BF16)
        else:
            grads[k] = jnp.zeros(grads.shape[1:], BF16)


def post_e_kernel(fused, g, recv, ka, base, out):
    out[0] = add_halo(fused, g, recv, ka, base).astype(BF16)


def add_kernel(recv, out):
    total = recv[0].astype(F32)
    for k in range(1, recv.shape[0]):
        total = total + recv[k].astype(F32)
    for k in range(out.shape[0]):
        out[k] = total.astype(BF16)


def finish_kernel(hid, factor, recv, gw, gb, cw, cb):
    rows = recv.shape[1]
    features = gw.shape[1]
    total = gw.shape[0] + cw.shape[0]
    for k in range(total // rows):
        part = recv[k].astype(F32)[:, :features] * factor
        at = k * rows
        if at < 2 * hid:
            gw[at : at + rows, :] = part
        else:
            cw[at - 2 * hid : at - 2 * hid + rows, :] = part
    flat = jnp.concatenate([recv[k].astype(F32) for k in range(total // rows)], axis=0)
    pick = jnp.where(iota((8, flat.shape[1]), 1) == features, 1.0, 0.0).astype(BF16)
    bias = nt(pick, flat.astype(BF16))[:1] * factor
    gb[...] = bias[:, : 2 * hid]
    cb[...] = bias[:, 2 * hid :]


def body(
    readings,
    previous,
    upstream,
    gate_weight,
    gate_bias,
    cand_weight,
    cand_bias,
    neighbours,
    edge_weight,
    send_rows,
):
    fin, hid = readings.shape[1], previous.shape[1]
    chans = fin + hid
    orders = gate_weight.shape[1] // chans
    n = readings.shape[2]
    nd = lax.axis_size("dom")
    devices = nd * lax.axis_size("snap")
    nh = send_rows.shape[1]
    cap = nh // nd
    block = hid + 16 * (-(-(fin + 1) // 16))
    one = hid + fin
    per = nh + 2 * cap
    fused = 3 * nh * nd * per <= 1 << 18
    move = functools.partial(lax.all_to_all, axis_name="dom", split_axis=0, concat_axis=0, tiled=True)

    e, s, b, pay = run(
        functools.partial(prep_kernel, cap), "prep",
        [((n + nh, n), BF16), ((nh, n), BF16), ((block, n), BF16), ((nd, cap, 2 * LANES), F32)],
        neighbours, edge_weight, send_rows, readings, previous,
    )
    recv = move(pay)
    fa, ra, gw, cw = run(
        functools.partial(mid_a_kernel, hid, fin, orders), "mid_a",
        [((block, n), F32), ((block, n), F32), ((2 * hid, orders * block), BF16), ((hid, orders * block), BF16)],
        e, b, gate_weight, cand_weight,
    )
    wide = 2 * LANES + 4 * nh
    f1, r1, ro, ri, pay = run(
        functools.partial(post_a_kernel, one, cap), "post_a",
        [((block, n), BF16), ((block, n), BF16), ((1, n), F32), ((1, n), F32), ((nd, cap, wide), F32)],
        recv, e, s, fa, ra, scratch=[pltpu.VMEM((nh, 2 * LANES), F32)],
    )
    recv_b = move(pay)
    f2l, r2l, kc, ke, ka = run(
        mid_b_kernel, "mid_b",
        [((block, n), F32), ((block, n), F32), ((2 * nh, n), BF16), ((2 * nh, n), BF16), ((4 * nh, n), BF16)],
        e, s, f1, r1, ro, ri,
    )
    pay_kind = ((nd, per, 2 * hid), BF16)
    field, field16 = ((hid, n), F32), ((hid, n), BF16)
    states, reset, update, y, f1l, r1l, pay = run(
        functools.partial(post_b_kernel, cap, one), "post_b",
        [((orders * block, n), BF16), field, field, field16, field, field, pay_kind],
        recv_b, e, s, b, f1, r1, f2l, r2l, ro, ri, gw, gate_bias[None, :],
        scratch=[pltpu.VMEM((nh, 2 * LANES), F32)],
    )
    recv = move(pay)
    table = ((3 * nh, nd * per), BF16)
    f2l, r2l, *tables = run(
        functools.partial(mid_c_kernel, nd, cap, per, fused), "mid_c",
        [field, field] + [table] * (2 if fused else 0),
        recv_b, e, f1l, r1l, scratch=[pltpu.VMEM((nh, 4 * nh), F32)] if fused else [],
    )
    if fused:
        inward, outward = tables
        halo_of = lambda got, first, factor: got
    else:
        inward = outward = jnp.zeros((8, LANES), BF16)
        coefs = recv_b[:, :, 2 * LANES :].reshape(nd, cap, 4, nd, cap)

        def halo_of(got, first, factor):
            rows = got[:, :nh].reshape(nd, nd, cap, 2, hid).astype(F32)
            two = jnp.einsum("psgrt,rptgk->psgk", coefs[:, :, first : first + 2], rows)
            two = factor * two.reshape(nh, 2 * hid) + got[:, nh + cap :].reshape(nh, 2 * hid).astype(F32)
            return jnp.concatenate([got[:, nh : nh + cap].reshape(nh, 2 * hid).astype(F32), two], axis=0)

    mixed, cand_grad, gate_update, z1, z2, direct, pay = run(
        functools.partial(post_c_kernel, fused, cap, orders), "post_c",
        [((orders * block, n), BF16), field16, field16, field16, field16, field, pay_kind],
        inward, halo_of(recv, 0, 1.0), e, s, kc, ke, y, f1l, r1l, f2l, r2l, ro, ri, states, cw, cand_bias[None, :], upstream, update,
    )
    recv = move(pay)
    width = -(-(orders * chans + 1) // LANES) * LANES
    base, part = run(
        functools.partial(mid_d_kernel, orders, fin), "mid_d", [field, ((2 * hid, width), BF16)],
        e, z1, z2, direct, cand_grad, mixed, gate_update, states,
    )
    gate_reset, z1, z2, direct, pay = run(
        functools.partial(post_d_kernel, fused, cap, orders), "post_d",
        [field16, field16, field16, field, pay_kind],
        outward, halo_of(recv, 2, 2.0), e, s, ka, base, ro, ri, states, gw, upstream, reset, update, gate_update,
    )
    recv = move(pay)
    rows = 8 * (-(-3 * hid // (8 * devices)))
    base, grads = run(
        functools.partial(mid_e_kernel, orders, fin, rows), "mid_e", [field, ((devices, rows, width), BF16)],
        e, z1, z2, direct, gate_reset, states, part,
    )
    (state_grad,) = run(
        functools.partial(post_e_kernel, fused), "post_e", [((1, hid, n), BF16)],
        outward, halo_of(recv, 2, 2.0), ka, base,
    )
    both = ("snap", "dom")
    grads = lax.all_to_all(grads, both, 0, 0, tiled=True)
    (grads,) = run(add_kernel, "add", [((devices, rows, width), BF16)], grads)
    grads = lax.all_to_all(grads, both, 0, 0, tiled=True)
    factor = 1.0 / math.sqrt(readings.shape[0] * lax.axis_size("snap") * n * nd)
    feats = orders * chans
    grad_gw, grad_gb, grad_cw, grad_cb = run(
        functools.partial(finish_kernel, hid, factor), "finish",
        [((2 * hid, feats), F32), ((1, 2 * hid), F32), ((hid, feats), F32), ((1, hid), F32)],
        grads,
    )
    return state_grad, grad_gw, grad_gb[0], grad_cw, grad_cb[0]


def solution(mesh):
    in_specs = (
        P("snap", None, "dom"),
        P("snap", None, "dom"),
        P("snap", None, "dom"),
        P(),
        P(),
        P(),
        P(),
        P(None, "dom"),
        P(None, "dom"),
        P("dom", None),
    )
    out_specs = (P("snap", None, "dom"), P(), P(), P(), P())
    return jax.shard_map(body, mesh=mesh, in_specs=in_specs, out_specs=out_specs, check_vma=False)
```

profile of v0, /device:TPU:0, one launch (start us, length us, event | category | flops | bytes accessed | tf_op | source)
XLA Modules:
  0.0 88.5 jit_solution(6488035151184874387)
XLA Ops:
  0.6 0.0 copy-start.1
  0.6 0.8 copy-done.1
  1.5 0.0 copy-start.3
  1.5 0.7 copy-done.3
  2.2 0.0 copy-start.4
  2.2 0.7 copy-done.4
  2.9 0.0 copy-start.5
  2.9 0.7 copy-done.5
  3.6 0.0 copy-start.7
  3.6 0.7 copy-done.7
  4.2 0.0 copy-start.9
  4.2 1.2 %prep.1 = (bf16[544,512]{1,0:T(8,128)(2,1)S(1)}, bf16[32,512]{1,0:T(8,128)(2,1)S(1)}, bf16[80,512]{1,0:T(8,128)(2,1)S(1)}, f32[8,4,256]{2,1,0:T(4,128)}) custom-call(s32[4,512]{1,0:T(4,128)S(1)} %copy-done.3, f32[4,512]{1,0:T(4,128)S(1)} %copy-done.4, s32[1,32]{1,0:T(1,128)S(1)} %copy-done.7, bf16[1,2,512]{2,1,0:T(2,128)(2,1)S(1)} %copy-done.5, ...), custom_call_target="tpu_custom_call" | custom-call | flops 20000000 | bytes 2000000 | tf_op jit(solution)/shard_map/prep/pallas_call | solution.py:40
  5.4 6.3 %all-to-all-start = ((f32[8,4,256]{2,1,0:T(4,128)}), f32[8,4,256]{2,1,0:T(4,128)S(1)}, u32[]{:S(2)}, u32[]{:S(2)}) async-start(f32[8,4,256]{2,1,0:T(4,128)} %get-tuple-element.54), calls=%async_computation | async-start | bytes 65536 | tf_op jit(solution)/shard_map/all_to_all | solution.py:431
  11.8 0.0 copy-done.9
  11.8 0.0 copy-start.2
  11.8 0.1 copy.15.gw
  11.9 0.7 copy-done.2
  12.6 0.5 mid_a.1
  13.1 4.4 %all-to-all-done.recv = f32[8,4,256]{2,1,0:T(4,128)S(1)} async-done(((f32[8,4,256]{2,1,0:T(4,128)}), f32[8,4,256]{2,1,0:T(4,128)S(1)}, u32[]{:S(2)}, u32[]{:S(2)}) %all-to-all-start) | async-done | bytes 32800 | tf_op jit(solution)/shard_map/all_to_all | solution.py:431
  17.5 1.1 %post_a.1 = (bf16[80,512]{1,0:T(8,128)(2,1)S(1)}, bf16[80,512]{1,0:T(8,128)(2,1)S(1)}, f32[1,512]{1,0:T(1,128)S(1)}, f32[1,512]{1,0:T(1,128)S(1)}, f32[8,4,384]{2,1,0:T(4,128)}) custom-call(f32[8,4,256]{2,1,0:T(4,128)S(1)} %all-to-all-done.recv, bf16[544,512]{1,0:T(8,128)(2,1)S(1)} %get-tuple-element.55.e, bf16[32,512]{1,0:T(8,128)(2,1)S(1)} %get-tuple-element.56.s, ...), custom_call_target="tpu_custom_call" | custom-call | flops 20000000 | bytes 2000000 | tf_op jit(solution)/shard_map/post_a/pallas_call | solution.py:40
  18.7 3.3 %all-to-all-start.1 = ((f32[8,4,384]{2,1,0:T(4,128)}), f32[8,4,384]{2,1,0:T(4,128)S(1)}, u32[]{:S(2)}, u32[]{:S(2)}) async-start(f32[8,4,384]{2,1,0:T(4,128)} %get-tuple-element.60), calls=%async_computation.1 | async-start | bytes 98304 | tf_op jit(solution)/shard_map/all_to_all | solution.py:443
  22.0 0.4 mid_b.1
  22.4 5.3 %all-to-all-done.1.recv = f32[8,4,384]{2,1,0:T(4,128)S(1)} async-done(((f32[8,4,384]{2,1,0:T(4,128)}), f32[8,4,384]{2,1,0:T(4,128)S(1)}, u32[]{:S(2)}, u32[]{:S(2)}) %all-to-all-start.1) | async-done | bytes 49184 | tf_op jit(solution)/shard_map/all_to_all | solution.py:443
  27.8 0.0 copy-start.6
  27.8 0.7 copy-done.6
  28.4 1.7 %post_b.1 = (bf16[400,512]{1,0:T(8,128)(2,1)S(1)}, f32[64,512]{1,0:T(8,128)S(1)}, f32[64,512]{1,0:T(8,128)S(1)}, bf16[64,512]{1,0:T(8,128)(2,1)S(1)}, f32[64,512...) custom-call(f32[8,4,384]{2,1,0:T(4,128)S(1)} %all-to-all-done.1.recv, ...), custom_call_target="tpu_custom_call" | custom-call | flops 20000000 | bytes 2000000 | tf_op jit(solution)/shard_map/post_b/pallas_call | solution.py:40
  30.1 3.4 %all-to-all-start.2 = ((bf16[8,40,128]{2,1,0:T(8,128)(2,1)}), bf16[8,40,128]{2,1,0:T(8,128)(2,1)S(1)}, u32[]{:S(2)}, u32[]{:S(2)}) async-start(bf16[8,40,128]{2,1,0:T(8,128)(2,1)} %get-tuple-element.72), calls=%async_computation.2 | async-start | bytes 163840 | tf_op jit(solution)/shard_map/all_to_all | solution.py:457
  33.5 0.0 copy-start
  33.5 0.4 mid_c.1
  33.9 5.6 %all-to-all-done.2.recv = bf16[8,40,128]{2,1,0:T(8,128)(2,1)S(1)} async-done(((bf16[8,40,128]{2,1,0:T(8,128)(2,1)}), bf16[8,40,128]{2,1,0:T(8,128)(2,1)S(1)}, u32[]{:S(2)}, u32[]{:S(2)}) %all-to-all-start.2) | async-done | bytes 81952 | tf_op jit(solution)/shard_map/all_to_all | solution.py:457
  39.5 0.0 copy-start.8
  39.5 0.0 copy-done
  39.5 0.7 copy-done.8
  40.2 2.1 %post_c.1 = (bf16[400,512]{1,0:T(8,128)(2,1)S(1)}, bf16[64,512]{1,0:T(8,128)(2,1)S(1)}, bf16[64,512]{1,0:T(8,128)(2,1)S(1)}, bf16[64,512]{1,0:T(8,128)(2,1)S(1)}...) custom-call(bf16[96,320]{1,0:T(8,128)(2,1)S(1)} %get-tuple-element.71.g, ...), custom_call_target="tpu_custom_call" | custom-call | flops 20000000 | bytes 2000000 | tf_op jit(solution)/shard_map/post_c/pallas_call | solution.py:40
  42.3 3.4 %all-to-all-start.3 = ((bf16[8,40,128]{2,1,0:T(8,128)(2,1)}), bf16[8,40,128]{2,1,0:T(8,128)(2,1)S(1)}, u32[]{:S(2)}, u32[]{:S(2)}) async-start(bf16[8,40,128]{2,1,0:T(8,128)(2,1)} %get-tuple-element.81), calls=%async_computation.3 | async-start | bytes 163840 | tf_op jit(solution)/shard_map/all_to_all | solution.py:482
  45.7 1.0 %mid_d.1 = (f32[64,512]{1,0:T(8,128)S(1)}, bf16[128,384]{1,0:T(8,128)(2,1)S(1)}) custom-call(bf16[544,512]{1,0:T(8,128)(2,1)S(1)} %get-tuple-element.55.e, bf16[64,512]{1,0:T(8,128)(2,1)S(1)} %get-tuple-element.83.z1, bf16[64,512]{1,0:T(8,128)(2,1)S(1)} %get-tuple-element.84.z2, f32[64,512]{1,0:T(8,128)S(1)} %get-tuple-element.85.direct, ...), custom_call_target="tpu_custom_call" | custom-call | flops 20000000 | bytes 2000000 | tf_op jit(solution)/shard_map/mid_d/pallas_call | solution.py:40
  46.7 5.0 %all-to-all-done.3.recv = bf16[8,40,128]{2,1,0:T(8,128)(2,1)S(1)} async-done(((bf16[8,40,128]{2,1,0:T(8,128)(2,1)}), bf16[8,40,128]{2,1,0:T(8,128)(2,1)S(1)}, u32[]{:S(2)}, u32[]{:S(2)}) %all-to-all-start.3) | async-done | bytes 81952 | tf_op jit(solution)/shard_map/all_to_all | solution.py:482
  51.8 2.0 %post_d.1 = (bf16[64,512]{1,0:T(8,128)(2,1)S(1)}, bf16[64,512]{1,0:T(8,128)(2,1)S(1)}, bf16[64,512]{1,0:T(8,128)(2,1)S(1)}, f32[64,512]{1,0:T(8,128)S(1)}, bf16[8,40,128]{2,1,0:T(8,128)(2,1)}) custom-call(bf16[96,320]{1,0:T(8,128)(2,1)S(1)} %get-tuple-element.70.g, bf16[8,40,128]{2,1,0:T(8,128)(2,1)S(1)} %all-to-all-done.3.recv, ...), custom_call_target="tpu_custom_call" | custom-call | flops 20000000 | bytes 2000000 | tf_op jit(solution)/shard_map/post_d/pallas_call | solution.py:40
  53.7 0.7 mid_e.1
  54.4 11.8 %all_to_all.35.recv = bf16[32,8,384]{2,1,0:T(8,128)(2,1)S(1)} all-to-all(bf16[32,8,384]{2,1,0:T(8,128)(2,1)S(1)} %get-tuple-element.98), channel_id=1, replica_groups=mesh['snap'=4,'dom'=8] {'snap','dom'}, dimensions={0} | all-to-all | bytes 393216 | tf_op jit(solution)/shard_map/all_to_all | solution.py:504
  66.2 3.4 %all-to-all-start.4 = ((bf16[8,40,128]{2,1,0:T(8,128)(2,1)}), bf16[8,40,128]{2,1,0:T(8,128)(2,1)S(1)}, u32[]{:S(2)}, u32[]{:S(2)}) async-start(bf16[8,40,128]{2,1,0:T(8,128)(2,1)} %get-tuple-element.91), calls=%async_computation.4 | async-start | bytes 163840 | tf_op jit(solution)/shard_map/all_to_all | solution.py:493
  69.6 0.7 add.1
  70.3 5.3 %all-to-all-done.4.recv = bf16[8,40,128]{2,1,0:T(8,128)(2,1)S(1)} async-done(((bf16[8,40,128]{2,1,0:T(8,128)(2,1)}), bf16[8,40,128]{2,1,0:T(8,128)(2,1)S(1)}, u32[]{:S(2)}, u32[]{:S(2)}) %all-to-all-start.4) | async-done | bytes 81952 | tf_op jit(solution)/shard_map/all_to_all | solution.py:493
  75.6 2.6 %all-to-all-start.6 = ((bf16[32,8,384]{2,1,0:T(8,128)(2,1)}), bf16[32,8,384]{2,1,0:T(8,128)(2,1)S(1)}, u32[]{:S(2)}, u32[]{:S(2)}) async-start(bf16[32,8,384]{2,1,0:T(8,128)(2,1)} %add.1), calls=%async_computation.6 | async-start | bytes 393216 | tf_op jit(solution)/shard_map/all_to_all | solution.py:506
  78.2 1.1 %post_e.1 = bf16[1,64,512]{2,1,0:T(8,128)(2,1)} custom-call(bf16[96,320]{1,0:T(8,128)(2,1)S(1)} %get-tuple-element.70.g, bf16[8,40,128]{2,1,0:T(8,128)(2,1)S(1)} %all-to-all-done.4.recv, bf16[128,512]{1,0:T(8,128)(2,1)S(1)} %get-tuple-element.82.ka, f32[64,512]{1,0:T(8,128)S(1)} %get-tuple-element.97.base), custom_call_target="tpu_custom_call" | custom-call | flops 20000000 | bytes 2000000 | tf_op jit(solution)/shard_map/post_e/pallas_call | solution.py:40
  79.3 7.7 %all-to-all-done.6.recv = bf16[32,8,384]{2,1,0:T(8,128)(2,1)S(1)} async-done(((bf16[32,8,384]{2,1,0:T(8,128)(2,1)}), bf16[32,8,384]{2,1,0:T(8,128)(2,1)S(1)}, u32[]{:S(2)}, u32[]{:S(2)}) %all-to-all-start.6) | async-done | bytes 196640 | tf_op jit(solution)/shard_map/all_to_all | solution.py:506
  87.0 0.7 finish.1
  87.7 0.8 copy.16
Async XLA Ops:
  0.6 0.8 copy-start.1
  1.5 0.7 copy-start.3
  2.2 0.7 copy-start.4
  2.9 0.7 copy-start.5
  3.6 0.7 copy-start.7
  4.2 7.6 %copy-start.9 = (bf16[128,330]{0,1:T(8,128)(2,1)S(1)}, bf16[128,330]{0,1:T(8,128)(2,1)}, u32[]{:S(2)}) copy-start(bf16[128,330]{0,1:T(8,128)(2,1)} %param.13) | copy-start | bytes 253444
  5.4 12.1 %all-to-all-start = ((f32[8,4,256]{2,1,0:T(4,128)}), f32[8,4,256]{2,1,0:T(4,128)S(1)}, u32[]{:S(2)}, u32[]{:S(2)}) async-start(f32[8,4,256]{2,1,0:T(4,128)} %get-tuple-element.54), calls=%async_computation | async-start | bytes 65536 | tf_op jit(solution)/shard_map/all_to_all | solution.py:431
  11.8 0.8 copy-start.2
  18.7 9.1 %all-to-all-start.1 = ((f32[8,4,384]{2,1,0:T(4,128)}), f32[8,4,384]{2,1,0:T(4,128)S(1)}, u32[]{:S(2)}, u32[]{:S(2)}) async-start(f32[8,4,384]{2,1,0:T(4,128)} %get-tuple-element.60), calls=%async_computation.1 | async-start | bytes 98304 | tf_op jit(solution)/shard_map/all_to_all | solution.py:443
  27.8 0.7 copy-start.6
  30.1 9.4 %all-to-all-start.2 = ((bf16[8,40,128]{2,1,0:T(8,128)(2,1)}), bf16[8,40,128]{2,1,0:T(8,128)(2,1)S(1)}, u32[]{:S(2)}, u32[]{:S(2)}) async-start(bf16[8,40,128]{2,1,0:T(8,128)(2,1)} %get-tuple-element.72), calls=%async_computation.2 | async-start | bytes 163840 | tf_op jit(solution)/shard_map/all_to_all | solution.py:457
  33.5 6.1 %copy-start = (bf16[1,64,512]{2,1,0:T(8,128)(2,1)S(1)}, bf16[1,64,512]{2,1,0:T(8,128)(2,1)}, u32[]{:S(2)}) copy-start(bf16[1,64,512]{2,1,0:T(8,128)(2,1)} %upstream.3) | copy-start | bytes 196612
  39.5 0.7 copy-start.8
  42.3 9.4 %all-to-all-start.3 = ((bf16[8,40,128]{2,1,0:T(8,128)(2,1)}), bf16[8,40,128]{2,1,0:T(8,128)(2,1)S(1)}, u32[]{:S(2)}, u32[]{:S(2)}) async-start(bf16[8,40,128]{2,1,0:T(8,128)(2,1)} %get-tuple-element.81), calls=%async_computation.3 | async-start | bytes 163840 | tf_op jit(solution)/shard_map/all_to_all | solution.py:482
  66.2 9.4 %all-to-all-start.4 = ((bf16[8,40,128]{2,1,0:T(8,128)(2,1)}), bf16[8,40,128]{2,1,0:T(8,128)(2,1)S(1)}, u32[]{:S(2)}, u32[]{:S(2)}) async-start(bf16[8,40,128]{2,1,0:T(8,128)(2,1)} %get-tuple-element.91), calls=%async_computation.4 | async-start | bytes 163840 | tf_op jit(solution)/shard_map/all_to_all | solution.py:493
  75.6 11.3 %all-to-all-start.6 = ((bf16[32,8,384]{2,1,0:T(8,128)(2,1)}), bf16[32,8,384]{2,1,0:T(8,128)(2,1)S(1)}, u32[]{:S(2)}, u32[]{:S(2)}) async-start(bf16[32,8,384]{2,1,0:T(8,128)(2,1)} %add.1), calls=%async_computation.6 | async-start | bytes 393216 | tf_op jit(solution)/shard_map/all_to_all | solution.py:506
where the time goes:
time: 89.6 us; the launch traced here: 88.5 us
  waiting for transfers between devices  33.4 us (37%)
  starting transfers between devices  22.3 us (25%)
  Pallas kernels  13.8 us (15%)
  blocking collectives  11.8 us (13%)
  local copies, waits for them, and re-layouts  6.46 us (7%)
    all_to_all x4, waiting for transfers between devices, body(): recv = move(pay)  20.3 us
    all_to_all x4, starting transfers between devices, body(): recv = move(pay)  16.4 us
    pallas_call x13, Pallas kernels, run(): pl.pallas_call(kernel, name=name, out_shape=[jax.ShapeDtypeStruct(shape,...  13.8 us
    all_to_all x1, blocking collectives, body(): grads = lax.all_to_all(grads, both, 0, 0, tiled=True)  11.8 us
    all_to_all x1, waiting for transfers between devices, body(): grads = lax.all_to_all(grads, both, 0, 0, tiled=True)  7.7 us
    unnamed x22, local copies, waits for them, and re-layouts  6.46 us
    all_to_all x1, waiting for transfers between devices, body(): recv_b = move(pay)  5.35 us
    all_to_all x1, starting transfers between devices, body(): recv_b = move(pay)  3.35 us
  transfers between devices with their start and end apart: 6, of which 6 were waited for; matrix products, arithmetic and copies ran while one was open for 0% of the time, Pallas kernels for 5%

commit v1 on v0

--- a/solution.py
+++ b/solution.py
@@ -35,7 +35,7 @@
     return jnp.sum(jnp.where(iota((k, k), 0) == iota((k, k), 1), spread, 0.0), axis=1, keepdims=True)
 
 
-def run(kernel, name, outs, *args, scratch=(), flops=20_000_000):
+def run(kernel, name, outs, *args, scratch=(), flops=20_000_000, vmem=24):
     whole = pl.BlockSpec(memory_space=pltpu.VMEM)
     return pl.pallas_call(
         kernel,
@@ -44,7 +44,7 @@
         in_specs=[whole] * len(args),
         out_specs=[whole] * len(outs),
         scratch_shapes=list(scratch),
-        compiler_params=pltpu.CompilerParams(vmem_limit_bytes=24 * 1024 * 1024),
+        compiler_params=pltpu.CompilerParams(vmem_limit_bytes=vmem * 1024 * 1024),
         cost_estimate=pl.CostEstimate(flops=flops, bytes_accessed=2_000_000, transcendentals=0),
     )(*args)
 
@@ -397,7 +397,7 @@
     cb[...] = bias[:, 2 * hid :]
 
 
-def body(
+def spread_body(
     readings,
     previous,
     upstream,
@@ -514,6 +514,449 @@
     return state_grad, grad_gw, grad_gb[0], grad_cw, grad_cb[0]
 
 
+def pack_kernel(own, nb, w, rows, readings, previous, tail):
+    degree = nb.shape[0]
+    nh = rows.shape[1]
+    hid = previous.shape[1]
+    fin = readings.shape[1]
+    tail[...] = jnp.zeros_like(tail)
+    tail[:fin, :] = readings[0].astype(F32)
+    high = lax.shift_right_logical(nb[...], 5)
+    tail[fin : fin + degree, :] = high.astype(F32)
+    tail[fin + degree : fin + 2 * degree, :] = (nb[...] - high * 32).astype(F32)
+    tail[fin + 2 * degree : fin + 3 * degree, :] = w[...]
+    at = fin + 3 * degree
+    high = lax.shift_right_logical(rows[...], 5)
+    tail[at : at + 1, :nh] = high.astype(F32)
+    tail[at + 1 : at + 2, :nh] = (rows[...] - high * 32).astype(F32)
+    own[:hid, :] = previous[0]
+    own[hid:, :] = tail[...].astype(BF16)
+
+
+def pack_entry(nb, w, rows, readings, previous, own, tail):
+    pack_kernel(own, nb, w, rows, readings, previous, tail)
+
+
+def exchange(first, second, e, sx, pay):
+    n = e.shape[2]
+    count = first[0].shape[0]
+    bound = sum(nt(first[p], sx[p]) for p in range(len(first)))
+    halo = sum(nt(second[p], e[p, n:, :]) for p in range(len(second)))
+    pay[:count, :] = bound.astype(BF16)
+    pay[count:, :] = halo.astype(BF16)
+
+
+def merged(mine, got):
+    half = mine.shape[1] // 2
+    value = jnp.where(iota(mine.shape, 1) < half, mine[...].astype(F32), got[...].astype(F32)).astype(BF16)
+    count = mine.shape[0] // 2
+    return value[:count, :], value[count:, :]
+
+
+def build_kernel(cap, hid, fin, degree, parts, *refs):
+    blocks_in, (e, sx, b, pay, blocks) = refs[:parts], refs[parts:]
+    n = e.shape[2]
+    slots = sx.shape[1]
+    half = slots // 2
+    nh = 2 * parts * cap
+    me = lax.axis_index("dom")
+    z = lax.shift_right_logical(me, 1)
+    core = me - 2 * z
+    for k in range(parts):
+        blocks[lax.bitwise_xor(z, jnp.int32(k))] = blocks_in[k][...]
+    lane = iota((slots, n), 1)
+    slot = iota((slots, 1), 0)
+    rel = lax.div(slot, jnp.int32(half))
+    rest = slot - rel * half
+    dest = lax.div(rest, jnp.int32(parts * cap))
+    rest = rest - dest * (parts * cap)
+    source = lax.div(rest, jnp.int32(cap))
+    t = rest - source * cap
+    other = lax.bitwise_xor(rel, core)
+    spot = (dest * 2 + other) * cap + t
+    width = -(-nh // LANES) * LANES
+    step = parts * cap
+    row = iota((32, n), 0).astype(F32)
+    for p in range(parts):
+        tail = blocks[p, hid:, :].astype(F32)
+        high, low = tail[fin : fin + degree], tail[fin + degree : fin + 2 * degree]
+        w = tail[fin + 2 * degree : fin + 3 * degree]
+        at = fin + 3 * degree
+        sent = tail[at : at + 1] * 32.0 + tail[at + 1 : at + 2]
+        low_is = [jnp.where(low[d : d + 1] == row, 1.0, 0.0).astype(BF16) for d in range(degree)]
+        for chunk in range(n // 32):
+            total = None
+            for d in range(degree):
+                term = low_is[d] * jnp.where(high[d : d + 1] == float(chunk), w[d : d + 1], 0.0).astype(BF16)
+                total = term if total is None else total + term
+            e[p, chunk * 32 : (chunk + 1) * 32, :] = total
+        names = high * 32.0 + low
+        e[p, n:, :] = jnp.zeros((slots, n), BF16)
+        line = iota((step, n), 0)
+        src = lax.div(line, jnp.int32(cap))
+        for r in range(2):
+            node = (n + (src * 2 + lax.bitwise_xor(jnp.int32(r), core)) * cap + line - src * cap).astype(F32)
+            total = jnp.zeros((step, n), F32)
+            for d in range(degree):
+                total = total + jnp.where(names[d : d + 1] == node, w[d : d + 1], 0.0)
+            start = n + r * half + p * step
+            e[p, start : start + step, :] = total.astype(BF16)
+        named = jnp.where(iota((slots, width), 1) == spot, sent[:, :width], 0.0)
+        target = jnp.sum(named, axis=1, keepdims=True).astype(jnp.int32)
+        target = jnp.where(source == p, target, -1)
+        sx[p] = jnp.where(lane == target, 1.0, 0.0).astype(BF16)
+        b[p, :hid, :] = blocks[p, :hid, :]
+        line = iota(tail.shape, 0)
+        b[p, hid:, :] = jnp.where(line < fin, tail, jnp.where(line == fin, 1.0, 0.0)).astype(BF16)
+    base = [b[p] for p in range(parts)]
+    exchange(base, base, e, sx, pay)
+
+
+def order_kernel(hid, fin, orders, block, gw, cw, own, gw_o, cw_o):
+    order = order_matrix((cw.shape[1], orders * block), hid + fin, hid, fin, block)
+    gw_o[...] = tn(gw[...], order).astype(BF16)
+    cw_o[...] = nn(cw[...], order).astype(BF16)
+
+
+def local_kernel(e, x1, x2, l1, l2):
+    n = e.shape[2]
+    for p in range(e.shape[0]):
+        l1[p] = nn(x1[p], e[p, :n, :])
+        l2[p] = nt(x2[p], e[p, :n, :])
+
+
+def chip_a_kernel(one, mine, got, e, sx, l1, l2, f1, r1, ro, ri, pay):
+    n = e.shape[2]
+    top, low = merged(mine, got)
+    firsts, seconds = [], []
+    for p in range(e.shape[0]):
+        pulled = l1[p] + nn(top, e[p, n:, :])
+        pushed = l2[p] + nn(low, sx[p])
+        inv_o = 1.0 / pushed[one : one + 1, :]
+        inv_i = 1.0 / pulled[one : one + 1, :]
+        ro[p] = inv_o
+        ri[p] = inv_i
+        out = (pushed * inv_o).astype(BF16)
+        into = (pulled * inv_i).astype(BF16)
+        f1[p] = out
+        r1[p] = into
+        firsts.append(into)
+        seconds.append(out)
+    exchange(firsts, seconds, e, sx, pay)
+
+
+def chip_b_kernel(mine, got, e, sx, b, f1, r1, l1, l2, ro, ri, gw, gb, states, reset, update, y, pay):
+    n = e.shape[2]
+    hid = y.shape[1]
+    chans = b.shape[1]
+    top, low = merged(mine, got)
+    bias = column(gb[...])
+    fields = []
+    for p in range(e.shape[0]):
+        base = b[p].astype(F32)
+        r2 = 2.0 * (l1[p] + nn(top, e[p, n:, :])) * ri[p] - base
+        f2 = 2.0 * (l2[p] + nn(low, sx[p])) * ro[p] - base
+        states[p, :chans, :] = b[p]
+        states[p, chans : 2 * chans, :] = f1[p]
+        states[p, 2 * chans : 3 * chans, :] = f2.astype(BF16)
+        states[p, 3 * chans : 4 * chans, :] = r1[p]
+        states[p, 4 * chans :, :] = r2.astype(BF16)
+        gates = jax.nn.sigmoid(nn(gw[...], states[p]) + bias)
+        reset[p] = gates[:hid]
+        update[p] = gates[hid:]
+        now = (gates[:hid] * base[:hid]).astype(BF16)
+        y[p] = now
+        fields.append(now)
+    exchange(fields, fields, e, sx, pay)
+
+
+def chip_c1_kernel(mine, got, e, sx, l1, l2, ro, ri, f1, r1, pay):
+    n = e.shape[2]
+    top, low = merged(mine, got)
+    firsts, seconds = [], []
+    for p in range(e.shape[0]):
+        into = ((l1[p] + nn(top, e[p, n:, :])) * ri[p]).astype(BF16)
+        out = ((l2[p] + nn(low, sx[p])) * ro[p]).astype(BF16)
+        f1[p] = out
+        r1[p] = into
+        firsts.append(into)
+        seconds.append(out)
+    exchange(firsts, seconds, e, sx, pay)
+
+
+def split_back(back, hid, inv_o, inv_i, y1, y2, g1, g3):
+    parts = [back[m * hid : (m + 1) * hid, :].astype(BF16) for m in range(5)]
+    y1[...] = (parts[2].astype(F32) * inv_o).astype(BF16)
+    y2[...] = (parts[4].astype(F32) * inv_i).astype(BF16)
+    g1[...] = parts[1]
+    g3[...] = parts[3]
+    return parts[0].astype(F32) - parts[2].astype(F32) - parts[4].astype(F32)
+
+
+def chip_c2_kernel(orders, parts, *refs):
+    ups, refs = refs[:parts], refs[parts:]
+    mine, got, e, sx, y, f1, r1, l1, l2, ro, ri, states, cw, cb, update = refs[:15]
+    mixed, cand_grad, gate_update, y1, y2, g1, g3, upstream, direct, pay = refs[15:]
+    n = e.shape[2]
+    hid = y.shape[1]
+    block = states.shape[1] // orders
+    z = lax.shift_right_logical(lax.axis_index("dom"), 1)
+    for k in range(parts):
+        upstream[lax.bitwise_xor(z, jnp.int32(k))] = ups[k][0]
+    top, low = merged(mine, got)
+    bias = column(cb[...])
+    hidden = hidden_weights(cw[...], hid, block, orders)
+    for p in range(e.shape[0]):
+        base = y[p].astype(F32)
+        r2 = 2.0 * (l1[p] + nn(top, e[p, n:, :])) * ri[p] - base
+        f2 = 2.0 * (l2[p] + nn(low, sx[p])) * ro[p] - base
+        for m, value in enumerate((y[p], f1[p], f2, r1[p], r2)):
+            mixed[p, m * block : m * block + hid, :] = value.astype(BF16)
+            mixed[p, m * block + hid : (m + 1) * block, :] = states[p, m * block + hid : (m + 1) * block, :]
+        cand = jnp.tanh(nn(cw[...], mixed[p]) + bias)
+        up = upstream[p].astype(F32)
+        gate = update[p]
+        grad = (up * (1.0 - gate) * (1.0 - cand * cand)).astype(BF16)
+        cand_grad[p] = grad
+        gate_update[p] = (up * (states[p, :hid, :].astype(F32) - cand) * gate * (1.0 - gate)).astype(BF16)
+        direct[p] = split_back(tn(hidden, grad), hid, ro[p], ri[p], y1.at[p], y2.at[p], g1.at[p], g3.at[p])
+    parts = range(e.shape[0])
+    exchange([y1[p] for p in parts], [y2[p] for p in parts], e, sx, pay)
+
+
+def chip_part(grads, features, orders, chans, hid, fin):
+    block = features.shape[1] // orders
+    width = -(-(orders * chans + 1) // LANES) * LANES
+    shape = (width, orders * block)
+    k = iota(shape, 0)
+    col = iota(shape, 1)
+    m = lax.div(col, jnp.int32(block))
+    c = col - m * block
+    source = jnp.where(c < hid, m * chans + fin + c, jnp.where(c < hid + fin, m * chans + c - hid, -1))
+    source = jnp.where(col == hid + fin, orders * chans, source)
+    order = jnp.where(k == source, 1.0, 0.0).astype(BF16)
+    total = sum(nt(grads[p], features[p]) for p in range(grads.shape[0]))
+    return nt(total.astype(BF16), order)
+
+
+def local_d_kernel(orders, fin, e, y1, y2, cand_grad, mixed, gate_update, states, l1, l2, part):
+    hid = y1.shape[1]
+    local_kernel(e, y1, y2, l1, l2)
+    part[:hid, :] = chip_part(gate_update, states, orders, hid + fin, hid, fin).astype(BF16)
+    part[hid:, :] = chip_part(cand_grad, mixed, orders, hid + fin, hid, fin).astype(BF16)
+
+
+def chip_e1_kernel(after, *refs):
+    chip_d1_kernel(*refs)
+
+
+def chip_d1_kernel(mine, got, e, sx, l1, l2, g1, g3, ro, ri, z1, z2, pay):
+    n = e.shape[2]
+    top, low = merged(mine, got)
+    firsts, seconds = [], []
+    for p in range(e.shape[0]):
+        one = ((g1[p].astype(F32) + 2.0 * (l1[p] + nn(top, e[p, n:, :]))) * ro[p]).astype(BF16)
+        two = ((g3[p].astype(F32) + 2.0 * (l2[p] + nn(low, sx[p]))) * ri[p]).astype(BF16)
+        z1[p] = one
+        z2[p] = two
+        firsts.append(one)
+        seconds.append(two)
+    exchange(firsts, seconds, e, sx, pay)
+
+
+def local_d2_kernel(e, z1, z2, direct, base):
+    n = e.shape[2]
+    for p in range(e.shape[0]):
+        base[p] = direct[p] + nn(z1[p], e[p, :n, :]) + nt(z2[p], e[p, :n, :])
+
+
+def chip_d2_kernel(orders, mine, got, e, sx, base, ro, ri, states, gw, upstream, reset, update, gate_update,
+                   gate_reset, y1, y2, g1, g3, direct, pay):
+    n = e.shape[2]
+    hid = base.shape[1]
+    block = states.shape[1] // orders
+    top, low = merged(mine, got)
+    hidden = hidden_weights(gw[...], hid, block, orders)
+    for p in range(e.shape[0]):
+        scaled_grad = base[p] + nn(top, e[p, n:, :]) + nn(low, sx[p])
+        gate = reset[p]
+        grad = (scaled_grad * states[p, :hid, :].astype(F32) * gate * (1.0 - gate)).astype(BF16)
+        gate_reset[p] = grad
+        back = tn(hidden, jnp.concatenate([grad, gate_update[p]], axis=0))
+        rest = split_back(back, hid, ro[p], ri[p], y1.at[p], y2.at[p], g1.at[p], g3.at[p])
+        direct[p] = rest + upstream[p].astype(F32) * update[p] + scaled_grad * gate
+    parts = range(e.shape[0])
+    exchange([y1[p] for p in parts], [y2[p] for p in parts], e, sx, pay)
+
+
+def grads_kernel(orders, fin, gate_reset, states, part, keep, give, flat):
+    hid = gate_reset.shape[1]
+    half = keep.shape[0]
+    core = lax.rem(lax.axis_index("dom"), 2)
+    flat[:hid, :] = chip_part(gate_reset, states, orders, hid + fin, hid, fin)
+    flat[hid:, :] = part[...].astype(F32)
+    keep[...] = flat[pl.ds(pl.multiple_of(core * half, 8), half), :].astype(BF16)
+    give[...] = flat[pl.ds(pl.multiple_of((1 - core) * half, 8), half), :].astype(BF16)
+
+
+def local_e_kernel(e, z1, z2, direct, base):
+    n = e.shape[2]
+    z = lax.shift_right_logical(lax.axis_index("dom"), 1)
+    a = e[z, :n, :]
+    base[...] = direct[z] + nn(z1[z], a) + nt(z2[z], a)
+
+
+def chip_e_kernel(mine, got, e, sx, base, out):
+    n = e.shape[2]
+    z = lax.shift_right_logical(lax.axis_index("dom"), 1)
+    top, low = merged(mine, got)
+    out[0] = (base[...] + nn(top, e[z, n:, :]) + nn(low, sx[z])).astype(BF16)
+
+
+def sum_kernel(*refs):
+    values = [ref[...].astype(F32) for ref in refs[:-1]]
+    while len(values) > 1:
+        values = [values[k] + values[k + 1] for k in range(0, len(values), 2)]
+    refs[-1][...] = values[0].astype(BF16)
+
+
+def end_kernel(factor, mine, got, gw, gb, cw, cb, flat):
+    half = mine.shape[0]
+    core = lax.rem(lax.axis_index("dom"), 2)
+    flat[pl.ds(pl.multiple_of(core * half, 8), half), :] = mine[...].astype(F32)
+    flat[pl.ds(pl.multiple_of((1 - core) * half, 8), half), :] = got[...].astype(F32)
+    features, rows = gw.shape
+    same = jnp.where(iota((features, flat.shape[1]), 0) == iota((features, flat.shape[1]), 1), 1.0, 0.0).astype(BF16)
+    gw[...] = nt(same, flat[:rows, :].astype(BF16)) * factor
+    cw[...] = flat[rows:, :features] * factor
+    pick = jnp.where(iota((8, flat.shape[1]), 1) == features, 1.0, 0.0).astype(BF16)
+    bias = nt(pick, flat[...].astype(BF16))[:1] * factor
+    gb[...] = bias[:, :rows]
+    cb[...] = bias[:, rows:]
+
+
+def chip_body(
+    readings,
+    previous,
+    upstream,
+    gate_weight,
+    gate_bias,
+    cand_weight,
+    cand_bias,
+    neighbours,
+    edge_weight,
+    send_rows,
+):
+    fin, hid = readings.shape[1], previous.shape[1]
+    chans = fin + hid
+    orders = gate_weight.shape[1] // chans
+    degree = neighbours.shape[0]
+    n = readings.shape[2]
+    nd = lax.axis_size("dom")
+    snaps = lax.axis_size("snap")
+    parts = nd // 2
+    cap = send_rows.shape[1] // nd
+    block = hid + 16 * (-(-(fin + 3 * degree + 2) // 16))
+    slots = 2 * parts * parts * cap
+
+    def swap(array, k, axis="dom", size=nd):
+        return lax.ppermute(array, axis, [(i, i ^ k) for i in range(size)])
+
+    (own,) = run(
+        pack_entry, "pack", [((block, n), BF16)], neighbours, edge_weight, send_rows, readings, previous,
+        scratch=[pltpu.VMEM((block - hid, n), F32)], vmem=56,
+    )
+    blocks = [own] + [swap(own, 2 * k) for k in range(1, parts)]
+    ups = [upstream] + [swap(upstream, 2 * k) for k in range(1, parts)]
+    gw, cw = run(
+        functools.partial(order_kernel, hid, fin, orders, block), "order",
+        [((2 * hid, orders * block), BF16), ((hid, orders * block), BF16)], gate_weight.T, cand_weight, own,
+    )
+    wide, wide16, wide_pay = ((parts, block, n), F32), ((parts, block, n), BF16), ((2 * block, slots), BF16)
+    field, field16, pay_kind = ((parts, hid, n), F32), ((parts, hid, n), BF16), ((2 * hid, slots), BF16)
+    line = ((parts, 1, n), F32)
+    e, sx, b, pay = run(
+        functools.partial(build_kernel, cap, hid, fin, degree, parts), "build",
+        [((parts, n + slots, n), BF16), ((parts, slots, n), BF16), wide16, wide_pay],
+        *blocks, scratch=[pltpu.VMEM((parts, block, n), BF16)],
+    )
+    got = swap(pay, 1)
+    l1, l2 = run(local_kernel, "local_a", [wide, wide], e, b, b)
+    f1, r1, ro, ri, pay = run(
+        functools.partial(chip_a_kernel, hid + fin), "chip_a", [wide16, wide16, line, line, wide_pay],
+        pay, got, e, sx, l1, l2,
+    )
+    got = swap(pay, 1)
+    l1, l2 = run(local_kernel, "local_b", [wide, wide], e, r1, f1)
+    states, reset, update, y, pay = run(
+        chip_b_kernel, "chip_b", [((parts, orders * block, n), BF16), field, field, field16, pay_kind],
+        pay, got, e, sx, b, f1, r1, l1, l2, ro, ri, gw, gate_bias[None, :],
+    )
+    got = swap(pay, 1)
+    l1, l2 = run(local_kernel, "local_c1", [field, field], e, y, y)
+    f1, r1, pay = run(
+        chip_c1_kernel, "chip_c1", [field16, field16, pay_kind], pay, got, e, sx, l1, l2, ro, ri
+    )
+    got = swap(pay, 1)
+    l1, l2 = run(local_kernel, "local_c2", [field, field], e, r1, f1)
+    mixed, cand_grad, gate_update, y1, y2, g1, g3, up, direct, pay = run(
+        functools.partial(chip_c2_kernel, orders, parts), "chip_c2",
+        [((parts, orders * block, n), BF16)] + [field16] * 7 + [field, pay_kind],
+        *ups, pay, got, e, sx, y, f1, r1, l1, l2, ro, ri, states, cw, cand_bias[None, :], update,
+    )
+    got = swap(pay, 1)
+    width = -(-(orders * chans + 1) // LANES) * LANES
+    l1, l2, part = run(
+        functools.partial(local_d_kernel, orders, fin), "local_d1", [field, field, ((2 * hid, width), BF16)],
+        e, y1, y2, cand_grad, mixed, gate_update, states,
+    )
+    z1, z2, pay = run(
+        chip_d1_kernel, "chip_d1", [field16, field16, pay_kind], pay, got, e, sx, l1, l2, g1, g3, ro, ri
+    )
+    got = swap(pay, 1)
+    (base,) = run(local_d2_kernel, "local_d2", [field], e, z1, z2, direct)
+    gate_reset, y1, y2, g1, g3, direct, pay = run(
+        functools.partial(chip_d2_kernel, orders), "chip_d2", [field16] * 5 + [field, pay_kind],
+        pay, got, e, sx, base, ro, ri, states, gw, up, reset, update, gate_update,
+    )
+    got = swap(pay, 1)
+    half = ((3 * hid // 2, width), BF16)
+    keep, give = run(
+        functools.partial(grads_kernel, orders, fin), "grads", [half, half], gate_reset, states, part,
+        scratch=[pltpu.VMEM((3 * hid, width), F32)],
+    )
+    (mine,) = run(sum_kernel, "sum_core", [half], keep, swap(give, 1))
+    every = [mine] + [swap(mine, k, "snap", snaps) for k in range(1, snaps)]
+    l1, l2 = run(local_kernel, "local_e1", [field, field], e, y1, y2)
+    z1, z2, pay = run(
+        chip_e1_kernel, "chip_e1", [field16, field16, pay_kind], mine, pay, got, e, sx, l1, l2, g1, g3, ro, ri
+    )
+    got = swap(pay, 1)
+    (base,) = run(local_e_kernel, "local_e2", [((hid, n), F32)], e, z1, z2, direct)
+    (state_grad,) = run(chip_e_kernel, "chip_e2", [((1, hid, n), BF16)], pay, got, e, sx, base)
+    (mine,) = run(sum_kernel, "sum_snap", [half], *every)
+    factor = 1.0 / math.sqrt(readings.shape[0] * snaps * n * nd)
+    feats = orders * chans
+    grad_gw, grad_gb, grad_cw, grad_cb = run(
+        functools.partial(end_kernel, factor), "end",
+        [((feats, 2 * hid), F32), ((1, 2 * hid), F32), ((hid, feats), F32), ((1, hid), F32)],
+        mine, swap(mine, 1), scratch=[pltpu.VMEM((3 * hid, width), F32)],
+    )
+    return state_grad, grad_gw.T, grad_gb[0], grad_cw, grad_cb[0]
+
+
+def body(*args):
+    neighbours, send_rows = args[7], args[9]
+    n = neighbours.shape[1]
+    nd, snaps = lax.axis_size("dom"), lax.axis_size("snap")
+    parts = nd // 2
+    slots = 2 * parts * parts * (send_rows.shape[1] // nd)
+    powers = nd & (nd - 1) == 0 and snaps & (snaps - 1) == 0 and nd > 1
+    if powers and parts * (n + slots) * n * 2 <= 4 << 20:
+        return chip_body(*args)
+    return spread_body(*args)
+
+
 def solution(mesh):
     in_specs = (
         P("snap", None, "dom"),

time: 89.6 us -> 56.4 us (0.63)
  waiting for transfers between devices: 33.4 us -> 14.4 us
  blocking collectives: 11.8 us -> 0 us
  Pallas kernels: 13.8 us -> 24.1 us
  starting transfers between devices: 22.3 us -> 15.9 us
  local copies, waits for them, and re-layouts: 6.46 us -> 0.92 us
    all_to_all x6 -> x0, waiting for transfers between devices: 33.4 us -> none  [the longest x4 20.3 us: body(): recv = move(pay)]
    all_to_all x6 -> x0, starting transfers between devices: 22.3 us -> none  [the longest x4 16.4 us: body(): recv = move(pay)]
    ppermute x0 -> x19, starting transfers between devices: none -> 15.9 us  [swap(): return lax.ppermute(array, axis, [(i, i ^ k) for i in range(size)])]
    ppermute x0 -> x19, waiting for transfers between devices: none -> 14.4 us  [swap(): return lax.ppermute(array, axis, [(i, i ^ k) for i in range(size)])]
    all_to_all x1 -> x0, blocking collectives: 11.8 us -> none  [body(): grads = lax.all_to_all(grads, both, 0, 0, tiled=True)]
    pallas_call x13 -> x23, Pallas kernels: 13.8 us -> 24.1 us  [run(): pl.pallas_call(kernel, name=name, out_shape=[jax.ShapeDtypeStruct(shape,...]
    unnamed x22 -> x14, local copies, waits for them, and re-layouts: 6.46 us -> 0.92 us
  transfers between devices with their start and end apart: 6 -> 19, of which waited for: 6 -> 9; matrix products, arithmetic and copies ran while one was open for 0% -> 0% of each run, Pallas kernels for 5% -> 21%
where the time goes in v1:
time: 56.4 us; the launch traced here: 56.2 us
  Pallas kernels  24.1 us (43%)
  starting transfers between devices  15.9 us (28%)
  waiting for transfers between devices  14.4 us (26%)
  local copies, waits for them, and re-layouts  0.92 us (2%)
  between operations  0.89 us (2%)
    pallas_call x23, Pallas kernels, run(): pl.pallas_call(kernel, name=name, out_shape=[jax.ShapeDtypeStruct(shape,...  24.1 us
    ppermute x19, starting transfers between devices, swap(): return lax.ppermute(array, axis, [(i, i ^ k) for i in range(size)])  15.9 us
    ppermute x19, waiting for transfers between devices, swap(): return lax.ppermute(array, axis, [(i, i ^ k) for i in range(size)])  14.4 us
  transfers between devices with their start and end apart: 19, of which 9 were waited for; matrix products, arithmetic and copies ran while one was open for 0% of the time, Pallas kernels for 21%

profile of v1, /device:TPU:0, one launch (start us, length us, event | category | flops | bytes accessed | tf_op | source)
XLA Modules:
  0.0 56.2 jit_solution(472900364389525592)
XLA Ops:
  0.6 1.6 %pack.1.refs_0_.own = bf16[80,512]{1,0:T(8,128)(2,1)} custom-call(s32[4,512]{1,0:T(4,128)} %nb.1, f32[4,512]{1,0:T(4,128)} %w.1, s32[1,32]{1,0:T(1,128)} %rows.1, bf16[1,2,512]{2,1,0:T(2,128)(2,1)} %readings.1, bf16[1,64,512]{2,1,0:T(8,128)(2,1)} %previous.1), custom_call_target="tpu_custom_call" | custom-call | flops 20000000 | bytes 2000000 | tf_op jit(solution)/shard_map/pack/pallas_call | solution.py:40
  2.2 5.0 %collective-permute-start.5 = (bf16[80,512]{1,0:T(8,128)(2,1)}, bf16[80,512]{1,0:T(8,128)(2,1)S(1)}, u32[]{:S(2)}, u32[]{:S(2)}) collective-permute-start(bf16[80,512]{1,0:T(8,128)(2,1)} %pack.1.refs_0_.own), channel_id=1, source_target_pairs={{0,6},{1,7},{2,4},{3,5},{4,2},{5,3},{6,0},{7,1},{8,14},{9,15},{10,... | collective-permute-start | bytes 245768 | tf_op jit(solution)/shard_map/ppermute | solution.py:863
  7.2 0.6 %collective-permute-start.3 = (bf16[80,512]{1,0:T(8,128)(2,1)}, bf16[80,512]{1,0:T(8,128)(2,1)S(1)}, u32[]{:S(2)}, u32[]{:S(2)}) collective-permute-start(bf16[80,512]{1,0:T(8,128)(2,1)} %pack.1.refs_0_.own), channel_id=1, source_target_pairs={{0,2},{1,3},{2,0},{3,1},{4,6},{5,7},{6,4},{7,5},{8,10},{9,11},{10,... | collective-permute-start | bytes 245768 | tf_op jit(solution)/shard_map/ppermute | solution.py:863
  7.8 2.7 %collective-permute-done.5.refs_3_ = bf16[80,512]{1,0:T(8,128)(2,1)S(1)} collective-permute-done((bf16[80,512]{1,0:T(8,128)(2,1)}, bf16[80,512]{1,0:T(8,128)(2,1)S(1)}, u32[]{:S(2)}, u32[]{:S(2)}) %collective-permute-start.5) | collective-permute-done | bytes 81952 | tf_op jit(solution)/shard_map/ppermute | solution.py:863
  10.5 3.8 %collective-permute-done.4.refs_2_ = bf16[80,512]{1,0:T(8,128)(2,1)S(1)} collective-permute-done((bf16[80,512]{1,0:T(8,128)(2,1)}, bf16[80,512]{1,0:T(8,128)(2,1)S(1)}, u32[]{:S(2)}, u32[]{:S(2)}) %collective-permute-start.4) | collective-permute-done | bytes 81952 | tf_op jit(solution)/shard_map/ppermute | solution.py:863
  14.3 0.9 %copy-done = bf16[80,512]{1,0:T(8,128)(2,1)S(1)} copy-done((bf16[80,512]{1,0:T(8,128)(2,1)S(1)}, bf16[80,512]{1,0:T(8,128)(2,1)}, u32[]{:S(2)}) %copy-start) | copy-done | bytes 81944
  15.2 1.6 %build.1 = (bf16[4,640,512]{2,1,0:T(8,128)(2,1)S(1)}, bf16[4,128,512]{2,1,0:T(8,128)(2,1)S(1)}, bf16[4,80,512]{2,1,0:T(8,128)(2,1)S(1)}, bf16[160,128]{1,0:T(8,128)(2,1)S(1)}) custom-call(bf16[80,512]{1,0:T(8,128)(2,1)S(1)} %copy-done, bf16[80,512]{1,0:T(8,128)(2,1)S(1)} %collective-permute-done.3.refs_1_, ...), custom_call_target="tpu_custom_call" | custom-call | flops 20000000 | bytes 2000000 | tf_op jit(solution)/shard_map/build/pallas_call | solution.py:40
  16.8 0.1 collective-permute-start.6
  16.9 1.1 %local_a.1 = (f32[4,80,512]{2,1,0:T(8,128)S(1)}, f32[4,80,512]{2,1,0:T(8,128)S(1)}) custom-call(bf16[4,640,512]{2,1,0:T(8,128)(2,1)S(1)} %get-tuple-element.67.e.refs_6_.refs_2_, bf16[4,80,512]{2,1,0:T(8,128)(2,1)S(1)} %get-tuple-element.69.x1.x2.b, bf16[4,80,512]{2,1,0:T(8,128)(2,1)S(1)} %get-tuple-element.69.x1.x2.b), custom_call_target="tpu_custom_call" | custom-call | flops 20000000 | bytes 2000000 | tf_op jit(solution)/shard_map/local_a/pallas_call | solution.py:40
  18.0 0.1 collective-permute-done.6.got
  18.1 0.6 %chip_a.1 = (bf16[4,80,512]{2,1,0:T(8,128)(2,1)S(1)}, bf16[4,80,512]{2,1,0:T(8,128)(2,1)S(1)}, f32[4,1,512]{2,1,0:T(1,128)S(1)}, f32[4,1,512]{2,1,0:T(1,128)S(1)}, bf16[160,128]{1,0:T(8,128)(2,1)S(1)}) custom-call(bf16[160,128]{1,0:T(8,128)(2,1)S(1)} %get-tuple-element.66.mine, bf16[160,128]{1,0:T(8,128)(2,1)S(1)} %collective-permute-done.6.got, ...), custom_call_target="tpu_custom_call" | custom-call | flops 20000000 | bytes 2000000 | tf_op jit(solution)/shard_map/chip_a/pallas_call | solution.py:40
  18.7 0.5 collective-permute-start.7
  19.2 0.3 order.1
  19.6 1.1 %local_b.1 = (f32[4,80,512]{2,1,0:T(8,128)S(1)}, f32[4,80,512]{2,1,0:T(8,128)S(1)}) custom-call(bf16[4,640,512]{2,1,0:T(8,128)(2,1)S(1)} %get-tuple-element.67.e.refs_6_.refs_2_, bf16[4,80,512]{2,1,0:T(8,128)(2,1)S(1)} %get-tuple-element.74.x1.r1, bf16[4,80,512]{2,1,0:T(8,128)(2,1)S(1)} %get-tuple-element.73.x2.f1), custom_call_target="tpu_custom_call" | custom-call | flops 20000000 | bytes 2000000 | tf_op jit(solution)/shard_map/local_b/pallas_call | solution.py:40
  20.7 1.6 %chip_b.1 = (bf16[4,400,512]{2,1,0:T(8,128)(2,1)S(1)}, f32[4,64,512]{2,1,0:T(8,128)S(1)}, f32[4,64,512]{2,1,0:T(8,128)S(1)}, bf16[4,64,512]{2,1,0:T(8,128)(2,1)S(1)}, bf16[128,128]{1,0:T(8,128)(2,1)S(1)}) custom-call(bf16[160,128]{1,0:T(8,128)(2,1)S(1)} %get-tuple-element.72.mine, bf16[160,128]{1,0:T(8,128)(2,1)S(1)} %collective-permute-done.7.got, ...), custom_call_target="tpu_custom_call" | custom-call | flops 20000000 | bytes 2000000 | tf_op jit(solution)/shard_map/chip_b/pallas_call | solution.py:40
  22.3 0.2 collective-permute-start.8
  22.5 0.9 %collective-permute-start.1 = (bf16[1,64,512]{2,1,0:T(8,128)(2,1)S(1)}, bf16[1,64,512]{2,1,0:T(8,128)(2,1)S(1)}, u32[]{:S(2)}, u32[]{:S(2)}) collective-permute-start(bf16[1,64,512]{2,1,0:T(8,128)(2,1)S(1)} %copy-done.3), channel_id=1, source_target_pairs={{0,4},{1,5},{2,6},{3,7},{4,0},{5,1},{6,2},{7,3},{8,12},{9,13},{10,... | collective-permute-start | bytes 196616 | tf_op jit(solution)/shard_map/ppermute | solution.py:863
  23.4 2.3 %collective-permute-start = (bf16[1,64,512]{2,1,0:T(8,128)(2,1)S(1)}, bf16[1,64,512]{2,1,0:T(8,128)(2,1)S(1)}, u32[]{:S(2)}, u32[]{:S(2)}) collective-permute-start(bf16[1,64,512]{2,1,0:T(8,128)(2,1)S(1)} %copy-done.3), channel_id=1, source_target_pairs={{0,2},{1,3},{2,0},{3,1},{4,6},{5,7},{6,4},{7,5},{8,10},{9,11},{10,... | collective-permute-start | bytes 196616 | tf_op jit(solution)/shard_map/ppermute | solution.py:863
  25.7 1.2 %collective-permute-start.2 = (bf16[1,64,512]{2,1,0:T(8,128)(2,1)S(1)}, bf16[1,64,512]{2,1,0:T(8,128)(2,1)S(1)}, u32[]{:S(2)}, u32[]{:S(2)}) collective-permute-start(bf16[1,64,512]{2,1,0:T(8,128)(2,1)S(1)} %copy-done.3), channel_id=1, source_target_pairs={{0,6},{1,7},{2,4},{3,5},{4,2},{5,3},{6,0},{7,1},{8,14},{9,15},{10,... | collective-permute-start | bytes 196616 | tf_op jit(solution)/shard_map/ppermute | solution.py:863
  26.9 1.1 %local_c1.1 = (f32[4,64,512]{2,1,0:T(8,128)S(1)}, f32[4,64,512]{2,1,0:T(8,128)S(1)}) custom-call(bf16[4,640,512]{2,1,0:T(8,128)(2,1)S(1)} %get-tuple-element.67.e.refs_6_.refs_2_, bf16[4,64,512]{2,1,0:T(8,128)(2,1)S(1)} %get-tuple-element.81.x1.x2.refs_8_, bf16[4,64,512]{2,1,0:T(8,128)(2,1)S(1)} %get-tuple-element.81.x1.x2.refs_8_), custom_call_target="tpu_custom_call" | custom-call | flops 20000000 | bytes 2000000 | tf_op jit(solution)/shard_map/local_c1/pallas_call | solution.py:40
  28.0 0.6 %chip_c1.1 = (bf16[4,64,512]{2,1,0:T(8,128)(2,1)S(1)}, bf16[4,64,512]{2,1,0:T(8,128)(2,1)S(1)}, bf16[128,128]{1,0:T(8,128)(2,1)S(1)}) custom-call(bf16[128,128]{1,0:T(8,128)(2,1)S(1)} %get-tuple-element.80.mine, bf16[128,128]{1,0:T(8,128)(2,1)S(1)} %collective-permute-done.8.got, bf16[4,640,512]{2,1,0:T(8,128)(2,1)S(1)} %get-tuple-element.67.e.refs_6_.refs_2_, ...), custom_call_target="tpu_custom_call" | custom-call | flops 20000000 | bytes 2000000 | tf_op jit(solution)/shard_map/chip_c1/pallas_call | solution.py:40
  28.6 0.1 collective-permute-start.9
  28.7 1.1 %local_c2.1 = (f32[4,64,512]{2,1,0:T(8,128)S(1)}, f32[4,64,512]{2,1,0:T(8,128)S(1)}) custom-call(bf16[4,640,512]{2,1,0:T(8,128)(2,1)S(1)} %get-tuple-element.67.e.refs_6_.refs_2_, bf16[4,64,512]{2,1,0:T(8,128)(2,1)S(1)} %get-tuple-element.86.x1.refs_10_, bf16[4,64,512]{2,1,0:T(8,128)(2,1)S(1)} %get-tuple-element.85.x2.refs_9_), custom_call_target="tpu_custom_call" | custom-call | flops 20000000 | bytes 2000000 | tf_op jit(solution)/shard_map/local_c2/pallas_call | solution.py:40
  29.8 2.0 %collective-permute-done.2.refs_3_ = bf16[1,64,512]{2,1,0:T(8,128)(2,1)S(1)} collective-permute-done((bf16[1,64,512]{2,1,0:T(8,128)(2,1)S(1)}, bf16[1,64,512]{2,1,0:T(8,128)(2,1)S(1)}, u32[]{:S(2)}, u32[]{:S(2)}) %collective-permute-start.2) | collective-permute-done | bytes 65568 | tf_op jit(solution)/shard_map/ppermute | solution.py:863
  31.8 2.4 %chip_c2.1 = (bf16[4,400,512]{2,1,0:T(8,128)(2,1)S(1)}, bf16[4,64,512]{2,1,0:T(8,128)(2,1)S(1)}, bf16[4,64,512]{2,1,0:T(8,128)(2,1)S(1)}, bf16[4,64,512]{2,1,0:T...) custom-call(bf16[1,64,512]{2,1,0:T(8,128)(2,1)S(1)} %copy-done.3, ...), custom_call_target="tpu_custom_call" | custom-call | flops 20000000 | bytes 2000000 | tf_op jit(solution)/shard_map/chip_c2/pallas_call | solution.py:40
  34.3 2.8 %local_d1.1 = (f32[4,64,512]{2,1,0:T(8,128)S(1)}, f32[4,64,512]{2,1,0:T(8,128)S(1)}, bf16[128,384]{1,0:T(8,128)(2,1)S(1)}) custom-call(bf16[4,640,512]{2,1,0:T(8,128)(2,1)S(1)} %get-tuple-element.67.e.refs_6_.refs_2_, bf16[4,64,512]{2,1,0:T(8,128)(2,1)S(1)} %get-tuple-element.93.y1, bf16[4,64,512]{2,1,0:T(8,128)(2,1)S(1)} %get-tuple-element.94.y2, ...), custom_call_target="tpu_custom_call" | custom-call | flops 20000000 | bytes 2000000 | tf_op jit(solution)/shard_map/local_d1/pallas_call | solution.py:40
  37.1 0.6 %chip_d1.1 = (bf16[4,64,512]{2,1,0:T(8,128)(2,1)S(1)}, bf16[4,64,512]{2,1,0:T(8,128)(2,1)S(1)}, bf16[128,128]{1,0:T(8,128)(2,1)S(1)}) custom-call(bf16[128,128]{1,0:T(8,128)(2,1)S(1)} %get-tuple-element.92.mine, bf16[128,128]{1,0:T(8,128)(2,1)S(1)} %collective-permute-done.10.got, bf16[4,640,512]{2,1,0:T(8,128)(2,1)S(1)} %get-tuple-element.67.e.refs_6_.refs_2_, ...), custom_call_target="tpu_custom_call" | custom-call | flops 20000000 | bytes 2000000 | tf_op jit(solution)/shard_map/chip_d1/pallas_call | solution.py:40
  37.7 0.6 collective-permute-start.11
  38.2 1.1 %local_d2.1.base = f32[4,64,512]{2,1,0:T(8,128)S(1)} custom-call(bf16[4,640,512]{2,1,0:T(8,128)(2,1)S(1)} %get-tuple-element.67.e.refs_6_.refs_2_, bf16[4,64,512]{2,1,0:T(8,128)(2,1)S(1)} %get-tuple-element.103.z1, bf16[4,64,512]{2,1,0:T(8,128)(2,1)S(1)} %get-tuple-element.104.z2, f32[4,64,512]{2,1,0:T(8,128)S(1)} %get-tuple-element.105.direct), custom_call_target="tpu_custom_call" | custom-call | flops 20000000 | bytes 2000000 | tf_op jit(solution)/shard_map/local_d2/pallas_call | solution.py:40
  39.4 1.6 %chip_d2.1 = (bf16[4,64,512]{2,1,0:T(8,128)(2,1)S(1)}, bf16[4,64,512]{2,1,0:T(8,128)(2,1)S(1)}, bf16[4,64,512]{2,1,0:T(8,128)(2,1)S(1)}, bf16[4,64,512]{2,1,0:T(...) custom-call(bf16[128,128]{1,0:T(8,128)(2,1)S(1)} %get-tuple-element.102.mi, ...), custom_call_target="tpu_custom_call" | custom-call | flops 20000000 | bytes 2000000 | tf_op jit(solution)/shard_map/chip_d2/pallas_call | solution.py:40
  41.0 1.0 %grads.1 = (bf16[96,384]{1,0:T(8,128)(2,1)S(1)}, bf16[96,384]{1,0:T(8,128)(2,1)S(1)}) custom-call(bf16[4,64,512]{2,1,0:T(8,128)(2,1)S(1)} %get-tuple-element.108.gate_reset, bf16[4,400,512]{2,1,0:T(8,128)(2,1)S(1)} %get-tuple-element.89.refs_15_.states, bf16[128,384]{1,0:T(8,128)(2,1)S(1)} %get-tuple-element.109.part), custom_call_target="tpu_custom_call" | custom-call | flops 20000000 | bytes 2000000 | tf_op jit(solution)/shard_map/grads/pallas_call | solution.py:40
  42.0 0.1 collective-permute-start.12
  42.1 1.2 %collective-permute-done.12.refs_1_ = bf16[96,384]{1,0:T(8,128)(2,1)S(1)} collective-permute-done((bf16[96,384]{1,0:T(8,128)(2,1)S(1)}, bf16[96,384]{1,0:T(8,128)(2,1)S(1)}, u32[]{:S(2)}, u32[]{:S(2)}) %collective-permute-start.12) | collective-permute-done | bytes 73760 | tf_op jit(solution)/shard_map/ppermute | solution.py:863
  43.3 2.5 %collective-permute-start.17 = (bf16[96,384]{1,0:T(8,128)(2,1)S(1)}, bf16[96,384]{1,0:T(8,128)(2,1)S(1)}, u32[]{:S(2)}, u32[]{:S(2)}) collective-permute-start(bf16[96,384]{1,0:T(8,128)(2,1)S(1)} %sum_core.1.after.refs_0_), channel_id=1, source_target_pairs={{0,24},{8,16},{16,8},{24,0},{1,25},{9,17},{17,9},{25,1},{2,26},{10... | collective-permute-start | bytes 221192 | tf_op jit(solution)/shard_map/ppermute | solution.py:863
  45.9 0.5 collective-permute-start.16
  46.4 0.5 collective-permute-start.15
  46.9 1.8 %collective-permute-done.17.refs_3_ = bf16[96,384]{1,0:T(8,128)(2,1)S(1)} collective-permute-done((bf16[96,384]{1,0:T(8,128)(2,1)S(1)}, bf16[96,384]{1,0:T(8,128)(2,1)S(1)}, u32[]{:S(2)}, u32[]{:S(2)}) %collective-permute-start.17) | collective-permute-done | bytes 73760 | tf_op jit(solution)/shard_map/ppermute | solution.py:863
  48.7 1.5 %collective-permute-done.16.refs_2_ = bf16[96,384]{1,0:T(8,128)(2,1)S(1)} collective-permute-done((bf16[96,384]{1,0:T(8,128)(2,1)S(1)}, bf16[96,384]{1,0:T(8,128)(2,1)S(1)}, u32[]{:S(2)}, u32[]{:S(2)}) %collective-permute-start.16) | collective-permute-done | bytes 73760 | tf_op jit(solution)/shard_map/ppermute | solution.py:863
  50.2 0.5 collective-permute-done.15.refs_1_
  50.8 0.1 collective-permute-start.18
  50.8 0.5 collective-permute-start.13
  51.3 1.1 %local_e1.1 = (f32[4,64,512]{2,1,0:T(8,128)S(1)}, f32[4,64,512]{2,1,0:T(8,128)S(1)}) custom-call(bf16[4,640,512]{2,1,0:T(8,128)(2,1)S(1)} %get-tuple-element.67.e.refs_6_.refs_2_, bf16[4,64,512]{2,1,0:T(8,128)(2,1)S(1)} %get-tuple-element.113.x1, bf16[4,64,512]{2,1,0:T(8,128)(2,1)S(1)} %get-tuple-element.114.x2), custom_call_target="tpu_custom_call" | custom-call | flops 20000000 | bytes 2000000 | tf_op jit(solution)/shard_map/local_e1/pallas_call | solution.py:40
  52.4 0.6 %chip_e1.1 = (bf16[4,64,512]{2,1,0:T(8,128)(2,1)S(1)}, bf16[4,64,512]{2,1,0:T(8,128)(2,1)S(1)}, bf16[128,128]{1,0:T(8,128)(2,1)S(1)}) custom-call(bf16[96,384]{1,0:T(8,128)(2,1)S(1)} %sum_core.1.after.refs_0_, bf16[128,128]{1,0:T(8,128)(2,1)S(1)} %get-tuple-element.112.refs_0_, bf16[128,128]{1,0:T(8,128)(2,1)S(1)} %collective-permute-done.13.refs_1_, ...), custom_call_target="tpu_custom_call" | custom-call | flops 20000000 | bytes 2000000 | tf_op jit(solution)/shard_map/chip_e1/pallas_call | solution.py:40
  53.1 0.2 collective-permute-start.14
  53.2 0.4 local_e2.1.base
  53.6 0.8 %collective-permute-done.14.got = bf16[128,128]{1,0:T(8,128)(2,1)S(1)} collective-permute-done((bf16[128,128]{1,0:T(8,128)(2,1)S(1)}, bf16[128,128]{1,0:T(8,128)(2,1)S(1)}, u32[]{:S(2)}, u32[]{:S(2)}) %collective-permute-start.14) | collective-permute-done | bytes 32800 | tf_op jit(solution)/shard_map/ppermute | solution.py:863
  54.3 0.8 %chip_e2.1 = bf16[1,64,512]{2,1,0:T(8,128)(2,1)} custom-call(bf16[128,128]{1,0:T(8,128)(2,1)S(1)} %get-tuple-element.119.mine, bf16[128,128]{1,0:T(8,128)(2,1)S(1)} %collective-permute-done.14.got, bf16[4,640,512]{2,1,0:T(8,128)(2,1)S(1)} %get-tuple-element.67.e.refs_6_.refs_2_, bf16[4,128,512]{2,1,0:T(8,128)(2,1)S(1)} %get-tuple-element.68.sx.refs_7_.refs_3_, ...), custom_call_target="tpu_custom_call" | custom-call | flops 20000000 | bytes 2000000 | tf_op jit(solution)/shard_map/chip_e2/pallas_call | solution.py:40
  55.1 1.0 %end.1 = (f32[330,128]{1,0:T(8,128)}, f32[1,128]{1,0:T(1,128)}, f32[64,330]{1,0:T(8,128)}, f32[1,64]{1,0:T(1,128)}) custom-call(bf16[96,384]{1,0:T(8,128)(2,1)S(1)} %sum_snap.1.mine, bf16[96,384]{1,0:T(8,128)(2,1)S(1)} %collective-permute-done.18.got), custom_call_target="tpu_custom_call" | custom-call | flops 20000000 | bytes 2000000 | tf_op jit(solution)/shard_map/end/pallas_call | solution.py:40
  (27 shorter events, 0.2 us)
Async XLA Ops:
  2.2 8.3 %collective-permute-start.5 = (bf16[80,512]{1,0:T(8,128)(2,1)}, bf16[80,512]{1,0:T(8,128)(2,1)S(1)}, u32[]{:S(2)}, u32[]{:S(2)}) collective-permute-start(bf16[80,512]{1,0:T(8,128)(2,1)} %pack.1.refs_0_.own), channel_id=1, source_target_pairs={{0,6},{1,7},{2,4},{3,5},{4,2},{5,3},{6,0},{7,1},{8,14},{9,15},{10,... | collective-permute-start | bytes 245768 | tf_op jit(solution)/shard_map/ppermute | solution.py:863
  7.2 7.1 %collective-permute-start.4 = (bf16[80,512]{1,0:T(8,128)(2,1)}, bf16[80,512]{1,0:T(8,128)(2,1)S(1)}, u32[]{:S(2)}, u32[]{:S(2)}) collective-permute-start(bf16[80,512]{1,0:T(8,128)(2,1)} %pack.1.refs_0_.own), channel_id=1, source_target_pairs={{0,4},{1,5},{2,6},{3,7},{4,0},{5,1},{6,2},{7,3},{8,12},{9,13},{10,... | collective-permute-start | bytes 245768 | tf_op jit(solution)/shard_map/ppermute | solution.py:863
  7.2 7.1 %collective-permute-start.3 = (bf16[80,512]{1,0:T(8,128)(2,1)}, bf16[80,512]{1,0:T(8,128)(2,1)S(1)}, u32[]{:S(2)}, u32[]{:S(2)}) collective-permute-start(bf16[80,512]{1,0:T(8,128)(2,1)} %pack.1.refs_0_.own), channel_id=1, source_target_pairs={{0,2},{1,3},{2,0},{3,1},{4,6},{5,7},{6,4},{7,5},{8,10},{9,11},{10,... | collective-permute-start | bytes 245768 | tf_op jit(solution)/shard_map/ppermute | solution.py:863
  14.3 0.9 %copy-start = (bf16[80,512]{1,0:T(8,128)(2,1)S(1)}, bf16[80,512]{1,0:T(8,128)(2,1)}, u32[]{:S(2)}) copy-start(bf16[80,512]{1,0:T(8,128)(2,1)} %pack.1.refs_0_.own) | copy-start | bytes 245764
  16.8 1.3 %collective-permute-start.6 = (bf16[160,128]{1,0:T(8,128)(2,1)S(1)}, bf16[160,128]{1,0:T(8,128)(2,1)S(1)}, u32[]{:S(2)}, u32[]{:S(2)}) collective-permute-start(bf16[160,128]{1,0:T(8,128)(2,1)S(1)} %get-tuple-element.66.mine), channel_id=1, source_target_pairs={{0,1},{1,0},{2,3},{3,2},{4,5},{5,4},{6,7},{7,6},{8,9},{9,8},{10,11... | collective-permute-start | bytes 122888 | tf_op jit(solution)/shard_map/ppermute | solution.py:863
  18.1 1.2 %copy-start.1 = (bf16[80,512]{1,0:T(8,128)(2,1)S(1)}, bf16[80,512]{1,0:T(8,128)(2,1)}, u32[]{:S(2)}) copy-start(bf16[80,512]{1,0:T(8,128)(2,1)} %pack.1.refs_0_.own) | copy-start | bytes 245764
  18.1 1.2 %copy-start.2 = (bf16[128,330]{0,1:T(8,128)(2,1)S(1)}, bf16[128,330]{0,1:T(8,128)(2,1)}, u32[]{:S(2)}) copy-start(bf16[128,330]{0,1:T(8,128)(2,1)} %param.13) | copy-start | bytes 253444
  18.1 1.2 %copy-start.4 = (bf16[64,330]{1,0:T(8,128)(2,1)S(1)}, bf16[64,330]{1,0:T(8,128)(2,1)}, u32[]{:S(2)}) copy-start(bf16[64,330]{1,0:T(8,128)(2,1)} %cw.1) | copy-start | bytes 126724
  18.7 1.9 %collective-permute-start.7 = (bf16[160,128]{1,0:T(8,128)(2,1)S(1)}, bf16[160,128]{1,0:T(8,128)(2,1)S(1)}, u32[]{:S(2)}, u32[]{:S(2)}) collective-permute-start(bf16[160,128]{1,0:T(8,128)(2,1)S(1)} %get-tuple-element.72.mine), channel_id=1, source_target_pairs={{0,1},{1,0},{2,3},{3,2},{4,5},{5,4},{6,7},{7,6},{8,9},{9,8},{10,11... | collective-permute-start | bytes 122888 | tf_op jit(solution)/shard_map/ppermute | solution.py:863
  19.6 1.1 %copy-start.5 = (f32[128]{0:T(128)S(1)}, f32[128]{0:T(128)}, u32[]{:S(2)}) copy-start(f32[128]{0:T(128)} %param.14) | copy-start | bytes 1540
  20.7 1.8 %copy-start.3 = (bf16[1,64,512]{2,1,0:T(8,128)(2,1)S(1)}, bf16[1,64,512]{2,1,0:T(8,128)(2,1)}, u32[]{:S(2)}) copy-start(bf16[1,64,512]{2,1,0:T(8,128)(2,1)} %refs_0_.1) | copy-start | bytes 196612
  22.3 5.7 %collective-permute-start.8 = (bf16[128,128]{1,0:T(8,128)(2,1)S(1)}, bf16[128,128]{1,0:T(8,128)(2,1)S(1)}, u32[]{:S(2)}, u32[]{:S(2)}) collective-permute-start(bf16[128,128]{1,0:T(8,128)(2,1)S(1)} %get-tuple-element.80.mine), channel_id=1, source_target_pairs={{0,1},{1,0},{2,3},{3,2},{4,5},{5,4},{6,7},{7,6},{8,9},{9,8},{10,11... | collective-permute-start | bytes 98312 | tf_op jit(solution)/shard_map/ppermute | solution.py:863
  22.5 7.3 %collective-permute-start.1 = (bf16[1,64,512]{2,1,0:T(8,128)(2,1)S(1)}, bf16[1,64,512]{2,1,0:T(8,128)(2,1)S(1)}, u32[]{:S(2)}, u32[]{:S(2)}) collective-permute-start(bf16[1,64,512]{2,1,0:T(8,128)(2,1)S(1)} %copy-done.3), channel_id=1, source_target_pairs={{0,4},{1,5},{2,6},{3,7},{4,0},{5,1},{6,2},{7,3},{8,12},{9,13},{10,... | collective-permute-start | bytes 196616 | tf_op jit(solution)/shard_map/ppermute | solution.py:863
  23.4 6.4 %collective-permute-start = (bf16[1,64,512]{2,1,0:T(8,128)(2,1)S(1)}, bf16[1,64,512]{2,1,0:T(8,128)(2,1)S(1)}, u32[]{:S(2)}, u32[]{:S(2)}) collective-permute-start(bf16[1,64,512]{2,1,0:T(8,128)(2,1)S(1)} %copy-done.3), channel_id=1, source_target_pairs={{0,2},{1,3},{2,0},{3,1},{4,6},{5,7},{6,4},{7,5},{8,10},{9,11},{10,... | collective-permute-start | bytes 196616 | tf_op jit(solution)/shard_map/ppermute | solution.py:863
  25.7 6.1 %collective-permute-start.2 = (bf16[1,64,512]{2,1,0:T(8,128)(2,1)S(1)}, bf16[1,64,512]{2,1,0:T(8,128)(2,1)S(1)}, u32[]{:S(2)}, u32[]{:S(2)}) collective-permute-start(bf16[1,64,512]{2,1,0:T(8,128)(2,1)S(1)} %copy-done.3), channel_id=1, source_target_pairs={{0,6},{1,7},{2,4},{3,5},{4,2},{5,3},{6,0},{7,1},{8,14},{9,15},{10,... | collective-permute-start | bytes 196616 | tf_op jit(solution)/shard_map/ppermute | solution.py:863
  28.6 3.2 %copy-start.6 = (f32[64]{0:T(128)S(1)}, f32[64]{0:T(128)}, u32[]{:S(2)}) copy-start(f32[64]{0:T(128)} %param.16) | copy-start | bytes 772
  28.6 3.2 %collective-permute-start.9 = (bf16[128,128]{1,0:T(8,128)(2,1)S(1)}, bf16[128,128]{1,0:T(8,128)(2,1)S(1)}, u32[]{:S(2)}, u32[]{:S(2)}) collective-permute-start(bf16[128,128]{1,0:T(8,128)(2,1)S(1)} %get-tuple-element.84.refs_4_), channel_id=1, source_target_pairs={{0,1},{1,0},{2,3},{3,2},{4,5},{5,4},{6,7},{7,6},{8,9},{9,8},{10,11... | collective-permute-start | bytes 98312 | tf_op jit(solution)/shard_map/ppermute | solution.py:863
  34.2 2.9 %collective-permute-start.10 = (bf16[128,128]{1,0:T(8,128)(2,1)S(1)}, bf16[128,128]{1,0:T(8,128)(2,1)S(1)}, u32[]{:S(2)}, u32[]{:S(2)}) collective-permute-start(bf16[128,128]{1,0:T(8,128)(2,1)S(1)} %get-tuple-element.92.mine), channel_id=1, source_target_pairs={{0,1},{1,0},{2,3},{3,2},{4,5},{5,4},{6,7},{7,6},{8,9},{9,8},{10,11... | collective-permute-start | bytes 98312 | tf_op jit(solution)/shard_map/ppermute | solution.py:863
  37.7 1.7 %collective-permute-start.11 = (bf16[128,128]{1,0:T(8,128)(2,1)S(1)}, bf16[128,128]{1,0:T(8,128)(2,1)S(1)}, u32[]{:S(2)}, u32[]{:S(2)}) collective-permute-start(bf16[128,128]{1,0:T(8,128)(2,1)S(1)} %get-tuple-element.102.mine), channel_id=1, source_target_pairs={{0,1},{1,0},{2,3},{3,2},{4,5},{5,4},{6,7},{7,6},{8,9},{9,8},{10,11... | collective-permute-start | bytes 98312 | tf_op jit(solution)/shard_map/ppermute | solution.py:863
  42.0 1.3 %collective-permute-start.12 = (bf16[96,384]{1,0:T(8,128)(2,1)S(1)}, bf16[96,384]{1,0:T(8,128)(2,1)S(1)}, u32[]{:S(2)}, u32[]{:S(2)}) collective-permute-start(bf16[96,384]{1,0:T(8,128)(2,1)S(1)} %get-tuple-element.111), channel_id=1, source_target_pairs={{0,1},{1,0},{2,3},{3,2},{4,5},{5,4},{6,7},{7,6},{8,9},{9,8},{10,11... | collective-permute-start | bytes 221192 | tf_op jit(solution)/shard_map/ppermute | solution.py:863
  43.3 5.4 %collective-permute-start.17 = (bf16[96,384]{1,0:T(8,128)(2,1)S(1)}, bf16[96,384]{1,0:T(8,128)(2,1)S(1)}, u32[]{:S(2)}, u32[]{:S(2)}) collective-permute-start(bf16[96,384]{1,0:T(8,128)(2,1)S(1)} %sum_core.1.after.refs_0_), channel_id=1, source_target_pairs={{0,24},{8,16},{16,8},{24,0},{1,25},{9,17},{17,9},{25,1},{2,26},{10... | collective-permute-start | bytes 221192 | tf_op jit(solution)/shard_map/ppermute | solution.py:863
  45.9 4.4 %collective-permute-start.16 = (bf16[96,384]{1,0:T(8,128)(2,1)S(1)}, bf16[96,384]{1,0:T(8,128)(2,1)S(1)}, u32[]{:S(2)}, u32[]{:S(2)}) collective-permute-start(bf16[96,384]{1,0:T(8,128)(2,1)S(1)} %sum_core.1.after.refs_0_), channel_id=1, source_target_pairs={{0,16},{8,24},{16,0},{24,8},{1,17},{9,25},{17,1},{25,9},{2,18},{10... | collective-permute-start | bytes 221192 | tf_op jit(solution)/shard_map/ppermute | solution.py:863
  46.4 4.4 %collective-permute-start.15 = (bf16[96,384]{1,0:T(8,128)(2,1)S(1)}, bf16[96,384]{1,0:T(8,128)(2,1)S(1)}, u32[]{:S(2)}, u32[]{:S(2)}) collective-permute-start(bf16[96,384]{1,0:T(8,128)(2,1)S(1)} %sum_core.1.after.refs_0_), channel_id=1, source_target_pairs={{0,8},{8,0},{16,24},{24,16},{1,9},{9,1},{17,25},{25,17},{2,10},{10... | collective-permute-start | bytes 221192 | tf_op jit(solution)/shard_map/ppermute | solution.py:863
  50.8 4.4 %collective-permute-start.18 = (bf16[96,384]{1,0:T(8,128)(2,1)S(1)}, bf16[96,384]{1,0:T(8,128)(2,1)S(1)}, u32[]{:S(2)}, u32[]{:S(2)}) collective-permute-start(bf16[96,384]{1,0:T(8,128)(2,1)S(1)} %sum_snap.1.mine), channel_id=1, source_target_pairs={{0,1},{1,0},{2,3},{3,2},{4,5},{5,4},{6,7},{7,6},{8,9},{9,8},{10,11... | collective-permute-start | bytes 221192 | tf_op jit(solution)/shard_map/ppermute | solution.py:863
  50.8 1.6 %collective-permute-start.13 = (bf16[128,128]{1,0:T(8,128)(2,1)S(1)}, bf16[128,128]{1,0:T(8,128)(2,1)S(1)}, u32[]{:S(2)}, u32[]{:S(2)}) collective-permute-start(bf16[128,128]{1,0:T(8,128)(2,1)S(1)} %get-tuple-element.112.refs_0_), channel_id=1, source_target_pairs={{0,1},{1,0},{2,3},{3,2},{4,5},{5,4},{6,7},{7,6},{8,9},{9,8},{10,11... | collective-permute-start | bytes 98312 | tf_op jit(solution)/shard_map/ppermute | solution.py:863
  53.1 1.3 %collective-permute-start.14 = (bf16[128,128]{1,0:T(8,128)(2,1)S(1)}, bf16[128,128]{1,0:T(8,128)(2,1)S(1)}, u32[]{:S(2)}, u32[]{:S(2)}) collective-permute-start(bf16[128,128]{1,0:T(8,128)(2,1)S(1)} %get-tuple-element.119.mine), channel_id=1, source_target_pairs={{0,1},{1,0},{2,3},{3,2},{4,5},{5,4},{6,7},{7,6},{8,9},{9,8},{10,11... | collective-permute-start | bytes 98312 | tf_op jit(solution)/shard_map/ppermute | solution.py:863

commit v2 on v1

--- a/solution.py
+++ b/solution.py
@@ -35,18 +35,18 @@
     return jnp.sum(jnp.where(iota((k, k), 0) == iota((k, k), 1), spread, 0.0), axis=1, keepdims=True)
 
 
-def run(kernel, name, outs, *args, scratch=(), flops=20_000_000, vmem=24):
+def run(kernel, name, outs, *args, scratch=(), flops=20_000_000, vmem=24, after=()):
     whole = pl.BlockSpec(memory_space=pltpu.VMEM)
     return pl.pallas_call(
-        kernel,
+        lambda *refs: kernel(*refs[len(after) :]),
         name=name,
         out_shape=[jax.ShapeDtypeStruct(shape, kind) for shape, kind in outs],
-        in_specs=[whole] * len(args),
+        in_specs=[pl.BlockSpec(memory_space=pl.ANY)] * len(after) + [whole] * len(args),
         out_specs=[whole] * len(outs),
         scratch_shapes=list(scratch),
         compiler_params=pltpu.CompilerParams(vmem_limit_bytes=vmem * 1024 * 1024),
         cost_estimate=pl.CostEstimate(flops=flops, bytes_accessed=2_000_000, transcendentals=0),
-    )(*args)
+    )(*after, *args)
 
 
 def prep_kernel(cap, nb, w, rows, readings, previous, e, s, b, pay):
@@ -533,104 +533,103 @@
     own[hid:, :] = tail[...].astype(BF16)
 
 
-def pack_entry(nb, w, rows, readings, previous, own, tail):
+def pack_entry(nb, w, rows, readings, previous, own, sent, tail):
     pack_kernel(own, nb, w, rows, readings, previous, tail)
-
-
-def exchange(first, second, e, sx, pay):
-    n = e.shape[2]
+    sent[...] = own[...]
+
+
+def exchange(first, second, hc, sc, pay):
     count = first[0].shape[0]
-    bound = sum(nt(first[p], sx[p]) for p in range(len(first)))
-    halo = sum(nt(second[p], e[p, n:, :]) for p in range(len(second)))
-    pay[:count, :] = bound.astype(BF16)
-    pay[count:, :] = halo.astype(BF16)
-
-
-def merged(mine, got):
-    half = mine.shape[1] // 2
-    value = jnp.where(iota(mine.shape, 1) < half, mine[...].astype(F32), got[...].astype(F32)).astype(BF16)
+    parts = len(first)
+    pay[:count, :] = jnp.concatenate([nt(first[p], sc[p]).astype(BF16) for p in range(parts)], axis=1)
+    pay[count:, :] = jnp.concatenate([nt(second[p], hc[p]).astype(BF16) for p in range(parts)], axis=1)
+
+
+def merged(parts, mine, got):
+    step = mine.shape[1] // (2 * parts)
+    here = lax.rem(lax.div(iota(mine.shape, 1), jnp.int32(step)), jnp.int32(2)) == 0
+    value = jnp.where(here, mine[...].astype(F32), got[...].astype(F32)).astype(BF16)
     count = mine.shape[0] // 2
     return value[:count, :], value[count:, :]
 
 
 def build_kernel(cap, hid, fin, degree, parts, *refs):
-    blocks_in, (e, sx, b, pay, blocks) = refs[:parts], refs[parts:]
-    n = e.shape[2]
+    blocks_in, (a, at, hc, hx, sc, sx, b, pay, blocks) = refs[:parts], refs[parts:]
+    n = a.shape[2]
     slots = sx.shape[1]
-    half = slots // 2
     nh = 2 * parts * cap
+    half = parts * cap
     me = lax.axis_index("dom")
     z = lax.shift_right_logical(me, 1)
     core = me - 2 * z
     for k in range(parts):
         blocks[lax.bitwise_xor(z, jnp.int32(k))] = blocks_in[k][...]
-    lane = iota((slots, n), 1)
-    slot = iota((slots, 1), 0)
-    rel = lax.div(slot, jnp.int32(half))
-    rest = slot - rel * half
-    dest = lax.div(rest, jnp.int32(parts * cap))
-    rest = rest - dest * (parts * cap)
-    source = lax.div(rest, jnp.int32(cap))
-    t = rest - source * cap
-    other = lax.bitwise_xor(rel, core)
-    spot = (dest * 2 + other) * cap + t
+    line = iota((nh, 1), 0)
+    rel = lax.div(line, jnp.int32(half))
+    k = lax.div(line - rel * half, jnp.int32(cap))
+    t = line - rel * half - k * cap
+    spot = (k * 2 + lax.bitwise_xor(rel, core)) * cap + t
+    node = (n + spot).astype(F32)
     width = -(-nh // LANES) * LANES
-    step = parts * cap
+    slot = iota((slots, nh), 0)
+    outer = lax.div(slot, jnp.int32(nh))
+    rest = slot - outer * nh
+    slot_rel = lax.div(rest, jnp.int32(half))
+    rest = rest - slot_rel * half
+    inner = lax.div(rest, jnp.int32(cap))
+    filled = iota((slots, nh), 1) == slot_rel * half + outer * cap + rest - inner * cap
     row = iota((32, n), 0).astype(F32)
     for p in range(parts):
         tail = blocks[p, hid:, :].astype(F32)
         high, low = tail[fin : fin + degree], tail[fin + degree : fin + 2 * degree]
         w = tail[fin + 2 * degree : fin + 3 * degree]
-        at = fin + 3 * degree
-        sent = tail[at : at + 1] * 32.0 + tail[at + 1 : at + 2]
+        start = fin + 3 * degree
+        sent = tail[start : start + 1] * 32.0 + tail[start + 1 : start + 2]
         low_is = [jnp.where(low[d : d + 1] == row, 1.0, 0.0).astype(BF16) for d in range(degree)]
         for chunk in range(n // 32):
             total = None
             for d in range(degree):
                 term = low_is[d] * jnp.where(high[d : d + 1] == float(chunk), w[d : d + 1], 0.0).astype(BF16)
                 total = term if total is None else total + term
-            e[p, chunk * 32 : (chunk + 1) * 32, :] = total
+            a[p, chunk * 32 : (chunk + 1) * 32, :] = total
+        at[p] = a[p].T
         names = high * 32.0 + low
-        e[p, n:, :] = jnp.zeros((slots, n), BF16)
-        line = iota((step, n), 0)
-        src = lax.div(line, jnp.int32(cap))
-        for r in range(2):
-            node = (n + (src * 2 + lax.bitwise_xor(jnp.int32(r), core)) * cap + line - src * cap).astype(F32)
-            total = jnp.zeros((step, n), F32)
-            for d in range(degree):
-                total = total + jnp.where(names[d : d + 1] == node, w[d : d + 1], 0.0)
-            start = n + r * half + p * step
-            e[p, start : start + step, :] = total.astype(BF16)
-        named = jnp.where(iota((slots, width), 1) == spot, sent[:, :width], 0.0)
+        total = jnp.zeros((nh, n), F32)
+        for d in range(degree):
+            total = total + jnp.where(names[d : d + 1] == node, w[d : d + 1], 0.0)
+        halo = total.astype(BF16)
+        hc[p] = halo
+        named = jnp.where(iota((nh, width), 1) == spot, sent[:, :width], 0.0)
         target = jnp.sum(named, axis=1, keepdims=True).astype(jnp.int32)
-        target = jnp.where(source == p, target, -1)
-        sx[p] = jnp.where(lane == target, 1.0, 0.0).astype(BF16)
+        picked = jnp.where(iota((nh, n), 1) == target, 1.0, 0.0).astype(BF16)
+        sc[p] = picked
+        place = jnp.where(filled & (inner == p), 1.0, 0.0).astype(BF16)
+        hx[p] = nn(place, halo).astype(BF16)
+        sx[p] = nn(place, picked).astype(BF16)
         b[p, :hid, :] = blocks[p, :hid, :]
         line = iota(tail.shape, 0)
         b[p, hid:, :] = jnp.where(line < fin, tail, jnp.where(line == fin, 1.0, 0.0)).astype(BF16)
     base = [b[p] for p in range(parts)]
-    exchange(base, base, e, sx, pay)
-
-
-def order_kernel(hid, fin, orders, block, gw, cw, own, gw_o, cw_o):
+    exchange(base, base, hc, sc, pay)
+
+
+def order_kernel(hid, fin, orders, block, gw, cw, gw_o, cw_o):
     order = order_matrix((cw.shape[1], orders * block), hid + fin, hid, fin, block)
     gw_o[...] = tn(gw[...], order).astype(BF16)
     cw_o[...] = nn(cw[...], order).astype(BF16)
 
 
-def local_kernel(e, x1, x2, l1, l2):
-    n = e.shape[2]
-    for p in range(e.shape[0]):
-        l1[p] = nn(x1[p], e[p, :n, :])
-        l2[p] = nt(x2[p], e[p, :n, :])
-
-
-def chip_a_kernel(one, mine, got, e, sx, l1, l2, f1, r1, ro, ri, pay):
-    n = e.shape[2]
-    top, low = merged(mine, got)
+def local_kernel(a, at, x1, x2, l1, l2):
+    for p in range(a.shape[0]):
+        l1[p] = nn(x1[p], a[p])
+        l2[p] = nn(x2[p], at[p])
+
+
+def chip_a_kernel(one, mine, got, hc, hx, sc, sx, l1, l2, f1, r1, ro, ri, pay):
+    top, low = merged(sx.shape[0], mine, got)
     firsts, seconds = [], []
-    for p in range(e.shape[0]):
-        pulled = l1[p] + nn(top, e[p, n:, :])
+    for p in range(sx.shape[0]):
+        pulled = l1[p] + nn(top, hx[p])
         pushed = l2[p] + nn(low, sx[p])
         inv_o = 1.0 / pushed[one : one + 1, :]
         inv_i = 1.0 / pulled[one : one + 1, :]
@@ -642,19 +641,18 @@
         r1[p] = into
         firsts.append(into)
         seconds.append(out)
-    exchange(firsts, seconds, e, sx, pay)
-
-
-def chip_b_kernel(mine, got, e, sx, b, f1, r1, l1, l2, ro, ri, gw, gb, states, reset, update, y, pay):
-    n = e.shape[2]
+    exchange(firsts, seconds, hc, sc, pay)
+
+
+def chip_b_kernel(mine, got, hc, hx, sc, sx, b, f1, r1, l1, l2, ro, ri, gw, gb, states, reset, update, y, pay):
     hid = y.shape[1]
     chans = b.shape[1]
-    top, low = merged(mine, got)
+    top, low = merged(sx.shape[0], mine, got)
     bias = column(gb[...])
     fields = []
-    for p in range(e.shape[0]):
+    for p in range(sx.shape[0]):
         base = b[p].astype(F32)
-        r2 = 2.0 * (l1[p] + nn(top, e[p, n:, :])) * ri[p] - base
+        r2 = 2.0 * (l1[p] + nn(top, hx[p])) * ri[p] - base
         f2 = 2.0 * (l2[p] + nn(low, sx[p])) * ro[p] - base
         states[p, :chans, :] = b[p]
         states[p, chans : 2 * chans, :] = f1[p]
@@ -667,21 +665,20 @@
         now = (gates[:hid] * base[:hid]).astype(BF16)
         y[p] = now
         fields.append(now)
-    exchange(fields, fields, e, sx, pay)
-
-
-def chip_c1_kernel(mine, got, e, sx, l1, l2, ro, ri, f1, r1, pay):
-    n = e.shape[2]
-    top, low = merged(mine, got)
+    exchange(fields, fields, hc, sc, pay)
+
+
+def chip_c1_kernel(mine, got, hc, hx, sc, sx, l1, l2, ro, ri, f1, r1, pay):
+    top, low = merged(sx.shape[0], mine, got)
     firsts, seconds = [], []
-    for p in range(e.shape[0]):
-        into = ((l1[p] + nn(top, e[p, n:, :])) * ri[p]).astype(BF16)
+    for p in range(sx.shape[0]):
+        into = ((l1[p] + nn(top, hx[p])) * ri[p]).astype(BF16)
         out = ((l2[p] + nn(low, sx[p])) * ro[p]).astype(BF16)
         f1[p] = out
         r1[p] = into
         firsts.append(into)
         seconds.append(out)
-    exchange(firsts, seconds, e, sx, pay)
+    exchange(firsts, seconds, hc, sc, pay)
 
 
 def split_back(back, hid, inv_o, inv_i, y1, y2, g1, g3):
@@ -695,20 +692,19 @@
 
 def chip_c2_kernel(orders, parts, *refs):
     ups, refs = refs[:parts], refs[parts:]
-    mine, got, e, sx, y, f1, r1, l1, l2, ro, ri, states, cw, cb, update = refs[:15]
-    mixed, cand_grad, gate_update, y1, y2, g1, g3, upstream, direct, pay = refs[15:]
-    n = e.shape[2]
+    mine, got, hc, hx, sc, sx, y, f1, r1, l1, l2, ro, ri, states, cw, cb, update = refs[:17]
+    mixed, cand_grad, gate_update, y1, y2, g1, g3, upstream, direct, pay = refs[17:]
     hid = y.shape[1]
     block = states.shape[1] // orders
     z = lax.shift_right_logical(lax.axis_index("dom"), 1)
     for k in range(parts):
         upstream[lax.bitwise_xor(z, jnp.int32(k))] = ups[k][0]
-    top, low = merged(mine, got)
+    top, low = merged(sx.shape[0], mine, got)
     bias = column(cb[...])
     hidden = hidden_weights(cw[...], hid, block, orders)
-    for p in range(e.shape[0]):
+    for p in range(sx.shape[0]):
         base = y[p].astype(F32)
-        r2 = 2.0 * (l1[p] + nn(top, e[p, n:, :])) * ri[p] - base
+        r2 = 2.0 * (l1[p] + nn(top, hx[p])) * ri[p] - base
         f2 = 2.0 * (l2[p] + nn(low, sx[p])) * ro[p] - base
         for m, value in enumerate((y[p], f1[p], f2, r1[p], r2)):
             mixed[p, m * block : m * block + hid, :] = value.astype(BF16)
@@ -720,8 +716,8 @@
         cand_grad[p] = grad
         gate_update[p] = (up * (states[p, :hid, :].astype(F32) - cand) * gate * (1.0 - gate)).astype(BF16)
         direct[p] = split_back(tn(hidden, grad), hid, ro[p], ri[p], y1.at[p], y2.at[p], g1.at[p], g3.at[p])
-    parts = range(e.shape[0])
-    exchange([y1[p] for p in parts], [y2[p] for p in parts], e, sx, pay)
+    parts = range(sx.shape[0])
+    exchange([y1[p] for p in parts], [y2[p] for p in parts], hc, sc, pay)
 
 
 def chip_part(grads, features, orders, chans, hid, fin):
@@ -735,89 +731,81 @@
     source = jnp.where(c < hid, m * chans + fin + c, jnp.where(c < hid + fin, m * chans + c - hid, -1))
     source = jnp.where(col == hid + fin, orders * chans, source)
     order = jnp.where(k == source, 1.0, 0.0).astype(BF16)
-    total = sum(nt(grads[p], features[p]) for p in range(grads.shape[0]))
+    total = sum(nt(grads[p], features[p]) for p in range(features.shape[0]))
     return nt(total.astype(BF16), order)
 
 
-def local_d_kernel(orders, fin, e, y1, y2, cand_grad, mixed, gate_update, states, l1, l2, part):
+def local_d_kernel(orders, fin, a, at, y1, y2, cand_grad, mixed, l1, l2, part):
     hid = y1.shape[1]
-    local_kernel(e, y1, y2, l1, l2)
-    part[:hid, :] = chip_part(gate_update, states, orders, hid + fin, hid, fin).astype(BF16)
-    part[hid:, :] = chip_part(cand_grad, mixed, orders, hid + fin, hid, fin).astype(BF16)
-
-
-def chip_e1_kernel(after, *refs):
-    chip_d1_kernel(*refs)
-
-
-def chip_d1_kernel(mine, got, e, sx, l1, l2, g1, g3, ro, ri, z1, z2, pay):
-    n = e.shape[2]
-    top, low = merged(mine, got)
+    local_kernel(a, at, y1, y2, l1, l2)
+    part[...] = chip_part(cand_grad, mixed, orders, hid + fin, hid, fin).astype(BF16)
+
+
+def chip_d1_kernel(mine, got, hc, hx, sc, sx, l1, l2, g1, g3, ro, ri, z1, z2, pay):
+    top, low = merged(sx.shape[0], mine, got)
     firsts, seconds = [], []
-    for p in range(e.shape[0]):
-        one = ((g1[p].astype(F32) + 2.0 * (l1[p] + nn(top, e[p, n:, :]))) * ro[p]).astype(BF16)
+    for p in range(sx.shape[0]):
+        one = ((g1[p].astype(F32) + 2.0 * (l1[p] + nn(top, hx[p]))) * ro[p]).astype(BF16)
         two = ((g3[p].astype(F32) + 2.0 * (l2[p] + nn(low, sx[p]))) * ri[p]).astype(BF16)
         z1[p] = one
         z2[p] = two
         firsts.append(one)
         seconds.append(two)
-    exchange(firsts, seconds, e, sx, pay)
-
-
-def local_d2_kernel(e, z1, z2, direct, base):
-    n = e.shape[2]
-    for p in range(e.shape[0]):
-        base[p] = direct[p] + nn(z1[p], e[p, :n, :]) + nt(z2[p], e[p, :n, :])
-
-
-def chip_d2_kernel(orders, mine, got, e, sx, base, ro, ri, states, gw, upstream, reset, update, gate_update,
-                   gate_reset, y1, y2, g1, g3, direct, pay):
-    n = e.shape[2]
+    exchange(firsts, seconds, hc, sc, pay)
+
+
+def local_d2_kernel(a, at, z1, z2, direct, base):
+    for p in range(a.shape[0]):
+        base[p] = direct[p] + nn(z1[p], a[p]) + nn(z2[p], at[p])
+
+
+def chip_d2_kernel(orders, mine, got, hc, hx, sc, sx, base, ro, ri, states, gw, upstream, reset, update, gate_update,
+                   gate_grad, y1, y2, g1, g3, direct, pay):
     hid = base.shape[1]
     block = states.shape[1] // orders
-    top, low = merged(mine, got)
+    top, low = merged(sx.shape[0], mine, got)
     hidden = hidden_weights(gw[...], hid, block, orders)
-    for p in range(e.shape[0]):
-        scaled_grad = base[p] + nn(top, e[p, n:, :]) + nn(low, sx[p])
+    for p in range(sx.shape[0]):
+        scaled_grad = base[p] + nn(top, hx[p]) + nn(low, sx[p])
         gate = reset[p]
         grad = (scaled_grad * states[p, :hid, :].astype(F32) * gate * (1.0 - gate)).astype(BF16)
-        gate_reset[p] = grad
-        back = tn(hidden, jnp.concatenate([grad, gate_update[p]], axis=0))
+        gate_grad[p, :hid, :] = grad
+        gate_grad[p, hid:, :] = gate_update[p]
+        back = tn(hidden, gate_grad[p])
         rest = split_back(back, hid, ro[p], ri[p], y1.at[p], y2.at[p], g1.at[p], g3.at[p])
         direct[p] = rest + upstream[p].astype(F32) * update[p] + scaled_grad * gate
-    parts = range(e.shape[0])
-    exchange([y1[p] for p in parts], [y2[p] for p in parts], e, sx, pay)
-
-
-def grads_kernel(orders, fin, gate_reset, states, part, keep, give, flat):
-    hid = gate_reset.shape[1]
+    parts = range(sx.shape[0])
+    exchange([y1[p] for p in parts], [y2[p] for p in parts], hc, sc, pay)
+
+
+def grads_kernel(orders, fin, gate_grad, states, part, keep, give, flat):
+    both = gate_grad.shape[1]
+    hid = both // 2
     half = keep.shape[0]
     core = lax.rem(lax.axis_index("dom"), 2)
-    flat[:hid, :] = chip_part(gate_reset, states, orders, hid + fin, hid, fin)
-    flat[hid:, :] = part[...].astype(F32)
+    flat[:both, :] = chip_part(gate_grad, states, orders, hid + fin, hid, fin)
+    flat[both:, :] = part[...].astype(F32)
     keep[...] = flat[pl.ds(pl.multiple_of(core * half, 8), half), :].astype(BF16)
     give[...] = flat[pl.ds(pl.multiple_of((1 - core) * half, 8), half), :].astype(BF16)
 
 
-def local_e_kernel(e, z1, z2, direct, base):
-    n = e.shape[2]
+def local_e_kernel(a, at, z1, z2, direct, base):
     z = lax.shift_right_logical(lax.axis_index("dom"), 1)
-    a = e[z, :n, :]
-    base[...] = direct[z] + nn(z1[z], a) + nt(z2[z], a)
-
-
-def chip_e_kernel(mine, got, e, sx, base, out):
-    n = e.shape[2]
+    base[...] = direct[z] + nn(z1[z], a[z]) + nn(z2[z], at[z])
+
+
+def chip_e_kernel(mine, got, hc, hx, sc, sx, base, out):
     z = lax.shift_right_logical(lax.axis_index("dom"), 1)
-    top, low = merged(mine, got)
-    out[0] = (base[...] + nn(top, e[z, n:, :]) + nn(low, sx[z])).astype(BF16)
+    top, low = merged(sx.shape[0], mine, got)
+    out[0] = (base[...] + nn(top, hx[z]) + nn(low, sx[z])).astype(BF16)
 
 
 def sum_kernel(*refs):
-    values = [ref[...].astype(F32) for ref in refs[:-1]]
+    values = [ref[...].astype(F32) for ref in refs[:-2]]
     while len(values) > 1:
         values = [values[k] + values[k + 1] for k in range(0, len(values), 2)]
     refs[-1][...] = values[0].astype(BF16)
+    refs[-2][...] = values[0].astype(BF16)
 
 
 def end_kernel(factor, mine, got, gw, gb, cw, cb, flat):
@@ -862,85 +850,87 @@
     def swap(array, k, axis="dom", size=nd):
         return lax.ppermute(array, axis, [(i, i ^ k) for i in range(size)])
 
-    (own,) = run(
-        pack_entry, "pack", [((block, n), BF16)], neighbours, edge_weight, send_rows, readings, previous,
+    own, sent = run(
+        pack_entry, "pack", [((block, n), BF16)] * 2, neighbours, edge_weight, send_rows, readings, previous,
         scratch=[pltpu.VMEM((block - hid, n), F32)], vmem=56,
     )
-    blocks = [own] + [swap(own, 2 * k) for k in range(1, parts)]
+    blocks = [own] + [swap(sent, 2 * k) for k in range(1, parts)]
     ups = [upstream] + [swap(upstream, 2 * k) for k in range(1, parts)]
     gw, cw = run(
         functools.partial(order_kernel, hid, fin, orders, block), "order",
-        [((2 * hid, orders * block), BF16), ((hid, orders * block), BF16)], gate_weight.T, cand_weight, own,
+        [((2 * hid, orders * block), BF16), ((hid, orders * block), BF16)], gate_weight.T, cand_weight, after=[own],
     )
     wide, wide16, wide_pay = ((parts, block, n), F32), ((parts, block, n), BF16), ((2 * block, slots), BF16)
     field, field16, pay_kind = ((parts, hid, n), F32), ((parts, hid, n), BF16), ((2 * hid, slots), BF16)
     line = ((parts, 1, n), F32)
-    e, sx, b, pay = run(
+    a, at, hc, hx, sc, sx, b, pay = run(
         functools.partial(build_kernel, cap, hid, fin, degree, parts), "build",
-        [((parts, n + slots, n), BF16), ((parts, slots, n), BF16), wide16, wide_pay],
-        *blocks, scratch=[pltpu.VMEM((parts, block, n), BF16)],
-    )
+        [((parts, n, n), BF16)] * 2 + [((parts, rows, n), BF16) for rows in (2 * parts * cap, slots)] * 2 + [wide16, wide_pay],
+        *blocks, scratch=[pltpu.VMEM((parts, block, n), BF16)], after=[gw],
+    )
+    edges = (hc, hx, sc, sx)
     got = swap(pay, 1)
-    l1, l2 = run(local_kernel, "local_a", [wide, wide], e, b, b)
+    l1, l2 = run(local_kernel, "local_a", [wide, wide], a, at, b, b)
     f1, r1, ro, ri, pay = run(
         functools.partial(chip_a_kernel, hid + fin), "chip_a", [wide16, wide16, line, line, wide_pay],
-        pay, got, e, sx, l1, l2,
+        pay, got, *edges, l1, l2, after=ups[1:],
     )
     got = swap(pay, 1)
-    l1, l2 = run(local_kernel, "local_b", [wide, wide], e, r1, f1)
+    l1, l2 = run(local_kernel, "local_b", [wide, wide], a, at, r1, f1)
     states, reset, update, y, pay = run(
         chip_b_kernel, "chip_b", [((parts, orders * block, n), BF16), field, field, field16, pay_kind],
-        pay, got, e, sx, b, f1, r1, l1, l2, ro, ri, gw, gate_bias[None, :],
+        pay, got, *edges, b, f1, r1, l1, l2, ro, ri, gw, gate_bias[None, :],
     )
     got = swap(pay, 1)
-    l1, l2 = run(local_kernel, "local_c1", [field, field], e, y, y)
+    l1, l2 = run(local_kernel, "local_c1", [field, field], a, at, y, y)
     f1, r1, pay = run(
-        chip_c1_kernel, "chip_c1", [field16, field16, pay_kind], pay, got, e, sx, l1, l2, ro, ri
+        chip_c1_kernel, "chip_c1", [field16, field16, pay_kind], pay, got, *edges, l1, l2, ro, ri
     )
     got = swap(pay, 1)
-    l1, l2 = run(local_kernel, "local_c2", [field, field], e, r1, f1)
+    l1, l2 = run(local_kernel, "local_c2", [field, field], a, at, r1, f1)
     mixed, cand_grad, gate_update, y1, y2, g1, g3, up, direct, pay = run(
         functools.partial(chip_c2_kernel, orders, parts), "chip_c2",
         [((parts, orders * block, n), BF16)] + [field16] * 7 + [field, pay_kind],
-        *ups, pay, got, e, sx, y, f1, r1, l1, l2, ro, ri, states, cw, cand_bias[None, :], update,
+        *ups, pay, got, *edges, y, f1, r1, l1, l2, ro, ri, states, cw, cand_bias[None, :], update,
     )
     got = swap(pay, 1)
     width = -(-(orders * chans + 1) // LANES) * LANES
     l1, l2, part = run(
-        functools.partial(local_d_kernel, orders, fin), "local_d1", [field, field, ((2 * hid, width), BF16)],
-        e, y1, y2, cand_grad, mixed, gate_update, states,
+        functools.partial(local_d_kernel, orders, fin), "local_d1", [field, field, ((hid, width), BF16)],
+        a, at, y1, y2, cand_grad, mixed,
     )
     z1, z2, pay = run(
-        chip_d1_kernel, "chip_d1", [field16, field16, pay_kind], pay, got, e, sx, l1, l2, g1, g3, ro, ri
+        chip_d1_kernel, "chip_d1", [field16, field16, pay_kind], pay, got, *edges, l1, l2, g1, g3, ro, ri
     )
     got = swap(pay, 1)
-    (base,) = run(local_d2_kernel, "local_d2", [field], e, z1, z2, direct)
-    gate_reset, y1, y2, g1, g3, direct, pay = run(
-        functools.partial(chip_d2_kernel, orders), "chip_d2", [field16] * 5 + [field, pay_kind],
-        pay, got, e, sx, base, ro, ri, states, gw, up, reset, update, gate_update,
+    (base,) = run(local_d2_kernel, "local_d2", [field], a, at, z1, z2, direct)
+    gate_grad, y1, y2, g1, g3, direct, pay = run(
+        functools.partial(chip_d2_kernel, orders), "chip_d2",
+        [((parts, 2 * hid, n), BF16)] + [field16] * 4 + [field, pay_kind],
+        pay, got, *edges, base, ro, ri, states, gw, up, reset, update, gate_update,
     )
     got = swap(pay, 1)
     half = ((3 * hid // 2, width), BF16)
     keep, give = run(
-        functools.partial(grads_kernel, orders, fin), "grads", [half, half], gate_reset, states, part,
+        functools.partial(grads_kernel, orders, fin), "grads", [half, half], gate_grad, states, part,
         scratch=[pltpu.VMEM((3 * hid, width), F32)],
     )
-    (mine,) = run(sum_kernel, "sum_core", [half], keep, swap(give, 1))
-    every = [mine] + [swap(mine, k, "snap", snaps) for k in range(1, snaps)]
-    l1, l2 = run(local_kernel, "local_e1", [field, field], e, y1, y2)
+    l1, l2 = run(local_kernel, "local_e1", [field, field], a, at, y1, y2)
+    mine, sent = run(sum_kernel, "sum_core", [half] * 2, keep, swap(give, 1), after=[l1, got])
+    every = [mine] + [swap(sent, k, "snap", snaps) for k in range(1, snaps)]
     z1, z2, pay = run(
-        chip_e1_kernel, "chip_e1", [field16, field16, pay_kind], mine, pay, got, e, sx, l1, l2, g1, g3, ro, ri
+        chip_d1_kernel, "chip_e1", [field16, field16, pay_kind], pay, got, *edges, l1, l2, g1, g3, ro, ri, after=[mine],
     )
     got = swap(pay, 1)
-    (base,) = run(local_e_kernel, "local_e2", [((hid, n), F32)], e, z1, z2, direct)
-    (state_grad,) = run(chip_e_kernel, "chip_e2", [((1, hid, n), BF16)], pay, got, e, sx, base)
-    (mine,) = run(sum_kernel, "sum_snap", [half], *every)
+    (base,) = run(local_e_kernel, "local_e2", [((hid, n), F32)], a, at, z1, z2, direct)
+    (state_grad,) = run(chip_e_kernel, "chip_e2", [((1, hid, n), BF16)], pay, got, *edges, base)
+    mine, sent = run(sum_kernel, "sum_snap", [half] * 2, *every, after=[state_grad])
     factor = 1.0 / math.sqrt(readings.shape[0] * snaps * n * nd)
     feats = orders * chans
     grad_gw, grad_gb, grad_cw, grad_cb = run(
         functools.partial(end_kernel, factor), "end",
         [((feats, 2 * hid), F32), ((1, 2 * hid), F32), ((hid, feats), F32), ((1, hid), F32)],
-        mine, swap(mine, 1), scratch=[pltpu.VMEM((3 * hid, width), F32)],
+        mine, swap(sent, 1), scratch=[pltpu.VMEM((3 * hid, width), F32)],
     )
     return state_grad, grad_gw.T, grad_gb[0], grad_cw, grad_cb[0]
 

time: 56.4 us -> 48.8 us (0.87)
  waiting for transfers between devices: 14.4 us -> 4.39 us
  local copies, waits for them, and re-layouts: 0.92 us -> 3.42 us
  Pallas kernels: 24.1 us -> 21.8 us
  starting transfers between devices: 15.9 us -> 18 us
    ppermute x19, waiting for transfers between devices: 14.4 us -> 4.39 us  [swap(): return lax.ppermute(array, axis, [(i, i ^ k) for i in range(size)])]
    unnamed x14, local copies, waits for them, and re-layouts: 0.92 us -> 3.42 us
    pallas_call x23, Pallas kernels: 24.1 us -> 21.8 us  [run(): pl.pallas_call(lambda *refs: kernel(*refs[len(after):]), name=name, out_s...]
    ppermute x19, starting transfers between devices: 15.9 us -> 18 us  [swap(): return lax.ppermute(array, axis, [(i, i ^ k) for i in range(size)])]
  transfers between devices with their start and end apart: 19 -> 19, of which waited for: 9 -> 9; matrix products, arithmetic and copies ran while one was open for 0% -> 0% of each run, Pallas kernels for 21% -> 22%
where the time goes in v2:
time: 48.8 us; the launch traced here: 48.4 us
  Pallas kernels  21.8 us (45%)
  starting transfers between devices  18 us (37%)
  waiting for transfers between devices  4.39 us (9%)
  local copies, waits for them, and re-layouts  3.42 us (7%)
  between operations  0.78 us (2%)
    pallas_call x23, Pallas kernels, run(): pl.pallas_call(lambda *refs: kernel(*refs[len(after):]), name=name, out_s...  21.8 us
    ppermute x19, starting transfers between devices, swap(): return lax.ppermute(array, axis, [(i, i ^ k) for i in range(size)])  18 us
    ppermute x19, waiting for transfers between devices, swap(): return lax.ppermute(array, axis, [(i, i ^ k) for i in range(size)])  4.39 us
    unnamed x14, local copies, waits for them, and re-layouts  3.42 us
  transfers between devices with their start and end apart: 19, of which 9 were waited for; matrix products, arithmetic and copies ran while one was open for 0% of the time, Pallas kernels for 22%

profile of v2, /device:TPU:0, one launch (start us, length us, event | category | flops | bytes accessed | tf_op | source)
XLA Modules:
  0.0 48.4 jit_solution(13055083784715198684)
XLA Ops:
  0.6 1.6 %pack.1 = (bf16[80,512]{1,0:T(8,128)(2,1)}, bf16[80,512]{1,0:T(8,128)(2,1)}) custom-call(s32[4,512]{1,0:T(4,128)} %refs_0_.2, f32[4,512]{1,0:T(4,128)} %refs_1_.1, s32[1,32]{1,0:T(1,128)} %refs_2_.2, bf16[1,2,512]{2,1,0:T(2,128)(2,1)} %refs_3_.1, bf16[1,64,512]{2,1,0:T(8,128)(2,1)} %refs_4_.1), custom_call_target="tpu_custom_call" | custom-call | flops 20000000 | bytes 2000000 | tf_op jit(solution)/shard_map/pack/pallas_call | solution.py:40
  2.2 5.0 %collective-permute-start.2 = (bf16[80,512]{1,0:T(8,128)(2,1)}, bf16[80,512]{1,0:T(8,128)(2,1)S(1)}, u32[]{:S(2)}, u32[]{:S(2)}) collective-permute-start(bf16[80,512]{1,0:T(8,128)(2,1)} %get-tuple-element.78), channel_id=1, source_target_pairs={{0,6},{1,7},{2,4},{3,5},{4,2},{5,3},{6,0},{7,1},{8,14},{9,15},{10,... | collective-permute-start | bytes 245768 | tf_op jit(solution)/shard_map/ppermute | solution.py:851
  7.3 0.6 %collective-permute-start = (bf16[80,512]{1,0:T(8,128)(2,1)}, bf16[80,512]{1,0:T(8,128)(2,1)S(1)}, u32[]{:S(2)}, u32[]{:S(2)}) collective-permute-start(bf16[80,512]{1,0:T(8,128)(2,1)} %get-tuple-element.78), channel_id=1, source_target_pairs={{0,2},{1,3},{2,0},{3,1},{4,6},{5,7},{6,4},{7,5},{8,10},{9,11},{10,... | collective-permute-start | bytes 245768 | tf_op jit(solution)/shard_map/ppermute | solution.py:851
  7.8 2.4 %collective-permute-start.4 = (bf16[1,64,512]{2,1,0:T(8,128)(2,1)}, bf16[1,64,512]{2,1,0:T(8,128)(2,1)S(1)}, u32[]{:S(2)}, u32[]{:S(2)}) collective-permute-start(bf16[1,64,512]{2,1,0:T(8,128)(2,1)} %refs_0_.3), channel_id=1, source_target_pairs={{0,4},{1,5},{2,6},{3,7},{4,0},{5,1},{6,2},{7,3},{8,12},{9,13},{10,... | collective-permute-start | bytes 196616 | tf_op jit(solution)/shard_map/ppermute | solution.py:851
  10.2 2.0 %collective-permute-start.3 = (bf16[1,64,512]{2,1,0:T(8,128)(2,1)}, bf16[1,64,512]{2,1,0:T(8,128)(2,1)S(1)}, u32[]{:S(2)}, u32[]{:S(2)}) collective-permute-start(bf16[1,64,512]{2,1,0:T(8,128)(2,1)} %refs_0_.3), channel_id=1, source_target_pairs={{0,2},{1,3},{2,0},{3,1},{4,6},{5,7},{6,4},{7,5},{8,10},{9,11},{10,... | collective-permute-start | bytes 196616 | tf_op jit(solution)/shard_map/ppermute | solution.py:851
  12.2 2.4 %collective-permute-start.5 = (bf16[1,64,512]{2,1,0:T(8,128)(2,1)}, bf16[1,64,512]{2,1,0:T(8,128)(2,1)S(1)}, u32[]{:S(2)}, u32[]{:S(2)}) collective-permute-start(bf16[1,64,512]{2,1,0:T(8,128)(2,1)} %refs_0_.3), channel_id=1, source_target_pairs={{0,6},{1,7},{2,4},{3,5},{4,2},{5,3},{6,0},{7,1},{8,14},{9,15},{10,... | collective-permute-start | bytes 196616 | tf_op jit(solution)/shard_map/ppermute | solution.py:851
  14.6 0.9 %copy-done = bf16[80,512]{1,0:T(8,128)(2,1)S(1)} copy-done((bf16[80,512]{1,0:T(8,128)(2,1)S(1)}, bf16[80,512]{1,0:T(8,128)(2,1)}, u32[]{:S(2)}) %copy-start) | copy-done | bytes 81944
  15.5 0.9 %copy-done.2 = bf16[128,330]{0,1:T(8,128)(2,1)S(1)} copy-done((bf16[128,330]{0,1:T(8,128)(2,1)S(1)}, bf16[128,330]{0,1:T(8,128)(2,1)}, u32[]{:S(2)}) %copy-start.2) | copy-done | bytes 84504
  16.4 0.8 %copy-done.4 = bf16[64,330]{1,0:T(8,128)(2,1)S(1)} copy-done((bf16[64,330]{1,0:T(8,128)(2,1)S(1)}, bf16[64,330]{1,0:T(8,128)(2,1)}, u32[]{:S(2)}) %copy-start.4) | copy-done | bytes 42264
  17.2 0.3 order.1
  17.5 2.0 %build.1 = (bf16[4,512,512]{2,1,0:T(8,128)(2,1)S(1)}, bf16[4,512,512]{2,1,0:T(8,128)(2,1)S(1)}, bf16[4,32,512]{2,1,0:T(8,128)(2,1)S(1)}, bf16[4,128,512]{2,1,0:T...) custom-call(bf16[128,400]{1,0:T(8,128)(2,1)S(1)} %get-tuple-element., ...), custom_call_target="tpu_custom_call" | custom-call | flops 20000000 | bytes 2000000 | tf_op jit(solution)/shard_map/build/pallas_call | solution.py:40
  19.7 0.8 %local_a.1 = (f32[4,80,512]{2,1,0:T(8,128)S(1)}, f32[4,80,512]{2,1,0:T(8,128)S(1)}) custom-call(bf16[4,512,512]{2,1,0:T(8,128)(2,1)S(1)} %get-tuple-element.79.refs_0_, bf16[4,512,512]{2,1,0:T(8,128)(2,1)S(1)} %get-tuple-element.80.refs_1_, bf16[4,80,512]{2,1,0:T(8,128)(2,1)S(1)} %get-tuple-element.86.refs_2_.refs_3_.refs_6_, ...), custom_call_target="tpu_custom_call" | custom-call | flops 20000000 | bytes 2000000 | tf_op jit(solution)/shard_map/local_a/pallas_call | solution.py:40
  20.5 0.3 collective-permute-done.6.refs_4_
  20.9 0.7 %chip_a.1 = (bf16[4,80,512]{2,1,0:T(8,128)(2,1)S(1)}, bf16[4,80,512]{2,1,0:T(8,128)(2,1)S(1)}, f32[4,1,512]{2,1,0:T(1,128)S(1)}, f32[4,1,512]{2,1,0:T(1,128)S(1)}, bf16[160,128]{1,0:T(8,128)(2,1)S(1)}) custom-call(bf16[1,64,512]{2,1,0:T(8,128)(2,1)S(1)} %collective-permute-done.3.refs_0_.refs_1_, ...), custom_call_target="tpu_custom_call" | custom-call | flops 20000000 | bytes 2000000 | tf_op jit(solution)/shard_map/chip_a/pallas_call | solution.py:40
  21.6 0.2 collective-permute-start.7
  21.8 0.8 %local_b.1 = (f32[4,80,512]{2,1,0:T(8,128)S(1)}, f32[4,80,512]{2,1,0:T(8,128)S(1)}) custom-call(bf16[4,512,512]{2,1,0:T(8,128)(2,1)S(1)} %get-tuple-element.79.refs_0_, bf16[4,512,512]{2,1,0:T(8,128)(2,1)S(1)} %get-tuple-element.80.refs_1_, bf16[4,80,512]{2,1,0:T(8,128)(2,1)S(1)} %get-tuple-element.91.refs_2_.refs_8_, ...), custom_call_target="tpu_custom_call" | custom-call | flops 20000000 | bytes 2000000 | tf_op jit(solution)/shard_map/local_b/pallas_call | solution.py:40
  22.6 0.2 collective-permute-done.7.refs_1_
  22.8 1.5 %chip_b.1 = (bf16[4,400,512]{2,1,0:T(8,128)(2,1)S(1)}, f32[4,64,512]{2,1,0:T(8,128)S(1)}, f32[4,64,512]{2,1,0:T(8,128)S(1)}, bf16[4,64,512]{2,1,0:T(8,128)(2,1)S(1)}, bf16[128,128]{1,0:T(8,128)(2,1)S(1)}) custom-call(bf16[160,128]{1,0:T(8,128)(2,1)S(1)} %get-tuple-element.89.refs_0_, bf16[160,128]{1,0:T(8,128)(2,1)S(1)} %collective-permute-done.7.refs_1_, ...), custom_call_target="tpu_custom_call" | custom-call | flops 20000000 | bytes 2000000 | tf_op jit(solution)/shard_map/chip_b/pallas_call | solution.py:40
  24.3 0.2 collective-permute-start.8
  24.6 0.8 %local_c1.1 = (f32[4,64,512]{2,1,0:T(8,128)S(1)}, f32[4,64,512]{2,1,0:T(8,128)S(1)}) custom-call(bf16[4,512,512]{2,1,0:T(8,128)(2,1)S(1)} %get-tuple-element.79.refs_0_, bf16[4,512,512]{2,1,0:T(8,128)(2,1)S(1)} %get-tuple-element.80.refs_1_, bf16[4,64,512]{2,1,0:T(8,128)(2,1)S(1)} %get-tuple-element.97.refs_2_.refs_3_.refs_10_, ...), custom_call_target="tpu_custom_call" | custom-call | flops 20000000 | bytes 2000000 | tf_op jit(solution)/shard_map/local_c1/pallas_call | solution.py:40
  25.4 0.2 collective-permute-done.8.refs_1_
  25.6 0.6 %chip_c1.1 = (bf16[4,64,512]{2,1,0:T(8,128)(2,1)S(1)}, bf16[4,64,512]{2,1,0:T(8,128)(2,1)S(1)}, bf16[128,128]{1,0:T(8,128)(2,1)S(1)}) custom-call(bf16[128,128]{1,0:T(8,128)(2,1)S(1)} %get-tuple-element.96.refs_0_, bf16[128,128]{1,0:T(8,128)(2,1)S(1)} %collective-permute-done.8.refs_1_, ...), custom_call_target="tpu_custom_call" | custom-call | flops 20000000 | bytes 2000000 | tf_op jit(solution)/shard_map/chip_c1/pallas_call | solution.py:40
  26.2 0.2 collective-permute-start.9
  26.4 0.8 %local_c2.1 = (f32[4,64,512]{2,1,0:T(8,128)S(1)}, f32[4,64,512]{2,1,0:T(8,128)S(1)}) custom-call(bf16[4,512,512]{2,1,0:T(8,128)(2,1)S(1)} %get-tuple-element.79.refs_0_, bf16[4,512,512]{2,1,0:T(8,128)(2,1)S(1)} %get-tuple-element.80.refs_1_, bf16[4,64,512]{2,1,0:T(8,128)(2,1)S(1)} %get-tuple-element.102.refs_2_.refs_12_, ...), custom_call_target="tpu_custom_call" | custom-call | flops 20000000 | bytes 2000000 | tf_op jit(solution)/shard_map/local_c2/pallas_call | solution.py:40
  27.4 2.3 %chip_c2.1 = (bf16[4,400,512]{2,1,0:T(8,128)(2,1)S(1)}, bf16[4,64,512]{2,1,0:T(8,128)(2,1)S(1)}, bf16[4,64,512]{2,1,0:T(8,128)(2,1)S(1)}, bf16[4,64,512]{2,1,0:T...) custom-call(bf16[1,64,512]{2,1,0:T(8,128)(2,1)S(1)} %copy-done.3, ...), custom_call_target="tpu_custom_call" | custom-call | flops 20000000 | bytes 2000000 | tf_op jit(solution)/shard_map/chip_c2/pallas_call | solution.py:40
  29.8 0.3 collective-permute-start.10
  30.0 1.7 %local_d1.1 = (f32[4,64,512]{2,1,0:T(8,128)S(1)}, f32[4,64,512]{2,1,0:T(8,128)S(1)}, bf16[64,384]{1,0:T(8,128)(2,1)S(1)}) custom-call(bf16[4,512,512]{2,1,0:T(8,128)(2,1)S(1)} %get-tuple-element.79.refs_0_, bf16[4,512,512]{2,1,0:T(8,128)(2,1)S(1)} %get-tuple-element.80.refs_1_, bf16[4,64,512]{2,1,0:T(8,128)(2,1)S(1)} %get-tuple-element.109.refs_2_, ...), custom_call_target="tpu_custom_call" | custom-call | flops 20000000 | bytes 2000000 | tf_op jit(solution)/shard_map/local_d1/pallas_call | solution.py:40
  31.7 0.6 %chip_d1.1 = (bf16[4,64,512]{2,1,0:T(8,128)(2,1)S(1)}, bf16[4,64,512]{2,1,0:T(8,128)(2,1)S(1)}, bf16[128,128]{1,0:T(8,128)(2,1)S(1)}) custom-call(bf16[128,128]{1,0:T(8,128)(2,1)S(1)} %get-tuple-element.108.refs_0_, bf16[128,128]{1,0:T(8,128)(2,1)S(1)} %collective-permute-done.10.refs_1_, ...), custom_call_target="tpu_custom_call" | custom-call | flops 20000000 | bytes 2000000 | tf_op jit(solution)/shard_map/chip_d1/pallas_call | solution.py:40
  32.3 0.4 collective-permute-start.11
  32.7 0.8 %local_d2.1.refs_6_ = f32[4,64,512]{2,1,0:T(8,128)S(1)} custom-call(bf16[4,512,512]{2,1,0:T(8,128)(2,1)S(1)} %get-tuple-element.79.refs_0_, bf16[4,512,512]{2,1,0:T(8,128)(2,1)S(1)} %get-tuple-element.80.refs_1_, bf16[4,64,512]{2,1,0:T(8,128)(2,1)S(1)} %get-tuple-element.118.refs_2_, bf16[4,64,512]{2,1,0:T(8,128)(2,1)S(1)} %get-tuple-element.119.refs_3_, ...), custom_call_target="tpu_custom_call" | custom-call | flops 20000000 | bytes 2000000 | tf_op jit(solution)/shard_map/local_d2/pallas_call | solution.py:40
  33.6 1.6 %chip_d2.1 = (bf16[4,128,512]{2,1,0:T(8,128)(2,1)S(1)}, bf16[4,64,512]{2,1,0:T(8,128)(2,1)S(1)}, bf16[4,64,512]{2,1,0:T(8,128)(2,1)S(1)}, bf16[4,64,512]{2,1,0:T...) custom-call(bf16[128,128]{1,0:T(8,128)(2,1)S(1)} %get-tuple-element.117.r, ...), custom_call_target="tpu_custom_call" | custom-call | flops 20000000 | bytes 2000000 | tf_op jit(solution)/shard_map/chip_d2/pallas_call | solution.py:40
  35.2 1.0 %grads.1 = (bf16[96,384]{1,0:T(8,128)(2,1)S(1)}, bf16[96,384]{1,0:T(8,128)(2,1)S(1)}) custom-call(bf16[4,128,512]{2,1,0:T(8,128)(2,1)S(1)} %get-tuple-element.128.refs_0_, bf16[4,400,512]{2,1,0:T(8,128)(2,1)S(1)} %get-tuple-element.105.refs_17_.refs_9_.refs_1_, bf16[64,384]{1,0:T(8,128)(2,1)S(1)} %get-tuple-element.129.refs_2_), custom_call_target="tpu_custom_call" | custom-call | flops 20000000 | bytes 2000000 | tf_op jit(solution)/shard_map/grads/pallas_call | solution.py:40
  36.2 0.4 collective-permute-start.13
  36.6 0.2 collective-permute-start.12
  36.8 0.8 %local_e1.1 = (f32[4,64,512]{2,1,0:T(8,128)S(1)}, f32[4,64,512]{2,1,0:T(8,128)S(1)}) custom-call(bf16[4,512,512]{2,1,0:T(8,128)(2,1)S(1)} %get-tuple-element.79.refs_0_, bf16[4,512,512]{2,1,0:T(8,128)(2,1)S(1)} %get-tuple-element.80.refs_1_, bf16[4,64,512]{2,1,0:T(8,128)(2,1)S(1)} %get-tuple-element.124.refs_2_, ...), custom_call_target="tpu_custom_call" | custom-call | flops 20000000 | bytes 2000000 | tf_op jit(solution)/shard_map/local_e1/pallas_call | solution.py:40
  37.6 0.2 collective-permute-done.12.refs_1_.refs_2_
  37.8 2.5 %collective-permute-start.17 = (bf16[96,384]{1,0:T(8,128)(2,1)S(1)}, bf16[96,384]{1,0:T(8,128)(2,1)S(1)}, u32[]{:S(2)}, u32[]{:S(2)}) collective-permute-start(bf16[96,384]{1,0:T(8,128)(2,1)S(1)} %get-tuple-element.140), channel_id=1, source_target_pairs={{0,24},{8,16},{16,8},{24,0},{1,25},{9,17},{17,9},{25,1},{2,26},{10... | collective-permute-start | bytes 221192 | tf_op jit(solution)/shard_map/ppermute | solution.py:851
  40.3 0.5 %collective-permute-start.16 = (bf16[96,384]{1,0:T(8,128)(2,1)S(1)}, bf16[96,384]{1,0:T(8,128)(2,1)S(1)}, u32[]{:S(2)}, u32[]{:S(2)}) collective-permute-start(bf16[96,384]{1,0:T(8,128)(2,1)S(1)} %get-tuple-element.140), channel_id=1, source_target_pairs={{0,16},{8,24},{16,0},{24,8},{1,17},{9,25},{17,1},{25,9},{2,18},{10... | collective-permute-start | bytes 221192 | tf_op jit(solution)/shard_map/ppermute | solution.py:851
  40.8 0.5 %collective-permute-start.15 = (bf16[96,384]{1,0:T(8,128)(2,1)S(1)}, bf16[96,384]{1,0:T(8,128)(2,1)S(1)}, u32[]{:S(2)}, u32[]{:S(2)}) collective-permute-start(bf16[96,384]{1,0:T(8,128)(2,1)S(1)} %get-tuple-element.140), channel_id=1, source_target_pairs={{0,8},{8,0},{16,24},{24,16},{1,9},{9,1},{17,25},{25,17},{2,10},{10... | collective-permute-start | bytes 221192 | tf_op jit(solution)/shard_map/ppermute | solution.py:851
  41.4 0.6 %chip_e1.1 = (bf16[4,64,512]{2,1,0:T(8,128)(2,1)S(1)}, bf16[4,64,512]{2,1,0:T(8,128)(2,1)S(1)}, bf16[128,128]{1,0:T(8,128)(2,1)S(1)}) custom-call(bf16[96,384]{1,0:T(8,128)(2,1)S(1)} %get-tuple-element.132.refs_0_.refs_1_, bf16[128,128]{1,0:T(8,128)(2,1)S(1)} %get-tuple-element.127.refs_1_, bf16[128,128]{1,0:T(8,128)(2,1)S(1)} %collective-permute-done.12.refs_1_.refs_2_, ...), custom_call_target="tpu_custom_call" | custom-call | flops 20000000 | bytes 2000000 | tf_op jit(solution)/shard_map/chip_e1/pallas_call | solution.py:40
  42.1 0.3 local_e2.1.refs_6_
  42.4 0.9 %collective-permute-done.14.refs_1_ = bf16[128,128]{1,0:T(8,128)(2,1)S(1)} collective-permute-done((bf16[128,128]{1,0:T(8,128)(2,1)S(1)}, bf16[128,128]{1,0:T(8,128)(2,1)S(1)}, u32[]{:S(2)}, u32[]{:S(2)}) %collective-permute-start.14) | collective-permute-done | bytes 32800 | tf_op jit(solution)/shard_map/ppermute | solution.py:851
  43.2 0.8 %chip_e2.1.refs_0_ = bf16[1,64,512]{2,1,0:T(8,128)(2,1)} custom-call(bf16[128,128]{1,0:T(8,128)(2,1)S(1)} %get-tuple-element.136.refs_0_, bf16[128,128]{1,0:T(8,128)(2,1)S(1)} %collective-permute-done.14.refs_1_, bf16[4,32,512]{2,1,0:T(8,128)(2,1)S(1)} %get-tuple-element.82.refs_5_.refs_2_.refs_6_.refs_3_, ...), custom_call_target="tpu_custom_call" | custom-call | flops 20000000 | bytes 2000000 | tf_op jit(solution)/shard_map/chip_e2/pallas_call | solution.py:40
  44.1 0.7 %collective-permute-done.16.refs_3_ = bf16[96,384]{1,0:T(8,128)(2,1)S(1)} collective-permute-done((bf16[96,384]{1,0:T(8,128)(2,1)S(1)}, bf16[96,384]{1,0:T(8,128)(2,1)S(1)}, u32[]{:S(2)}, u32[]{:S(2)}) %collective-permute-start.16) | collective-permute-done | bytes 73760 | tf_op jit(solution)/shard_map/ppermute | solution.py:851
  44.7 0.5 collective-permute-done.15.refs_2_
  45.2 0.8 %copy-done.1 = bf16[1,64,512]{2,1,0:T(8,128)(2,1)S(1)} copy-done((bf16[1,64,512]{2,1,0:T(8,128)(2,1)S(1)}, bf16[1,64,512]{2,1,0:T(8,128)(2,1)}, u32[]{:S(2)}) %copy-start.1) | copy-done | bytes 65560
  46.1 1.3 %collective-permute-done.18.refs_1_ = bf16[96,384]{1,0:T(8,128)(2,1)S(1)} collective-permute-done((bf16[96,384]{1,0:T(8,128)(2,1)S(1)}, bf16[96,384]{1,0:T(8,128)(2,1)S(1)}, u32[]{:S(2)}, u32[]{:S(2)}) %collective-permute-start.18) | collective-permute-done | bytes 73760 | tf_op jit(solution)/shard_map/ppermute | solution.py:851
  47.4 1.0 %end.1 = (f32[330,128]{1,0:T(8,128)}, f32[1,128]{1,0:T(1,128)}, f32[64,330]{1,0:T(8,128)}, f32[1,64]{1,0:T(1,128)}) custom-call(bf16[96,384]{1,0:T(8,128)(2,1)S(1)} %get-tuple-element.141.refs_0_, bf16[96,384]{1,0:T(8,128)(2,1)S(1)} %collective-permute-done.18.refs_1_), custom_call_target="tpu_custom_call" | custom-call | flops 20000000 | bytes 2000000 | tf_op jit(solution)/shard_map/end/pallas_call | solution.py:40
  (27 shorter events, 0.5 us)
Async XLA Ops:
  2.2 10.0 %collective-permute-start.2 = (bf16[80,512]{1,0:T(8,128)(2,1)}, bf16[80,512]{1,0:T(8,128)(2,1)S(1)}, u32[]{:S(2)}, u32[]{:S(2)}) collective-permute-start(bf16[80,512]{1,0:T(8,128)(2,1)} %get-tuple-element.78), channel_id=1, source_target_pairs={{0,6},{1,7},{2,4},{3,5},{4,2},{5,3},{6,0},{7,1},{8,14},{9,15},{10,... | collective-permute-start | bytes 245768 | tf_op jit(solution)/shard_map/ppermute | solution.py:851
  7.3 10.2 %collective-permute-start.1 = (bf16[80,512]{1,0:T(8,128)(2,1)}, bf16[80,512]{1,0:T(8,128)(2,1)S(1)}, u32[]{:S(2)}, u32[]{:S(2)}) collective-permute-start(bf16[80,512]{1,0:T(8,128)(2,1)} %get-tuple-element.78), channel_id=1, source_target_pairs={{0,4},{1,5},{2,6},{3,7},{4,0},{5,1},{6,2},{7,3},{8,12},{9,13},{10,... | collective-permute-start | bytes 245768 | tf_op jit(solution)/shard_map/ppermute | solution.py:851
  7.3 10.2 %collective-permute-start = (bf16[80,512]{1,0:T(8,128)(2,1)}, bf16[80,512]{1,0:T(8,128)(2,1)S(1)}, u32[]{:S(2)}, u32[]{:S(2)}) collective-permute-start(bf16[80,512]{1,0:T(8,128)(2,1)} %get-tuple-element.78), channel_id=1, source_target_pairs={{0,2},{1,3},{2,0},{3,1},{4,6},{5,7},{6,4},{7,5},{8,10},{9,11},{10,... | collective-permute-start | bytes 245768 | tf_op jit(solution)/shard_map/ppermute | solution.py:851
  7.8 12.7 %collective-permute-start.4 = (bf16[1,64,512]{2,1,0:T(8,128)(2,1)}, bf16[1,64,512]{2,1,0:T(8,128)(2,1)S(1)}, u32[]{:S(2)}, u32[]{:S(2)}) collective-permute-start(bf16[1,64,512]{2,1,0:T(8,128)(2,1)} %refs_0_.3), channel_id=1, source_target_pairs={{0,4},{1,5},{2,6},{3,7},{4,0},{5,1},{6,2},{7,3},{8,12},{9,13},{10,... | collective-permute-start | bytes 196616 | tf_op jit(solution)/shard_map/ppermute | solution.py:851
  10.2 10.3 %collective-permute-start.3 = (bf16[1,64,512]{2,1,0:T(8,128)(2,1)}, bf16[1,64,512]{2,1,0:T(8,128)(2,1)S(1)}, u32[]{:S(2)}, u32[]{:S(2)}) collective-permute-start(bf16[1,64,512]{2,1,0:T(8,128)(2,1)} %refs_0_.3), channel_id=1, source_target_pairs={{0,2},{1,3},{2,0},{3,1},{4,6},{5,7},{6,4},{7,5},{8,10},{9,11},{10,... | collective-permute-start | bytes 196616 | tf_op jit(solution)/shard_map/ppermute | solution.py:851
  12.2 8.3 %collective-permute-start.5 = (bf16[1,64,512]{2,1,0:T(8,128)(2,1)}, bf16[1,64,512]{2,1,0:T(8,128)(2,1)S(1)}, u32[]{:S(2)}, u32[]{:S(2)}) collective-permute-start(bf16[1,64,512]{2,1,0:T(8,128)(2,1)} %refs_0_.3), channel_id=1, source_target_pairs={{0,6},{1,7},{2,4},{3,5},{4,2},{5,3},{6,0},{7,1},{8,14},{9,15},{10,... | collective-permute-start | bytes 196616 | tf_op jit(solution)/shard_map/ppermute | solution.py:851
  14.6 0.9 %copy-start = (bf16[80,512]{1,0:T(8,128)(2,1)S(1)}, bf16[80,512]{1,0:T(8,128)(2,1)}, u32[]{:S(2)}) copy-start(bf16[80,512]{1,0:T(8,128)(2,1)} %get-tuple-element.76.refs_0_.refs_1_) | copy-start | bytes 245764
  15.5 0.9 %copy-start.2 = (bf16[128,330]{0,1:T(8,128)(2,1)S(1)}, bf16[128,330]{0,1:T(8,128)(2,1)}, u32[]{:S(2)}) copy-start(bf16[128,330]{0,1:T(8,128)(2,1)} %param.13) | copy-start | bytes 253444
  16.4 0.8 %copy-start.4 = (bf16[64,330]{1,0:T(8,128)(2,1)S(1)}, bf16[64,330]{1,0:T(8,128)(2,1)}, u32[]{:S(2)}) copy-start(bf16[64,330]{1,0:T(8,128)(2,1)} %refs_2_.3) | copy-start | bytes 126724
  19.6 1.3 %collective-permute-start.6 = (bf16[160,128]{1,0:T(8,128)(2,1)S(1)}, bf16[160,128]{1,0:T(8,128)(2,1)S(1)}, u32[]{:S(2)}, u32[]{:S(2)}) collective-permute-start(bf16[160,128]{1,0:T(8,128)(2,1)S(1)} %get-tuple-element.81.refs_3_), channel_id=1, source_target_pairs={{0,1},{1,0},{2,3},{3,2},{4,5},{5,4},{6,7},{7,6},{8,9},{9,8},{10,11... | collective-permute-start | bytes 122888 | tf_op jit(solution)/shard_map/ppermute | solution.py:851
  21.6 1.3 %collective-permute-start.7 = (bf16[160,128]{1,0:T(8,128)(2,1)S(1)}, bf16[160,128]{1,0:T(8,128)(2,1)S(1)}, u32[]{:S(2)}, u32[]{:S(2)}) collective-permute-start(bf16[160,128]{1,0:T(8,128)(2,1)S(1)} %get-tuple-element.89.refs_0_), channel_id=1, source_target_pairs={{0,1},{1,0},{2,3},{3,2},{4,5},{5,4},{6,7},{7,6},{8,9},{9,8},{10,11... | collective-permute-start | bytes 122888 | tf_op jit(solution)/shard_map/ppermute | solution.py:851
  21.8 1.1 %copy-start.5 = (f32[128]{0:T(128)S(1)}, f32[128]{0:T(128)}, u32[]{:S(2)}) copy-start(f32[128]{0:T(128)} %param.14) | copy-start | bytes 1540
  24.3 1.3 %collective-permute-start.8 = (bf16[128,128]{1,0:T(8,128)(2,1)S(1)}, bf16[128,128]{1,0:T(8,128)(2,1)S(1)}, u32[]{:S(2)}, u32[]{:S(2)}) collective-permute-start(bf16[128,128]{1,0:T(8,128)(2,1)S(1)} %get-tuple-element.96.refs_0_), channel_id=1, source_target_pairs={{0,1},{1,0},{2,3},{3,2},{4,5},{5,4},{6,7},{7,6},{8,9},{9,8},{10,11... | collective-permute-start | bytes 98312 | tf_op jit(solution)/shard_map/ppermute | solution.py:851
  26.2 1.3 %collective-permute-start.9 = (bf16[128,128]{1,0:T(8,128)(2,1)S(1)}, bf16[128,128]{1,0:T(8,128)(2,1)S(1)}, u32[]{:S(2)}, u32[]{:S(2)}) collective-permute-start(bf16[128,128]{1,0:T(8,128)(2,1)S(1)} %get-tuple-element.100.refs_4_), channel_id=1, source_target_pairs={{0,1},{1,0},{2,3},{3,2},{4,5},{5,4},{6,7},{7,6},{8,9},{9,8},{10,11... | collective-permute-start | bytes 98312 | tf_op jit(solution)/shard_map/ppermute | solution.py:851
  26.4 1.0 %copy-start.3 = (bf16[1,64,512]{2,1,0:T(8,128)(2,1)S(1)}, bf16[1,64,512]{2,1,0:T(8,128)(2,1)}, u32[]{:S(2)}) copy-start(bf16[1,64,512]{2,1,0:T(8,128)(2,1)} %refs_0_.3) | copy-start | bytes 196612
  26.4 1.0 %copy-start.6 = (f32[64]{0:T(128)S(1)}, f32[64]{0:T(128)}, u32[]{:S(2)}) copy-start(f32[64]{0:T(128)} %param.16) | copy-start | bytes 772
  29.8 1.9 %collective-permute-start.10 = (bf16[128,128]{1,0:T(8,128)(2,1)S(1)}, bf16[128,128]{1,0:T(8,128)(2,1)S(1)}, u32[]{:S(2)}, u32[]{:S(2)}) collective-permute-start(bf16[128,128]{1,0:T(8,128)(2,1)S(1)} %get-tuple-element.108.refs_0_), channel_id=1, source_target_pairs={{0,1},{1,0},{2,3},{3,2},{4,5},{5,4},{6,7},{7,6},{8,9},{9,8},{10,11... | collective-permute-start | bytes 98312 | tf_op jit(solution)/shard_map/ppermute | solution.py:851
  32.3 1.3 %collective-permute-start.11 = (bf16[128,128]{1,0:T(8,128)(2,1)S(1)}, bf16[128,128]{1,0:T(8,128)(2,1)S(1)}, u32[]{:S(2)}, u32[]{:S(2)}) collective-permute-start(bf16[128,128]{1,0:T(8,128)(2,1)S(1)} %get-tuple-element.117.refs_0_), channel_id=1, source_target_pairs={{0,1},{1,0},{2,3},{3,2},{4,5},{5,4},{6,7},{7,6},{8,9},{9,8},{10,11... | collective-permute-start | bytes 98312 | tf_op jit(solution)/shard_map/ppermute | solution.py:851
  36.2 1.6 %collective-permute-start.13 = (bf16[96,384]{1,0:T(8,128)(2,1)S(1)}, bf16[96,384]{1,0:T(8,128)(2,1)S(1)}, u32[]{:S(2)}, u32[]{:S(2)}) collective-permute-start(bf16[96,384]{1,0:T(8,128)(2,1)S(1)} %get-tuple-element.131), channel_id=1, source_target_pairs={{0,1},{1,0},{2,3},{3,2},{4,5},{5,4},{6,7},{7,6},{8,9},{9,8},{10,11... | collective-permute-start | bytes 221192 | tf_op jit(solution)/shard_map/ppermute | solution.py:851
  36.6 1.2 %collective-permute-start.12 = (bf16[128,128]{1,0:T(8,128)(2,1)S(1)}, bf16[128,128]{1,0:T(8,128)(2,1)S(1)}, u32[]{:S(2)}, u32[]{:S(2)}) collective-permute-start(bf16[128,128]{1,0:T(8,128)(2,1)S(1)} %get-tuple-element.127.refs_1_), channel_id=1, source_target_pairs={{0,1},{1,0},{2,3},{3,2},{4,5},{5,4},{6,7},{7,6},{8,9},{9,8},{10,11... | collective-permute-start | bytes 98312 | tf_op jit(solution)/shard_map/ppermute | solution.py:851
  37.8 6.2 %collective-permute-start.17 = (bf16[96,384]{1,0:T(8,128)(2,1)S(1)}, bf16[96,384]{1,0:T(8,128)(2,1)S(1)}, u32[]{:S(2)}, u32[]{:S(2)}) collective-permute-start(bf16[96,384]{1,0:T(8,128)(2,1)S(1)} %get-tuple-element.140), channel_id=1, source_target_pairs={{0,24},{8,16},{16,8},{24,0},{1,25},{9,17},{17,9},{25,1},{2,26},{10... | collective-permute-start | bytes 221192 | tf_op jit(solution)/shard_map/ppermute | solution.py:851
  40.3 4.4 %collective-permute-start.16 = (bf16[96,384]{1,0:T(8,128)(2,1)S(1)}, bf16[96,384]{1,0:T(8,128)(2,1)S(1)}, u32[]{:S(2)}, u32[]{:S(2)}) collective-permute-start(bf16[96,384]{1,0:T(8,128)(2,1)S(1)} %get-tuple-element.140), channel_id=1, source_target_pairs={{0,16},{8,24},{16,0},{24,8},{1,17},{9,25},{17,1},{25,9},{2,18},{10... | collective-permute-start | bytes 221192 | tf_op jit(solution)/shard_map/ppermute | solution.py:851
  40.8 4.4 %collective-permute-start.15 = (bf16[96,384]{1,0:T(8,128)(2,1)S(1)}, bf16[96,384]{1,0:T(8,128)(2,1)S(1)}, u32[]{:S(2)}, u32[]{:S(2)}) collective-permute-start(bf16[96,384]{1,0:T(8,128)(2,1)S(1)} %get-tuple-element.140), channel_id=1, source_target_pairs={{0,8},{8,0},{16,24},{24,16},{1,9},{9,1},{17,25},{25,17},{2,10},{10... | collective-permute-start | bytes 221192 | tf_op jit(solution)/shard_map/ppermute | solution.py:851
  42.0 1.3 %collective-permute-start.14 = (bf16[128,128]{1,0:T(8,128)(2,1)S(1)}, bf16[128,128]{1,0:T(8,128)(2,1)S(1)}, u32[]{:S(2)}, u32[]{:S(2)}) collective-permute-start(bf16[128,128]{1,0:T(8,128)(2,1)S(1)} %get-tuple-element.136.refs_0_), channel_id=1, source_target_pairs={{0,1},{1,0},{2,3},{3,2},{4,5},{5,4},{6,7},{7,6},{8,9},{9,8},{10,11... | collective-permute-start | bytes 98312 | tf_op jit(solution)/shard_map/ppermute | solution.py:851
  45.2 0.8 %copy-start.1 = (bf16[1,64,512]{2,1,0:T(8,128)(2,1)S(1)}, bf16[1,64,512]{2,1,0:T(8,128)(2,1)}, u32[]{:S(2)}) copy-start(bf16[1,64,512]{2,1,0:T(8,128)(2,1)} %chip_e2.1.refs_0_) | copy-start | bytes 196612
  46.1 1.3 %collective-permute-start.18 = (bf16[96,384]{1,0:T(8,128)(2,1)S(1)}, bf16[96,384]{1,0:T(8,128)(2,1)S(1)}, u32[]{:S(2)}, u32[]{:S(2)}) collective-permute-start(bf16[96,384]{1,0:T(8,128)(2,1)S(1)} %get-tuple-element.142), channel_id=1, source_target_pairs={{0,1},{1,0},{2,3},{3,2},{4,5},{5,4},{6,7},{7,6},{8,9},{9,8},{10,11... | collective-permute-start | bytes 221192 | tf_op jit(solution)/shard_map/ppermute | solution.py:851

commit v3 on v0

--- a/solution.py
+++ b/solution.py
@@ -35,18 +35,18 @@
     return jnp.sum(jnp.where(iota((k, k), 0) == iota((k, k), 1), spread, 0.0), axis=1, keepdims=True)
 
 
-def run(kernel, name, outs, *args, scratch=(), flops=20_000_000):
+def run(kernel, name, outs, *args, scratch=(), flops=20_000_000, vmem=24, after=()):
     whole = pl.BlockSpec(memory_space=pltpu.VMEM)
     return pl.pallas_call(
-        kernel,
+        lambda *refs: kernel(*refs[len(after) :]),
         name=name,
         out_shape=[jax.ShapeDtypeStruct(shape, kind) for shape, kind in outs],
-        in_specs=[whole] * len(args),
+        in_specs=[pl.BlockSpec(memory_space=pl.ANY)] * len(after) + [whole] * len(args),
         out_specs=[whole] * len(outs),
         scratch_shapes=list(scratch),
-        compiler_params=pltpu.CompilerParams(vmem_limit_bytes=24 * 1024 * 1024),
+        compiler_params=pltpu.CompilerParams(vmem_limit_bytes=vmem * 1024 * 1024),
         cost_estimate=pl.CostEstimate(flops=flops, bytes_accessed=2_000_000, transcendentals=0),
-    )(*args)
+    )(*after, *args)
 
 
 def prep_kernel(cap, nb, w, rows, readings, previous, e, s, b, pay):
@@ -397,7 +397,7 @@
     cb[...] = bias[:, 2 * hid :]
 
 
-def body(
+def spread_body(
     readings,
     previous,
     upstream,
@@ -514,6 +514,494 @@
     return state_grad, grad_gw, grad_gb[0], grad_cw, grad_cb[0]
 
 
+def pack_kernel(own, nb, w, rows, readings, previous, tail):
+    degree = nb.shape[0]
+    nh = rows.shape[1]
+    hid = previous.shape[1]
+    fin = readings.shape[1]
+    tail[...] = jnp.zeros_like(tail)
+    tail[:fin, :] = readings[0].astype(F32)
+    high = lax.shift_right_logical(nb[...], 5)
+    tail[fin : fin + degree, :] = high.astype(F32)
+    tail[fin + degree : fin + 2 * degree, :] = (nb[...] - high * 32).astype(F32)
+    tail[fin + 2 * degree : fin + 3 * degree, :] = w[...]
+    at = fin + 3 * degree
+    high = lax.shift_right_logical(rows[...], 5)
+    tail[at : at + 1, :nh] = high.astype(F32)
+    tail[at + 1 : at + 2, :nh] = (rows[...] - high * 32).astype(F32)
+    own[:hid, :] = previous[0]
+    own[hid:, :] = tail[...].astype(BF16)
+
+
+def pack_entry(nb, w, rows, readings, previous, own, sent, tail):
+    pack_kernel(own, nb, w, rows, readings, previous, tail)
+    sent[...] = own[...]
+
+
+def exchange(first, second, hc, sc, pay):
+    count = first[0].shape[0]
+    parts = len(first)
+    pay[:count, :] = jnp.concatenate([nt(first[p], sc[p]).astype(BF16) for p in range(parts)], axis=1)
+    pay[count:, :] = jnp.concatenate([nt(second[p], hc[p]).astype(BF16) for p in range(parts)], axis=1)
+
+
+def merged(parts, mine, got):
+    step = mine.shape[1] // (2 * parts)
+    here = lax.rem(lax.div(iota(mine.shape, 1), jnp.int32(step)), jnp.int32(2)) == 0
+    value = jnp.where(here, mine[...].astype(F32), got[...].astype(F32)).astype(BF16)
+    count = mine.shape[0] // 2
+    return value[:count, :], value[count:, :]
+
+
+def build_part(cap, hid, fin, degree, parts, p, block, a, at, hc, hx, sc, sx, b):
+    n = a.shape[1]
+    slots = sx.shape[0]
+    nh = 2 * parts * cap
+    half = parts * cap
+    core = lax.rem(lax.axis_index("dom"), 2)
+    line = iota((nh, 1), 0)
+    rel = lax.div(line, jnp.int32(half))
+    k = lax.div(line - rel * half, jnp.int32(cap))
+    t = line - rel * half - k * cap
+    spot = (k * 2 + lax.bitwise_xor(rel, core)) * cap + t
+    node = (n + spot).astype(F32)
+    width = -(-nh // LANES) * LANES
+    slot = iota((slots, nh), 0)
+    outer = lax.div(slot, jnp.int32(nh))
+    rest = slot - outer * nh
+    slot_rel = lax.div(rest, jnp.int32(half))
+    rest = rest - slot_rel * half
+    inner = lax.div(rest, jnp.int32(cap))
+    filled = iota((slots, nh), 1) == slot_rel * half + outer * cap + rest - inner * cap
+    row = iota((32, n), 0).astype(F32)
+    edges = hid + fin + 3 * degree + 2
+    tail = block[hid : hid + 16 * (-(-(edges - hid) // 16)), :].astype(F32)
+    high, low = tail[fin : fin + degree], tail[fin + degree : fin + 2 * degree]
+    w = tail[fin + 2 * degree : fin + 3 * degree]
+    start = fin + 3 * degree
+    sent = tail[start : start + 1] * 32.0 + tail[start + 1 : start + 2]
+    low_is = [jnp.where(low[d : d + 1] == row, 1.0, 0.0).astype(BF16) for d in range(degree)]
+    for chunk in range(n // 32):
+        total = None
+        for d in range(degree):
+            term = low_is[d] * jnp.where(high[d : d + 1] == float(chunk), w[d : d + 1], 0.0).astype(BF16)
+            total = term if total is None else total + term
+        a[chunk * 32 : (chunk + 1) * 32, :] = total
+    at[...] = a[...].T
+    names = high * 32.0 + low
+    total = jnp.zeros((nh, n), F32)
+    for d in range(degree):
+        total = total + jnp.where(names[d : d + 1] == node, w[d : d + 1], 0.0)
+    halo = total.astype(BF16)
+    hc[...] = halo
+    named = jnp.where(iota((nh, width), 1) == spot, sent[:, :width], 0.0)
+    target = jnp.sum(named, axis=1, keepdims=True).astype(jnp.int32)
+    picked = jnp.where(iota((nh, n), 1) == target, 1.0, 0.0).astype(BF16)
+    sc[...] = picked
+    place = jnp.where(filled & (inner == p), 1.0, 0.0).astype(BF16)
+    hx[...] = nn(place, halo).astype(BF16)
+    sx[...] = nn(place, picked).astype(BF16)
+    b[:hid, :] = block[:hid, :]
+    line = iota(tail.shape, 0)
+    b[hid:, :] = jnp.where(line < fin, tail, jnp.where(line == fin, 1.0, 0.0)).astype(BF16)
+
+
+def build_early_kernel(cap, hid, fin, degree, parts, *refs):
+    count = parts - 1
+    z = lax.shift_right_logical(lax.axis_index("dom"), 1)
+    for k in range(count):
+        p = lax.bitwise_xor(z, jnp.int32(k))
+        build_part(cap, hid, fin, degree, parts, p, refs[k], *(ref.at[k] for ref in refs[count:]))
+
+
+def build_late_kernel(cap, hid, fin, degree, parts, last, *refs):
+    early, outs, pay = refs[:7], refs[7:14], refs[14]
+    z = lax.shift_right_logical(lax.axis_index("dom"), 1)
+    for k in range(parts - 1):
+        p = lax.bitwise_xor(z, jnp.int32(k))
+        for source, to in zip(early, outs):
+            to[p] = source[k]
+    p = lax.bitwise_xor(z, jnp.int32(parts - 1))
+    build_part(cap, hid, fin, degree, parts, p, last, *(ref.at[p] for ref in outs))
+    hc, sc, b = outs[2], outs[4], outs[6]
+    base = [b[p] for p in range(parts)]
+    exchange(base, base, hc, sc, pay)
+
+
+def chip_source(col, chans, hid, fin, block):
+    m = lax.div(col, jnp.int32(block))
+    c = col - m * block
+    m = jnp.where(m == 2, 3, jnp.where(m == 3, 2, m))
+    return m, c, jnp.where(c < hid, m * chans + fin + c, jnp.where(c < hid + fin, m * chans + c - hid, -1))
+
+
+def order_kernel(hid, fin, orders, block, gw, cw, gw_o, cw_o, gw_b, cw_b, order):
+    chans = hid + fin
+    feats = cw.shape[1]
+    shape = (feats, orders * block)
+    source = chip_source(iota(shape, 1), chans, hid, fin, block)[2]
+    pick = jnp.where(iota(shape, 0) == source, 1.0, 0.0).astype(BF16)
+    gw_o[...] = tn(gw[...], pick).astype(BF16)
+    cw_o[...] = nn(cw[...], pick).astype(BF16)
+    shape = (orders * hid, feats)
+    line = iota(shape, 0)
+    m = lax.div(line, jnp.int32(hid))
+    pick = jnp.where(iota(shape, 1) == m * chans + fin + line - m * hid, 1.0, 0.0).astype(BF16)
+    gw_b[...] = nn(pick, gw[...]).astype(BF16)
+    cw_b[...] = nt(pick, cw[...]).astype(BF16)
+    m, c, source = chip_source(iota(order.shape, 0), chans, hid, fin, block)
+    source = jnp.where((m == 0) & (c == hid + fin), feats, source)
+    order[...] = jnp.where(iota(order.shape, 1) == source, 1.0, 0.0).astype(BF16)
+
+
+def local_kernel(a, at, x1, x2, l1, l2):
+    for p in range(a.shape[0]):
+        l1[p] = nn(x1[p], a[p])
+        l2[p] = nn(x2[p], at[p])
+
+
+def arrive(sx, hx, mine, got, l1, l2):
+    parts = range(sx.shape[0])
+    top, low = merged(sx.shape[0], mine, got)
+    pulled = [l1[p] + nn(top, hx[p]) for p in parts]
+    pushed = [l2[p] + nn(low, sx[p]) for p in parts]
+    return parts, pulled, pushed
+
+
+def chip_a_kernel(one, mine, got, hc, hx, sc, sx, b, l1, l2, sa, ro, ri, pay):
+    chans = b.shape[1]
+    parts, pulled, pushed = arrive(sx, hx, mine, got, l1, l2)
+    inv_o = [1.0 / pushed[p][one : one + 1, :] for p in parts]
+    inv_i = [1.0 / pulled[p][one : one + 1, :] for p in parts]
+    outs = [(pushed[p] * inv_o[p]).astype(BF16) for p in parts]
+    ins = [(pulled[p] * inv_i[p]).astype(BF16) for p in parts]
+    for p in parts:
+        ro[p] = inv_o[p]
+        ri[p] = inv_i[p]
+        sa[p, :chans, :] = b[p]
+        sa[p, chans : 2 * chans, :] = outs[p]
+        sa[p, 2 * chans :, :] = ins[p]
+    exchange(ins, outs, hc, sc, pay)
+
+
+def local_b_kernel(a, at, sa, gw, l1, l2, gp):
+    chans = l1.shape[1]
+    weights = gw[:, : 3 * chans]
+    for p in range(a.shape[0]):
+        l1[p] = nn(sa[p, 2 * chans :, :], a[p])
+        l2[p] = nn(sa[p, chans : 2 * chans, :], at[p])
+        gp[p] = nn(weights, sa[p])
+
+
+def chip_b_kernel(mine, got, hc, hx, sc, sx, sa, l1, l2, ro, ri, gw, gb, gp, sb, reset, update, y, pay):
+    hid = y.shape[1]
+    chans = l1.shape[1]
+    bias = column(gb[...])
+    weights = gw[:, 3 * chans :]
+    parts, pulled, pushed = arrive(sx, hx, mine, got, l1, l2)
+    base = [sa[p, :chans, :].astype(F32) for p in parts]
+    r2 = [(pulled[p] * (2.0 * ri[p]) - base[p]).astype(BF16) for p in parts]
+    f2 = [(pushed[p] * (2.0 * ro[p]) - base[p]).astype(BF16) for p in parts]
+    second = [jnp.concatenate([f2[p], r2[p]], axis=0) for p in parts]
+    gates = [jax.nn.sigmoid(gp[p] + nn(weights, second[p]) + bias) for p in parts]
+    now = [(gates[p][:hid] * base[p][:hid]).astype(BF16) for p in parts]
+    for p in parts:
+        sb[p] = second[p]
+        reset[p] = gates[p][:hid]
+        update[p] = gates[p][hid:]
+        y[p] = now[p]
+    exchange(now, now, hc, sc, pay)
+
+
+def chip_c1_kernel(mine, got, hc, hx, sc, sx, y, sa, l1, l2, ro, ri, ma, pay):
+    hid = y.shape[1]
+    chans = ma.shape[1] // 3
+    parts, pulled, pushed = arrive(sx, hx, mine, got, l1, l2)
+    ins = [(pulled[p] * ri[p]).astype(BF16) for p in parts]
+    outs = [(pushed[p] * ro[p]).astype(BF16) for p in parts]
+    exchange(ins, outs, hc, sc, pay)
+    for p in parts:
+        for m, value in enumerate((y[p], outs[p], ins[p])):
+            ma[p, m * chans : m * chans + hid, :] = value
+            ma[p, m * chans + hid : (m + 1) * chans, :] = sa[p, m * chans + hid : (m + 1) * chans, :]
+
+
+def local_c2_kernel(a, at, ma, cw, l1, l2, cp):
+    hid = l1.shape[1]
+    chans = ma.shape[1] // 3
+    weights = cw[:, : 3 * chans]
+    for p in range(a.shape[0]):
+        l1[p] = nn(ma[p, 2 * chans : 2 * chans + hid, :], a[p])
+        l2[p] = nn(ma[p, chans : chans + hid, :], at[p])
+        cp[p] = nn(weights, ma[p])
+
+
+def split_back(back, hid, ro, ri, y1, y2, g1, g3, direct):
+    parts = range(len(back))
+    blocks = [[back[p][m * hid : (m + 1) * hid, :] for m in range(5)] for p in parts]
+    one = [(blocks[p][2] * (2.0 * ro[p])).astype(BF16) for p in parts]
+    two = [(blocks[p][4] * (2.0 * ri[p])).astype(BF16) for p in parts]
+    for p in parts:
+        y1[p] = one[p]
+        y2[p] = two[p]
+        g1[p] = blocks[p][1].astype(BF16)
+        g3[p] = blocks[p][3].astype(BF16)
+        direct[p] = blocks[p][0] - blocks[p][2] - blocks[p][4]
+    return one, two
+
+
+def chip_c2_kernel(parts, *refs):
+    ups, refs = refs[:parts], refs[parts:]
+    mine, got, hc, hx, sc, sx, ma, sa, sb, l1, l2, ro, ri, cw, cw_b, cb, cp, update = refs[:18]
+    mb, cand_grad, gate_update, y1, y2, g1, g3, upstream, direct, pay = refs[18:]
+    hid = l1.shape[1]
+    chans = ma.shape[1] // 3
+    z = lax.shift_right_logical(lax.axis_index("dom"), 1)
+    for k in range(parts):
+        upstream[lax.bitwise_xor(z, jnp.int32(k))] = ups[k][0]
+    bias = column(cb[...])
+    weights = cw[:, 3 * chans :]
+    parts, pulled, pushed = arrive(sx, hx, mine, got, l1, l2)
+    base = [ma[p, :hid, :].astype(F32) for p in parts]
+    r2 = [(pulled[p] * (2.0 * ri[p]) - base[p]).astype(BF16) for p in parts]
+    f2 = [(pushed[p] * (2.0 * ro[p]) - base[p]).astype(BF16) for p in parts]
+    second = [
+        jnp.concatenate([f2[p], sb[p, hid:chans, :], r2[p], sb[p, chans + hid :, :]], axis=0) for p in parts
+    ]
+    cand = [jnp.tanh(cp[p] + nn(weights, second[p]) + bias) for p in parts]
+    rest = [upstream[p].astype(F32) * (1.0 - update[p]) for p in parts]
+    grad = [(rest[p] - rest[p] * cand[p] * cand[p]).astype(BF16) for p in parts]
+    back = [nn(cw_b[...], grad[p]) for p in parts]
+    for p in parts:
+        mb[p] = second[p]
+        cand_grad[p] = grad[p]
+        gate_update[p] = ((sa[p, :hid, :].astype(F32) - cand[p]) * (rest[p] * update[p])).astype(BF16)
+    one, two = split_back(back, hid, ro, ri, y1, y2, g1, g3, direct)
+    exchange(one, two, hc, sc, pay)
+
+
+def chip_part(grads, first, second, order):
+    parts = range(first.shape[0])
+    split = first.shape[1]
+    one = sum(nt(grads[p], first[p]) for p in parts).astype(BF16)
+    two = sum(nt(grads[p], second[p]) for p in parts).astype(BF16)
+    return nn(one, order[:split, :]) + nn(two, order[split:, :])
+
+
+def local_d_kernel(a, at, y1, y2, cand_grad, ma, mb, order, l1, l2, part):
+    local_kernel(a, at, y1, y2, l1, l2)
+    part[...] = chip_part(cand_grad, ma, mb, order).astype(BF16)
+
+
+def chip_d1_kernel(mine, got, hc, hx, sc, sx, l1, l2, g1, g3, ro, ri, z1, z2, pay):
+    parts, pulled, pushed = arrive(sx, hx, mine, got, l1, l2)
+    one = [((g1[p].astype(F32) + pulled[p]) * ro[p]).astype(BF16) for p in parts]
+    two = [((g3[p].astype(F32) + pushed[p]) * ri[p]).astype(BF16) for p in parts]
+    exchange(one, two, hc, sc, pay)
+    for p in parts:
+        z1[p] = one[p]
+        z2[p] = two[p]
+
+
+def local_d2_kernel(a, at, z1, z2, direct, base):
+    for p in range(a.shape[0]):
+        base[p] = direct[p] + nn(z1[p], a[p]) + nn(z2[p], at[p])
+
+
+def chip_d2_kernel(mine, got, hc, hx, sc, sx, base, ro, ri, sa, gw_b, upstream, reset, update, gate_update,
+                   gate_grad, y1, y2, g1, g3, direct, pay):
+    hid = base.shape[1]
+    parts = range(sx.shape[0])
+    top, low = merged(sx.shape[0], mine, got)
+    scaled_grad = [base[p] + nn(top, hx[p]) + nn(low, sx[p]) for p in parts]
+    kept = [scaled_grad[p] * reset[p] for p in parts]
+    grad = [
+        jnp.concatenate([(sa[p, :hid, :].astype(F32) * (kept[p] - kept[p] * reset[p])).astype(BF16), gate_update[p]], axis=0)
+        for p in parts
+    ]
+    back = [nn(gw_b[...], grad[p]) for p in parts]
+    one, two = split_back(back, hid, ro, ri, y1, y2, g1, g3, direct)
+    for p in parts:
+        gate_grad[p] = grad[p]
+        direct[p] = direct[p] + upstream[p].astype(F32) * update[p] + kept[p]
+    exchange(one, two, hc, sc, pay)
+
+
+def grads_kernel(gate_grad, sa, sb, order, part, keep, give, flat):
+    both = gate_grad.shape[1]
+    half = keep.shape[0]
+    core = lax.rem(lax.axis_index("dom"), 2)
+    flat[:both, :] = chip_part(gate_grad, sa, sb, order)
+    flat[both:, :] = part[...].astype(F32)
+    keep[...] = flat[pl.ds(pl.multiple_of(core * half, 8), half), :].astype(BF16)
+    give[...] = flat[pl.ds(pl.multiple_of((1 - core) * half, 8), half), :].astype(BF16)
+
+
+def local_e_kernel(a, at, z1, z2, direct, base):
+    z = lax.shift_right_logical(lax.axis_index("dom"), 1)
+    base[...] = direct[z] + nn(z1[z], a[z]) + nn(z2[z], at[z])
+
+
+def chip_e_kernel(mine, got, hc, hx, sc, sx, base, out, done):
+    done[...] = jnp.zeros_like(done)
+    z = lax.shift_right_logical(lax.axis_index("dom"), 1)
+    top, low = merged(sx.shape[0], mine, got)
+    out[0] = (base[...] + nn(top, hx[z]) + nn(low, sx[z])).astype(BF16)
+
+
+def sum_kernel(*refs):
+    values = [ref[...].astype(F32) for ref in refs[:-2]]
+    while len(values) > 1:
+        values = [values[k] + values[k + 1] for k in range(0, len(values), 2)]
+    refs[-1][...] = values[0].astype(BF16)
+    refs[-2][...] = values[0].astype(BF16)
+
+
+def end_kernel(factor, mine, got, gw, gb, cw, cb, flat):
+    half = mine.shape[0]
+    core = lax.rem(lax.axis_index("dom"), 2)
+    flat[pl.ds(pl.multiple_of(core * half, 8), half), :] = mine[...].astype(F32)
+    flat[pl.ds(pl.multiple_of((1 - core) * half, 8), half), :] = got[...].astype(F32)
+    features, rows = gw.shape
+    same = jnp.where(iota((features, flat.shape[1]), 0) == iota((features, flat.shape[1]), 1), 1.0, 0.0).astype(BF16)
+    gw[...] = nt(same, flat[:rows, :].astype(BF16)) * factor
+    cw[...] = flat[rows:, :features] * factor
+    pick = jnp.where(iota((8, flat.shape[1]), 1) == features, 1.0, 0.0).astype(BF16)
+    bias = nt(pick, flat[...].astype(BF16))[:1] * factor
+    gb[...] = bias[:, :rows]
+    cb[...] = bias[:, rows:]
+
+
+def chip_body(
+    readings,
+    previous,
+    upstream,
+    gate_weight,
+    gate_bias,
+    cand_weight,
+    cand_bias,
+    neighbours,
+    edge_weight,
+    send_rows,
+):
+    fin, hid = readings.shape[1], previous.shape[1]
+    chans = fin + hid
+    orders = gate_weight.shape[1] // chans
+    degree = neighbours.shape[0]
+    n = readings.shape[2]
+    nd = lax.axis_size("dom")
+    snaps = lax.axis_size("snap")
+    parts = nd // 2
+    cap = send_rows.shape[1] // nd
+    block = hid + 16 * (-(-(fin + 3 * degree + 2) // 16))
+    slots = 2 * parts * parts * cap
+
+    def swap(array, k, axis="dom", size=nd):
+        return lax.ppermute(array, axis, [(i, i ^ k) for i in range(size)])
+
+    own, sent = run(
+        pack_entry, "pack", [((block, n), BF16)] * 2, neighbours, edge_weight, send_rows, readings, previous,
+        scratch=[pltpu.VMEM((block - hid, n), F32)], vmem=56,
+    )
+    blocks = [own] + [swap(sent, 2 * k) for k in range(1, parts - 1)]
+    relay = blocks[-1] if parts > 2 else sent
+    ups = [upstream] + [swap(upstream, 2 * k) for k in range(1, parts - 1)]
+    ups.append(swap(ups[-1], 2))
+    width = -(-(orders * chans + 1) // LANES) * LANES
+    gw, cw, gw_b, cw_b, order = run(
+        functools.partial(order_kernel, hid, fin, orders, block), "order",
+        [((2 * hid, orders * block), BF16), ((hid, orders * block), BF16), ((orders * hid, 2 * hid), BF16), ((orders * hid, hid), BF16),
+         ((orders * block, width), BF16)],
+        gate_weight.T, cand_weight, after=[own],
+    )
+    relay, gw = lax.optimization_barrier((relay, gw))
+    wide, wide16, wide_pay = ((parts, block, n), F32), ((parts, block, n), BF16), ((2 * block, slots), BF16)
+    field, field16, pay_kind = ((parts, hid, n), F32), ((parts, hid, n), BF16), ((2 * hid, slots), BF16)
+    first, second = ((parts, 3 * block, n), BF16), ((parts, 2 * block, n), BF16)
+    line = ((parts, 1, n), F32)
+    built = [((n, n), BF16)] * 2 + [((rows, n), BF16) for rows in (2 * parts * cap, slots)] * 2 + [((block, n), BF16)]
+    early = run(
+        functools.partial(build_early_kernel, cap, hid, fin, degree, parts), "build_early",
+        [((parts - 1, *shape), kind) for shape, kind in built], *blocks[:-1], relay if parts > 2 else own,
+    )
+    a, at, hc, hx, sc, sx, b, pay = run(
+        functools.partial(build_late_kernel, cap, hid, fin, degree, parts), "build_late",
+        [((parts, *shape), kind) for shape, kind in built] + [wide_pay], swap(relay, 2), *early,
+    )
+    edges = (hc, hx, sc, sx)
+    got = swap(pay, 1)
+    l1, l2 = run(local_kernel, "local_a", [wide, wide], a, at, b, b)
+    sa, ro, ri, pay = run(
+        functools.partial(chip_a_kernel, hid + fin), "chip_a", [first, line, line, wide_pay],
+        pay, got, *edges, b, l1, l2, after=ups[1:],
+    )
+    got = swap(pay, 1)
+    l1, l2, gp = run(local_b_kernel, "local_b", [wide, wide, ((parts, 2 * hid, n), F32)], a, at, sa, gw)
+    sb, reset, update, y, pay = run(
+        chip_b_kernel, "chip_b", [second, field, field, field16, pay_kind],
+        pay, got, *edges, sa, l1, l2, ro, ri, gw, gate_bias[None, :], gp,
+    )
+    got = swap(pay, 1)
+    l1, l2 = run(local_kernel, "local_c1", [field, field], a, at, y, y)
+    ma, pay = run(chip_c1_kernel, "chip_c1", [first, pay_kind], pay, got, *edges, y, sa, l1, l2, ro, ri)
+    got = swap(pay, 1)
+    l1, l2, cp = run(local_c2_kernel, "local_c2", [field, field, field], a, at, ma, cw)
+    mb, cand_grad, gate_update, y1, y2, g1, g3, up, direct, pay = run(
+        functools.partial(chip_c2_kernel, parts), "chip_c2", [second] + [field16] * 7 + [field, pay_kind],
+        *ups, pay, got, *edges, ma, sa, sb, l1, l2, ro, ri, cw, cw_b, cand_bias[None, :], cp, update,
+    )
+    got = swap(pay, 1)
+    l1, l2, part = run(
+        local_d_kernel, "local_d1", [field, field, ((hid, width), BF16)], a, at, y1, y2, cand_grad, ma, mb, order
+    )
+    z1, z2, pay = run(
+        chip_d1_kernel, "chip_d1", [field16, field16, pay_kind], pay, got, *edges, l1, l2, g1, g3, ro, ri
+    )
+    got = swap(pay, 1)
+    (base,) = run(local_d2_kernel, "local_d2", [field], a, at, z1, z2, direct)
+    gate_grad, y1, y2, g1, g3, direct, pay = run(
+        chip_d2_kernel, "chip_d2", [((parts, 2 * hid, n), BF16)] + [field16] * 4 + [field, pay_kind],
+        pay, got, *edges, base, ro, ri, sa, gw_b, up, reset, update, gate_update,
+    )
+    got = swap(pay, 1)
+    half = ((3 * hid // 2, width), BF16)
+    keep, give = run(
+        grads_kernel, "grads", [half, half], gate_grad, sa, sb, order, part, scratch=[pltpu.VMEM((3 * hid, width), F32)]
+    )
+    l1, l2 = run(local_kernel, "local_e1", [field, field], a, at, y1, y2)
+    mine, sent = run(sum_kernel, "sum_core", [half] * 2, keep, swap(give, 1), after=[l1, got])
+    every = [mine] + [swap(sent, k, "snap", snaps) for k in range(1, snaps)]
+    z1, z2, pay = run(
+        chip_d1_kernel, "chip_e1", [field16, field16, pay_kind], pay, got, *edges, l1, l2, g1, g3, ro, ri, after=[mine],
+    )
+    got = swap(pay, 1)
+    (base,) = run(local_e_kernel, "local_e2", [((hid, n), F32)], a, at, z1, z2, direct)
+    state_grad, done = run(
+        chip_e_kernel, "chip_e2", [((1, hid, n), BF16), ((8, LANES), F32)], pay, got, *edges, base
+    )
+    mine, sent = run(sum_kernel, "sum_snap", [half] * 2, *every, after=[done])
+    factor = 1.0 / math.sqrt(readings.shape[0] * snaps * n * nd)
+    feats = orders * chans
+    grad_gw, grad_gb, grad_cw, grad_cb = run(
+        functools.partial(end_kernel, factor), "end",
+        [((feats, 2 * hid), F32), ((1, 2 * hid), F32), ((hid, feats), F32), ((1, hid), F32)],
+        mine, swap(sent, 1), scratch=[pltpu.VMEM((3 * hid, width), F32)],
+    )
+    return state_grad, grad_gw.T, grad_gb[0], grad_cw, grad_cb[0]
+
+
+def body(*args):
+    neighbours, send_rows = args[7], args[9]
+    n = neighbours.shape[1]
+    nd, snaps = lax.axis_size("dom"), lax.axis_size("snap")
+    parts = nd // 2
+    slots = 2 * parts * parts * (send_rows.shape[1] // nd)
+    powers = nd & (nd - 1) == 0 and snaps & (snaps - 1) == 0 and nd > 2
+    if powers and parts * (n + slots) * n * 2 <= 4 << 20:
+        return chip_body(*args)
+    return spread_body(*args)
+
+
 def solution(mesh):
     in_specs = (
         P("snap", None, "dom"),

time: 89.6 us -> 44.6 us (0.50)
  waiting for transfers between devices: 33.4 us -> 5.49 us
  blocking collectives: 11.8 us -> 0 us
  starting transfers between devices: 22.3 us -> 15.3 us
  Pallas kernels: 13.8 us -> 20.1 us
  local copies, waits for them, and re-layouts: 6.46 us -> 2.58 us
    all_to_all x6 -> x0, waiting for transfers between devices: 33.4 us -> none  [the longest x4 20.3 us: body(): recv = move(pay)]
    all_to_all x6 -> x0, starting transfers between devices: 22.3 us -> none  [the longest x4 16.4 us: body(): recv = move(pay)]
    ppermute x0 -> x19, starting transfers between devices: none -> 15.3 us  [swap(): return lax.ppermute(array, axis, [(i, i ^ k) for i in range(size)])]
    all_to_all x1 -> x0, blocking collectives: 11.8 us -> none  [body(): grads = lax.all_to_all(grads, both, 0, 0, tiled=True)]
    pallas_call x13 -> x24, Pallas kernels: 13.8 us -> 20.1 us  [run(): pl.pallas_call(lambda *refs: kernel(*refs[len(after):]), name=name, out_s...]
    ppermute x0 -> x19, waiting for transfers between devices: none -> 5.49 us  [swap(): return lax.ppermute(array, axis, [(i, i ^ k) for i in range(size)])]
    unnamed x22 -> x12, local copies, waits for them, and re-layouts: 6.46 us -> 2.58 us
  transfers between devices with their start and end apart: 6 -> 19, of which waited for: 6 -> 8; matrix products, arithmetic and copies ran while one was open for 0% -> 0% of each run, Pallas kernels for 5% -> 26%
where the time goes in v3:
time: 44.6 us; the launch traced here: 44.3 us
  Pallas kernels  20.1 us (45%)
  starting transfers between devices  15.3 us (34%)
  waiting for transfers between devices  5.49 us (12%)
  local copies, waits for them, and re-layouts  2.58 us (6%)
  between operations  0.82 us (2%)
    pallas_call x24, Pallas kernels, run(): pl.pallas_call(lambda *refs: kernel(*refs[len(after):]), name=name, out_s...  20.1 us
    ppermute x19, starting transfers between devices, swap(): return lax.ppermute(array, axis, [(i, i ^ k) for i in range(size)])  15.3 us
    ppermute x19, waiting for transfers between devices, swap(): return lax.ppermute(array, axis, [(i, i ^ k) for i in range(size)])  5.49 us
    unnamed x12, local copies, waits for them, and re-layouts  2.58 us
  transfers between devices with their start and end apart: 19, of which 8 were waited for; matrix products, arithmetic and copies ran while one was open for 0% of the time, Pallas kernels for 26%

profile of v3, /device:TPU:0, one launch (start us, length us, event | category | flops | bytes accessed | tf_op | source)
XLA Modules:
  0.0 44.3 jit_solution(3856055855979694717)
XLA Ops:
  0.6 1.6 %pack.1 = (bf16[80,512]{1,0:T(8,128)(2,1)}, bf16[80,512]{1,0:T(8,128)(2,1)}) custom-call(s32[4,512]{1,0:T(4,128)} %refs_0_.2, f32[4,512]{1,0:T(4,128)} %refs_1_.1, s32[1,32]{1,0:T(1,128)} %refs_2_.2, bf16[1,2,512]{2,1,0:T(2,128)(2,1)} %refs_3_.1, bf16[1,64,512]{2,1,0:T(8,128)(2,1)} %refs_4_.1), custom_call_target="tpu_custom_call" | custom-call | flops 20000000 | bytes 2000000 | tf_op jit(solution)/shard_map/pack/pallas_call | solution.py:40
  2.2 4.0 %collective-permute-start = (bf16[80,512]{1,0:T(8,128)(2,1)}, bf16[80,512]{1,0:T(8,128)(2,1)S(1)}, u32[]{:S(2)}, u32[]{:S(2)}) collective-permute-start(bf16[80,512]{1,0:T(8,128)(2,1)} %get-tuple-element.90), channel_id=1, source_target_pairs={{0,4},{1,5},{2,6},{3,7},{4,0},{5,1},{6,2},{7,3},{8,12},{9,13},{10,... | collective-permute-start | bytes 245768 | tf_op jit(solution)/shard_map/ppermute | solution.py:900
  6.3 1.9 %collective-permute-start.2 = (bf16[80,512]{1,0:T(8,128)(2,1)}, bf16[80,512]{1,0:T(8,128)(2,1)S(1)}, u32[]{:S(2)}, u32[]{:S(2)}) collective-permute-start(bf16[80,512]{1,0:T(8,128)(2,1)} %get-tuple-element.90), channel_id=1, source_target_pairs={{0,2},{1,3},{2,0},{3,1},{4,6},{5,7},{6,4},{7,5},{8,10},{9,11},{10,... | collective-permute-start | bytes 245768 | tf_op jit(solution)/shard_map/ppermute | solution.py:900
  8.2 0.9 %copy-done = bf16[80,512]{1,0:T(8,128)(2,1)S(1)} copy-done((bf16[80,512]{1,0:T(8,128)(2,1)S(1)}, bf16[80,512]{1,0:T(8,128)(2,1)}, u32[]{:S(2)}) %copy-start) | copy-done | bytes 81944
  9.1 0.9 %copy-done.1 = bf16[128,330]{0,1:T(8,128)(2,1)S(1)} copy-done((bf16[128,330]{0,1:T(8,128)(2,1)S(1)}, bf16[128,330]{0,1:T(8,128)(2,1)}, u32[]{:S(2)}) %copy-start.1) | copy-done | bytes 84504
  10.0 0.8 %copy-done.3 = bf16[64,330]{1,0:T(8,128)(2,1)S(1)} copy-done((bf16[64,330]{1,0:T(8,128)(2,1)S(1)}, bf16[64,330]{1,0:T(8,128)(2,1)}, u32[]{:S(2)}) %copy-start.3) | copy-done | bytes 42264
  10.8 0.6 %order.1 = (bf16[128,400]{1,0:T(8,128)(2,1)S(1)}, bf16[64,400]{1,0:T(8,128)(2,1)S(1)}, bf16[320,128]{1,0:T(8,128)(2,1)S(1)}, bf16[320,64]{1,0:T(8,128)(2,1)S(1)}, bf16[400,384]{1,0:T(8,128)(2,1)S(1)}) custom-call(bf16[80,512]{1,0:T(8,128)(2,1)S(1)} %copy-done, bf16[330,128]{1,0:T(8,128)(2,1)S(1)} %bitcast.6, bf16[64,330]{1,0:T(8,128)(2,1)S(1)} %copy-done.3), custom_call_target="tpu_custom_call" | custom-call | flops 20000000 | bytes 2000000 | tf_op jit(solution)/shard_map/order/pallas_call | solution.py:40
  11.4 0.3 collective-permute-done.refs_2_
  11.7 1.3 %collective-permute-start.1 = (bf16[80,512]{1,0:T(8,128)(2,1)S(1)}, bf16[80,512]{1,0:T(8,128)(2,1)S(1)}, u32[]{:S(2)}, u32[]{:S(2)}) collective-permute-start(bf16[80,512]{1,0:T(8,128)(2,1)S(1)} %collective-permute-done.refs_2_), channel_id=1, source_target_pairs={{0,2},{1,3},{2,0},{3,1},{4,6},{5,7},{6,4},{7,5},{8,10},{9,11},{10,... | collective-permute-start | bytes 245768 | tf_op jit(solution)/shard_map/ppermute | solution.py:900
  13.0 0.8 %collective-permute-start.3 = (bf16[1,64,512]{2,1,0:T(8,128)(2,1)}, bf16[1,64,512]{2,1,0:T(8,128)(2,1)S(1)}, u32[]{:S(2)}, u32[]{:S(2)}) collective-permute-start(bf16[1,64,512]{2,1,0:T(8,128)(2,1)} %refs_0_.3), channel_id=1, source_target_pairs={{0,2},{1,3},{2,0},{3,1},{4,6},{5,7},{6,4},{7,5},{8,10},{9,11},{10,... | collective-permute-start | bytes 196616 | tf_op jit(solution)/shard_map/ppermute | solution.py:900
  13.8 1.3 %collective-permute-start.5 = (bf16[1,64,512]{2,1,0:T(8,128)(2,1)S(1)}, bf16[1,64,512]{2,1,0:T(8,128)(2,1)S(1)}, u32[]{:S(2)}, u32[]{:S(2)}) collective-permute-start(bf16[1,64,512]{2,1,0:T(8,128)(2,1)S(1)} %collective-permute-done.4.refs_1_.refs_2_), channel_id=1, source_target_pairs={{0,2},{1,3},{2,0},{3,1},{4,6},{5,7},{6,4},{7,5},{8,10},{9,11},{10,... | collective-permute-start | bytes 196616 | tf_op jit(solution)/shard_map/ppermute | solution.py:900
  15.0 1.2 %build_early.1 = (bf16[3,512,512]{2,1,0:T(8,128)(2,1)S(1)}, bf16[3,512,512]{2,1,0:T(8,128)(2,1)S(1)}, bf16[3,32,512]{2,1,0:T(8,128)(2,1)S(1)}, bf16[3,128,512]{2...) custom-call(bf16[80,512]{1,0:T(8,128)(2,1)S(1)} %copy-done, ...), custom_call_target="tpu_custom_call" | custom-call | flops 20000000 | bytes 2000000 | tf_op jit(solution)/shard_map/build_early/pallas_call | solution.py:40
  16.2 0.8 %collective-permute-done.1.refs_0_ = bf16[80,512]{1,0:T(8,128)(2,1)S(1)} collective-permute-done((bf16[80,512]{1,0:T(8,128)(2,1)S(1)}, bf16[80,512]{1,0:T(8,128)(2,1)S(1)}, u32[]{:S(2)}, u32[]{:S(2)}) %collective-permute-start.1) | collective-permute-done | bytes 81952 | tf_op jit(solution)/shard_map/ppermute | solution.py:900
  17.1 1.0 %build_late.1 = (bf16[4,512,512]{2,1,0:T(8,128)(2,1)S(1)}, bf16[4,512,512]{2,1,0:T(8,128)(2,1)S(1)}, bf16[4,32,512]{2,1,0:T(8,128)(2,1)S(1)}, bf16[4,128,512]{2,...) custom-call(bf16[80,512]{1,0:T(8,128)(2,1)S(1)} %collective-permute-, ...), custom_call_target="tpu_custom_call" | custom-call | flops 20000000 | bytes 2000000 | tf_op jit(solution)/shard_map/build_late/pallas_call | solution.py:40
  18.2 0.8 %local_a.1 = (f32[4,80,512]{2,1,0:T(8,128)S(1)}, f32[4,80,512]{2,1,0:T(8,128)S(1)}) custom-call(bf16[4,512,512]{2,1,0:T(8,128)(2,1)S(1)} %get-tuple-element.101.refs_0_, bf16[4,512,512]{2,1,0:T(8,128)(2,1)S(1)} %get-tuple-element.102.refs_1_, bf16[4,80,512]{2,1,0:T(8,128)(2,1)S(1)} %get-tuple-element.108.refs_2_.refs_3_.refs_9_, ...), custom_call_target="tpu_custom_call" | custom-call | flops 20000000 | bytes 2000000 | tf_op jit(solution)/shard_map/local_a/pallas_call | solution.py:40
  19.0 0.3 collective-permute-done.6.refs_4_
  19.4 0.6 %chip_a.1 = (bf16[4,240,512]{2,1,0:T(8,128)(2,1)S(1)}, f32[4,1,512]{2,1,0:T(1,128)S(1)}, f32[4,1,512]{2,1,0:T(1,128)S(1)}, bf16[160,128]{1,0:T(8,128)(2,1)S(1)}) custom-call(bf16[1,64,512]{2,1,0:T(8,128)(2,1)S(1)} %collective-permute-done.3.refs_0_.refs_1_, bf16[1,64,512]{2,1,0:T(8,128)(2,1)S(1)} %collective-permute-done.4.refs_1_.refs_2_, ...), custom_call_target="tpu_custom_call" | custom-call | flops 20000000 | bytes 2000000 | tf_op jit(solution)/shard_map/chip_a/pallas_call | solution.py:40
  20.0 0.2 collective-permute-start.7
  20.3 1.0 %local_b.1 = (f32[4,80,512]{2,1,0:T(8,128)S(1)}, f32[4,80,512]{2,1,0:T(8,128)S(1)}, f32[4,128,512]{2,1,0:T(8,128)S(1)}) custom-call(bf16[4,512,512]{2,1,0:T(8,128)(2,1)S(1)} %get-tuple-element.101.refs_0_, bf16[4,512,512]{2,1,0:T(8,128)(2,1)S(1)} %get-tuple-element.102.refs_1_, ...), custom_call_target="tpu_custom_call" | custom-call | flops 20000000 | bytes 2000000 | tf_op jit(solution)/shard_map/local_b/pallas_call | solution.py:40
  21.3 1.0 %chip_b.1 = (bf16[4,160,512]{2,1,0:T(8,128)(2,1)S(1)}, f32[4,64,512]{2,1,0:T(8,128)S(1)}, f32[4,64,512]{2,1,0:T(8,128)S(1)}, bf16[4,64,512]{2,1,0:T(8,128)(2,1)S(1)}, bf16[128,128]{1,0:T(8,128)(2,1)S(1)}) custom-call(bf16[160,128]{1,0:T(8,128)(2,1)S(1)} %get-tuple-element.111.refs_0_, bf16[160,128]{1,0:T(8,128)(2,1)S(1)} %collective-permute-done.7.refs_1_, ...), custom_call_target="tpu_custom_call" | custom-call | flops 20000000 | bytes 2000000 | tf_op jit(solution)/shard_map/chip_b/pallas_call | solution.py:40
  22.3 0.4 collective-permute-start.8
  22.7 0.8 %local_c1.1 = (f32[4,64,512]{2,1,0:T(8,128)S(1)}, f32[4,64,512]{2,1,0:T(8,128)S(1)}) custom-call(bf16[4,512,512]{2,1,0:T(8,128)(2,1)S(1)} %get-tuple-element.101.refs_0_, bf16[4,512,512]{2,1,0:T(8,128)(2,1)S(1)} %get-tuple-element.102.refs_1_, bf16[4,64,512]{2,1,0:T(8,128)(2,1)S(1)} %get-tuple-element.120.refs_2_.refs_3_.refs_6_, ...), custom_call_target="tpu_custom_call" | custom-call | flops 20000000 | bytes 2000000 | tf_op jit(solution)/shard_map/local_c1/pallas_call | solution.py:40
  23.6 0.5 %chip_c1.1 = (bf16[4,240,512]{2,1,0:T(8,128)(2,1)S(1)}, bf16[128,128]{1,0:T(8,128)(2,1)S(1)}) custom-call(bf16[128,128]{1,0:T(8,128)(2,1)S(1)} %get-tuple-element.119.refs_0_, bf16[128,128]{1,0:T(8,128)(2,1)S(1)} %collective-permute-done.8.refs_1_, bf16[4,32,512]{2,1,0:T(8,128)(2,1)S(1)} %get-tuple-element.104.refs_5_.refs_2_.refs_6_.refs_3_, ...), custom_call_target="tpu_custom_call" | custom-call | flops 20000000 | bytes 2000000 | tf_op jit(solution)/shard_map/chip_c1/pallas_call | solution.py:40
  24.1 0.4 collective-permute-start.9
  24.5 1.0 %local_c2.1 = (f32[4,64,512]{2,1,0:T(8,128)S(1)}, f32[4,64,512]{2,1,0:T(8,128)S(1)}, f32[4,64,512]{2,1,0:T(8,128)S(1)}) custom-call(bf16[4,512,512]{2,1,0:T(8,128)(2,1)S(1)} %get-tuple-element.101.refs_0_, bf16[4,512,512]{2,1,0:T(8,128)(2,1)S(1)} %get-tuple-element.102.refs_1_, bf16[4,240,512]{2,1,0:T(8,128)(2,1)S(1)} %get-tuple-element.124.refs_2_.refs_10_.refs_5_, ...), custom_call_target="tpu_custom_call" | custom-call | flops 20000000 | bytes 2000000 | tf_op jit(solution)/shard_map/local_c2/pallas_call | solution.py:40
  25.5 1.3 %chip_c2.1 = (bf16[4,160,512]{2,1,0:T(8,128)(2,1)S(1)}, bf16[4,64,512]{2,1,0:T(8,128)(2,1)S(1)}, bf16[4,64,512]{2,1,0:T(8,128)(2,1)S(1)}, bf16[4,64,512]{2,1,0:T...) custom-call(bf16[1,64,512]{2,1,0:T(8,128)(2,1)S(1)} %copy-done.2, ...), custom_call_target="tpu_custom_call" | custom-call | flops 20000000 | bytes 2000000 | tf_op jit(solution)/shard_map/chip_c2/pallas_call | solution.py:40
  26.8 0.3 collective-permute-start.10
  27.0 1.5 %local_d1.1 = (f32[4,64,512]{2,1,0:T(8,128)S(1)}, f32[4,64,512]{2,1,0:T(8,128)S(1)}, bf16[64,384]{1,0:T(8,128)(2,1)S(1)}) custom-call(bf16[4,512,512]{2,1,0:T(8,128)(2,1)S(1)} %get-tuple-element.101.refs_0_, bf16[4,512,512]{2,1,0:T(8,128)(2,1)S(1)} %get-tuple-element.102.refs_1_, bf16[4,64,512]{2,1,0:T(8,128)(2,1)S(1)} %get-tuple-element.133.refs_2_, ...), custom_call_target="tpu_custom_call" | custom-call | flops 20000000 | bytes 2000000 | tf_op jit(solution)/shard_map/local_d1/pallas_call | solution.py:40
  28.6 0.6 %chip_d1.1 = (bf16[4,64,512]{2,1,0:T(8,128)(2,1)S(1)}, bf16[4,64,512]{2,1,0:T(8,128)(2,1)S(1)}, bf16[128,128]{1,0:T(8,128)(2,1)S(1)}) custom-call(bf16[128,128]{1,0:T(8,128)(2,1)S(1)} %get-tuple-element.132.refs_0_, bf16[128,128]{1,0:T(8,128)(2,1)S(1)} %collective-permute-done.10.refs_1_, ...), custom_call_target="tpu_custom_call" | custom-call | flops 20000000 | bytes 2000000 | tf_op jit(solution)/shard_map/chip_d1/pallas_call | solution.py:40
  29.2 0.4 collective-permute-start.11
  29.5 0.9 %local_d2.1.refs_6_ = f32[4,64,512]{2,1,0:T(8,128)S(1)} custom-call(bf16[4,512,512]{2,1,0:T(8,128)(2,1)S(1)} %get-tuple-element.101.refs_0_, bf16[4,512,512]{2,1,0:T(8,128)(2,1)S(1)} %get-tuple-element.102.refs_1_, bf16[4,64,512]{2,1,0:T(8,128)(2,1)S(1)} %get-tuple-element.143.refs_2_, bf16[4,64,512]{2,1,0:T(8,128)(2,1)S(1)} %get-tuple-element.144.refs_3_, ...), custom_call_target="tpu_custom_call" | custom-call | flops 20000000 | bytes 2000000 | tf_op jit(solution)/shard_map/local_d2/pallas_call | solution.py:40
  30.4 1.0 %chip_d2.1 = (bf16[4,128,512]{2,1,0:T(8,128)(2,1)S(1)}, bf16[4,64,512]{2,1,0:T(8,128)(2,1)S(1)}, bf16[4,64,512]{2,1,0:T(8,128)(2,1)S(1)}, bf16[4,64,512]{2,1,0:T...) custom-call(bf16[128,128]{1,0:T(8,128)(2,1)S(1)} %get-tuple-element.142.r, ...), custom_call_target="tpu_custom_call" | custom-call | flops 20000000 | bytes 2000000 | tf_op jit(solution)/shard_map/chip_d2/pallas_call | solution.py:40
  31.5 0.9 %grads.1 = (bf16[96,384]{1,0:T(8,128)(2,1)S(1)}, bf16[96,384]{1,0:T(8,128)(2,1)S(1)}) custom-call(bf16[4,128,512]{2,1,0:T(8,128)(2,1)S(1)} %get-tuple-element.154.refs_0_, bf16[4,240,512]{2,1,0:T(8,128)(2,1)S(1)} %get-tuple-element.112.refs_2_.refs_6_.refs_7_.refs_11_.refs_9_.refs_1_, bf16[4,160,512]{2,1,0:T(8,128)(2,1)S(1)} %get-tuple-element.125.refs_12_.refs_2_, ...), custom_call_target="tpu_custom_call" | custom-call | flops 20000000 | bytes 2000000 | tf_op jit(solution)/shard_map/grads/pallas_call | solution.py:40
  32.4 0.4 collective-permute-start.13
  32.7 0.2 collective-permute-start.12
  32.9 0.8 %local_e1.1 = (f32[4,64,512]{2,1,0:T(8,128)S(1)}, f32[4,64,512]{2,1,0:T(8,128)S(1)}) custom-call(bf16[4,512,512]{2,1,0:T(8,128)(2,1)S(1)} %get-tuple-element.101.refs_0_, bf16[4,512,512]{2,1,0:T(8,128)(2,1)S(1)} %get-tuple-element.102.refs_1_, bf16[4,64,512]{2,1,0:T(8,128)(2,1)S(1)} %get-tuple-element.150.refs_2_, ...), custom_call_target="tpu_custom_call" | custom-call | flops 20000000 | bytes 2000000 | tf_op jit(solution)/shard_map/local_e1/pallas_call | solution.py:40
  33.8 0.2 collective-permute-done.12.refs_1_.refs_2_
  34.0 3.0 %collective-permute-start.17 = (bf16[96,384]{1,0:T(8,128)(2,1)S(1)}, bf16[96,384]{1,0:T(8,128)(2,1)S(1)}, u32[]{:S(2)}, u32[]{:S(2)}) collective-permute-start(bf16[96,384]{1,0:T(8,128)(2,1)S(1)} %get-tuple-element.168), channel_id=1, source_target_pairs={{0,24},{8,16},{16,8},{24,0},{1,25},{9,17},{17,9},{25,1},{2,26},{10... | collective-permute-start | bytes 221192 | tf_op jit(solution)/shard_map/ppermute | solution.py:900
  37.0 0.5 %collective-permute-start.16 = (bf16[96,384]{1,0:T(8,128)(2,1)S(1)}, bf16[96,384]{1,0:T(8,128)(2,1)S(1)}, u32[]{:S(2)}, u32[]{:S(2)}) collective-permute-start(bf16[96,384]{1,0:T(8,128)(2,1)S(1)} %get-tuple-element.168), channel_id=1, source_target_pairs={{0,16},{8,24},{16,0},{24,8},{1,17},{9,25},{17,1},{25,9},{2,18},{10... | collective-permute-start | bytes 221192 | tf_op jit(solution)/shard_map/ppermute | solution.py:900
  37.5 0.1 collective-permute-start.15
  37.6 0.6 %chip_e1.1 = (bf16[4,64,512]{2,1,0:T(8,128)(2,1)S(1)}, bf16[4,64,512]{2,1,0:T(8,128)(2,1)S(1)}, bf16[128,128]{1,0:T(8,128)(2,1)S(1)}) custom-call(bf16[96,384]{1,0:T(8,128)(2,1)S(1)} %get-tuple-element.158.refs_0_.refs_1_, bf16[128,128]{1,0:T(8,128)(2,1)S(1)} %get-tuple-element.153.refs_1_, bf16[128,128]{1,0:T(8,128)(2,1)S(1)} %collective-permute-done.12.refs_1_.refs_2_, ...), custom_call_target="tpu_custom_call" | custom-call | flops 20000000 | bytes 2000000 | tf_op jit(solution)/shard_map/chip_e1/pallas_call | solution.py:40
  38.3 0.3 local_e2.1.refs_6_
  38.6 0.9 %collective-permute-done.14.refs_1_ = bf16[128,128]{1,0:T(8,128)(2,1)S(1)} collective-permute-done((bf16[128,128]{1,0:T(8,128)(2,1)S(1)}, bf16[128,128]{1,0:T(8,128)(2,1)S(1)}, u32[]{:S(2)}, u32[]{:S(2)}) %collective-permute-start.14) | collective-permute-done | bytes 32800 | tf_op jit(solution)/shard_map/ppermute | solution.py:900
  39.5 0.8 %chip_e2.1 = (bf16[1,64,512]{2,1,0:T(8,128)(2,1)}, f32[8,128]{1,0:T(8,128)S(1)}) custom-call(bf16[128,128]{1,0:T(8,128)(2,1)S(1)} %get-tuple-element.162.refs_0_, bf16[128,128]{1,0:T(8,128)(2,1)S(1)} %collective-permute-done.14.refs_1_, bf16[4,32,512]{2,1,0:T(8,128)(2,1)S(1)} %get-tuple-element.104.refs_5_.refs_2_.refs_6_.refs_3_, ...), custom_call_target="tpu_custom_call" | custom-call | flops 20000000 | bytes 2000000 | tf_op jit(solution)/shard_map/chip_e2/pallas_call | solution.py:40
  40.3 1.1 %collective-permute-done.16.refs_3_ = bf16[96,384]{1,0:T(8,128)(2,1)S(1)} collective-permute-done((bf16[96,384]{1,0:T(8,128)(2,1)S(1)}, bf16[96,384]{1,0:T(8,128)(2,1)S(1)}, u32[]{:S(2)}, u32[]{:S(2)}) %collective-permute-start.16) | collective-permute-done | bytes 73760 | tf_op jit(solution)/shard_map/ppermute | solution.py:900
  41.4 0.5 %collective-permute-done.15.refs_2_ = bf16[96,384]{1,0:T(8,128)(2,1)S(1)} collective-permute-done((bf16[96,384]{1,0:T(8,128)(2,1)S(1)}, bf16[96,384]{1,0:T(8,128)(2,1)S(1)}, u32[]{:S(2)}, u32[]{:S(2)}) %collective-permute-start.15) | collective-permute-done | bytes 73760 | tf_op jit(solution)/shard_map/ppermute | solution.py:900
  42.0 1.3 %collective-permute-done.18.refs_1_ = bf16[96,384]{1,0:T(8,128)(2,1)S(1)} collective-permute-done((bf16[96,384]{1,0:T(8,128)(2,1)S(1)}, bf16[96,384]{1,0:T(8,128)(2,1)S(1)}, u32[]{:S(2)}, u32[]{:S(2)}) %collective-permute-start.18) | collective-permute-done | bytes 73760 | tf_op jit(solution)/shard_map/ppermute | solution.py:900
  43.2 1.0 %end.1 = (f32[330,128]{1,0:T(8,128)}, f32[1,128]{1,0:T(1,128)}, f32[64,330]{1,0:T(8,128)}, f32[1,64]{1,0:T(1,128)}) custom-call(bf16[96,384]{1,0:T(8,128)(2,1)S(1)} %get-tuple-element.169.refs_0_, bf16[96,384]{1,0:T(8,128)(2,1)S(1)} %collective-permute-done.18.refs_1_), custom_call_target="tpu_custom_call" | custom-call | flops 20000000 | bytes 2000000 | tf_op jit(solution)/shard_map/end/pallas_call | solution.py:40
  (26 shorter events, 0.5 us)
Async XLA Ops:
  2.2 9.5 %collective-permute-start = (bf16[80,512]{1,0:T(8,128)(2,1)}, bf16[80,512]{1,0:T(8,128)(2,1)S(1)}, u32[]{:S(2)}, u32[]{:S(2)}) collective-permute-start(bf16[80,512]{1,0:T(8,128)(2,1)} %get-tuple-element.90), channel_id=1, source_target_pairs={{0,4},{1,5},{2,6},{3,7},{4,0},{5,1},{6,2},{7,3},{8,12},{9,13},{10,... | collective-permute-start | bytes 245768 | tf_op jit(solution)/shard_map/ppermute | solution.py:900
  6.3 7.5 %collective-permute-start.4 = (bf16[1,64,512]{2,1,0:T(8,128)(2,1)}, bf16[1,64,512]{2,1,0:T(8,128)(2,1)S(1)}, u32[]{:S(2)}, u32[]{:S(2)}) collective-permute-start(bf16[1,64,512]{2,1,0:T(8,128)(2,1)} %refs_0_.3), channel_id=1, source_target_pairs={{0,4},{1,5},{2,6},{3,7},{4,0},{5,1},{6,2},{7,3},{8,12},{9,13},{10,... | collective-permute-start | bytes 196616 | tf_op jit(solution)/shard_map/ppermute | solution.py:900
  6.3 8.7 %collective-permute-start.2 = (bf16[80,512]{1,0:T(8,128)(2,1)}, bf16[80,512]{1,0:T(8,128)(2,1)S(1)}, u32[]{:S(2)}, u32[]{:S(2)}) collective-permute-start(bf16[80,512]{1,0:T(8,128)(2,1)} %get-tuple-element.90), channel_id=1, source_target_pairs={{0,2},{1,3},{2,0},{3,1},{4,6},{5,7},{6,4},{7,5},{8,10},{9,11},{10,... | collective-permute-start | bytes 245768 | tf_op jit(solution)/shard_map/ppermute | solution.py:900
  8.2 0.9 %copy-start = (bf16[80,512]{1,0:T(8,128)(2,1)S(1)}, bf16[80,512]{1,0:T(8,128)(2,1)}, u32[]{:S(2)}) copy-start(bf16[80,512]{1,0:T(8,128)(2,1)} %get-tuple-element.91.refs_0_) | copy-start | bytes 245764
  9.1 0.9 %copy-start.1 = (bf16[128,330]{0,1:T(8,128)(2,1)S(1)}, bf16[128,330]{0,1:T(8,128)(2,1)}, u32[]{:S(2)}) copy-start(bf16[128,330]{0,1:T(8,128)(2,1)} %param.13) | copy-start | bytes 253444
  10.0 0.8 %copy-start.3 = (bf16[64,330]{1,0:T(8,128)(2,1)S(1)}, bf16[64,330]{1,0:T(8,128)(2,1)}, u32[]{:S(2)}) copy-start(bf16[64,330]{1,0:T(8,128)(2,1)} %refs_2_.3) | copy-start | bytes 126724
  11.7 5.3 %collective-permute-start.1 = (bf16[80,512]{1,0:T(8,128)(2,1)S(1)}, bf16[80,512]{1,0:T(8,128)(2,1)S(1)}, u32[]{:S(2)}, u32[]{:S(2)}) collective-permute-start(bf16[80,512]{1,0:T(8,128)(2,1)S(1)} %collective-permute-done.refs_2_), channel_id=1, source_target_pairs={{0,2},{1,3},{2,0},{3,1},{4,6},{5,7},{6,4},{7,5},{8,10},{9,11},{10,... | collective-permute-start | bytes 245768 | tf_op jit(solution)/shard_map/ppermute | solution.py:900
  13.0 6.0 %collective-permute-start.3 = (bf16[1,64,512]{2,1,0:T(8,128)(2,1)}, bf16[1,64,512]{2,1,0:T(8,128)(2,1)S(1)}, u32[]{:S(2)}, u32[]{:S(2)}) collective-permute-start(bf16[1,64,512]{2,1,0:T(8,128)(2,1)} %refs_0_.3), channel_id=1, source_target_pairs={{0,2},{1,3},{2,0},{3,1},{4,6},{5,7},{6,4},{7,5},{8,10},{9,11},{10,... | collective-permute-start | bytes 196616 | tf_op jit(solution)/shard_map/ppermute | solution.py:900
  13.8 5.3 %collective-permute-start.5 = (bf16[1,64,512]{2,1,0:T(8,128)(2,1)S(1)}, bf16[1,64,512]{2,1,0:T(8,128)(2,1)S(1)}, u32[]{:S(2)}, u32[]{:S(2)}) collective-permute-start(bf16[1,64,512]{2,1,0:T(8,128)(2,1)S(1)} %collective-permute-done.4.refs_1_.refs_2_), channel_id=1, source_target_pairs={{0,2},{1,3},{2,0},{3,1},{4,6},{5,7},{6,4},{7,5},{8,10},{9,11},{10,... | collective-permute-start | bytes 196616 | tf_op jit(solution)/shard_map/ppermute | solution.py:900
  18.1 1.3 %collective-permute-start.6 = (bf16[160,128]{1,0:T(8,128)(2,1)S(1)}, bf16[160,128]{1,0:T(8,128)(2,1)S(1)}, u32[]{:S(2)}, u32[]{:S(2)}) collective-permute-start(bf16[160,128]{1,0:T(8,128)(2,1)S(1)} %get-tuple-element.103.refs_3_), channel_id=1, source_target_pairs={{0,1},{1,0},{2,3},{3,2},{4,5},{5,4},{6,7},{7,6},{8,9},{9,8},{10,11... | collective-permute-start | bytes 122888 | tf_op jit(solution)/shard_map/ppermute | solution.py:900
  20.0 1.3 %collective-permute-start.7 = (bf16[160,128]{1,0:T(8,128)(2,1)S(1)}, bf16[160,128]{1,0:T(8,128)(2,1)S(1)}, u32[]{:S(2)}, u32[]{:S(2)}) collective-permute-start(bf16[160,128]{1,0:T(8,128)(2,1)S(1)} %get-tuple-element.111.refs_0_), channel_id=1, source_target_pairs={{0,1},{1,0},{2,3},{3,2},{4,5},{5,4},{6,7},{7,6},{8,9},{9,8},{10,11... | collective-permute-start | bytes 122888 | tf_op jit(solution)/shard_map/ppermute | solution.py:900
  20.3 1.0 %copy-start.4 = (f32[128]{0:T(128)S(1)}, f32[128]{0:T(128)}, u32[]{:S(2)}) copy-start(f32[128]{0:T(128)} %param.14) | copy-start | bytes 1540
  22.3 1.3 %collective-permute-start.8 = (bf16[128,128]{1,0:T(8,128)(2,1)S(1)}, bf16[128,128]{1,0:T(8,128)(2,1)S(1)}, u32[]{:S(2)}, u32[]{:S(2)}) collective-permute-start(bf16[128,128]{1,0:T(8,128)(2,1)S(1)} %get-tuple-element.119.refs_0_), channel_id=1, source_target_pairs={{0,1},{1,0},{2,3},{3,2},{4,5},{5,4},{6,7},{7,6},{8,9},{9,8},{10,11... | collective-permute-start | bytes 98312 | tf_op jit(solution)/shard_map/ppermute | solution.py:900
  24.1 1.4 %collective-permute-start.9 = (bf16[128,128]{1,0:T(8,128)(2,1)S(1)}, bf16[128,128]{1,0:T(8,128)(2,1)S(1)}, u32[]{:S(2)}, u32[]{:S(2)}) collective-permute-start(bf16[128,128]{1,0:T(8,128)(2,1)S(1)} %get-tuple-element.123.refs_4_), channel_id=1, source_target_pairs={{0,1},{1,0},{2,3},{3,2},{4,5},{5,4},{6,7},{7,6},{8,9},{9,8},{10,11... | collective-permute-start | bytes 98312 | tf_op jit(solution)/shard_map/ppermute | solution.py:900
  24.5 1.0 %copy-start.2 = (bf16[1,64,512]{2,1,0:T(8,128)(2,1)S(1)}, bf16[1,64,512]{2,1,0:T(8,128)(2,1)}, u32[]{:S(2)}) copy-start(bf16[1,64,512]{2,1,0:T(8,128)(2,1)} %refs_0_.3) | copy-start | bytes 196612
  24.5 1.0 %copy-start.5 = (f32[64]{0:T(128)S(1)}, f32[64]{0:T(128)}, u32[]{:S(2)}) copy-start(f32[64]{0:T(128)} %param.16) | copy-start | bytes 772
  26.8 1.8 %collective-permute-start.10 = (bf16[128,128]{1,0:T(8,128)(2,1)S(1)}, bf16[128,128]{1,0:T(8,128)(2,1)S(1)}, u32[]{:S(2)}, u32[]{:S(2)}) collective-permute-start(bf16[128,128]{1,0:T(8,128)(2,1)S(1)} %get-tuple-element.132.refs_0_), channel_id=1, source_target_pairs={{0,1},{1,0},{2,3},{3,2},{4,5},{5,4},{6,7},{7,6},{8,9},{9,8},{10,11... | collective-permute-start | bytes 98312 | tf_op jit(solution)/shard_map/ppermute | solution.py:900
  29.2 1.3 %collective-permute-start.11 = (bf16[128,128]{1,0:T(8,128)(2,1)S(1)}, bf16[128,128]{1,0:T(8,128)(2,1)S(1)}, u32[]{:S(2)}, u32[]{:S(2)}) collective-permute-start(bf16[128,128]{1,0:T(8,128)(2,1)S(1)} %get-tuple-element.142.refs_0_), channel_id=1, source_target_pairs={{0,1},{1,0},{2,3},{3,2},{4,5},{5,4},{6,7},{7,6},{8,9},{9,8},{10,11... | collective-permute-start | bytes 98312 | tf_op jit(solution)/shard_map/ppermute | solution.py:900
  32.4 1.6 %collective-permute-start.13 = (bf16[96,384]{1,0:T(8,128)(2,1)S(1)}, bf16[96,384]{1,0:T(8,128)(2,1)S(1)}, u32[]{:S(2)}, u32[]{:S(2)}) collective-permute-start(bf16[96,384]{1,0:T(8,128)(2,1)S(1)} %get-tuple-element.157), channel_id=1, source_target_pairs={{0,1},{1,0},{2,3},{3,2},{4,5},{5,4},{6,7},{7,6},{8,9},{9,8},{10,11... | collective-permute-start | bytes 221192 | tf_op jit(solution)/shard_map/ppermute | solution.py:900
  32.7 1.2 %collective-permute-start.12 = (bf16[128,128]{1,0:T(8,128)(2,1)S(1)}, bf16[128,128]{1,0:T(8,128)(2,1)S(1)}, u32[]{:S(2)}, u32[]{:S(2)}) collective-permute-start(bf16[128,128]{1,0:T(8,128)(2,1)S(1)} %get-tuple-element.153.refs_1_), channel_id=1, source_target_pairs={{0,1},{1,0},{2,3},{3,2},{4,5},{5,4},{6,7},{7,6},{8,9},{9,8},{10,11... | collective-permute-start | bytes 98312 | tf_op jit(solution)/shard_map/ppermute | solution.py:900
  34.0 6.3 %collective-permute-start.17 = (bf16[96,384]{1,0:T(8,128)(2,1)S(1)}, bf16[96,384]{1,0:T(8,128)(2,1)S(1)}, u32[]{:S(2)}, u32[]{:S(2)}) collective-permute-start(bf16[96,384]{1,0:T(8,128)(2,1)S(1)} %get-tuple-element.168), channel_id=1, source_target_pairs={{0,24},{8,16},{16,8},{24,0},{1,25},{9,17},{17,9},{25,1},{2,26},{10... | collective-permute-start | bytes 221192 | tf_op jit(solution)/shard_map/ppermute | solution.py:900
  37.0 4.4 %collective-permute-start.16 = (bf16[96,384]{1,0:T(8,128)(2,1)S(1)}, bf16[96,384]{1,0:T(8,128)(2,1)S(1)}, u32[]{:S(2)}, u32[]{:S(2)}) collective-permute-start(bf16[96,384]{1,0:T(8,128)(2,1)S(1)} %get-tuple-element.168), channel_id=1, source_target_pairs={{0,16},{8,24},{16,0},{24,8},{1,17},{9,25},{17,1},{25,9},{2,18},{10... | collective-permute-start | bytes 221192 | tf_op jit(solution)/shard_map/ppermute | solution.py:900
  37.5 4.4 %collective-permute-start.15 = (bf16[96,384]{1,0:T(8,128)(2,1)S(1)}, bf16[96,384]{1,0:T(8,128)(2,1)S(1)}, u32[]{:S(2)}, u32[]{:S(2)}) collective-permute-start(bf16[96,384]{1,0:T(8,128)(2,1)S(1)} %get-tuple-element.168), channel_id=1, source_target_pairs={{0,8},{8,0},{16,24},{24,16},{1,9},{9,1},{17,25},{25,17},{2,10},{10... | collective-permute-start | bytes 221192 | tf_op jit(solution)/shard_map/ppermute | solution.py:900
  38.2 1.3 %collective-permute-start.14 = (bf16[128,128]{1,0:T(8,128)(2,1)S(1)}, bf16[128,128]{1,0:T(8,128)(2,1)S(1)}, u32[]{:S(2)}, u32[]{:S(2)}) collective-permute-start(bf16[128,128]{1,0:T(8,128)(2,1)S(1)} %get-tuple-element.162.refs_0_), channel_id=1, source_target_pairs={{0,1},{1,0},{2,3},{3,2},{4,5},{5,4},{6,7},{7,6},{8,9},{9,8},{10,11... | collective-permute-start | bytes 98312 | tf_op jit(solution)/shard_map/ppermute | solution.py:900
  41.9 1.3 %collective-permute-start.18 = (bf16[96,384]{1,0:T(8,128)(2,1)S(1)}, bf16[96,384]{1,0:T(8,128)(2,1)S(1)}, u32[]{:S(2)}, u32[]{:S(2)}) collective-permute-start(bf16[96,384]{1,0:T(8,128)(2,1)S(1)} %get-tuple-element.170), channel_id=1, source_target_pairs={{0,1},{1,0},{2,3},{3,2},{4,5},{5,4},{6,7},{7,6},{8,9},{9,8},{10,11... | collective-permute-start | bytes 221192 | tf_op jit(solution)/shard_map/ppermute | solution.py:900

commit v4 on v3

--- a/solution.py
+++ b/solution.py
@@ -36,13 +36,12 @@
 
 
 def run(kernel, name, outs, *args, scratch=(), flops=20_000_000, vmem=24, after=()):
-    whole = pl.BlockSpec(memory_space=pltpu.VMEM)
     return pl.pallas_call(
         lambda *refs: kernel(*refs[len(after) :]),
         name=name,
         out_shape=[jax.ShapeDtypeStruct(shape, kind) for shape, kind in outs],
-        in_specs=[pl.BlockSpec(memory_space=pl.ANY)] * len(after) + [whole] * len(args),
-        out_specs=[whole] * len(outs),
+        in_specs=[pl.BlockSpec(memory_space=pl.ANY)] * len(after) + [pl.BlockSpec(memory_space=pltpu.VMEM)] * len(args),
+        out_specs=[pl.BlockSpec(memory_space=pltpu.VMEM)] * len(outs),
         scratch_shapes=list(scratch),
         compiler_params=pltpu.CompilerParams(vmem_limit_bytes=vmem * 1024 * 1024),
         cost_estimate=pl.CostEstimate(flops=flops, bytes_accessed=2_000_000, transcendentals=0),
@@ -514,11 +513,12 @@
     return state_grad, grad_gw, grad_gb[0], grad_cw, grad_cb[0]
 
 
-def pack_kernel(own, nb, w, rows, readings, previous, tail):
+def pack_kernel(nb, w, rows, readings, previous, upstream, own, both, tail):
     degree = nb.shape[0]
     nh = rows.shape[1]
     hid = previous.shape[1]
     fin = readings.shape[1]
+    block = own.shape[0]
     tail[...] = jnp.zeros_like(tail)
     tail[:fin, :] = readings[0].astype(F32)
     high = lax.shift_right_logical(nb[...], 5)
@@ -529,13 +529,10 @@
     high = lax.shift_right_logical(rows[...], 5)
     tail[at : at + 1, :nh] = high.astype(F32)
     tail[at + 1 : at + 2, :nh] = (rows[...] - high * 32).astype(F32)
-    own[:hid, :] = previous[0]
-    own[hid:, :] = tail[...].astype(BF16)
-
-
-def pack_entry(nb, w, rows, readings, previous, own, sent, tail):
-    pack_kernel(own, nb, w, rows, readings, previous, tail)
-    sent[...] = own[...]
+    for to in (own, both):
+        to[:hid, :] = previous[0]
+        to[hid:block, :] = tail[...].astype(BF16)
+    both[block:, :] = upstream[0]
 
 
 def exchange(first, second, hc, sc, pay):
@@ -615,14 +612,14 @@
 
 
 def build_late_kernel(cap, hid, fin, degree, parts, last, *refs):
-    early, outs, pay = refs[:7], refs[7:14], refs[14]
+    early, outs, pay = refs[:5], refs[5:12], refs[12]
     z = lax.shift_right_logical(lax.axis_index("dom"), 1)
     for k in range(parts - 1):
         p = lax.bitwise_xor(z, jnp.int32(k))
-        for source, to in zip(early, outs):
+        for source, to in zip(early, outs[2:]):
             to[p] = source[k]
     p = lax.bitwise_xor(z, jnp.int32(parts - 1))
-    build_part(cap, hid, fin, degree, parts, p, last, *(ref.at[p] for ref in outs))
+    build_part(cap, hid, fin, degree, parts, p, last, outs[0].at[0], outs[1].at[0], *(ref.at[p] for ref in outs[2:]))
     hc, sc, b = outs[2], outs[4], outs[6]
     base = [b[p] for p in range(parts)]
     exchange(base, base, hc, sc, pay)
@@ -654,10 +651,19 @@
     order[...] = jnp.where(iota(order.shape, 1) == source, 1.0, 0.0).astype(BF16)
 
 
-def local_kernel(a, at, x1, x2, l1, l2):
-    for p in range(a.shape[0]):
-        l1[p] = nn(x1[p], a[p])
-        l2[p] = nn(x2[p], at[p])
+def here(early, late, k):
+    z = lax.shift_right_logical(lax.axis_index("dom"), 1)
+    count = early.shape[0]
+    return lax.bitwise_xor(z, jnp.int32(k)), early[k] if k < count else late[k - count]
+
+
+def local_kernel(a0, at0, a1, at1, x1, x2, l1, l2):
+    for k in range(x1.shape[0]):
+        p, a = here(a0, a1, k)
+        l1[p] = nn(x1[p], a)
+    for k in range(x1.shape[0]):
+        p, at = here(at0, at1, k)
+        l2[p] = nn(x2[p], at)
 
 
 def arrive(sx, hx, mine, got, l1, l2):
@@ -684,12 +690,16 @@
     exchange(ins, outs, hc, sc, pay)
 
 
-def local_b_kernel(a, at, sa, gw, l1, l2, gp):
+def local_b_kernel(a0, at0, a1, at1, sa, gw, l1, l2, gp):
     chans = l1.shape[1]
     weights = gw[:, : 3 * chans]
-    for p in range(a.shape[0]):
-        l1[p] = nn(sa[p, 2 * chans :, :], a[p])
-        l2[p] = nn(sa[p, chans : 2 * chans, :], at[p])
+    for k in range(sa.shape[0]):
+        p, a = here(a0, a1, k)
+        l1[p] = nn(sa[p, 2 * chans :, :], a)
+    for k in range(sa.shape[0]):
+        p, at = here(at0, at1, k)
+        l2[p] = nn(sa[p, chans : 2 * chans, :], at)
+    for p in range(sa.shape[0]):
         gp[p] = nn(weights, sa[p])
 
 
@@ -726,13 +736,17 @@
             ma[p, m * chans + hid : (m + 1) * chans, :] = sa[p, m * chans + hid : (m + 1) * chans, :]
 
 
-def local_c2_kernel(a, at, ma, cw, l1, l2, cp):
+def local_c2_kernel(a0, at0, a1, at1, ma, cw, l1, l2, cp):
     hid = l1.shape[1]
     chans = ma.shape[1] // 3
     weights = cw[:, : 3 * chans]
-    for p in range(a.shape[0]):
-        l1[p] = nn(ma[p, 2 * chans : 2 * chans + hid, :], a[p])
-        l2[p] = nn(ma[p, chans : chans + hid, :], at[p])
+    for k in range(ma.shape[0]):
+        p, a = here(a0, a1, k)
+        l1[p] = nn(ma[p, 2 * chans : 2 * chans + hid, :], a)
+    for k in range(ma.shape[0]):
+        p, at = here(at0, at1, k)
+        l2[p] = nn(ma[p, chans : chans + hid, :], at)
+    for p in range(ma.shape[0]):
         cp[p] = nn(weights, ma[p])
 
 
@@ -758,7 +772,7 @@
     chans = ma.shape[1] // 3
     z = lax.shift_right_logical(lax.axis_index("dom"), 1)
     for k in range(parts):
-        upstream[lax.bitwise_xor(z, jnp.int32(k))] = ups[k][0]
+        upstream[lax.bitwise_xor(z, jnp.int32(k))] = ups[k][0] if len(ups[k].shape) == 3 else ups[k][ups[k].shape[0] - hid :, :]
     bias = column(cb[...])
     weights = cw[:, 3 * chans :]
     parts, pulled, pushed = arrive(sx, hx, mine, got, l1, l2)
@@ -788,8 +802,8 @@
     return nn(one, order[:split, :]) + nn(two, order[split:, :])
 
 
-def local_d_kernel(a, at, y1, y2, cand_grad, ma, mb, order, l1, l2, part):
-    local_kernel(a, at, y1, y2, l1, l2)
+def local_d_kernel(a0, at0, a1, at1, y1, y2, cand_grad, ma, mb, order, l1, l2, part):
+    local_kernel(a0, at0, a1, at1, y1, y2, l1, l2)
     part[...] = chip_part(cand_grad, ma, mb, order).astype(BF16)
 
 
@@ -803,9 +817,11 @@
         z2[p] = two[p]
 
 
-def local_d2_kernel(a, at, z1, z2, direct, base):
-    for p in range(a.shape[0]):
-        base[p] = direct[p] + nn(z1[p], a[p]) + nn(z2[p], at[p])
+def local_d2_kernel(a0, at0, a1, at1, z1, z2, direct, base):
+    for k in range(z1.shape[0]):
+        p, a = here(a0, a1, k)
+        _, at = here(at0, at1, k)
+        base[p] = direct[p] + nn(z1[p], a) + nn(z2[p], at)
 
 
 def chip_d2_kernel(mine, got, hc, hx, sc, sx, base, ro, ri, sa, gw_b, upstream, reset, update, gate_update,
@@ -839,7 +855,7 @@
 
 def local_e_kernel(a, at, z1, z2, direct, base):
     z = lax.shift_right_logical(lax.axis_index("dom"), 1)
-    base[...] = direct[z] + nn(z1[z], a[z]) + nn(z2[z], at[z])
+    base[...] = direct[z] + nn(z1[z], a[0]) + nn(z2[z], at[0])
 
 
 def chip_e_kernel(mine, got, hc, hx, sc, sx, base, out, done):
@@ -899,13 +915,15 @@
     def swap(array, k, axis="dom", size=nd):
         return lax.ppermute(array, axis, [(i, i ^ k) for i in range(size)])
 
-    own, sent = run(
-        pack_entry, "pack", [((block, n), BF16)] * 2, neighbours, edge_weight, send_rows, readings, previous,
+    own, both = run(
+        pack_kernel, "pack", [((block, n), BF16), ((block + hid, n), BF16)],
+        neighbours, edge_weight, send_rows, readings, previous, upstream,
         scratch=[pltpu.VMEM((block - hid, n), F32)], vmem=56,
     )
-    blocks = [own] + [swap(sent, 2 * k) for k in range(1, parts - 1)]
-    relay = blocks[-1] if parts > 2 else sent
-    ups = [upstream] + [swap(upstream, 2 * k) for k in range(1, parts - 1)]
+    near = swap(both, 2)
+    blocks = [own] + [near if k == 1 else swap(own, 2 * k) for k in range(1, parts - 1)]
+    relay = blocks[-1]
+    ups = [upstream] + [near if k == 1 else swap(upstream, 2 * k) for k in range(1, parts - 1)]
     ups.append(swap(ups[-1], 2))
     width = -(-(orders * chans + 1) // LANES) * LANES
     gw, cw, gw_b, cw_b, order = run(
@@ -922,43 +940,45 @@
     built = [((n, n), BF16)] * 2 + [((rows, n), BF16) for rows in (2 * parts * cap, slots)] * 2 + [((block, n), BF16)]
     early = run(
         functools.partial(build_early_kernel, cap, hid, fin, degree, parts), "build_early",
-        [((parts - 1, *shape), kind) for shape, kind in built], *blocks[:-1], relay if parts > 2 else own,
+        [((parts - 1, *shape), kind) for shape, kind in built], *blocks[:-1], relay,
     )
     a, at, hc, hx, sc, sx, b, pay = run(
         functools.partial(build_late_kernel, cap, hid, fin, degree, parts), "build_late",
-        [((parts, *shape), kind) for shape, kind in built] + [wide_pay], swap(relay, 2), *early,
-    )
+        [((1 if shape == (n, n) else parts, *shape), kind) for shape, kind in built] + [wide_pay],
+        swap(relay, 2), *early[2:],
+    )
+    local = (early[0], early[1], a, at)
     edges = (hc, hx, sc, sx)
     got = swap(pay, 1)
-    l1, l2 = run(local_kernel, "local_a", [wide, wide], a, at, b, b)
+    l1, l2 = run(local_kernel, "local_a", [wide, wide], *local, b, b)
     sa, ro, ri, pay = run(
         functools.partial(chip_a_kernel, hid + fin), "chip_a", [first, line, line, wide_pay],
-        pay, got, *edges, b, l1, l2, after=ups[1:],
+        pay, got, *edges, b, l1, l2, after=ups[2:],
     )
     got = swap(pay, 1)
-    l1, l2, gp = run(local_b_kernel, "local_b", [wide, wide, ((parts, 2 * hid, n), F32)], a, at, sa, gw)
+    l1, l2, gp = run(local_b_kernel, "local_b", [wide, wide, ((parts, 2 * hid, n), F32)], *local, sa, gw)
     sb, reset, update, y, pay = run(
         chip_b_kernel, "chip_b", [second, field, field, field16, pay_kind],
         pay, got, *edges, sa, l1, l2, ro, ri, gw, gate_bias[None, :], gp,
     )
     got = swap(pay, 1)
-    l1, l2 = run(local_kernel, "local_c1", [field, field], a, at, y, y)
+    l1, l2 = run(local_kernel, "local_c1", [field, field], *local, y, y)
     ma, pay = run(chip_c1_kernel, "chip_c1", [first, pay_kind], pay, got, *edges, y, sa, l1, l2, ro, ri)
     got = swap(pay, 1)
-    l1, l2, cp = run(local_c2_kernel, "local_c2", [field, field, field], a, at, ma, cw)
+    l1, l2, cp = run(local_c2_kernel, "local_c2", [field, field, field], *local, ma, cw)
     mb, cand_grad, gate_update, y1, y2, g1, g3, up, direct, pay = run(
         functools.partial(chip_c2_kernel, parts), "chip_c2", [second] + [field16] * 7 + [field, pay_kind],
         *ups, pay, got, *edges, ma, sa, sb, l1, l2, ro, ri, cw, cw_b, cand_bias[None, :], cp, update,
     )
     got = swap(pay, 1)
     l1, l2, part = run(
-        local_d_kernel, "local_d1", [field, field, ((hid, width), BF16)], a, at, y1, y2, cand_grad, ma, mb, order
+        local_d_kernel, "local_d1", [field, field, ((hid, width), BF16)], *local, y1, y2, cand_grad, ma, mb, order
     )
     z1, z2, pay = run(
         chip_d1_kernel, "chip_d1", [field16, field16, pay_kind], pay, got, *edges, l1, l2, g1, g3, ro, ri
     )
     got = swap(pay, 1)
-    (base,) = run(local_d2_kernel, "local_d2", [field], a, at, z1, z2, direct)
+    (base,) = run(local_d2_kernel, "local_d2", [field], *local, z1, z2, direct)
     gate_grad, y1, y2, g1, g3, direct, pay = run(
         chip_d2_kernel, "chip_d2", [((parts, 2 * hid, n), BF16)] + [field16] * 4 + [field, pay_kind],
         pay, got, *edges, base, ro, ri, sa, gw_b, up, reset, update, gate_update,
@@ -968,14 +988,14 @@
     keep, give = run(
         grads_kernel, "grads", [half, half], gate_grad, sa, sb, order, part, scratch=[pltpu.VMEM((3 * hid, width), F32)]
     )
-    l1, l2 = run(local_kernel, "local_e1", [field, field], a, at, y1, y2)
+    l1, l2 = run(local_kernel, "local_e1", [field, field], *local, y1, y2)
     mine, sent = run(sum_kernel, "sum_core", [half] * 2, keep, swap(give, 1), after=[l1, got])
     every = [mine] + [swap(sent, k, "snap", snaps) for k in range(1, snaps)]
     z1, z2, pay = run(
         chip_d1_kernel, "chip_e1", [field16, field16, pay_kind], pay, got, *edges, l1, l2, g1, g3, ro, ri, after=[mine],
     )
     got = swap(pay, 1)
-    (base,) = run(local_e_kernel, "local_e2", [((hid, n), F32)], a, at, z1, z2, direct)
+    (base,) = run(local_e_kernel, "local_e2", [((hid, n), F32)], early[0], early[1], z1, z2, direct)
     state_grad, done = run(
         chip_e_kernel, "chip_e2", [((1, hid, n), BF16), ((8, LANES), F32)], pay, got, *edges, base
     )

time: 44.6 us -> 43.3 us (0.971)
  starting transfers between devices: 15.3 us -> 13.6 us
  waiting for transfers between devices: 5.49 us -> 6.3 us
    ppermute x19 -> x18, starting transfers between devices: 15.3 us -> 13.6 us  [swap(): return lax.ppermute(array, axis, [(i, i ^ k) for i in range(size)])]
    ppermute x19 -> x18, waiting for transfers between devices: 5.49 us -> 6.3 us  [swap(): return lax.ppermute(array, axis, [(i, i ^ k) for i in range(size)])]
  transfers between devices with their start and end apart: 19 -> 18, of which waited for: 8 -> 8; matrix products, arithmetic and copies ran while one was open for 0% -> 0% of each run, Pallas kernels for 26% -> 26%
where the time goes in v4:
time: 43.3 us; the launch traced here: 43 us
  Pallas kernels  19.7 us (45%)
  starting transfers between devices  13.6 us (31%)
  waiting for transfers between devices  6.3 us (15%)
  local copies, waits for them, and re-layouts  2.58 us (6%)
  between operations  0.81 us (2%)
    pallas_call x24, Pallas kernels, run(): pl.pallas_call(lambda *refs: kernel(*refs[len(after):]), name=name, out_s...  19.7 us
    ppermute x18, starting transfers between devices, swap(): return lax.ppermute(array, axis, [(i, i ^ k) for i in range(size)])  13.6 us
    ppermute x18, waiting for transfers between devices, swap(): return lax.ppermute(array, axis, [(i, i ^ k) for i in range(size)])  6.3 us
    unnamed x12, local copies, waits for them, and re-layouts  2.58 us
  transfers between devices with their start and end apart: 18, of which 8 were waited for; matrix products, arithmetic and copies ran while one was open for 0% of the time, Pallas kernels for 26%

profile of v4, /device:TPU:0, one launch (start us, length us, event | category | flops | bytes accessed | tf_op | source)
XLA Modules:
  0.0 43.0 jit_solution(7527805785243787089)
XLA Ops:
  0.6 1.7 %pack.1 = (bf16[80,512]{1,0:T(8,128)(2,1)}, bf16[144,512]{1,0:T(8,128)(2,1)}) custom-call(s32[4,512]{1,0:T(4,128)} %refs_0_.2, f32[4,512]{1,0:T(4,128)} %refs_1_.1, s32[1,32]{1,0:T(1,128)} %refs_2_.2, bf16[1,2,512]{2,1,0:T(2,128)(2,1)} %refs_3_.1, bf16[1,64,512]{2,1,0:T(8,128)(2,1)} %refs_4_.1, bf16[1,64,512]{2,1,0:T(8,128)(2,1)} %refs_0_.3), custom_call_target="tpu_custom_call" | custom-call | flops 20000000 | bytes 2000000 | tf_op jit(solution)/shard_map/pack/pallas_call | solution.py:39
  2.3 4.0 %collective-permute-start.1 = (bf16[80,512]{1,0:T(8,128)(2,1)}, bf16[80,512]{1,0:T(8,128)(2,1)S(1)}, u32[]{:S(2)}, u32[]{:S(2)}) collective-permute-start(bf16[80,512]{1,0:T(8,128)(2,1)} %get-tuple-element.90.refs_0_), channel_id=1, source_target_pairs={{0,4},{1,5},{2,6},{3,7},{4,0},{5,1},{6,2},{7,3},{8,12},{9,13},{10,... | collective-permute-start | bytes 245768 | tf_op jit(solution)/shard_map/ppermute | solution.py:916
  6.3 1.6 %collective-permute-start = (bf16[144,512]{1,0:T(8,128)(2,1)}, bf16[144,512]{1,0:T(8,128)(2,1)S(1)}, u32[]{:S(2)}, u32[]{:S(2)}) collective-permute-start(bf16[144,512]{1,0:T(8,128)(2,1)} %get-tuple-element.91), channel_id=1, source_target_pairs={{0,2},{1,3},{2,0},{3,1},{4,6},{5,7},{6,4},{7,5},{8,10},{9,11},{10,... | collective-permute-start | bytes 442376 | tf_op jit(solution)/shard_map/ppermute | solution.py:916
  7.9 0.3 collective-permute-start.3
  8.2 0.9 %copy-done = bf16[80,512]{1,0:T(8,128)(2,1)S(1)} copy-done((bf16[80,512]{1,0:T(8,128)(2,1)S(1)}, bf16[80,512]{1,0:T(8,128)(2,1)}, u32[]{:S(2)}) %copy-start) | copy-done | bytes 81944
  9.1 0.9 %copy-done.2 = bf16[128,330]{0,1:T(8,128)(2,1)S(1)} copy-done((bf16[128,330]{0,1:T(8,128)(2,1)S(1)}, bf16[128,330]{0,1:T(8,128)(2,1)}, u32[]{:S(2)}) %copy-start.2) | copy-done | bytes 84504
  10.0 0.8 %copy-done.3 = bf16[64,330]{1,0:T(8,128)(2,1)S(1)} copy-done((bf16[64,330]{1,0:T(8,128)(2,1)S(1)}, bf16[64,330]{1,0:T(8,128)(2,1)}, u32[]{:S(2)}) %copy-start.3) | copy-done | bytes 42264
  10.8 0.6 %order.1 = (bf16[128,400]{1,0:T(8,128)(2,1)S(1)}, bf16[64,400]{1,0:T(8,128)(2,1)S(1)}, bf16[320,128]{1,0:T(8,128)(2,1)S(1)}, bf16[320,64]{1,0:T(8,128)(2,1)S(1)}, bf16[400,384]{1,0:T(8,128)(2,1)S(1)}) custom-call(bf16[80,512]{1,0:T(8,128)(2,1)S(1)} %copy-done, bf16[330,128]{1,0:T(8,128)(2,1)S(1)} %bitcast.6, bf16[64,330]{1,0:T(8,128)(2,1)S(1)} %copy-done.3), custom_call_target="tpu_custom_call" | custom-call | flops 20000000 | bytes 2000000 | tf_op jit(solution)/shard_map/order/pallas_call | solution.py:39
  11.5 0.3 collective-permute-start.2
  11.8 2.1 %collective-permute-done.3.refs_0_.refs_2_ = bf16[1,64,512]{2,1,0:T(8,128)(2,1)S(1)} collective-permute-done((bf16[1,64,512]{2,1,0:T(8,128)(2,1)}, bf16[1,64,512]{2,1,0:T(8,128)(2,1)S(1)}, u32[]{:S(2)}, u32[]{:S(2)}) %collective-permute-start.3) | collective-permute-done | bytes 65568 | tf_op jit(solution)/shard_map/ppermute | solution.py:916
  13.9 1.3 %collective-permute-start.4 = (bf16[1,64,512]{2,1,0:T(8,128)(2,1)S(1)}, bf16[1,64,512]{2,1,0:T(8,128)(2,1)S(1)}, u32[]{:S(2)}, u32[]{:S(2)}) collective-permute-start(bf16[1,64,512]{2,1,0:T(8,128)(2,1)S(1)} %collective-permute-done.3.refs_0_.refs_2_), channel_id=1, source_target_pairs={{0,2},{1,3},{2,0},{3,1},{4,6},{5,7},{6,4},{7,5},{8,10},{9,11},{10,... | collective-permute-start | bytes 196616 | tf_op jit(solution)/shard_map/ppermute | solution.py:916
  15.2 1.2 %build_early.1 = (bf16[3,512,512]{2,1,0:T(8,128)(2,1)S(1)}, bf16[3,512,512]{2,1,0:T(8,128)(2,1)S(1)}, bf16[3,32,512]{2,1,0:T(8,128)(2,1)S(1)}, bf16[3,128,512]{2...) custom-call(bf16[80,512]{1,0:T(8,128)(2,1)S(1)} %copy-done, ...), custom_call_target="tpu_custom_call" | custom-call | flops 20000000 | bytes 2000000 | tf_op jit(solution)/shard_map/build_early/pallas_call | solution.py:39
  16.4 0.3 collective-permute-done.2.refs_0_
  16.7 0.6 %build_late.1 = (bf16[1,512,512]{2,1,0:T(8,128)(2,1)S(1)}, bf16[1,512,512]{2,1,0:T(8,128)(2,1)S(1)}, bf16[4,32,512]{2,1,0:T(8,128)(2,1)S(1)}, bf16[4,128,512]{2,...) custom-call(bf16[80,512]{1,0:T(8,128)(2,1)S(1)} %collective-permute-, ...), custom_call_target="tpu_custom_call" | custom-call | flops 20000000 | bytes 2000000 | tf_op jit(solution)/shard_map/build_late/pallas_call | solution.py:39
  17.4 0.9 %local_a.1 = (f32[4,80,512]{2,1,0:T(8,128)S(1)}, f32[4,80,512]{2,1,0:T(8,128)S(1)}) custom-call(bf16[3,512,512]{2,1,0:T(8,128)(2,1)S(1)} %get-tuple-element.94.refs_0_, bf16[3,512,512]{2,1,0:T(8,128)(2,1)S(1)} %get-tuple-element.95.refs_1_, bf16[1,512,512]{2,1,0:T(8,128)(2,1)S(1)} %get-tuple-element.101.refs_2_, ...), custom_call_target="tpu_custom_call" | custom-call | flops 20000000 | bytes 2000000 | tf_op jit(solution)/shard_map/local_a/pallas_call | solution.py:39
  18.2 0.3 collective-permute-done.5.refs_3_
  18.6 0.7 %chip_a.1 = (bf16[4,240,512]{2,1,0:T(8,128)(2,1)S(1)}, f32[4,1,512]{2,1,0:T(1,128)S(1)}, f32[4,1,512]{2,1,0:T(1,128)S(1)}, bf16[160,128]{1,0:T(8,128)(2,1)S(1)}) custom-call(bf16[1,64,512]{2,1,0:T(8,128)(2,1)S(1)} %collective-permute-done.3.refs_0_.refs_2_, bf16[1,64,512]{2,1,0:T(8,128)(2,1)S(1)} %collective-permute-done.4.refs_1_.refs_3_, ...), custom_call_target="tpu_custom_call" | custom-call | flops 20000000 | bytes 2000000 | tf_op jit(solution)/shard_map/chip_a/pallas_call | solution.py:39
  19.2 0.2 collective-permute-start.6
  19.5 1.0 %local_b.1 = (f32[4,80,512]{2,1,0:T(8,128)S(1)}, f32[4,80,512]{2,1,0:T(8,128)S(1)}, f32[4,128,512]{2,1,0:T(8,128)S(1)}) custom-call(bf16[3,512,512]{2,1,0:T(8,128)(2,1)S(1)} %get-tuple-element.94.refs_0_, bf16[3,512,512]{2,1,0:T(8,128)(2,1)S(1)} %get-tuple-element.95.refs_1_, bf16[1,512,512]{2,1,0:T(8,128)(2,1)S(1)} %get-tuple-element.101.refs_2_, ...), custom_call_target="tpu_custom_call" | custom-call | flops 20000000 | bytes 2000000 | tf_op jit(solution)/shard_map/local_b/pallas_call | solution.py:39
  20.5 1.0 %chip_b.1 = (bf16[4,160,512]{2,1,0:T(8,128)(2,1)S(1)}, f32[4,64,512]{2,1,0:T(8,128)S(1)}, f32[4,64,512]{2,1,0:T(8,128)S(1)}, bf16[4,64,512]{2,1,0:T(8,128)(2,1)S(1)}, bf16[128,128]{1,0:T(8,128)(2,1)S(1)}) custom-call(bf16[160,128]{1,0:T(8,128)(2,1)S(1)} %get-tuple-element.111.refs_0_, bf16[160,128]{1,0:T(8,128)(2,1)S(1)} %collective-permute-done.6.refs_1_, ...), custom_call_target="tpu_custom_call" | custom-call | flops 20000000 | bytes 2000000 | tf_op jit(solution)/shard_map/chip_b/pallas_call | solution.py:39
  21.5 0.4 collective-permute-start.7
  21.9 0.8 %local_c1.1 = (f32[4,64,512]{2,1,0:T(8,128)S(1)}, f32[4,64,512]{2,1,0:T(8,128)S(1)}) custom-call(bf16[3,512,512]{2,1,0:T(8,128)(2,1)S(1)} %get-tuple-element.94.refs_0_, bf16[3,512,512]{2,1,0:T(8,128)(2,1)S(1)} %get-tuple-element.95.refs_1_, bf16[1,512,512]{2,1,0:T(8,128)(2,1)S(1)} %get-tuple-element.101.refs_2_, ...), custom_call_target="tpu_custom_call" | custom-call | flops 20000000 | bytes 2000000 | tf_op jit(solution)/shard_map/local_c1/pallas_call | solution.py:39
  22.8 0.5 %chip_c1.1 = (bf16[4,240,512]{2,1,0:T(8,128)(2,1)S(1)}, bf16[128,128]{1,0:T(8,128)(2,1)S(1)}) custom-call(bf16[128,128]{1,0:T(8,128)(2,1)S(1)} %get-tuple-element.119.refs_0_, bf16[128,128]{1,0:T(8,128)(2,1)S(1)} %collective-permute-done.7.refs_1_, bf16[4,32,512]{2,1,0:T(8,128)(2,1)S(1)} %get-tuple-element.104.refs_4_.refs_2_.refs_6_.refs_3_, ...), custom_call_target="tpu_custom_call" | custom-call | flops 20000000 | bytes 2000000 | tf_op jit(solution)/shard_map/chip_c1/pallas_call | solution.py:39
  23.3 0.4 collective-permute-start.8
  23.7 1.0 %local_c2.1 = (f32[4,64,512]{2,1,0:T(8,128)S(1)}, f32[4,64,512]{2,1,0:T(8,128)S(1)}, f32[4,64,512]{2,1,0:T(8,128)S(1)}) custom-call(bf16[3,512,512]{2,1,0:T(8,128)(2,1)S(1)} %get-tuple-element.94.refs_0_, bf16[3,512,512]{2,1,0:T(8,128)(2,1)S(1)} %get-tuple-element.95.refs_1_, bf16[1,512,512]{2,1,0:T(8,128)(2,1)S(1)} %get-tuple-element.101.refs_2_, ...), custom_call_target="tpu_custom_call" | custom-call | flops 20000000 | bytes 2000000 | tf_op jit(solution)/shard_map/local_c2/pallas_call | solution.py:39
  24.8 1.3 %chip_c2.1 = (bf16[4,160,512]{2,1,0:T(8,128)(2,1)S(1)}, bf16[4,64,512]{2,1,0:T(8,128)(2,1)S(1)}, bf16[4,64,512]{2,1,0:T(8,128)(2,1)S(1)}, bf16[4,64,512]{2,1,0:T...) custom-call(bf16[1,64,512]{2,1,0:T(8,128)(2,1)S(1)} %copy-done.1, ...), custom_call_target="tpu_custom_call" | custom-call | flops 20000000 | bytes 2000000 | tf_op jit(solution)/shard_map/chip_c2/pallas_call | solution.py:39
  26.1 0.2 collective-permute-start.9
  26.3 1.5 %local_d1.1 = (f32[4,64,512]{2,1,0:T(8,128)S(1)}, f32[4,64,512]{2,1,0:T(8,128)S(1)}, bf16[64,384]{1,0:T(8,128)(2,1)S(1)}) custom-call(bf16[3,512,512]{2,1,0:T(8,128)(2,1)S(1)} %get-tuple-element.94.refs_0_, bf16[3,512,512]{2,1,0:T(8,128)(2,1)S(1)} %get-tuple-element.95.refs_1_, bf16[1,512,512]{2,1,0:T(8,128)(2,1)S(1)} %get-tuple-element.101.refs_2_, ...), custom_call_target="tpu_custom_call" | custom-call | flops 20000000 | bytes 2000000 | tf_op jit(solution)/shard_map/local_d1/pallas_call | solution.py:39
  27.8 0.6 %chip_d1.1 = (bf16[4,64,512]{2,1,0:T(8,128)(2,1)S(1)}, bf16[4,64,512]{2,1,0:T(8,128)(2,1)S(1)}, bf16[128,128]{1,0:T(8,128)(2,1)S(1)}) custom-call(bf16[128,128]{1,0:T(8,128)(2,1)S(1)} %get-tuple-element.132.refs_0_, bf16[128,128]{1,0:T(8,128)(2,1)S(1)} %collective-permute-done.9.refs_1_, ...), custom_call_target="tpu_custom_call" | custom-call | flops 20000000 | bytes 2000000 | tf_op jit(solution)/shard_map/chip_d1/pallas_call | solution.py:39
  28.3 0.4 collective-permute-start.10
  28.8 0.8 %local_d2.1.refs_6_ = f32[4,64,512]{2,1,0:T(8,128)S(1)} custom-call(bf16[3,512,512]{2,1,0:T(8,128)(2,1)S(1)} %get-tuple-element.94.refs_0_, bf16[3,512,512]{2,1,0:T(8,128)(2,1)S(1)} %get-tuple-element.95.refs_1_, bf16[1,512,512]{2,1,0:T(8,128)(2,1)S(1)} %get-tuple-element.101.refs_2_, bf16[1,512,512]{2,1,0:T(8,128)(2,1)S(1)} %get-tuple-element.102.refs_3_, ...), custom_call_target="tpu_custom_call" | custom-call | flops 20000000 | bytes 2000000 | tf_op jit(solution)/shard_map/local_d2/pallas_call | solution.py:39
  29.6 1.0 %chip_d2.1 = (bf16[4,128,512]{2,1,0:T(8,128)(2,1)S(1)}, bf16[4,64,512]{2,1,0:T(8,128)(2,1)S(1)}, bf16[4,64,512]{2,1,0:T(8,128)(2,1)S(1)}, bf16[4,64,512]{2,1,0:T...) custom-call(bf16[128,128]{1,0:T(8,128)(2,1)S(1)} %get-tuple-element.142.r, ...), custom_call_target="tpu_custom_call" | custom-call | flops 20000000 | bytes 2000000 | tf_op jit(solution)/shard_map/chip_d2/pallas_call | solution.py:39
  30.7 0.9 %grads.1 = (bf16[96,384]{1,0:T(8,128)(2,1)S(1)}, bf16[96,384]{1,0:T(8,128)(2,1)S(1)}) custom-call(bf16[4,128,512]{2,1,0:T(8,128)(2,1)S(1)} %get-tuple-element.154.refs_0_, bf16[4,240,512]{2,1,0:T(8,128)(2,1)S(1)} %get-tuple-element.112.refs_4_.refs_6_.refs_7_.refs_11_.refs_9_.refs_1_, bf16[4,160,512]{2,1,0:T(8,128)(2,1)S(1)} %get-tuple-element.125.refs_12_.refs_2_, ...), custom_call_target="tpu_custom_call" | custom-call | flops 20000000 | bytes 2000000 | tf_op jit(solution)/shard_map/grads/pallas_call | solution.py:39
  31.6 0.4 collective-permute-start.12
  32.0 0.2 collective-permute-start.11
  32.1 0.8 %local_e1.1 = (f32[4,64,512]{2,1,0:T(8,128)S(1)}, f32[4,64,512]{2,1,0:T(8,128)S(1)}) custom-call(bf16[3,512,512]{2,1,0:T(8,128)(2,1)S(1)} %get-tuple-element.94.refs_0_, bf16[3,512,512]{2,1,0:T(8,128)(2,1)S(1)} %get-tuple-element.95.refs_1_, bf16[1,512,512]{2,1,0:T(8,128)(2,1)S(1)} %get-tuple-element.101.refs_2_, ...), custom_call_target="tpu_custom_call" | custom-call | flops 20000000 | bytes 2000000 | tf_op jit(solution)/shard_map/local_e1/pallas_call | solution.py:39
  33.0 0.2 collective-permute-done.11.refs_1_.refs_2_
  33.2 2.5 %collective-permute-start.16 = (bf16[96,384]{1,0:T(8,128)(2,1)S(1)}, bf16[96,384]{1,0:T(8,128)(2,1)S(1)}, u32[]{:S(2)}, u32[]{:S(2)}) collective-permute-start(bf16[96,384]{1,0:T(8,128)(2,1)S(1)} %get-tuple-element.168), channel_id=1, source_target_pairs={{0,24},{8,16},{16,8},{24,0},{1,25},{9,17},{17,9},{25,1},{2,26},{10... | collective-permute-start | bytes 221192 | tf_op jit(solution)/shard_map/ppermute | solution.py:916
  35.7 0.5 %collective-permute-start.15 = (bf16[96,384]{1,0:T(8,128)(2,1)S(1)}, bf16[96,384]{1,0:T(8,128)(2,1)S(1)}, u32[]{:S(2)}, u32[]{:S(2)}) collective-permute-start(bf16[96,384]{1,0:T(8,128)(2,1)S(1)} %get-tuple-element.168), channel_id=1, source_target_pairs={{0,16},{8,24},{16,0},{24,8},{1,17},{9,25},{17,1},{25,9},{2,18},{10... | collective-permute-start | bytes 221192 | tf_op jit(solution)/shard_map/ppermute | solution.py:916
  36.2 0.5 %collective-permute-start.14 = (bf16[96,384]{1,0:T(8,128)(2,1)S(1)}, bf16[96,384]{1,0:T(8,128)(2,1)S(1)}, u32[]{:S(2)}, u32[]{:S(2)}) collective-permute-start(bf16[96,384]{1,0:T(8,128)(2,1)S(1)} %get-tuple-element.168), channel_id=1, source_target_pairs={{0,8},{8,0},{16,24},{24,16},{1,9},{9,1},{17,25},{25,17},{2,10},{10... | collective-permute-start | bytes 221192 | tf_op jit(solution)/shard_map/ppermute | solution.py:916
  36.8 0.6 %chip_e1.1 = (bf16[4,64,512]{2,1,0:T(8,128)(2,1)S(1)}, bf16[4,64,512]{2,1,0:T(8,128)(2,1)S(1)}, bf16[128,128]{1,0:T(8,128)(2,1)S(1)}) custom-call(bf16[96,384]{1,0:T(8,128)(2,1)S(1)} %get-tuple-element.158.refs_0_.refs_1_, bf16[128,128]{1,0:T(8,128)(2,1)S(1)} %get-tuple-element.153.refs_1_, bf16[128,128]{1,0:T(8,128)(2,1)S(1)} %collective-permute-done.11.refs_1_.refs_2_, ...), custom_call_target="tpu_custom_call" | custom-call | flops 20000000 | bytes 2000000 | tf_op jit(solution)/shard_map/chip_e1/pallas_call | solution.py:39
  37.4 0.3 local_e2.1.refs_6_
  37.7 0.9 %collective-permute-done.13.refs_1_ = bf16[128,128]{1,0:T(8,128)(2,1)S(1)} collective-permute-done((bf16[128,128]{1,0:T(8,128)(2,1)S(1)}, bf16[128,128]{1,0:T(8,128)(2,1)S(1)}, u32[]{:S(2)}, u32[]{:S(2)}) %collective-permute-start.13) | collective-permute-done | bytes 32800 | tf_op jit(solution)/shard_map/ppermute | solution.py:916
  38.6 0.8 %chip_e2.1 = (bf16[1,64,512]{2,1,0:T(8,128)(2,1)}, f32[8,128]{1,0:T(8,128)S(1)}) custom-call(bf16[128,128]{1,0:T(8,128)(2,1)S(1)} %get-tuple-element.162.refs_0_, bf16[128,128]{1,0:T(8,128)(2,1)S(1)} %collective-permute-done.13.refs_1_, bf16[4,32,512]{2,1,0:T(8,128)(2,1)S(1)} %get-tuple-element.104.refs_4_.refs_2_.refs_6_.refs_3_, ...), custom_call_target="tpu_custom_call" | custom-call | flops 20000000 | bytes 2000000 | tf_op jit(solution)/shard_map/chip_e2/pallas_call | solution.py:39
  39.4 0.7 %collective-permute-done.15.refs_3_ = bf16[96,384]{1,0:T(8,128)(2,1)S(1)} collective-permute-done((bf16[96,384]{1,0:T(8,128)(2,1)S(1)}, bf16[96,384]{1,0:T(8,128)(2,1)S(1)}, u32[]{:S(2)}, u32[]{:S(2)}) %collective-permute-start.15) | collective-permute-done | bytes 73760 | tf_op jit(solution)/shard_map/ppermute | solution.py:916
  40.1 0.5 %collective-permute-done.14.refs_2_ = bf16[96,384]{1,0:T(8,128)(2,1)S(1)} collective-permute-done((bf16[96,384]{1,0:T(8,128)(2,1)S(1)}, bf16[96,384]{1,0:T(8,128)(2,1)S(1)}, u32[]{:S(2)}, u32[]{:S(2)}) %collective-permute-start.14) | collective-permute-done | bytes 73760 | tf_op jit(solution)/shard_map/ppermute | solution.py:916
  40.7 1.3 %collective-permute-done.17.refs_1_ = bf16[96,384]{1,0:T(8,128)(2,1)S(1)} collective-permute-done((bf16[96,384]{1,0:T(8,128)(2,1)S(1)}, bf16[96,384]{1,0:T(8,128)(2,1)S(1)}, u32[]{:S(2)}, u32[]{:S(2)}) %collective-permute-start.17) | collective-permute-done | bytes 73760 | tf_op jit(solution)/shard_map/ppermute | solution.py:916
  42.0 1.0 %end.1 = (f32[330,128]{1,0:T(8,128)}, f32[1,128]{1,0:T(1,128)}, f32[64,330]{1,0:T(8,128)}, f32[1,64]{1,0:T(1,128)}) custom-call(bf16[96,384]{1,0:T(8,128)(2,1)S(1)} %get-tuple-element.169.refs_0_, bf16[96,384]{1,0:T(8,128)(2,1)S(1)} %collective-permute-done.17.refs_1_), custom_call_target="tpu_custom_call" | custom-call | flops 20000000 | bytes 2000000 | tf_op jit(solution)/shard_map/end/pallas_call | solution.py:39
  (24 shorter events, 0.4 us)
Async XLA Ops:
  2.3 9.2 %collective-permute-start.1 = (bf16[80,512]{1,0:T(8,128)(2,1)}, bf16[80,512]{1,0:T(8,128)(2,1)S(1)}, u32[]{:S(2)}, u32[]{:S(2)}) collective-permute-start(bf16[80,512]{1,0:T(8,128)(2,1)} %get-tuple-element.90.refs_0_), channel_id=1, source_target_pairs={{0,4},{1,5},{2,6},{3,7},{4,0},{5,1},{6,2},{7,3},{8,12},{9,13},{10,... | collective-permute-start | bytes 245768 | tf_op jit(solution)/shard_map/ppermute | solution.py:916
  6.3 8.8 %collective-permute-start = (bf16[144,512]{1,0:T(8,128)(2,1)}, bf16[144,512]{1,0:T(8,128)(2,1)S(1)}, u32[]{:S(2)}, u32[]{:S(2)}) collective-permute-start(bf16[144,512]{1,0:T(8,128)(2,1)} %get-tuple-element.91), channel_id=1, source_target_pairs={{0,2},{1,3},{2,0},{3,1},{4,6},{5,7},{6,4},{7,5},{8,10},{9,11},{10,... | collective-permute-start | bytes 442376 | tf_op jit(solution)/shard_map/ppermute | solution.py:916
  7.9 6.0 %collective-permute-start.3 = (bf16[1,64,512]{2,1,0:T(8,128)(2,1)}, bf16[1,64,512]{2,1,0:T(8,128)(2,1)S(1)}, u32[]{:S(2)}, u32[]{:S(2)}) collective-permute-start(bf16[1,64,512]{2,1,0:T(8,128)(2,1)} %refs_0_.3), channel_id=1, source_target_pairs={{0,4},{1,5},{2,6},{3,7},{4,0},{5,1},{6,2},{7,3},{8,12},{9,13},{10,... | collective-permute-start | bytes 196616 | tf_op jit(solution)/shard_map/ppermute | solution.py:916
  8.2 0.9 %copy-start = (bf16[80,512]{1,0:T(8,128)(2,1)S(1)}, bf16[80,512]{1,0:T(8,128)(2,1)}, u32[]{:S(2)}) copy-start(bf16[80,512]{1,0:T(8,128)(2,1)} %get-tuple-element.90.refs_0_) | copy-start | bytes 245764
  9.1 0.9 %copy-start.2 = (bf16[128,330]{0,1:T(8,128)(2,1)S(1)}, bf16[128,330]{0,1:T(8,128)(2,1)}, u32[]{:S(2)}) copy-start(bf16[128,330]{0,1:T(8,128)(2,1)} %param.13) | copy-start | bytes 253444
  10.0 0.8 %copy-start.3 = (bf16[64,330]{1,0:T(8,128)(2,1)S(1)}, bf16[64,330]{1,0:T(8,128)(2,1)}, u32[]{:S(2)}) copy-start(bf16[64,330]{1,0:T(8,128)(2,1)} %refs_2_.3) | copy-start | bytes 126724
  11.5 5.2 %collective-permute-start.2 = (bf16[80,512]{1,0:T(8,128)(2,1)S(1)}, bf16[80,512]{1,0:T(8,128)(2,1)S(1)}, u32[]{:S(2)}, u32[]{:S(2)}) collective-permute-start(bf16[80,512]{1,0:T(8,128)(2,1)S(1)} %collective-permute-done.1.refs_2_), channel_id=1, source_target_pairs={{0,2},{1,3},{2,0},{3,1},{4,6},{5,7},{6,4},{7,5},{8,10},{9,11},{10,... | collective-permute-start | bytes 245768 | tf_op jit(solution)/shard_map/ppermute | solution.py:916
  13.9 4.4 %collective-permute-start.4 = (bf16[1,64,512]{2,1,0:T(8,128)(2,1)S(1)}, bf16[1,64,512]{2,1,0:T(8,128)(2,1)S(1)}, u32[]{:S(2)}, u32[]{:S(2)}) collective-permute-start(bf16[1,64,512]{2,1,0:T(8,128)(2,1)S(1)} %collective-permute-done.3.refs_0_.refs_2_), channel_id=1, source_target_pairs={{0,2},{1,3},{2,0},{3,1},{4,6},{5,7},{6,4},{7,5},{8,10},{9,11},{10,... | collective-permute-start | bytes 196616 | tf_op jit(solution)/shard_map/ppermute | solution.py:916
  17.3 1.3 %collective-permute-start.5 = (bf16[160,128]{1,0:T(8,128)(2,1)S(1)}, bf16[160,128]{1,0:T(8,128)(2,1)S(1)}, u32[]{:S(2)}, u32[]{:S(2)}) collective-permute-start(bf16[160,128]{1,0:T(8,128)(2,1)S(1)} %get-tuple-element.103.refs_2_), channel_id=1, source_target_pairs={{0,1},{1,0},{2,3},{3,2},{4,5},{5,4},{6,7},{7,6},{8,9},{9,8},{10,11... | collective-permute-start | bytes 122888 | tf_op jit(solution)/shard_map/ppermute | solution.py:916
  19.2 1.3 %collective-permute-start.6 = (bf16[160,128]{1,0:T(8,128)(2,1)S(1)}, bf16[160,128]{1,0:T(8,128)(2,1)S(1)}, u32[]{:S(2)}, u32[]{:S(2)}) collective-permute-start(bf16[160,128]{1,0:T(8,128)(2,1)S(1)} %get-tuple-element.111.refs_0_), channel_id=1, source_target_pairs={{0,1},{1,0},{2,3},{3,2},{4,5},{5,4},{6,7},{7,6},{8,9},{9,8},{10,11... | collective-permute-start | bytes 122888 | tf_op jit(solution)/shard_map/ppermute | solution.py:916
  19.5 1.1 %copy-start.4 = (f32[128]{0:T(128)S(1)}, f32[128]{0:T(128)}, u32[]{:S(2)}) copy-start(f32[128]{0:T(128)} %param.14) | copy-start | bytes 1540
  21.5 1.3 %collective-permute-start.7 = (bf16[128,128]{1,0:T(8,128)(2,1)S(1)}, bf16[128,128]{1,0:T(8,128)(2,1)S(1)}, u32[]{:S(2)}, u32[]{:S(2)}) collective-permute-start(bf16[128,128]{1,0:T(8,128)(2,1)S(1)} %get-tuple-element.119.refs_0_), channel_id=1, source_target_pairs={{0,1},{1,0},{2,3},{3,2},{4,5},{5,4},{6,7},{7,6},{8,9},{9,8},{10,11... | collective-permute-start | bytes 98312 | tf_op jit(solution)/shard_map/ppermute | solution.py:916
  23.3 1.4 %collective-permute-start.8 = (bf16[128,128]{1,0:T(8,128)(2,1)S(1)}, bf16[128,128]{1,0:T(8,128)(2,1)S(1)}, u32[]{:S(2)}, u32[]{:S(2)}) collective-permute-start(bf16[128,128]{1,0:T(8,128)(2,1)S(1)} %get-tuple-element.123.refs_4_), channel_id=1, source_target_pairs={{0,1},{1,0},{2,3},{3,2},{4,5},{5,4},{6,7},{7,6},{8,9},{9,8},{10,11... | collective-permute-start | bytes 98312 | tf_op jit(solution)/shard_map/ppermute | solution.py:916
  23.7 1.0 %copy-start.1 = (bf16[1,64,512]{2,1,0:T(8,128)(2,1)S(1)}, bf16[1,64,512]{2,1,0:T(8,128)(2,1)}, u32[]{:S(2)}) copy-start(bf16[1,64,512]{2,1,0:T(8,128)(2,1)} %refs_0_.3) | copy-start | bytes 196612
  23.7 1.0 %copy-start.5 = (f32[64]{0:T(128)S(1)}, f32[64]{0:T(128)}, u32[]{:S(2)}) copy-start(f32[64]{0:T(128)} %param.16) | copy-start | bytes 772
  26.1 1.7 %collective-permute-start.9 = (bf16[128,128]{1,0:T(8,128)(2,1)S(1)}, bf16[128,128]{1,0:T(8,128)(2,1)S(1)}, u32[]{:S(2)}, u32[]{:S(2)}) collective-permute-start(bf16[128,128]{1,0:T(8,128)(2,1)S(1)} %get-tuple-element.132.refs_0_), channel_id=1, source_target_pairs={{0,1},{1,0},{2,3},{3,2},{4,5},{5,4},{6,7},{7,6},{8,9},{9,8},{10,11... | collective-permute-start | bytes 98312 | tf_op jit(solution)/shard_map/ppermute | solution.py:916
  28.3 1.3 %collective-permute-start.10 = (bf16[128,128]{1,0:T(8,128)(2,1)S(1)}, bf16[128,128]{1,0:T(8,128)(2,1)S(1)}, u32[]{:S(2)}, u32[]{:S(2)}) collective-permute-start(bf16[128,128]{1,0:T(8,128)(2,1)S(1)} %get-tuple-element.142.refs_0_), channel_id=1, source_target_pairs={{0,1},{1,0},{2,3},{3,2},{4,5},{5,4},{6,7},{7,6},{8,9},{9,8},{10,11... | collective-permute-start | bytes 98312 | tf_op jit(solution)/shard_map/ppermute | solution.py:916
  31.6 1.6 %collective-permute-start.12 = (bf16[96,384]{1,0:T(8,128)(2,1)S(1)}, bf16[96,384]{1,0:T(8,128)(2,1)S(1)}, u32[]{:S(2)}, u32[]{:S(2)}) collective-permute-start(bf16[96,384]{1,0:T(8,128)(2,1)S(1)} %get-tuple-element.157), channel_id=1, source_target_pairs={{0,1},{1,0},{2,3},{3,2},{4,5},{5,4},{6,7},{7,6},{8,9},{9,8},{10,11... | collective-permute-start | bytes 221192 | tf_op jit(solution)/shard_map/ppermute | solution.py:916
  32.0 1.2 %collective-permute-start.11 = (bf16[128,128]{1,0:T(8,128)(2,1)S(1)}, bf16[128,128]{1,0:T(8,128)(2,1)S(1)}, u32[]{:S(2)}, u32[]{:S(2)}) collective-permute-start(bf16[128,128]{1,0:T(8,128)(2,1)S(1)} %get-tuple-element.153.refs_1_), channel_id=1, source_target_pairs={{0,1},{1,0},{2,3},{3,2},{4,5},{5,4},{6,7},{7,6},{8,9},{9,8},{10,11... | collective-permute-start | bytes 98312 | tf_op jit(solution)/shard_map/ppermute | solution.py:916
  33.2 6.2 %collective-permute-start.16 = (bf16[96,384]{1,0:T(8,128)(2,1)S(1)}, bf16[96,384]{1,0:T(8,128)(2,1)S(1)}, u32[]{:S(2)}, u32[]{:S(2)}) collective-permute-start(bf16[96,384]{1,0:T(8,128)(2,1)S(1)} %get-tuple-element.168), channel_id=1, source_target_pairs={{0,24},{8,16},{16,8},{24,0},{1,25},{9,17},{17,9},{25,1},{2,26},{10... | collective-permute-start | bytes 221192 | tf_op jit(solution)/shard_map/ppermute | solution.py:916
  35.7 4.4 %collective-permute-start.15 = (bf16[96,384]{1,0:T(8,128)(2,1)S(1)}, bf16[96,384]{1,0:T(8,128)(2,1)S(1)}, u32[]{:S(2)}, u32[]{:S(2)}) collective-permute-start(bf16[96,384]{1,0:T(8,128)(2,1)S(1)} %get-tuple-element.168), channel_id=1, source_target_pairs={{0,16},{8,24},{16,0},{24,8},{1,17},{9,25},{17,1},{25,9},{2,18},{10... | collective-permute-start | bytes 221192 | tf_op jit(solution)/shard_map/ppermute | solution.py:916
  36.2 4.4 %collective-permute-start.14 = (bf16[96,384]{1,0:T(8,128)(2,1)S(1)}, bf16[96,384]{1,0:T(8,128)(2,1)S(1)}, u32[]{:S(2)}, u32[]{:S(2)}) collective-permute-start(bf16[96,384]{1,0:T(8,128)(2,1)S(1)} %get-tuple-element.168), channel_id=1, source_target_pairs={{0,8},{8,0},{16,24},{24,16},{1,9},{9,1},{17,25},{25,17},{2,10},{10... | collective-permute-start | bytes 221192 | tf_op jit(solution)/shard_map/ppermute | solution.py:916
  37.3 1.3 %collective-permute-start.13 = (bf16[128,128]{1,0:T(8,128)(2,1)S(1)}, bf16[128,128]{1,0:T(8,128)(2,1)S(1)}, u32[]{:S(2)}, u32[]{:S(2)}) collective-permute-start(bf16[128,128]{1,0:T(8,128)(2,1)S(1)} %get-tuple-element.162.refs_0_), channel_id=1, source_target_pairs={{0,1},{1,0},{2,3},{3,2},{4,5},{5,4},{6,7},{7,6},{8,9},{9,8},{10,11... | collective-permute-start | bytes 98312 | tf_op jit(solution)/shard_map/ppermute | solution.py:916
  40.6 1.3 %collective-permute-start.17 = (bf16[96,384]{1,0:T(8,128)(2,1)S(1)}, bf16[96,384]{1,0:T(8,128)(2,1)S(1)}, u32[]{:S(2)}, u32[]{:S(2)}) collective-permute-start(bf16[96,384]{1,0:T(8,128)(2,1)S(1)} %get-tuple-element.170), channel_id=1, source_target_pairs={{0,1},{1,0},{2,3},{3,2},{4,5},{5,4},{6,7},{7,6},{8,9},{9,8},{10,11... | collective-permute-start | bytes 221192 | tf_op jit(solution)/shard_map/ppermute | solution.py:916

commit v5 on v4

--- a/solution.py
+++ b/solution.py
@@ -824,33 +824,36 @@
         base[p] = direct[p] + nn(z1[p], a) + nn(z2[p], at)
 
 
-def chip_d2_kernel(mine, got, hc, hx, sc, sx, base, ro, ri, sa, gw_b, upstream, reset, update, gate_update,
-                   gate_grad, y1, y2, g1, g3, direct, pay):
+def chip_d2_kernel(mine, got, hx, sx, base, sa, sb, reset, gate_update, order, part, gate_grad, kept, keep, give, flat):
     hid = base.shape[1]
+    both = 2 * hid
+    half = keep.shape[0]
+    core = lax.rem(lax.axis_index("dom"), 2)
     parts = range(sx.shape[0])
     top, low = merged(sx.shape[0], mine, got)
     scaled_grad = [base[p] + nn(top, hx[p]) + nn(low, sx[p]) for p in parts]
-    kept = [scaled_grad[p] * reset[p] for p in parts]
+    through = [scaled_grad[p] * reset[p] for p in parts]
     grad = [
-        jnp.concatenate([(sa[p, :hid, :].astype(F32) * (kept[p] - kept[p] * reset[p])).astype(BF16), gate_update[p]], axis=0)
+        jnp.concatenate([(sa[p, :hid, :].astype(F32) * (through[p] - through[p] * reset[p])).astype(BF16), gate_update[p]], axis=0)
         for p in parts
     ]
-    back = [nn(gw_b[...], grad[p]) for p in parts]
-    one, two = split_back(back, hid, ro, ri, y1, y2, g1, g3, direct)
     for p in parts:
         gate_grad[p] = grad[p]
-        direct[p] = direct[p] + upstream[p].astype(F32) * update[p] + kept[p]
-    exchange(one, two, hc, sc, pay)
-
-
-def grads_kernel(gate_grad, sa, sb, order, part, keep, give, flat):
-    both = gate_grad.shape[1]
-    half = keep.shape[0]
-    core = lax.rem(lax.axis_index("dom"), 2)
-    flat[:both, :] = chip_part(gate_grad, sa, sb, order)
+        kept[p] = through[p]
+    flat[:both, :] = chip_part(grad, sa, sb, order)
     flat[both:, :] = part[...].astype(F32)
     keep[...] = flat[pl.ds(pl.multiple_of(core * half, 8), half), :].astype(BF16)
     give[...] = flat[pl.ds(pl.multiple_of((1 - core) * half, 8), half), :].astype(BF16)
+
+
+def back_e_kernel(hc, sc, gate_grad, kept, ro, ri, gw_b, upstream, update, y1, y2, g1, g3, direct, pay):
+    hid = kept.shape[1]
+    parts = range(sc.shape[0])
+    back = [nn(gw_b[...], gate_grad[p]) for p in parts]
+    one, two = split_back(back, hid, ro, ri, y1, y2, g1, g3, direct)
+    for p in parts:
+        direct[p] = direct[p] + upstream[p].astype(F32) * update[p] + kept[p]
+    exchange(one, two, hc, sc, pay)
 
 
 def local_e_kernel(a, at, z1, z2, direct, base):
@@ -979,17 +982,17 @@
     )
     got = swap(pay, 1)
     (base,) = run(local_d2_kernel, "local_d2", [field], *local, z1, z2, direct)
-    gate_grad, y1, y2, g1, g3, direct, pay = run(
-        chip_d2_kernel, "chip_d2", [((parts, 2 * hid, n), BF16)] + [field16] * 4 + [field, pay_kind],
-        pay, got, *edges, base, ro, ri, sa, gw_b, up, reset, update, gate_update,
+    half = ((3 * hid // 2, width), BF16)
+    gate_grad, kept, keep, give = run(
+        chip_d2_kernel, "chip_d2", [((parts, 2 * hid, n), BF16), field, half, half],
+        pay, got, hx, sx, base, sa, sb, reset, gate_update, order, part, scratch=[pltpu.VMEM((3 * hid, width), F32)],
+    )
+    y1, y2, g1, g3, direct, pay = run(
+        back_e_kernel, "back_e", [field16] * 4 + [field, pay_kind], hc, sc, gate_grad, kept, ro, ri, gw_b, up, update
     )
     got = swap(pay, 1)
-    half = ((3 * hid // 2, width), BF16)
-    keep, give = run(
-        grads_kernel, "grads", [half, half], gate_grad, sa, sb, order, part, scratch=[pltpu.VMEM((3 * hid, width), F32)]
-    )
     l1, l2 = run(local_kernel, "local_e1", [field, field], *local, y1, y2)
-    mine, sent = run(sum_kernel, "sum_core", [half] * 2, keep, swap(give, 1), after=[l1, got])
+    mine, sent = run(sum_kernel, "sum_core", [half] * 2, keep, swap(give, 1), after=[direct])
     every = [mine] + [swap(sent, k, "snap", snaps) for k in range(1, snaps)]
     z1, z2, pay = run(
         chip_d1_kernel, "chip_e1", [field16, field16, pay_kind], pay, got, *edges, l1, l2, g1, g3, ro, ri, after=[mine],

time: 43.3 us -> 42.2 us (0.975)
  waiting for transfers between devices: 6.3 us -> 5.12 us
    ppermute x18, waiting for transfers between devices: 6.3 us -> 5.12 us  [swap(): return lax.ppermute(array, axis, [(i, i ^ k) for i in range(size)])]
  transfers between devices with their start and end apart: 18 -> 18, of which waited for: 8 -> 7; matrix products, arithmetic and copies ran while one was open for 0% -> 0% of each run, Pallas kernels for 26% -> 28%
where the time goes in v5:
time: 42.2 us; the launch traced here: 41.9 us
  Pallas kernels  19.7 us (47%)
  starting transfers between devices  13.8 us (33%)
  waiting for transfers between devices  5.12 us (12%)
  local copies, waits for them, and re-layouts  2.58 us (6%)
  between operations  0.8 us (2%)
    pallas_call x24, Pallas kernels, run(): pl.pallas_call(lambda *refs: kernel(*refs[len(after):]), name=name, out_s...  19.7 us
    ppermute x18, starting transfers between devices, swap(): return lax.ppermute(array, axis, [(i, i ^ k) for i in range(size)])  13.8 us
    ppermute x18, waiting for transfers between devices, swap(): return lax.ppermute(array, axis, [(i, i ^ k) for i in range(size)])  5.12 us
    unnamed x12, local copies, waits for them, and re-layouts  2.58 us
  transfers between devices with their start and end apart: 18, of which 7 were waited for; matrix products, arithmetic and copies ran while one was open for 0% of the time, Pallas kernels for 28%

profile of v5, /device:TPU:0, one launch (start us, length us, event | category | flops | bytes accessed | tf_op | source)
XLA Modules:
  0.0 41.9 jit_solution(6081689198205845337)
XLA Ops:
  0.6 1.7 %pack.1 = (bf16[80,512]{1,0:T(8,128)(2,1)}, bf16[144,512]{1,0:T(8,128)(2,1)}) custom-call(s32[4,512]{1,0:T(4,128)} %refs_0_.2, f32[4,512]{1,0:T(4,128)} %refs_1_.1, s32[1,32]{1,0:T(1,128)} %refs_2_.2, bf16[1,2,512]{2,1,0:T(2,128)(2,1)} %refs_3_.1, bf16[1,64,512]{2,1,0:T(8,128)(2,1)} %refs_4_.1, bf16[1,64,512]{2,1,0:T(8,128)(2,1)} %refs_0_.3), custom_call_target="tpu_custom_call" | custom-call | flops 20000000 | bytes 2000000 | tf_op jit(solution)/shard_map/pack/pallas_call | solution.py:39
  2.3 4.0 %collective-permute-start = (bf16[80,512]{1,0:T(8,128)(2,1)}, bf16[80,512]{1,0:T(8,128)(2,1)S(1)}, u32[]{:S(2)}, u32[]{:S(2)}) collective-permute-start(bf16[80,512]{1,0:T(8,128)(2,1)} %get-tuple-element.91.refs_0_), channel_id=1, source_target_pairs={{0,4},{1,5},{2,6},{3,7},{4,0},{5,1},{6,2},{7,3},{8,12},{9,13},{10,... | collective-permute-start | bytes 245768 | tf_op jit(solution)/shard_map/ppermute | solution.py:919
  6.3 1.6 %collective-permute-start.2 = (bf16[144,512]{1,0:T(8,128)(2,1)}, bf16[144,512]{1,0:T(8,128)(2,1)S(1)}, u32[]{:S(2)}, u32[]{:S(2)}) collective-permute-start(bf16[144,512]{1,0:T(8,128)(2,1)} %get-tuple-element.94), channel_id=1, source_target_pairs={{0,2},{1,3},{2,0},{3,1},{4,6},{5,7},{6,4},{7,5},{8,10},{9,11},{10,... | collective-permute-start | bytes 442376 | tf_op jit(solution)/shard_map/ppermute | solution.py:919
  7.9 0.3 collective-permute-start.3
  8.2 0.9 %copy-done = bf16[80,512]{1,0:T(8,128)(2,1)S(1)} copy-done((bf16[80,512]{1,0:T(8,128)(2,1)S(1)}, bf16[80,512]{1,0:T(8,128)(2,1)}, u32[]{:S(2)}) %copy-start) | copy-done | bytes 81944
  9.1 0.9 %copy-done.2 = bf16[128,330]{0,1:T(8,128)(2,1)S(1)} copy-done((bf16[128,330]{0,1:T(8,128)(2,1)S(1)}, bf16[128,330]{0,1:T(8,128)(2,1)}, u32[]{:S(2)}) %copy-start.2) | copy-done | bytes 84504
  10.0 0.8 %copy-done.3 = bf16[64,330]{1,0:T(8,128)(2,1)S(1)} copy-done((bf16[64,330]{1,0:T(8,128)(2,1)S(1)}, bf16[64,330]{1,0:T(8,128)(2,1)}, u32[]{:S(2)}) %copy-start.3) | copy-done | bytes 42264
  10.8 0.6 %order.1 = (bf16[128,400]{1,0:T(8,128)(2,1)S(1)}, bf16[64,400]{1,0:T(8,128)(2,1)S(1)}, bf16[320,128]{1,0:T(8,128)(2,1)S(1)}, bf16[320,64]{1,0:T(8,128)(2,1)S(1)}, bf16[400,384]{1,0:T(8,128)(2,1)S(1)}) custom-call(bf16[80,512]{1,0:T(8,128)(2,1)S(1)} %copy-done, bf16[330,128]{1,0:T(8,128)(2,1)S(1)} %bitcast.6, bf16[64,330]{1,0:T(8,128)(2,1)S(1)} %copy-done.3), custom_call_target="tpu_custom_call" | custom-call | flops 20000000 | bytes 2000000 | tf_op jit(solution)/shard_map/order/pallas_call | solution.py:39
  11.5 0.3 collective-permute-start.1
  11.8 2.1 %collective-permute-done.3.refs_0_.refs_2_ = bf16[1,64,512]{2,1,0:T(8,128)(2,1)S(1)} collective-permute-done((bf16[1,64,512]{2,1,0:T(8,128)(2,1)}, bf16[1,64,512]{2,1,0:T(8,128)(2,1)S(1)}, u32[]{:S(2)}, u32[]{:S(2)}) %collective-permute-start.3) | collective-permute-done | bytes 65568 | tf_op jit(solution)/shard_map/ppermute | solution.py:919
  13.9 1.3 %collective-permute-start.4 = (bf16[1,64,512]{2,1,0:T(8,128)(2,1)S(1)}, bf16[1,64,512]{2,1,0:T(8,128)(2,1)S(1)}, u32[]{:S(2)}, u32[]{:S(2)}) collective-permute-start(bf16[1,64,512]{2,1,0:T(8,128)(2,1)S(1)} %collective-permute-done.3.refs_0_.refs_2_), channel_id=1, source_target_pairs={{0,2},{1,3},{2,0},{3,1},{4,6},{5,7},{6,4},{7,5},{8,10},{9,11},{10,... | collective-permute-start | bytes 196616 | tf_op jit(solution)/shard_map/ppermute | solution.py:919
  15.2 1.2 %build_early.1 = (bf16[3,512,512]{2,1,0:T(8,128)(2,1)S(1)}, bf16[3,512,512]{2,1,0:T(8,128)(2,1)S(1)}, bf16[3,32,512]{2,1,0:T(8,128)(2,1)S(1)}, bf16[3,128,512]{2...) custom-call(bf16[80,512]{1,0:T(8,128)(2,1)S(1)} %copy-done, ...), custom_call_target="tpu_custom_call" | custom-call | flops 20000000 | bytes 2000000 | tf_op jit(solution)/shard_map/build_early/pallas_call | solution.py:39
  16.4 0.3 collective-permute-done.1.refs_0_
  16.7 0.6 %build_late.1 = (bf16[1,512,512]{2,1,0:T(8,128)(2,1)S(1)}, bf16[1,512,512]{2,1,0:T(8,128)(2,1)S(1)}, bf16[4,32,512]{2,1,0:T(8,128)(2,1)S(1)}, bf16[4,128,512]{2,...) custom-call(bf16[80,512]{1,0:T(8,128)(2,1)S(1)} %collective-permute-, ...), custom_call_target="tpu_custom_call" | custom-call | flops 20000000 | bytes 2000000 | tf_op jit(solution)/shard_map/build_late/pallas_call | solution.py:39
  17.4 0.9 %local_a.1 = (f32[4,80,512]{2,1,0:T(8,128)S(1)}, f32[4,80,512]{2,1,0:T(8,128)S(1)}) custom-call(bf16[3,512,512]{2,1,0:T(8,128)(2,1)S(1)} %get-tuple-element.106.refs_0_, bf16[3,512,512]{2,1,0:T(8,128)(2,1)S(1)} %get-tuple-element.107.refs_1_, bf16[1,512,512]{2,1,0:T(8,128)(2,1)S(1)} %get-tuple-element.108.refs_2_, ...), custom_call_target="tpu_custom_call" | custom-call | flops 20000000 | bytes 2000000 | tf_op jit(solution)/shard_map/local_a/pallas_call | solution.py:39
  18.2 0.3 collective-permute-done.5.refs_3_
  18.6 0.7 %chip_a.1 = (bf16[4,240,512]{2,1,0:T(8,128)(2,1)S(1)}, f32[4,1,512]{2,1,0:T(1,128)S(1)}, f32[4,1,512]{2,1,0:T(1,128)S(1)}, bf16[160,128]{1,0:T(8,128)(2,1)S(1)}) custom-call(bf16[1,64,512]{2,1,0:T(8,128)(2,1)S(1)} %collective-permute-done.3.refs_0_.refs_2_, bf16[1,64,512]{2,1,0:T(8,128)(2,1)S(1)} %collective-permute-done.4.refs_1_.refs_3_, ...), custom_call_target="tpu_custom_call" | custom-call | flops 20000000 | bytes 2000000 | tf_op jit(solution)/shard_map/chip_a/pallas_call | solution.py:39
  19.2 0.2 collective-permute-start.6
  19.5 1.0 %local_b.1 = (f32[4,80,512]{2,1,0:T(8,128)S(1)}, f32[4,80,512]{2,1,0:T(8,128)S(1)}, f32[4,128,512]{2,1,0:T(8,128)S(1)}) custom-call(bf16[3,512,512]{2,1,0:T(8,128)(2,1)S(1)} %get-tuple-element.106.refs_0_, bf16[3,512,512]{2,1,0:T(8,128)(2,1)S(1)} %get-tuple-element.107.refs_1_, bf16[1,512,512]{2,1,0:T(8,128)(2,1)S(1)} %get-tuple-element.108.refs_2_, ...), custom_call_target="tpu_custom_call" | custom-call | flops 20000000 | bytes 2000000 | tf_op jit(solution)/shard_map/local_b/pallas_call | solution.py:39
  20.5 1.0 %chip_b.1 = (bf16[4,160,512]{2,1,0:T(8,128)(2,1)S(1)}, f32[4,64,512]{2,1,0:T(8,128)S(1)}, f32[4,64,512]{2,1,0:T(8,128)S(1)}, bf16[4,64,512]{2,1,0:T(8,128)(2,1)S(1)}, bf16[128,128]{1,0:T(8,128)(2,1)S(1)}) custom-call(bf16[160,128]{1,0:T(8,128)(2,1)S(1)} %get-tuple-element.112.refs_0_, bf16[160,128]{1,0:T(8,128)(2,1)S(1)} %collective-permute-done.6.refs_1_, ...), custom_call_target="tpu_custom_call" | custom-call | flops 20000000 | bytes 2000000 | tf_op jit(solution)/shard_map/chip_b/pallas_call | solution.py:39
  21.5 0.4 collective-permute-start.7
  21.9 0.8 %local_c1.1 = (f32[4,64,512]{2,1,0:T(8,128)S(1)}, f32[4,64,512]{2,1,0:T(8,128)S(1)}) custom-call(bf16[3,512,512]{2,1,0:T(8,128)(2,1)S(1)} %get-tuple-element.106.refs_0_, bf16[3,512,512]{2,1,0:T(8,128)(2,1)S(1)} %get-tuple-element.107.refs_1_, bf16[1,512,512]{2,1,0:T(8,128)(2,1)S(1)} %get-tuple-element.108.refs_2_, ...), custom_call_target="tpu_custom_call" | custom-call | flops 20000000 | bytes 2000000 | tf_op jit(solution)/shard_map/local_c1/pallas_call | solution.py:39
  22.8 0.5 %chip_c1.1 = (bf16[4,240,512]{2,1,0:T(8,128)(2,1)S(1)}, bf16[128,128]{1,0:T(8,128)(2,1)S(1)}) custom-call(bf16[128,128]{1,0:T(8,128)(2,1)S(1)} %get-tuple-element.120.refs_0_, bf16[128,128]{1,0:T(8,128)(2,1)S(1)} %collective-permute-done.7.refs_1_, bf16[4,32,512]{2,1,0:T(8,128)(2,1)S(1)} %get-tuple-element.100.refs_4_.refs_2_.refs_6_.refs_0_.refs_3_, ...), custom_call_target="tpu_custom_call" | custom-call | flops 20000000 | bytes 2000000 | tf_op jit(solution)/shard_map/chip_c1/pallas_call | solution.py:39
  23.3 0.4 collective-permute-start.8
  23.7 1.0 %local_c2.1 = (f32[4,64,512]{2,1,0:T(8,128)S(1)}, f32[4,64,512]{2,1,0:T(8,128)S(1)}, f32[4,64,512]{2,1,0:T(8,128)S(1)}) custom-call(bf16[3,512,512]{2,1,0:T(8,128)(2,1)S(1)} %get-tuple-element.106.refs_0_, bf16[3,512,512]{2,1,0:T(8,128)(2,1)S(1)} %get-tuple-element.107.refs_1_, bf16[1,512,512]{2,1,0:T(8,128)(2,1)S(1)} %get-tuple-element.108.refs_2_, ...), custom_call_target="tpu_custom_call" | custom-call | flops 20000000 | bytes 2000000 | tf_op jit(solution)/shard_map/local_c2/pallas_call | solution.py:39
  24.8 1.3 %chip_c2.1 = (bf16[4,160,512]{2,1,0:T(8,128)(2,1)S(1)}, bf16[4,64,512]{2,1,0:T(8,128)(2,1)S(1)}, bf16[4,64,512]{2,1,0:T(8,128)(2,1)S(1)}, bf16[4,64,512]{2,1,0:T...) custom-call(bf16[1,64,512]{2,1,0:T(8,128)(2,1)S(1)} %copy-done.1, ...), custom_call_target="tpu_custom_call" | custom-call | flops 20000000 | bytes 2000000 | tf_op jit(solution)/shard_map/chip_c2/pallas_call | solution.py:39
  26.0 0.2 collective-permute-start.9
  26.3 1.5 %local_d1.1 = (f32[4,64,512]{2,1,0:T(8,128)S(1)}, f32[4,64,512]{2,1,0:T(8,128)S(1)}, bf16[64,384]{1,0:T(8,128)(2,1)S(1)}) custom-call(bf16[3,512,512]{2,1,0:T(8,128)(2,1)S(1)} %get-tuple-element.106.refs_0_, bf16[3,512,512]{2,1,0:T(8,128)(2,1)S(1)} %get-tuple-element.107.refs_1_, bf16[1,512,512]{2,1,0:T(8,128)(2,1)S(1)} %get-tuple-element.108.refs_2_, ...), custom_call_target="tpu_custom_call" | custom-call | flops 20000000 | bytes 2000000 | tf_op jit(solution)/shard_map/local_d1/pallas_call | solution.py:39
  27.8 0.6 %chip_d1.1 = (bf16[4,64,512]{2,1,0:T(8,128)(2,1)S(1)}, bf16[4,64,512]{2,1,0:T(8,128)(2,1)S(1)}, bf16[128,128]{1,0:T(8,128)(2,1)S(1)}) custom-call(bf16[128,128]{1,0:T(8,128)(2,1)S(1)} %get-tuple-element.133.refs_0_, bf16[128,128]{1,0:T(8,128)(2,1)S(1)} %collective-permute-done.9.refs_1_, ...), custom_call_target="tpu_custom_call" | custom-call | flops 20000000 | bytes 2000000 | tf_op jit(solution)/shard_map/chip_d1/pallas_call | solution.py:39
  28.3 0.4 %collective-permute-start.10 = (bf16[128,128]{1,0:T(8,128)(2,1)S(1)}, bf16[128,128]{1,0:T(8,128)(2,1)S(1)}, u32[]{:S(2)}, u32[]{:S(2)}) collective-permute-start(bf16[128,128]{1,0:T(8,128)(2,1)S(1)} %get-tuple-element.143.refs_0_), channel_id=1, source_target_pairs={{0,1},{1,0},{2,3},{3,2},{4,5},{5,4},{6,7},{7,6},{8,9},{9,8},{10,11... | collective-permute-start | bytes 98312 | tf_op jit(solution)/shard_map/ppermute | solution.py:919
  28.8 0.8 %local_d2.1.refs_4_ = f32[4,64,512]{2,1,0:T(8,128)S(1)} custom-call(bf16[3,512,512]{2,1,0:T(8,128)(2,1)S(1)} %get-tuple-element.106.refs_0_, bf16[3,512,512]{2,1,0:T(8,128)(2,1)S(1)} %get-tuple-element.107.refs_1_, bf16[1,512,512]{2,1,0:T(8,128)(2,1)S(1)} %get-tuple-element.108.refs_2_, bf16[1,512,512]{2,1,0:T(8,128)(2,1)S(1)} %get-tuple-element.109.refs_3_, ...), custom_call_target="tpu_custom_call" | custom-call | flops 20000000 | bytes 2000000 | tf_op jit(solution)/shard_map/local_d2/pallas_call | solution.py:39
  29.6 1.1 %chip_d2.1 = (bf16[4,128,512]{2,1,0:T(8,128)(2,1)S(1)}, f32[4,64,512]{2,1,0:T(8,128)S(1)}, bf16[96,384]{1,0:T(8,128)(2,1)S(1)}, bf16[96,384]{1,0:T(8,128)(2,1)S(1)}) custom-call(bf16[128,128]{1,0:T(8,128)(2,1)S(1)} %get-tuple-element.143.refs_0_, bf16[128,128]{1,0:T(8,128)(2,1)S(1)} %collective-permute-done.10.refs_1_, ...), custom_call_target="tpu_custom_call" | custom-call | flops 20000000 | bytes 2000000 | tf_op jit(solution)/shard_map/chip_d2/pallas_call | solution.py:39
  30.7 0.4 collective-permute-start.11
  31.1 0.8 %back_e.1 = (bf16[4,64,512]{2,1,0:T(8,128)(2,1)S(1)}, bf16[4,64,512]{2,1,0:T(8,128)(2,1)S(1)}, bf16[4,64,512]{2,1,0:T(8,128)(2,1)S(1)}, bf16[4,64,512]{2,1,0:T(8...) custom-call(bf16[4,32,512]{2,1,0:T(8,128)(2,1)S(1)} %get-tuple-element.100.refs_4_.refs_2_.refs_6_.refs_0_.refs_3_, ...), custom_call_target="tpu_custom_call" | custom-call | flops 20000000 | bytes 2000000 | tf_op jit(solution)/shard_map/back_e/pallas_call | solution.py:39
  31.9 0.1 collective-permute-done.11.refs_2_
  32.1 2.5 %collective-permute-start.16 = (bf16[96,384]{1,0:T(8,128)(2,1)S(1)}, bf16[96,384]{1,0:T(8,128)(2,1)S(1)}, u32[]{:S(2)}, u32[]{:S(2)}) collective-permute-start(bf16[96,384]{1,0:T(8,128)(2,1)S(1)} %get-tuple-element.170), channel_id=1, source_target_pairs={{0,24},{8,16},{16,8},{24,0},{1,25},{9,17},{17,9},{25,1},{2,26},{10... | collective-permute-start | bytes 221192 | tf_op jit(solution)/shard_map/ppermute | solution.py:919
  34.6 0.5 %collective-permute-start.15 = (bf16[96,384]{1,0:T(8,128)(2,1)S(1)}, bf16[96,384]{1,0:T(8,128)(2,1)S(1)}, u32[]{:S(2)}, u32[]{:S(2)}) collective-permute-start(bf16[96,384]{1,0:T(8,128)(2,1)S(1)} %get-tuple-element.170), channel_id=1, source_target_pairs={{0,16},{8,24},{16,0},{24,8},{1,17},{9,25},{17,1},{25,9},{2,18},{10... | collective-permute-start | bytes 221192 | tf_op jit(solution)/shard_map/ppermute | solution.py:919
  35.1 0.5 %collective-permute-start.14 = (bf16[96,384]{1,0:T(8,128)(2,1)S(1)}, bf16[96,384]{1,0:T(8,128)(2,1)S(1)}, u32[]{:S(2)}, u32[]{:S(2)}) collective-permute-start(bf16[96,384]{1,0:T(8,128)(2,1)S(1)} %get-tuple-element.170), channel_id=1, source_target_pairs={{0,8},{8,0},{16,24},{24,16},{1,9},{9,1},{17,25},{25,17},{2,10},{10... | collective-permute-start | bytes 221192 | tf_op jit(solution)/shard_map/ppermute | solution.py:919
  35.6 0.8 %local_e1.1 = (f32[4,64,512]{2,1,0:T(8,128)S(1)}, f32[4,64,512]{2,1,0:T(8,128)S(1)}) custom-call(bf16[3,512,512]{2,1,0:T(8,128)(2,1)S(1)} %get-tuple-element.106.refs_0_, bf16[3,512,512]{2,1,0:T(8,128)(2,1)S(1)} %get-tuple-element.107.refs_1_, bf16[1,512,512]{2,1,0:T(8,128)(2,1)S(1)} %get-tuple-element.108.refs_2_, ...), custom_call_target="tpu_custom_call" | custom-call | flops 20000000 | bytes 2000000 | tf_op jit(solution)/shard_map/local_e1/pallas_call | solution.py:39
  36.5 0.4 collective-permute-done.12.refs_2_
  36.8 0.6 %chip_e1.1 = (bf16[4,64,512]{2,1,0:T(8,128)(2,1)S(1)}, bf16[4,64,512]{2,1,0:T(8,128)(2,1)S(1)}, bf16[128,128]{1,0:T(8,128)(2,1)S(1)}) custom-call(bf16[96,384]{1,0:T(8,128)(2,1)S(1)} %get-tuple-element.157.refs_0_.refs_1_, bf16[128,128]{1,0:T(8,128)(2,1)S(1)} %get-tuple-element.158.refs_1_, bf16[128,128]{1,0:T(8,128)(2,1)S(1)} %collective-permute-done.12.refs_2_, ...), custom_call_target="tpu_custom_call" | custom-call | flops 20000000 | bytes 2000000 | tf_op jit(solution)/shard_map/chip_e1/pallas_call | solution.py:39
  37.4 0.2 collective-permute-start.13
  37.7 0.3 local_e2.1.refs_6_
  38.0 0.7 %collective-permute-done.13.refs_1_ = bf16[128,128]{1,0:T(8,128)(2,1)S(1)} collective-permute-done((bf16[128,128]{1,0:T(8,128)(2,1)S(1)}, bf16[128,128]{1,0:T(8,128)(2,1)S(1)}, u32[]{:S(2)}, u32[]{:S(2)}) %collective-permute-start.13) | collective-permute-done | bytes 32800 | tf_op jit(solution)/shard_map/ppermute | solution.py:919
  38.7 0.8 %chip_e2.1 = (bf16[1,64,512]{2,1,0:T(8,128)(2,1)}, f32[8,128]{1,0:T(8,128)S(1)}) custom-call(bf16[128,128]{1,0:T(8,128)(2,1)S(1)} %get-tuple-element.165.refs_0_, bf16[128,128]{1,0:T(8,128)(2,1)S(1)} %collective-permute-done.13.refs_1_, bf16[4,32,512]{2,1,0:T(8,128)(2,1)S(1)} %get-tuple-element.100.refs_4_.refs_2_.refs_6_.refs_0_.refs_3_, ...), custom_call_target="tpu_custom_call" | custom-call | flops 20000000 | bytes 2000000 | tf_op jit(solution)/shard_map/chip_e2/pallas_call | solution.py:39
  39.6 0.2 collective-permute-start.17
  39.8 1.1 %collective-permute-done.17.refs_1_ = bf16[96,384]{1,0:T(8,128)(2,1)S(1)} collective-permute-done((bf16[96,384]{1,0:T(8,128)(2,1)S(1)}, bf16[96,384]{1,0:T(8,128)(2,1)S(1)}, u32[]{:S(2)}, u32[]{:S(2)}) %collective-permute-start.17) | collective-permute-done | bytes 73760 | tf_op jit(solution)/shard_map/ppermute | solution.py:919
  40.9 1.0 %end.1 = (f32[330,128]{1,0:T(8,128)}, f32[1,128]{1,0:T(1,128)}, f32[64,330]{1,0:T(8,128)}, f32[1,64]{1,0:T(1,128)}) custom-call(bf16[96,384]{1,0:T(8,128)(2,1)S(1)} %get-tuple-element.171.refs_0_, bf16[96,384]{1,0:T(8,128)(2,1)S(1)} %collective-permute-done.17.refs_1_), custom_call_target="tpu_custom_call" | custom-call | flops 20000000 | bytes 2000000 | tf_op jit(solution)/shard_map/end/pallas_call | solution.py:39
  (24 shorter events, 0.3 us)
Async XLA Ops:
  2.3 9.2 %collective-permute-start = (bf16[80,512]{1,0:T(8,128)(2,1)}, bf16[80,512]{1,0:T(8,128)(2,1)S(1)}, u32[]{:S(2)}, u32[]{:S(2)}) collective-permute-start(bf16[80,512]{1,0:T(8,128)(2,1)} %get-tuple-element.91.refs_0_), channel_id=1, source_target_pairs={{0,4},{1,5},{2,6},{3,7},{4,0},{5,1},{6,2},{7,3},{8,12},{9,13},{10,... | collective-permute-start | bytes 245768 | tf_op jit(solution)/shard_map/ppermute | solution.py:919
  6.3 8.8 %collective-permute-start.2 = (bf16[144,512]{1,0:T(8,128)(2,1)}, bf16[144,512]{1,0:T(8,128)(2,1)S(1)}, u32[]{:S(2)}, u32[]{:S(2)}) collective-permute-start(bf16[144,512]{1,0:T(8,128)(2,1)} %get-tuple-element.94), channel_id=1, source_target_pairs={{0,2},{1,3},{2,0},{3,1},{4,6},{5,7},{6,4},{7,5},{8,10},{9,11},{10,... | collective-permute-start | bytes 442376 | tf_op jit(solution)/shard_map/ppermute | solution.py:919
  7.9 6.0 %collective-permute-start.3 = (bf16[1,64,512]{2,1,0:T(8,128)(2,1)}, bf16[1,64,512]{2,1,0:T(8,128)(2,1)S(1)}, u32[]{:S(2)}, u32[]{:S(2)}) collective-permute-start(bf16[1,64,512]{2,1,0:T(8,128)(2,1)} %refs_0_.3), channel_id=1, source_target_pairs={{0,4},{1,5},{2,6},{3,7},{4,0},{5,1},{6,2},{7,3},{8,12},{9,13},{10,... | collective-permute-start | bytes 196616 | tf_op jit(solution)/shard_map/ppermute | solution.py:919
  8.2 0.9 %copy-start = (bf16[80,512]{1,0:T(8,128)(2,1)S(1)}, bf16[80,512]{1,0:T(8,128)(2,1)}, u32[]{:S(2)}) copy-start(bf16[80,512]{1,0:T(8,128)(2,1)} %get-tuple-element.91.refs_0_) | copy-start | bytes 245764
  9.1 0.9 %copy-start.2 = (bf16[128,330]{0,1:T(8,128)(2,1)S(1)}, bf16[128,330]{0,1:T(8,128)(2,1)}, u32[]{:S(2)}) copy-start(bf16[128,330]{0,1:T(8,128)(2,1)} %param.13) | copy-start | bytes 253444
  10.0 0.8 %copy-start.3 = (bf16[64,330]{1,0:T(8,128)(2,1)S(1)}, bf16[64,330]{1,0:T(8,128)(2,1)}, u32[]{:S(2)}) copy-start(bf16[64,330]{1,0:T(8,128)(2,1)} %refs_2_.3) | copy-start | bytes 126724
  11.5 5.2 %collective-permute-start.1 = (bf16[80,512]{1,0:T(8,128)(2,1)S(1)}, bf16[80,512]{1,0:T(8,128)(2,1)S(1)}, u32[]{:S(2)}, u32[]{:S(2)}) collective-permute-start(bf16[80,512]{1,0:T(8,128)(2,1)S(1)} %collective-permute-done.refs_2_), channel_id=1, source_target_pairs={{0,2},{1,3},{2,0},{3,1},{4,6},{5,7},{6,4},{7,5},{8,10},{9,11},{10,... | collective-permute-start | bytes 245768 | tf_op jit(solution)/shard_map/ppermute | solution.py:919
  13.9 4.4 %collective-permute-start.4 = (bf16[1,64,512]{2,1,0:T(8,128)(2,1)S(1)}, bf16[1,64,512]{2,1,0:T(8,128)(2,1)S(1)}, u32[]{:S(2)}, u32[]{:S(2)}) collective-permute-start(bf16[1,64,512]{2,1,0:T(8,128)(2,1)S(1)} %collective-permute-done.3.refs_0_.refs_2_), channel_id=1, source_target_pairs={{0,2},{1,3},{2,0},{3,1},{4,6},{5,7},{6,4},{7,5},{8,10},{9,11},{10,... | collective-permute-start | bytes 196616 | tf_op jit(solution)/shard_map/ppermute | solution.py:919
  17.3 1.3 %collective-permute-start.5 = (bf16[160,128]{1,0:T(8,128)(2,1)S(1)}, bf16[160,128]{1,0:T(8,128)(2,1)S(1)}, u32[]{:S(2)}, u32[]{:S(2)}) collective-permute-start(bf16[160,128]{1,0:T(8,128)(2,1)S(1)} %get-tuple-element.102.refs_2_), channel_id=1, source_target_pairs={{0,1},{1,0},{2,3},{3,2},{4,5},{5,4},{6,7},{7,6},{8,9},{9,8},{10,11... | collective-permute-start | bytes 122888 | tf_op jit(solution)/shard_map/ppermute | solution.py:919
  19.2 1.3 %collective-permute-start.6 = (bf16[160,128]{1,0:T(8,128)(2,1)S(1)}, bf16[160,128]{1,0:T(8,128)(2,1)S(1)}, u32[]{:S(2)}, u32[]{:S(2)}) collective-permute-start(bf16[160,128]{1,0:T(8,128)(2,1)S(1)} %get-tuple-element.112.refs_0_), channel_id=1, source_target_pairs={{0,1},{1,0},{2,3},{3,2},{4,5},{5,4},{6,7},{7,6},{8,9},{9,8},{10,11... | collective-permute-start | bytes 122888 | tf_op jit(solution)/shard_map/ppermute | solution.py:919
  19.5 1.1 %copy-start.4 = (f32[128]{0:T(128)S(1)}, f32[128]{0:T(128)}, u32[]{:S(2)}) copy-start(f32[128]{0:T(128)} %param.14) | copy-start | bytes 1540
  21.5 1.3 %collective-permute-start.7 = (bf16[128,128]{1,0:T(8,128)(2,1)S(1)}, bf16[128,128]{1,0:T(8,128)(2,1)S(1)}, u32[]{:S(2)}, u32[]{:S(2)}) collective-permute-start(bf16[128,128]{1,0:T(8,128)(2,1)S(1)} %get-tuple-element.120.refs_0_), channel_id=1, source_target_pairs={{0,1},{1,0},{2,3},{3,2},{4,5},{5,4},{6,7},{7,6},{8,9},{9,8},{10,11... | collective-permute-start | bytes 98312 | tf_op jit(solution)/shard_map/ppermute | solution.py:919
  23.3 1.4 %collective-permute-start.8 = (bf16[128,128]{1,0:T(8,128)(2,1)S(1)}, bf16[128,128]{1,0:T(8,128)(2,1)S(1)}, u32[]{:S(2)}, u32[]{:S(2)}) collective-permute-start(bf16[128,128]{1,0:T(8,128)(2,1)S(1)} %get-tuple-element.124.refs_4_), channel_id=1, source_target_pairs={{0,1},{1,0},{2,3},{3,2},{4,5},{5,4},{6,7},{7,6},{8,9},{9,8},{10,11... | collective-permute-start | bytes 98312 | tf_op jit(solution)/shard_map/ppermute | solution.py:919
  23.7 1.0 %copy-start.1 = (bf16[1,64,512]{2,1,0:T(8,128)(2,1)S(1)}, bf16[1,64,512]{2,1,0:T(8,128)(2,1)}, u32[]{:S(2)}) copy-start(bf16[1,64,512]{2,1,0:T(8,128)(2,1)} %refs_0_.3) | copy-start | bytes 196612
  23.7 1.0 %copy-start.5 = (f32[64]{0:T(128)S(1)}, f32[64]{0:T(128)}, u32[]{:S(2)}) copy-start(f32[64]{0:T(128)} %param.16) | copy-start | bytes 772
  26.0 1.7 %collective-permute-start.9 = (bf16[128,128]{1,0:T(8,128)(2,1)S(1)}, bf16[128,128]{1,0:T(8,128)(2,1)S(1)}, u32[]{:S(2)}, u32[]{:S(2)}) collective-permute-start(bf16[128,128]{1,0:T(8,128)(2,1)S(1)} %get-tuple-element.133.refs_0_), channel_id=1, source_target_pairs={{0,1},{1,0},{2,3},{3,2},{4,5},{5,4},{6,7},{7,6},{8,9},{9,8},{10,11... | collective-permute-start | bytes 98312 | tf_op jit(solution)/shard_map/ppermute | solution.py:919
  28.3 1.3 %collective-permute-start.10 = (bf16[128,128]{1,0:T(8,128)(2,1)S(1)}, bf16[128,128]{1,0:T(8,128)(2,1)S(1)}, u32[]{:S(2)}, u32[]{:S(2)}) collective-permute-start(bf16[128,128]{1,0:T(8,128)(2,1)S(1)} %get-tuple-element.143.refs_0_), channel_id=1, source_target_pairs={{0,1},{1,0},{2,3},{3,2},{4,5},{5,4},{6,7},{7,6},{8,9},{9,8},{10,11... | collective-permute-start | bytes 98312 | tf_op jit(solution)/shard_map/ppermute | solution.py:919
  30.7 1.3 %collective-permute-start.11 = (bf16[96,384]{1,0:T(8,128)(2,1)S(1)}, bf16[96,384]{1,0:T(8,128)(2,1)S(1)}, u32[]{:S(2)}, u32[]{:S(2)}) collective-permute-start(bf16[96,384]{1,0:T(8,128)(2,1)S(1)} %get-tuple-element.156), channel_id=1, source_target_pairs={{0,1},{1,0},{2,3},{3,2},{4,5},{5,4},{6,7},{7,6},{8,9},{9,8},{10,11... | collective-permute-start | bytes 221192 | tf_op jit(solution)/shard_map/ppermute | solution.py:919
  32.1 7.4 %collective-permute-start.16 = (bf16[96,384]{1,0:T(8,128)(2,1)S(1)}, bf16[96,384]{1,0:T(8,128)(2,1)S(1)}, u32[]{:S(2)}, u32[]{:S(2)}) collective-permute-start(bf16[96,384]{1,0:T(8,128)(2,1)S(1)} %get-tuple-element.170), channel_id=1, source_target_pairs={{0,24},{8,16},{16,8},{24,0},{1,25},{9,17},{17,9},{25,1},{2,26},{10... | collective-permute-start | bytes 221192 | tf_op jit(solution)/shard_map/ppermute | solution.py:919
  34.6 4.9 %collective-permute-start.15 = (bf16[96,384]{1,0:T(8,128)(2,1)S(1)}, bf16[96,384]{1,0:T(8,128)(2,1)S(1)}, u32[]{:S(2)}, u32[]{:S(2)}) collective-permute-start(bf16[96,384]{1,0:T(8,128)(2,1)S(1)} %get-tuple-element.170), channel_id=1, source_target_pairs={{0,16},{8,24},{16,0},{24,8},{1,17},{9,25},{17,1},{25,9},{2,18},{10... | collective-permute-start | bytes 221192 | tf_op jit(solution)/shard_map/ppermute | solution.py:919
  35.1 4.4 %collective-permute-start.14 = (bf16[96,384]{1,0:T(8,128)(2,1)S(1)}, bf16[96,384]{1,0:T(8,128)(2,1)S(1)}, u32[]{:S(2)}, u32[]{:S(2)}) collective-permute-start(bf16[96,384]{1,0:T(8,128)(2,1)S(1)} %get-tuple-element.170), channel_id=1, source_target_pairs={{0,8},{8,0},{16,24},{24,16},{1,9},{9,1},{17,25},{25,17},{2,10},{10... | collective-permute-start | bytes 221192 | tf_op jit(solution)/shard_map/ppermute | solution.py:919
  35.6 1.2 %collective-permute-start.12 = (bf16[128,128]{1,0:T(8,128)(2,1)S(1)}, bf16[128,128]{1,0:T(8,128)(2,1)S(1)}, u32[]{:S(2)}, u32[]{:S(2)}) collective-permute-start(bf16[128,128]{1,0:T(8,128)(2,1)S(1)} %get-tuple-element.158.refs_1_), channel_id=1, source_target_pairs={{0,1},{1,0},{2,3},{3,2},{4,5},{5,4},{6,7},{7,6},{8,9},{9,8},{10,11... | collective-permute-start | bytes 98312 | tf_op jit(solution)/shard_map/ppermute | solution.py:919
  37.4 1.3 %collective-permute-start.13 = (bf16[128,128]{1,0:T(8,128)(2,1)S(1)}, bf16[128,128]{1,0:T(8,128)(2,1)S(1)}, u32[]{:S(2)}, u32[]{:S(2)}) collective-permute-start(bf16[128,128]{1,0:T(8,128)(2,1)S(1)} %get-tuple-element.165.refs_0_), channel_id=1, source_target_pairs={{0,1},{1,0},{2,3},{3,2},{4,5},{5,4},{6,7},{7,6},{8,9},{9,8},{10,11... | collective-permute-start | bytes 98312 | tf_op jit(solution)/shard_map/ppermute | solution.py:919
  39.6 1.3 %collective-permute-start.17 = (bf16[96,384]{1,0:T(8,128)(2,1)S(1)}, bf16[96,384]{1,0:T(8,128)(2,1)S(1)}, u32[]{:S(2)}, u32[]{:S(2)}) collective-permute-start(bf16[96,384]{1,0:T(8,128)(2,1)S(1)} %get-tuple-element.172), channel_id=1, source_target_pairs={{0,1},{1,0},{2,3},{3,2},{4,5},{5,4},{6,7},{7,6},{8,9},{9,8},{10,11... | collective-permute-start | bytes 221192 | tf_op jit(solution)/shard_map/ppermute | solution.py:919

commit v6 on v5

--- a/solution.py
+++ b/solution.py
@@ -872,23 +872,22 @@
     values = [ref[...].astype(F32) for ref in refs[:-2]]
     while len(values) > 1:
         values = [values[k] + values[k + 1] for k in range(0, len(values), 2)]
-    refs[-1][...] = values[0].astype(BF16)
-    refs[-2][...] = values[0].astype(BF16)
+    refs[-1][...] = values[0].astype(refs[-1].dtype)
+    refs[-2][...] = values[0].astype(refs[-2].dtype)
 
 
 def end_kernel(factor, mine, got, gw, gb, cw, cb, flat):
     half = mine.shape[0]
     core = lax.rem(lax.axis_index("dom"), 2)
-    flat[pl.ds(pl.multiple_of(core * half, 8), half), :] = mine[...].astype(F32)
-    flat[pl.ds(pl.multiple_of((1 - core) * half, 8), half), :] = got[...].astype(F32)
+    flat[pl.ds(pl.multiple_of(core * half, 8), half), :] = mine[...] * factor
+    flat[pl.ds(pl.multiple_of((1 - core) * half, 8), half), :] = got[...] * factor
     features, rows = gw.shape
-    same = jnp.where(iota((features, flat.shape[1]), 0) == iota((features, flat.shape[1]), 1), 1.0, 0.0).astype(BF16)
-    gw[...] = nt(same, flat[:rows, :].astype(BF16)) * factor
-    cw[...] = flat[rows:, :features] * factor
-    pick = jnp.where(iota((8, flat.shape[1]), 1) == features, 1.0, 0.0).astype(BF16)
-    bias = nt(pick, flat[...].astype(BF16))[:1] * factor
-    gb[...] = bias[:, :rows]
-    cb[...] = bias[:, rows:]
+    gates = flat[:rows, :].T
+    gw[...] = gates[:features, :]
+    gb[...] = gates[features : features + 1, :]
+    cw[...] = flat[rows:, :features]
+    last = (features // LANES) * LANES
+    cb[...] = flat[rows:, last : last + LANES].T[features - last : features - last + 1, :]
 
 
 def chip_body(
@@ -1002,7 +1001,7 @@
     state_grad, done = run(
         chip_e_kernel, "chip_e2", [((1, hid, n), BF16), ((8, LANES), F32)], pay, got, *edges, base
     )
-    mine, sent = run(sum_kernel, "sum_snap", [half] * 2, *every, after=[done])
+    mine, sent = run(sum_kernel, "sum_snap", [(half[0], F32)] * 2, *every, after=[done])
     factor = 1.0 / math.sqrt(readings.shape[0] * snaps * n * nd)
     feats = orders * chans
     grad_gw, grad_gb, grad_cw, grad_cb = run(

time: 42.2 us -> 42.2 us (level)
  no operation moved by 1% of the time
where the time goes in v6:
time: 42.2 us; the launch traced here: 41.9 us
  Pallas kernels  19.5 us (46%)
  starting transfers between devices  13.8 us (33%)
  waiting for transfers between devices  5.22 us (12%)
  local copies, waits for them, and re-layouts  2.58 us (6%)
  between operations  0.79 us (2%)
    pallas_call x24, Pallas kernels, run(): pl.pallas_call(lambda *refs: kernel(*refs[len(after):]), name=name, out_s...  19.5 us
    ppermute x18, starting transfers between devices, swap(): return lax.ppermute(array, axis, [(i, i ^ k) for i in range(size)])  13.8 us
    ppermute x18, waiting for transfers between devices, swap(): return lax.ppermute(array, axis, [(i, i ^ k) for i in range(size)])  5.22 us
    unnamed x12, local copies, waits for them, and re-layouts  2.58 us
  transfers between devices with their start and end apart: 18, of which 7 were waited for; matrix products, arithmetic and copies ran while one was open for 0% of the time, Pallas kernels for 28%

profile of v6, /device:TPU:0, one launch (start us, length us, event | category | flops | bytes accessed | tf_op | source)
XLA Modules:
  0.0 41.9 jit_solution(5511707399913261868)
XLA Ops:
  0.6 1.7 %pack.1 = (bf16[80,512]{1,0:T(8,128)(2,1)}, bf16[144,512]{1,0:T(8,128)(2,1)}) custom-call(s32[4,512]{1,0:T(4,128)} %refs_0_.2, f32[4,512]{1,0:T(4,128)} %refs_1_.1, s32[1,32]{1,0:T(1,128)} %refs_2_.2, bf16[1,2,512]{2,1,0:T(2,128)(2,1)} %refs_3_.1, bf16[1,64,512]{2,1,0:T(8,128)(2,1)} %refs_4_.1, bf16[1,64,512]{2,1,0:T(8,128)(2,1)} %refs_0_.3), custom_call_target="tpu_custom_call" | custom-call | flops 20000000 | bytes 2000000 | tf_op jit(solution)/shard_map/pack/pallas_call | solution.py:39
  2.3 4.0 %collective-permute-start = (bf16[80,512]{1,0:T(8,128)(2,1)}, bf16[80,512]{1,0:T(8,128)(2,1)S(1)}, u32[]{:S(2)}, u32[]{:S(2)}) collective-permute-start(bf16[80,512]{1,0:T(8,128)(2,1)} %get-tuple-element.91.refs_0_), channel_id=1, source_target_pairs={{0,4},{1,5},{2,6},{3,7},{4,0},{5,1},{6,2},{7,3},{8,12},{9,13},{10,... | collective-permute-start | bytes 245768 | tf_op jit(solution)/shard_map/ppermute | solution.py:918
  6.3 1.6 %collective-permute-start.2 = (bf16[144,512]{1,0:T(8,128)(2,1)}, bf16[144,512]{1,0:T(8,128)(2,1)S(1)}, u32[]{:S(2)}, u32[]{:S(2)}) collective-permute-start(bf16[144,512]{1,0:T(8,128)(2,1)} %get-tuple-element.94), channel_id=1, source_target_pairs={{0,2},{1,3},{2,0},{3,1},{4,6},{5,7},{6,4},{7,5},{8,10},{9,11},{10,... | collective-permute-start | bytes 442376 | tf_op jit(solution)/shard_map/ppermute | solution.py:918
  7.9 0.3 collective-permute-start.3
  8.2 0.9 %copy-done = bf16[80,512]{1,0:T(8,128)(2,1)S(1)} copy-done((bf16[80,512]{1,0:T(8,128)(2,1)S(1)}, bf16[80,512]{1,0:T(8,128)(2,1)}, u32[]{:S(2)}) %copy-start) | copy-done | bytes 81944
  9.1 0.9 %copy-done.2 = bf16[128,330]{0,1:T(8,128)(2,1)S(1)} copy-done((bf16[128,330]{0,1:T(8,128)(2,1)S(1)}, bf16[128,330]{0,1:T(8,128)(2,1)}, u32[]{:S(2)}) %copy-start.2) | copy-done | bytes 84504
  10.0 0.8 %copy-done.3 = bf16[64,330]{1,0:T(8,128)(2,1)S(1)} copy-done((bf16[64,330]{1,0:T(8,128)(2,1)S(1)}, bf16[64,330]{1,0:T(8,128)(2,1)}, u32[]{:S(2)}) %copy-start.3) | copy-done | bytes 42264
  10.8 0.6 %order.1 = (bf16[128,400]{1,0:T(8,128)(2,1)S(1)}, bf16[64,400]{1,0:T(8,128)(2,1)S(1)}, bf16[320,128]{1,0:T(8,128)(2,1)S(1)}, bf16[320,64]{1,0:T(8,128)(2,1)S(1)}, bf16[400,384]{1,0:T(8,128)(2,1)S(1)}) custom-call(bf16[80,512]{1,0:T(8,128)(2,1)S(1)} %copy-done, bf16[330,128]{1,0:T(8,128)(2,1)S(1)} %bitcast.6, bf16[64,330]{1,0:T(8,128)(2,1)S(1)} %copy-done.3), custom_call_target="tpu_custom_call" | custom-call | flops 20000000 | bytes 2000000 | tf_op jit(solution)/shard_map/order/pallas_call | solution.py:39
  11.5 0.3 collective-permute-start.1
  11.8 2.1 %collective-permute-done.3.refs_0_.refs_2_ = bf16[1,64,512]{2,1,0:T(8,128)(2,1)S(1)} collective-permute-done((bf16[1,64,512]{2,1,0:T(8,128)(2,1)}, bf16[1,64,512]{2,1,0:T(8,128)(2,1)S(1)}, u32[]{:S(2)}, u32[]{:S(2)}) %collective-permute-start.3) | collective-permute-done | bytes 65568 | tf_op jit(solution)/shard_map/ppermute | solution.py:918
  13.9 1.3 %collective-permute-start.4 = (bf16[1,64,512]{2,1,0:T(8,128)(2,1)S(1)}, bf16[1,64,512]{2,1,0:T(8,128)(2,1)S(1)}, u32[]{:S(2)}, u32[]{:S(2)}) collective-permute-start(bf16[1,64,512]{2,1,0:T(8,128)(2,1)S(1)} %collective-permute-done.3.refs_0_.refs_2_), channel_id=1, source_target_pairs={{0,2},{1,3},{2,0},{3,1},{4,6},{5,7},{6,4},{7,5},{8,10},{9,11},{10,... | collective-permute-start | bytes 196616 | tf_op jit(solution)/shard_map/ppermute | solution.py:918
  15.2 1.2 %build_early.1 = (bf16[3,512,512]{2,1,0:T(8,128)(2,1)S(1)}, bf16[3,512,512]{2,1,0:T(8,128)(2,1)S(1)}, bf16[3,32,512]{2,1,0:T(8,128)(2,1)S(1)}, bf16[3,128,512]{2...) custom-call(bf16[80,512]{1,0:T(8,128)(2,1)S(1)} %copy-done, ...), custom_call_target="tpu_custom_call" | custom-call | flops 20000000 | bytes 2000000 | tf_op jit(solution)/shard_map/build_early/pallas_call | solution.py:39
  16.4 0.3 collective-permute-done.1.refs_0_
  16.7 0.6 %build_late.1 = (bf16[1,512,512]{2,1,0:T(8,128)(2,1)S(1)}, bf16[1,512,512]{2,1,0:T(8,128)(2,1)S(1)}, bf16[4,32,512]{2,1,0:T(8,128)(2,1)S(1)}, bf16[4,128,512]{2,...) custom-call(bf16[80,512]{1,0:T(8,128)(2,1)S(1)} %collective-permute-, ...), custom_call_target="tpu_custom_call" | custom-call | flops 20000000 | bytes 2000000 | tf_op jit(solution)/shard_map/build_late/pallas_call | solution.py:39
  17.4 0.9 %local_a.1 = (f32[4,80,512]{2,1,0:T(8,128)S(1)}, f32[4,80,512]{2,1,0:T(8,128)S(1)}) custom-call(bf16[3,512,512]{2,1,0:T(8,128)(2,1)S(1)} %get-tuple-element.106.refs_0_, bf16[3,512,512]{2,1,0:T(8,128)(2,1)S(1)} %get-tuple-element.107.refs_1_, bf16[1,512,512]{2,1,0:T(8,128)(2,1)S(1)} %get-tuple-element.108.refs_2_, ...), custom_call_target="tpu_custom_call" | custom-call | flops 20000000 | bytes 2000000 | tf_op jit(solution)/shard_map/local_a/pallas_call | solution.py:39
  18.2 0.3 collective-permute-done.5.refs_3_
  18.6 0.7 %chip_a.1 = (bf16[4,240,512]{2,1,0:T(8,128)(2,1)S(1)}, f32[4,1,512]{2,1,0:T(1,128)S(1)}, f32[4,1,512]{2,1,0:T(1,128)S(1)}, bf16[160,128]{1,0:T(8,128)(2,1)S(1)}) custom-call(bf16[1,64,512]{2,1,0:T(8,128)(2,1)S(1)} %collective-permute-done.3.refs_0_.refs_2_, bf16[1,64,512]{2,1,0:T(8,128)(2,1)S(1)} %collective-permute-done.4.refs_1_.refs_3_, ...), custom_call_target="tpu_custom_call" | custom-call | flops 20000000 | bytes 2000000 | tf_op jit(solution)/shard_map/chip_a/pallas_call | solution.py:39
  19.2 0.2 collective-permute-start.6
  19.5 1.0 %local_b.1 = (f32[4,80,512]{2,1,0:T(8,128)S(1)}, f32[4,80,512]{2,1,0:T(8,128)S(1)}, f32[4,128,512]{2,1,0:T(8,128)S(1)}) custom-call(bf16[3,512,512]{2,1,0:T(8,128)(2,1)S(1)} %get-tuple-element.106.refs_0_, bf16[3,512,512]{2,1,0:T(8,128)(2,1)S(1)} %get-tuple-element.107.refs_1_, bf16[1,512,512]{2,1,0:T(8,128)(2,1)S(1)} %get-tuple-element.108.refs_2_, ...), custom_call_target="tpu_custom_call" | custom-call | flops 20000000 | bytes 2000000 | tf_op jit(solution)/shard_map/local_b/pallas_call | solution.py:39
  20.5 1.0 %chip_b.1 = (bf16[4,160,512]{2,1,0:T(8,128)(2,1)S(1)}, f32[4,64,512]{2,1,0:T(8,128)S(1)}, f32[4,64,512]{2,1,0:T(8,128)S(1)}, bf16[4,64,512]{2,1,0:T(8,128)(2,1)S(1)}, bf16[128,128]{1,0:T(8,128)(2,1)S(1)}) custom-call(bf16[160,128]{1,0:T(8,128)(2,1)S(1)} %get-tuple-element.112.refs_0_, bf16[160,128]{1,0:T(8,128)(2,1)S(1)} %collective-permute-done.6.refs_1_, ...), custom_call_target="tpu_custom_call" | custom-call | flops 20000000 | bytes 2000000 | tf_op jit(solution)/shard_map/chip_b/pallas_call | solution.py:39
  21.5 0.4 collective-permute-start.7
  21.9 0.8 %local_c1.1 = (f32[4,64,512]{2,1,0:T(8,128)S(1)}, f32[4,64,512]{2,1,0:T(8,128)S(1)}) custom-call(bf16[3,512,512]{2,1,0:T(8,128)(2,1)S(1)} %get-tuple-element.106.refs_0_, bf16[3,512,512]{2,1,0:T(8,128)(2,1)S(1)} %get-tuple-element.107.refs_1_, bf16[1,512,512]{2,1,0:T(8,128)(2,1)S(1)} %get-tuple-element.108.refs_2_, ...), custom_call_target="tpu_custom_call" | custom-call | flops 20000000 | bytes 2000000 | tf_op jit(solution)/shard_map/local_c1/pallas_call | solution.py:39
  22.8 0.5 %chip_c1.1 = (bf16[4,240,512]{2,1,0:T(8,128)(2,1)S(1)}, bf16[128,128]{1,0:T(8,128)(2,1)S(1)}) custom-call(bf16[128,128]{1,0:T(8,128)(2,1)S(1)} %get-tuple-element.120.refs_0_, bf16[128,128]{1,0:T(8,128)(2,1)S(1)} %collective-permute-done.7.refs_1_, bf16[4,32,512]{2,1,0:T(8,128)(2,1)S(1)} %get-tuple-element.100.refs_4_.refs_2_.refs_6_.refs_0_.refs_3_, ...), custom_call_target="tpu_custom_call" | custom-call | flops 20000000 | bytes 2000000 | tf_op jit(solution)/shard_map/chip_c1/pallas_call | solution.py:39
  23.3 0.4 collective-permute-start.8
  23.7 1.0 %local_c2.1 = (f32[4,64,512]{2,1,0:T(8,128)S(1)}, f32[4,64,512]{2,1,0:T(8,128)S(1)}, f32[4,64,512]{2,1,0:T(8,128)S(1)}) custom-call(bf16[3,512,512]{2,1,0:T(8,128)(2,1)S(1)} %get-tuple-element.106.refs_0_, bf16[3,512,512]{2,1,0:T(8,128)(2,1)S(1)} %get-tuple-element.107.refs_1_, bf16[1,512,512]{2,1,0:T(8,128)(2,1)S(1)} %get-tuple-element.108.refs_2_, ...), custom_call_target="tpu_custom_call" | custom-call | flops 20000000 | bytes 2000000 | tf_op jit(solution)/shard_map/local_c2/pallas_call | solution.py:39
  24.8 1.3 %chip_c2.1 = (bf16[4,160,512]{2,1,0:T(8,128)(2,1)S(1)}, bf16[4,64,512]{2,1,0:T(8,128)(2,1)S(1)}, bf16[4,64,512]{2,1,0:T(8,128)(2,1)S(1)}, bf16[4,64,512]{2,1,0:T...) custom-call(bf16[1,64,512]{2,1,0:T(8,128)(2,1)S(1)} %copy-done.1, ...), custom_call_target="tpu_custom_call" | custom-call | flops 20000000 | bytes 2000000 | tf_op jit(solution)/shard_map/chip_c2/pallas_call | solution.py:39
  26.0 0.2 collective-permute-start.9
  26.3 1.5 %local_d1.1 = (f32[4,64,512]{2,1,0:T(8,128)S(1)}, f32[4,64,512]{2,1,0:T(8,128)S(1)}, bf16[64,384]{1,0:T(8,128)(2,1)S(1)}) custom-call(bf16[3,512,512]{2,1,0:T(8,128)(2,1)S(1)} %get-tuple-element.106.refs_0_, bf16[3,512,512]{2,1,0:T(8,128)(2,1)S(1)} %get-tuple-element.107.refs_1_, bf16[1,512,512]{2,1,0:T(8,128)(2,1)S(1)} %get-tuple-element.108.refs_2_, ...), custom_call_target="tpu_custom_call" | custom-call | flops 20000000 | bytes 2000000 | tf_op jit(solution)/shard_map/local_d1/pallas_call | solution.py:39
  27.8 0.6 %chip_d1.1 = (bf16[4,64,512]{2,1,0:T(8,128)(2,1)S(1)}, bf16[4,64,512]{2,1,0:T(8,128)(2,1)S(1)}, bf16[128,128]{1,0:T(8,128)(2,1)S(1)}) custom-call(bf16[128,128]{1,0:T(8,128)(2,1)S(1)} %get-tuple-element.133.refs_0_, bf16[128,128]{1,0:T(8,128)(2,1)S(1)} %collective-permute-done.9.refs_1_, ...), custom_call_target="tpu_custom_call" | custom-call | flops 20000000 | bytes 2000000 | tf_op jit(solution)/shard_map/chip_d1/pallas_call | solution.py:39
  28.3 0.4 %collective-permute-start.10 = (bf16[128,128]{1,0:T(8,128)(2,1)S(1)}, bf16[128,128]{1,0:T(8,128)(2,1)S(1)}, u32[]{:S(2)}, u32[]{:S(2)}) collective-permute-start(bf16[128,128]{1,0:T(8,128)(2,1)S(1)} %get-tuple-element.143.refs_0_), channel_id=1, source_target_pairs={{0,1},{1,0},{2,3},{3,2},{4,5},{5,4},{6,7},{7,6},{8,9},{9,8},{10,11... | collective-permute-start | bytes 98312 | tf_op jit(solution)/shard_map/ppermute | solution.py:918
  28.8 0.8 %local_d2.1.refs_4_ = f32[4,64,512]{2,1,0:T(8,128)S(1)} custom-call(bf16[3,512,512]{2,1,0:T(8,128)(2,1)S(1)} %get-tuple-element.106.refs_0_, bf16[3,512,512]{2,1,0:T(8,128)(2,1)S(1)} %get-tuple-element.107.refs_1_, bf16[1,512,512]{2,1,0:T(8,128)(2,1)S(1)} %get-tuple-element.108.refs_2_, bf16[1,512,512]{2,1,0:T(8,128)(2,1)S(1)} %get-tuple-element.109.refs_3_, ...), custom_call_target="tpu_custom_call" | custom-call | flops 20000000 | bytes 2000000 | tf_op jit(solution)/shard_map/local_d2/pallas_call | solution.py:39
  29.6 1.1 %chip_d2.1 = (bf16[4,128,512]{2,1,0:T(8,128)(2,1)S(1)}, f32[4,64,512]{2,1,0:T(8,128)S(1)}, bf16[96,384]{1,0:T(8,128)(2,1)S(1)}, bf16[96,384]{1,0:T(8,128)(2,1)S(1)}) custom-call(bf16[128,128]{1,0:T(8,128)(2,1)S(1)} %get-tuple-element.143.refs_0_, bf16[128,128]{1,0:T(8,128)(2,1)S(1)} %collective-permute-done.10.refs_1_, ...), custom_call_target="tpu_custom_call" | custom-call | flops 20000000 | bytes 2000000 | tf_op jit(solution)/shard_map/chip_d2/pallas_call | solution.py:39
  30.7 0.4 collective-permute-start.11
  31.1 0.8 %back_e.1 = (bf16[4,64,512]{2,1,0:T(8,128)(2,1)S(1)}, bf16[4,64,512]{2,1,0:T(8,128)(2,1)S(1)}, bf16[4,64,512]{2,1,0:T(8,128)(2,1)S(1)}, bf16[4,64,512]{2,1,0:T(8...) custom-call(bf16[4,32,512]{2,1,0:T(8,128)(2,1)S(1)} %get-tuple-element.100.refs_4_.refs_2_.refs_6_.refs_0_.refs_3_, ...), custom_call_target="tpu_custom_call" | custom-call | flops 20000000 | bytes 2000000 | tf_op jit(solution)/shard_map/back_e/pallas_call | solution.py:39
  31.9 0.1 collective-permute-done.11.refs_2_
  32.1 2.5 %collective-permute-start.16 = (bf16[96,384]{1,0:T(8,128)(2,1)S(1)}, bf16[96,384]{1,0:T(8,128)(2,1)S(1)}, u32[]{:S(2)}, u32[]{:S(2)}) collective-permute-start(bf16[96,384]{1,0:T(8,128)(2,1)S(1)} %get-tuple-element.170), channel_id=1, source_target_pairs={{0,24},{8,16},{16,8},{24,0},{1,25},{9,17},{17,9},{25,1},{2,26},{10... | collective-permute-start | bytes 221192 | tf_op jit(solution)/shard_map/ppermute | solution.py:918
  34.6 0.5 %collective-permute-start.15 = (bf16[96,384]{1,0:T(8,128)(2,1)S(1)}, bf16[96,384]{1,0:T(8,128)(2,1)S(1)}, u32[]{:S(2)}, u32[]{:S(2)}) collective-permute-start(bf16[96,384]{1,0:T(8,128)(2,1)S(1)} %get-tuple-element.170), channel_id=1, source_target_pairs={{0,16},{8,24},{16,0},{24,8},{1,17},{9,25},{17,1},{25,9},{2,18},{10... | collective-permute-start | bytes 221192 | tf_op jit(solution)/shard_map/ppermute | solution.py:918
  35.1 0.5 %collective-permute-start.14 = (bf16[96,384]{1,0:T(8,128)(2,1)S(1)}, bf16[96,384]{1,0:T(8,128)(2,1)S(1)}, u32[]{:S(2)}, u32[]{:S(2)}) collective-permute-start(bf16[96,384]{1,0:T(8,128)(2,1)S(1)} %get-tuple-element.170), channel_id=1, source_target_pairs={{0,8},{8,0},{16,24},{24,16},{1,9},{9,1},{17,25},{25,17},{2,10},{10... | collective-permute-start | bytes 221192 | tf_op jit(solution)/shard_map/ppermute | solution.py:918
  35.6 0.8 %local_e1.1 = (f32[4,64,512]{2,1,0:T(8,128)S(1)}, f32[4,64,512]{2,1,0:T(8,128)S(1)}) custom-call(bf16[3,512,512]{2,1,0:T(8,128)(2,1)S(1)} %get-tuple-element.106.refs_0_, bf16[3,512,512]{2,1,0:T(8,128)(2,1)S(1)} %get-tuple-element.107.refs_1_, bf16[1,512,512]{2,1,0:T(8,128)(2,1)S(1)} %get-tuple-element.108.refs_2_, ...), custom_call_target="tpu_custom_call" | custom-call | flops 20000000 | bytes 2000000 | tf_op jit(solution)/shard_map/local_e1/pallas_call | solution.py:39
  36.5 0.4 collective-permute-done.12.refs_2_
  36.8 0.6 %chip_e1.1 = (bf16[4,64,512]{2,1,0:T(8,128)(2,1)S(1)}, bf16[4,64,512]{2,1,0:T(8,128)(2,1)S(1)}, bf16[128,128]{1,0:T(8,128)(2,1)S(1)}) custom-call(bf16[96,384]{1,0:T(8,128)(2,1)S(1)} %get-tuple-element.157.refs_0_.refs_1_, bf16[128,128]{1,0:T(8,128)(2,1)S(1)} %get-tuple-element.158.refs_1_, bf16[128,128]{1,0:T(8,128)(2,1)S(1)} %collective-permute-done.12.refs_2_, ...), custom_call_target="tpu_custom_call" | custom-call | flops 20000000 | bytes 2000000 | tf_op jit(solution)/shard_map/chip_e1/pallas_call | solution.py:39
  37.4 0.2 collective-permute-start.13
  37.7 0.3 local_e2.1.refs_6_
  38.0 0.7 %collective-permute-done.13.refs_1_ = bf16[128,128]{1,0:T(8,128)(2,1)S(1)} collective-permute-done((bf16[128,128]{1,0:T(8,128)(2,1)S(1)}, bf16[128,128]{1,0:T(8,128)(2,1)S(1)}, u32[]{:S(2)}, u32[]{:S(2)}) %collective-permute-start.13) | collective-permute-done | bytes 32800 | tf_op jit(solution)/shard_map/ppermute | solution.py:918
  38.7 0.8 %chip_e2.1 = (bf16[1,64,512]{2,1,0:T(8,128)(2,1)}, f32[8,128]{1,0:T(8,128)S(1)}) custom-call(bf16[128,128]{1,0:T(8,128)(2,1)S(1)} %get-tuple-element.165.refs_0_, bf16[128,128]{1,0:T(8,128)(2,1)S(1)} %collective-permute-done.13.refs_1_, bf16[4,32,512]{2,1,0:T(8,128)(2,1)S(1)} %get-tuple-element.100.refs_4_.refs_2_.refs_6_.refs_0_.refs_3_, ...), custom_call_target="tpu_custom_call" | custom-call | flops 20000000 | bytes 2000000 | tf_op jit(solution)/shard_map/chip_e2/pallas_call | solution.py:39
  39.6 0.2 collective-permute-start.17
  39.8 1.2 %collective-permute-done.17.refs_1_ = f32[96,384]{1,0:T(8,128)S(1)} collective-permute-done((f32[96,384]{1,0:T(8,128)S(1)}, f32[96,384]{1,0:T(8,128)S(1)}, u32[]{:S(2)}, u32[]{:S(2)}) %collective-permute-start.17) | collective-permute-done | bytes 147488 | tf_op jit(solution)/shard_map/ppermute | solution.py:918
  41.0 0.9 %end.1 = (f32[330,128]{1,0:T(8,128)}, f32[1,128]{1,0:T(1,128)}, f32[64,330]{1,0:T(8,128)}, f32[1,64]{1,0:T(1,128)}) custom-call(f32[96,384]{1,0:T(8,128)S(1)} %get-tuple-element.171.refs_0_, f32[96,384]{1,0:T(8,128)S(1)} %collective-permute-done.17.refs_1_), custom_call_target="tpu_custom_call" | custom-call | flops 20000000 | bytes 2000000 | tf_op jit(solution)/shard_map/end/pallas_call | solution.py:39
  (24 shorter events, 0.3 us)
Async XLA Ops:
  2.3 9.2 %collective-permute-start = (bf16[80,512]{1,0:T(8,128)(2,1)}, bf16[80,512]{1,0:T(8,128)(2,1)S(1)}, u32[]{:S(2)}, u32[]{:S(2)}) collective-permute-start(bf16[80,512]{1,0:T(8,128)(2,1)} %get-tuple-element.91.refs_0_), channel_id=1, source_target_pairs={{0,4},{1,5},{2,6},{3,7},{4,0},{5,1},{6,2},{7,3},{8,12},{9,13},{10,... | collective-permute-start | bytes 245768 | tf_op jit(solution)/shard_map/ppermute | solution.py:918
  6.3 8.8 %collective-permute-start.2 = (bf16[144,512]{1,0:T(8,128)(2,1)}, bf16[144,512]{1,0:T(8,128)(2,1)S(1)}, u32[]{:S(2)}, u32[]{:S(2)}) collective-permute-start(bf16[144,512]{1,0:T(8,128)(2,1)} %get-tuple-element.94), channel_id=1, source_target_pairs={{0,2},{1,3},{2,0},{3,1},{4,6},{5,7},{6,4},{7,5},{8,10},{9,11},{10,... | collective-permute-start | bytes 442376 | tf_op jit(solution)/shard_map/ppermute | solution.py:918
  7.9 6.0 %collective-permute-start.3 = (bf16[1,64,512]{2,1,0:T(8,128)(2,1)}, bf16[1,64,512]{2,1,0:T(8,128)(2,1)S(1)}, u32[]{:S(2)}, u32[]{:S(2)}) collective-permute-start(bf16[1,64,512]{2,1,0:T(8,128)(2,1)} %refs_0_.3), channel_id=1, source_target_pairs={{0,4},{1,5},{2,6},{3,7},{4,0},{5,1},{6,2},{7,3},{8,12},{9,13},{10,... | collective-permute-start | bytes 196616 | tf_op jit(solution)/shard_map/ppermute | solution.py:918
  8.2 0.9 %copy-start = (bf16[80,512]{1,0:T(8,128)(2,1)S(1)}, bf16[80,512]{1,0:T(8,128)(2,1)}, u32[]{:S(2)}) copy-start(bf16[80,512]{1,0:T(8,128)(2,1)} %get-tuple-element.91.refs_0_) | copy-start | bytes 245764
  9.1 0.9 %copy-start.2 = (bf16[128,330]{0,1:T(8,128)(2,1)S(1)}, bf16[128,330]{0,1:T(8,128)(2,1)}, u32[]{:S(2)}) copy-start(bf16[128,330]{0,1:T(8,128)(2,1)} %param.13) | copy-start | bytes 253444
  10.0 0.8 %copy-start.3 = (bf16[64,330]{1,0:T(8,128)(2,1)S(1)}, bf16[64,330]{1,0:T(8,128)(2,1)}, u32[]{:S(2)}) copy-start(bf16[64,330]{1,0:T(8,128)(2,1)} %refs_2_.3) | copy-start | bytes 126724
  11.5 5.2 %collective-permute-start.1 = (bf16[80,512]{1,0:T(8,128)(2,1)S(1)}, bf16[80,512]{1,0:T(8,128)(2,1)S(1)}, u32[]{:S(2)}, u32[]{:S(2)}) collective-permute-start(bf16[80,512]{1,0:T(8,128)(2,1)S(1)} %collective-permute-done.refs_2_), channel_id=1, source_target_pairs={{0,2},{1,3},{2,0},{3,1},{4,6},{5,7},{6,4},{7,5},{8,10},{9,11},{10,... | collective-permute-start | bytes 245768 | tf_op jit(solution)/shard_map/ppermute | solution.py:918
  13.9 4.4 %collective-permute-start.4 = (bf16[1,64,512]{2,1,0:T(8,128)(2,1)S(1)}, bf16[1,64,512]{2,1,0:T(8,128)(2,1)S(1)}, u32[]{:S(2)}, u32[]{:S(2)}) collective-permute-start(bf16[1,64,512]{2,1,0:T(8,128)(2,1)S(1)} %collective-permute-done.3.refs_0_.refs_2_), channel_id=1, source_target_pairs={{0,2},{1,3},{2,0},{3,1},{4,6},{5,7},{6,4},{7,5},{8,10},{9,11},{10,... | collective-permute-start | bytes 196616 | tf_op jit(solution)/shard_map/ppermute | solution.py:918
  17.3 1.3 %collective-permute-start.5 = (bf16[160,128]{1,0:T(8,128)(2,1)S(1)}, bf16[160,128]{1,0:T(8,128)(2,1)S(1)}, u32[]{:S(2)}, u32[]{:S(2)}) collective-permute-start(bf16[160,128]{1,0:T(8,128)(2,1)S(1)} %get-tuple-element.102.refs_2_), channel_id=1, source_target_pairs={{0,1},{1,0},{2,3},{3,2},{4,5},{5,4},{6,7},{7,6},{8,9},{9,8},{10,11... | collective-permute-start | bytes 122888 | tf_op jit(solution)/shard_map/ppermute | solution.py:918
  19.2 1.3 %collective-permute-start.6 = (bf16[160,128]{1,0:T(8,128)(2,1)S(1)}, bf16[160,128]{1,0:T(8,128)(2,1)S(1)}, u32[]{:S(2)}, u32[]{:S(2)}) collective-permute-start(bf16[160,128]{1,0:T(8,128)(2,1)S(1)} %get-tuple-element.112.refs_0_), channel_id=1, source_target_pairs={{0,1},{1,0},{2,3},{3,2},{4,5},{5,4},{6,7},{7,6},{8,9},{9,8},{10,11... | collective-permute-start | bytes 122888 | tf_op jit(solution)/shard_map/ppermute | solution.py:918
  19.5 1.1 %copy-start.4 = (f32[128]{0:T(128)S(1)}, f32[128]{0:T(128)}, u32[]{:S(2)}) copy-start(f32[128]{0:T(128)} %param.14) | copy-start | bytes 1540
  21.5 1.3 %collective-permute-start.7 = (bf16[128,128]{1,0:T(8,128)(2,1)S(1)}, bf16[128,128]{1,0:T(8,128)(2,1)S(1)}, u32[]{:S(2)}, u32[]{:S(2)}) collective-permute-start(bf16[128,128]{1,0:T(8,128)(2,1)S(1)} %get-tuple-element.120.refs_0_), channel_id=1, source_target_pairs={{0,1},{1,0},{2,3},{3,2},{4,5},{5,4},{6,7},{7,6},{8,9},{9,8},{10,11... | collective-permute-start | bytes 98312 | tf_op jit(solution)/shard_map/ppermute | solution.py:918
  23.3 1.4 %collective-permute-start.8 = (bf16[128,128]{1,0:T(8,128)(2,1)S(1)}, bf16[128,128]{1,0:T(8,128)(2,1)S(1)}, u32[]{:S(2)}, u32[]{:S(2)}) collective-permute-start(bf16[128,128]{1,0:T(8,128)(2,1)S(1)} %get-tuple-element.124.refs_4_), channel_id=1, source_target_pairs={{0,1},{1,0},{2,3},{3,2},{4,5},{5,4},{6,7},{7,6},{8,9},{9,8},{10,11... | collective-permute-start | bytes 98312 | tf_op jit(solution)/shard_map/ppermute | solution.py:918
  23.7 1.0 %copy-start.1 = (bf16[1,64,512]{2,1,0:T(8,128)(2,1)S(1)}, bf16[1,64,512]{2,1,0:T(8,128)(2,1)}, u32[]{:S(2)}) copy-start(bf16[1,64,512]{2,1,0:T(8,128)(2,1)} %refs_0_.3) | copy-start | bytes 196612
  23.7 1.0 %copy-start.5 = (f32[64]{0:T(128)S(1)}, f32[64]{0:T(128)}, u32[]{:S(2)}) copy-start(f32[64]{0:T(128)} %param.16) | copy-start | bytes 772
  26.0 1.7 %collective-permute-start.9 = (bf16[128,128]{1,0:T(8,128)(2,1)S(1)}, bf16[128,128]{1,0:T(8,128)(2,1)S(1)}, u32[]{:S(2)}, u32[]{:S(2)}) collective-permute-start(bf16[128,128]{1,0:T(8,128)(2,1)S(1)} %get-tuple-element.133.refs_0_), channel_id=1, source_target_pairs={{0,1},{1,0},{2,3},{3,2},{4,5},{5,4},{6,7},{7,6},{8,9},{9,8},{10,11... | collective-permute-start | bytes 98312 | tf_op jit(solution)/shard_map/ppermute | solution.py:918
  28.3 1.3 %collective-permute-start.10 = (bf16[128,128]{1,0:T(8,128)(2,1)S(1)}, bf16[128,128]{1,0:T(8,128)(2,1)S(1)}, u32[]{:S(2)}, u32[]{:S(2)}) collective-permute-start(bf16[128,128]{1,0:T(8,128)(2,1)S(1)} %get-tuple-element.143.refs_0_), channel_id=1, source_target_pairs={{0,1},{1,0},{2,3},{3,2},{4,5},{5,4},{6,7},{7,6},{8,9},{9,8},{10,11... | collective-permute-start | bytes 98312 | tf_op jit(solution)/shard_map/ppermute | solution.py:918
  30.7 1.3 %collective-permute-start.11 = (bf16[96,384]{1,0:T(8,128)(2,1)S(1)}, bf16[96,384]{1,0:T(8,128)(2,1)S(1)}, u32[]{:S(2)}, u32[]{:S(2)}) collective-permute-start(bf16[96,384]{1,0:T(8,128)(2,1)S(1)} %get-tuple-element.156), channel_id=1, source_target_pairs={{0,1},{1,0},{2,3},{3,2},{4,5},{5,4},{6,7},{7,6},{8,9},{9,8},{10,11... | collective-permute-start | bytes 221192 | tf_op jit(solution)/shard_map/ppermute | solution.py:918
  32.1 7.4 %collective-permute-start.16 = (bf16[96,384]{1,0:T(8,128)(2,1)S(1)}, bf16[96,384]{1,0:T(8,128)(2,1)S(1)}, u32[]{:S(2)}, u32[]{:S(2)}) collective-permute-start(bf16[96,384]{1,0:T(8,128)(2,1)S(1)} %get-tuple-element.170), channel_id=1, source_target_pairs={{0,24},{8,16},{16,8},{24,0},{1,25},{9,17},{17,9},{25,1},{2,26},{10... | collective-permute-start | bytes 221192 | tf_op jit(solution)/shard_map/ppermute | solution.py:918
  34.6 4.9 %collective-permute-start.15 = (bf16[96,384]{1,0:T(8,128)(2,1)S(1)}, bf16[96,384]{1,0:T(8,128)(2,1)S(1)}, u32[]{:S(2)}, u32[]{:S(2)}) collective-permute-start(bf16[96,384]{1,0:T(8,128)(2,1)S(1)} %get-tuple-element.170), channel_id=1, source_target_pairs={{0,16},{8,24},{16,0},{24,8},{1,17},{9,25},{17,1},{25,9},{2,18},{10... | collective-permute-start | bytes 221192 | tf_op jit(solution)/shard_map/ppermute | solution.py:918
  35.1 4.4 %collective-permute-start.14 = (bf16[96,384]{1,0:T(8,128)(2,1)S(1)}, bf16[96,384]{1,0:T(8,128)(2,1)S(1)}, u32[]{:S(2)}, u32[]{:S(2)}) collective-permute-start(bf16[96,384]{1,0:T(8,128)(2,1)S(1)} %get-tuple-element.170), channel_id=1, source_target_pairs={{0,8},{8,0},{16,24},{24,16},{1,9},{9,1},{17,25},{25,17},{2,10},{10... | collective-permute-start | bytes 221192 | tf_op jit(solution)/shard_map/ppermute | solution.py:918
  35.6 1.2 %collective-permute-start.12 = (bf16[128,128]{1,0:T(8,128)(2,1)S(1)}, bf16[128,128]{1,0:T(8,128)(2,1)S(1)}, u32[]{:S(2)}, u32[]{:S(2)}) collective-permute-start(bf16[128,128]{1,0:T(8,128)(2,1)S(1)} %get-tuple-element.158.refs_1_), channel_id=1, source_target_pairs={{0,1},{1,0},{2,3},{3,2},{4,5},{5,4},{6,7},{7,6},{8,9},{9,8},{10,11... | collective-permute-start | bytes 98312 | tf_op jit(solution)/shard_map/ppermute | solution.py:918
  37.4 1.3 %collective-permute-start.13 = (bf16[128,128]{1,0:T(8,128)(2,1)S(1)}, bf16[128,128]{1,0:T(8,128)(2,1)S(1)}, u32[]{:S(2)}, u32[]{:S(2)}) collective-permute-start(bf16[128,128]{1,0:T(8,128)(2,1)S(1)} %get-tuple-element.165.refs_0_), channel_id=1, source_target_pairs={{0,1},{1,0},{2,3},{3,2},{4,5},{5,4},{6,7},{7,6},{8,9},{9,8},{10,11... | collective-permute-start | bytes 98312 | tf_op jit(solution)/shard_map/ppermute | solution.py:918
  39.6 1.4 %collective-permute-start.17 = (f32[96,384]{1,0:T(8,128)S(1)}, f32[96,384]{1,0:T(8,128)S(1)}, u32[]{:S(2)}, u32[]{:S(2)}) collective-permute-start(f32[96,384]{1,0:T(8,128)S(1)} %get-tuple-element.172), channel_id=1, source_target_pairs={{0,1},{1,0},{2,3},{3,2},{4,5},{5,4},{6,7},{7,6},{8,9},{9,8},{10,11... | collective-permute-start | bytes 442376 | tf_op jit(solution)/shard_map/ppermute | solution.py:918

commit v7 on v6

--- a/solution.py
+++ b/solution.py
@@ -802,9 +802,14 @@
     return nn(one, order[:split, :]) + nn(two, order[split:, :])
 
 
-def local_d_kernel(a0, at0, a1, at1, y1, y2, cand_grad, ma, mb, order, l1, l2, part):
+def cand_sums(cand_grad, features, parts):
+    return sum(nt(cand_grad[p], features[p]) for p in parts)
+
+
+def local_d_kernel(count, a0, at0, a1, at1, y1, y2, cand_grad, ma, mb, l1, l2, one, two):
     local_kernel(a0, at0, a1, at1, y1, y2, l1, l2)
-    part[...] = chip_part(cand_grad, ma, mb, order).astype(BF16)
+    one[...] = cand_sums(cand_grad, ma, range(count))
+    two[...] = cand_sums(cand_grad, mb, range(count))
 
 
 def chip_d1_kernel(mine, got, hc, hx, sc, sx, l1, l2, g1, g3, ro, ri, z1, z2, pay):
@@ -817,7 +822,12 @@
         z2[p] = two[p]
 
 
-def local_d2_kernel(a0, at0, a1, at1, z1, z2, direct, base):
+def local_d2_kernel(count, a0, at0, a1, at1, z1, z2, direct, cand_grad, ma, mb, one, two, order, base, part):
+    rest = range(count, z1.shape[0])
+    split = one.shape[1]
+    first = (one[...] + cand_sums(cand_grad, ma, rest)).astype(BF16)
+    second = (two[...] + cand_sums(cand_grad, mb, rest)).astype(BF16)
+    part[...] = (nn(first, order[:split, :]) + nn(second, order[split:, :])).astype(BF16)
     for k in range(z1.shape[0]):
         p, a = here(a0, a1, k)
         _, at = here(at0, at1, k)
@@ -973,14 +983,19 @@
         *ups, pay, got, *edges, ma, sa, sb, l1, l2, ro, ri, cw, cw_b, cand_bias[None, :], cp, update,
     )
     got = swap(pay, 1)
-    l1, l2, part = run(
-        local_d_kernel, "local_d1", [field, field, ((hid, width), BF16)], *local, y1, y2, cand_grad, ma, mb, order
+    count = parts // 2
+    l1, l2, one, two = run(
+        functools.partial(local_d_kernel, count), "local_d1",
+        [field, field, ((hid, 3 * block), F32), ((hid, (orders - 3) * block), F32)], *local, y1, y2, cand_grad, ma, mb
     )
     z1, z2, pay = run(
         chip_d1_kernel, "chip_d1", [field16, field16, pay_kind], pay, got, *edges, l1, l2, g1, g3, ro, ri
     )
     got = swap(pay, 1)
-    (base,) = run(local_d2_kernel, "local_d2", [field], *local, z1, z2, direct)
+    base, part = run(
+        functools.partial(local_d2_kernel, count), "local_d2", [field, ((hid, width), BF16)],
+        *local, z1, z2, direct, cand_grad, ma, mb, one, two, order,
+    )
     half = ((3 * hid // 2, width), BF16)
     gate_grad, kept, keep, give = run(
         chip_d2_kernel, "chip_d2", [((parts, 2 * hid, n), BF16), field, half, half],

time: 42.2 us -> 42.1 us (level)
  no operation moved by 1% of the time
where the time goes in v7:
time: 42.1 us; the launch traced here: 41.8 us
  Pallas kernels  19.4 us (46%)
  starting transfers between devices  13.6 us (32%)
  waiting for transfers between devices  5.41 us (13%)
  local copies, waits for them, and re-layouts  2.58 us (6%)
  between operations  0.8 us (2%)
    pallas_call x24, Pallas kernels, run(): pl.pallas_call(lambda *refs: kernel(*refs[len(after):]), name=name, out_s...  19.4 us
    ppermute x18, starting transfers between devices, swap(): return lax.ppermute(array, axis, [(i, i ^ k) for i in range(size)])  13.6 us
    ppermute x18, waiting for transfers between devices, swap(): return lax.ppermute(array, axis, [(i, i ^ k) for i in range(size)])  5.41 us
    unnamed x12, local copies, waits for them, and re-layouts  2.58 us
  transfers between devices with their start and end apart: 18, of which 7 were waited for; matrix products, arithmetic and copies ran while one was open for 0% of the time, Pallas kernels for 28%

profile of v7, /device:TPU:0, one launch (start us, length us, event | category | flops | bytes accessed | tf_op | source)
XLA Modules:
  0.0 41.8 jit_solution(6623643017717684095)
XLA Ops:
  0.6 1.7 %pack.1 = (bf16[80,512]{1,0:T(8,128)(2,1)}, bf16[144,512]{1,0:T(8,128)(2,1)}) custom-call(s32[4,512]{1,0:T(4,128)} %refs_0_.2, f32[4,512]{1,0:T(4,128)} %refs_1_.1, s32[1,32]{1,0:T(1,128)} %refs_2_.2, bf16[1,2,512]{2,1,0:T(2,128)(2,1)} %refs_3_.1, bf16[1,64,512]{2,1,0:T(8,128)(2,1)} %refs_4_.1, bf16[1,64,512]{2,1,0:T(8,128)(2,1)} %refs_0_.3), custom_call_target="tpu_custom_call" | custom-call | flops 20000000 | bytes 2000000 | tf_op jit(solution)/shard_map/pack/pallas_call | solution.py:39
  2.3 4.0 %collective-permute-start = (bf16[80,512]{1,0:T(8,128)(2,1)}, bf16[80,512]{1,0:T(8,128)(2,1)S(1)}, u32[]{:S(2)}, u32[]{:S(2)}) collective-permute-start(bf16[80,512]{1,0:T(8,128)(2,1)} %get-tuple-element.94.refs_0_), channel_id=1, source_target_pairs={{0,4},{1,5},{2,6},{3,7},{4,0},{5,1},{6,2},{7,3},{8,12},{9,13},{10,... | collective-permute-start | bytes 245768 | tf_op jit(solution)/shard_map/ppermute | solution.py:928
  6.3 1.6 %collective-permute-start.2 = (bf16[144,512]{1,0:T(8,128)(2,1)}, bf16[144,512]{1,0:T(8,128)(2,1)S(1)}, u32[]{:S(2)}, u32[]{:S(2)}) collective-permute-start(bf16[144,512]{1,0:T(8,128)(2,1)} %get-tuple-element.97), channel_id=1, source_target_pairs={{0,2},{1,3},{2,0},{3,1},{4,6},{5,7},{6,4},{7,5},{8,10},{9,11},{10,... | collective-permute-start | bytes 442376 | tf_op jit(solution)/shard_map/ppermute | solution.py:928
  7.9 0.3 collective-permute-start.3
  8.2 0.9 %copy-done = bf16[80,512]{1,0:T(8,128)(2,1)S(1)} copy-done((bf16[80,512]{1,0:T(8,128)(2,1)S(1)}, bf16[80,512]{1,0:T(8,128)(2,1)}, u32[]{:S(2)}) %copy-start) | copy-done | bytes 81944
  9.1 0.9 %copy-done.2 = bf16[128,330]{0,1:T(8,128)(2,1)S(1)} copy-done((bf16[128,330]{0,1:T(8,128)(2,1)S(1)}, bf16[128,330]{0,1:T(8,128)(2,1)}, u32[]{:S(2)}) %copy-start.2) | copy-done | bytes 84504
  10.0 0.8 %copy-done.3 = bf16[64,330]{1,0:T(8,128)(2,1)S(1)} copy-done((bf16[64,330]{1,0:T(8,128)(2,1)S(1)}, bf16[64,330]{1,0:T(8,128)(2,1)}, u32[]{:S(2)}) %copy-start.3) | copy-done | bytes 42264
  10.8 0.6 %order.1 = (bf16[128,400]{1,0:T(8,128)(2,1)S(1)}, bf16[64,400]{1,0:T(8,128)(2,1)S(1)}, bf16[320,128]{1,0:T(8,128)(2,1)S(1)}, bf16[320,64]{1,0:T(8,128)(2,1)S(1)}, bf16[400,384]{1,0:T(8,128)(2,1)S(1)}) custom-call(bf16[80,512]{1,0:T(8,128)(2,1)S(1)} %copy-done, bf16[330,128]{1,0:T(8,128)(2,1)S(1)} %bitcast.6, bf16[64,330]{1,0:T(8,128)(2,1)S(1)} %copy-done.3), custom_call_target="tpu_custom_call" | custom-call | flops 20000000 | bytes 2000000 | tf_op jit(solution)/shard_map/order/pallas_call | solution.py:39
  11.5 0.3 collective-permute-start.1
  11.8 2.1 %collective-permute-done.3.refs_0_.refs_2_ = bf16[1,64,512]{2,1,0:T(8,128)(2,1)S(1)} collective-permute-done((bf16[1,64,512]{2,1,0:T(8,128)(2,1)}, bf16[1,64,512]{2,1,0:T(8,128)(2,1)S(1)}, u32[]{:S(2)}, u32[]{:S(2)}) %collective-permute-start.3) | collective-permute-done | bytes 65568 | tf_op jit(solution)/shard_map/ppermute | solution.py:928
  13.9 1.3 %collective-permute-start.4 = (bf16[1,64,512]{2,1,0:T(8,128)(2,1)S(1)}, bf16[1,64,512]{2,1,0:T(8,128)(2,1)S(1)}, u32[]{:S(2)}, u32[]{:S(2)}) collective-permute-start(bf16[1,64,512]{2,1,0:T(8,128)(2,1)S(1)} %collective-permute-done.3.refs_0_.refs_2_), channel_id=1, source_target_pairs={{0,2},{1,3},{2,0},{3,1},{4,6},{5,7},{6,4},{7,5},{8,10},{9,11},{10,... | collective-permute-start | bytes 196616 | tf_op jit(solution)/shard_map/ppermute | solution.py:928
  15.2 1.2 %build_early.1 = (bf16[3,512,512]{2,1,0:T(8,128)(2,1)S(1)}, bf16[3,512,512]{2,1,0:T(8,128)(2,1)S(1)}, bf16[3,32,512]{2,1,0:T(8,128)(2,1)S(1)}, bf16[3,128,512]{2...) custom-call(bf16[80,512]{1,0:T(8,128)(2,1)S(1)} %copy-done, ...), custom_call_target="tpu_custom_call" | custom-call | flops 20000000 | bytes 2000000 | tf_op jit(solution)/shard_map/build_early/pallas_call | solution.py:39
  16.4 0.3 collective-permute-done.1.refs_0_
  16.7 0.6 %build_late.1 = (bf16[1,512,512]{2,1,0:T(8,128)(2,1)S(1)}, bf16[1,512,512]{2,1,0:T(8,128)(2,1)S(1)}, bf16[4,32,512]{2,1,0:T(8,128)(2,1)S(1)}, bf16[4,128,512]{2,...) custom-call(bf16[80,512]{1,0:T(8,128)(2,1)S(1)} %collective-permute-, ...), custom_call_target="tpu_custom_call" | custom-call | flops 20000000 | bytes 2000000 | tf_op jit(solution)/shard_map/build_late/pallas_call | solution.py:39
  17.4 0.9 %local_a.1 = (f32[4,80,512]{2,1,0:T(8,128)S(1)}, f32[4,80,512]{2,1,0:T(8,128)S(1)}) custom-call(bf16[3,512,512]{2,1,0:T(8,128)(2,1)S(1)} %get-tuple-element.109.refs_0_, bf16[3,512,512]{2,1,0:T(8,128)(2,1)S(1)} %get-tuple-element.110.refs_1_, bf16[1,512,512]{2,1,0:T(8,128)(2,1)S(1)} %get-tuple-element.111.refs_2_, ...), custom_call_target="tpu_custom_call" | custom-call | flops 20000000 | bytes 2000000 | tf_op jit(solution)/shard_map/local_a/pallas_call | solution.py:39
  18.2 0.3 collective-permute-done.5.refs_3_
  18.6 0.7 %chip_a.1 = (bf16[4,240,512]{2,1,0:T(8,128)(2,1)S(1)}, f32[4,1,512]{2,1,0:T(1,128)S(1)}, f32[4,1,512]{2,1,0:T(1,128)S(1)}, bf16[160,128]{1,0:T(8,128)(2,1)S(1)}) custom-call(bf16[1,64,512]{2,1,0:T(8,128)(2,1)S(1)} %collective-permute-done.3.refs_0_.refs_2_, bf16[1,64,512]{2,1,0:T(8,128)(2,1)S(1)} %collective-permute-done.4.refs_1_.refs_3_, ...), custom_call_target="tpu_custom_call" | custom-call | flops 20000000 | bytes 2000000 | tf_op jit(solution)/shard_map/chip_a/pallas_call | solution.py:39
  19.2 0.2 collective-permute-start.6
  19.5 1.0 %local_b.1 = (f32[4,80,512]{2,1,0:T(8,128)S(1)}, f32[4,80,512]{2,1,0:T(8,128)S(1)}, f32[4,128,512]{2,1,0:T(8,128)S(1)}) custom-call(bf16[3,512,512]{2,1,0:T(8,128)(2,1)S(1)} %get-tuple-element.109.refs_0_, bf16[3,512,512]{2,1,0:T(8,128)(2,1)S(1)} %get-tuple-element.110.refs_1_, bf16[1,512,512]{2,1,0:T(8,128)(2,1)S(1)} %get-tuple-element.111.refs_2_, ...), custom_call_target="tpu_custom_call" | custom-call | flops 20000000 | bytes 2000000 | tf_op jit(solution)/shard_map/local_b/pallas_call | solution.py:39
  20.5 1.0 %chip_b.1 = (bf16[4,160,512]{2,1,0:T(8,128)(2,1)S(1)}, f32[4,64,512]{2,1,0:T(8,128)S(1)}, f32[4,64,512]{2,1,0:T(8,128)S(1)}, bf16[4,64,512]{2,1,0:T(8,128)(2,1)S(1)}, bf16[128,128]{1,0:T(8,128)(2,1)S(1)}) custom-call(bf16[160,128]{1,0:T(8,128)(2,1)S(1)} %get-tuple-element.115.refs_0_, bf16[160,128]{1,0:T(8,128)(2,1)S(1)} %collective-permute-done.6.refs_1_, ...), custom_call_target="tpu_custom_call" | custom-call | flops 20000000 | bytes 2000000 | tf_op jit(solution)/shard_map/chip_b/pallas_call | solution.py:39
  21.5 0.4 collective-permute-start.7
  21.9 0.8 %local_c1.1 = (f32[4,64,512]{2,1,0:T(8,128)S(1)}, f32[4,64,512]{2,1,0:T(8,128)S(1)}) custom-call(bf16[3,512,512]{2,1,0:T(8,128)(2,1)S(1)} %get-tuple-element.109.refs_0_, bf16[3,512,512]{2,1,0:T(8,128)(2,1)S(1)} %get-tuple-element.110.refs_1_, bf16[1,512,512]{2,1,0:T(8,128)(2,1)S(1)} %get-tuple-element.111.refs_2_, ...), custom_call_target="tpu_custom_call" | custom-call | flops 20000000 | bytes 2000000 | tf_op jit(solution)/shard_map/local_c1/pallas_call | solution.py:39
  22.8 0.5 %chip_c1.1 = (bf16[4,240,512]{2,1,0:T(8,128)(2,1)S(1)}, bf16[128,128]{1,0:T(8,128)(2,1)S(1)}) custom-call(bf16[128,128]{1,0:T(8,128)(2,1)S(1)} %get-tuple-element.123.refs_0_, bf16[128,128]{1,0:T(8,128)(2,1)S(1)} %collective-permute-done.7.refs_1_, bf16[4,32,512]{2,1,0:T(8,128)(2,1)S(1)} %get-tuple-element.103.refs_4_.refs_2_.refs_6_.refs_0_.refs_3_, ...), custom_call_target="tpu_custom_call" | custom-call | flops 20000000 | bytes 2000000 | tf_op jit(solution)/shard_map/chip_c1/pallas_call | solution.py:39
  23.3 0.4 collective-permute-start.8
  23.7 1.0 %local_c2.1 = (f32[4,64,512]{2,1,0:T(8,128)S(1)}, f32[4,64,512]{2,1,0:T(8,128)S(1)}, f32[4,64,512]{2,1,0:T(8,128)S(1)}) custom-call(bf16[3,512,512]{2,1,0:T(8,128)(2,1)S(1)} %get-tuple-element.109.refs_0_, bf16[3,512,512]{2,1,0:T(8,128)(2,1)S(1)} %get-tuple-element.110.refs_1_, bf16[1,512,512]{2,1,0:T(8,128)(2,1)S(1)} %get-tuple-element.111.refs_2_, ...), custom_call_target="tpu_custom_call" | custom-call | flops 20000000 | bytes 2000000 | tf_op jit(solution)/shard_map/local_c2/pallas_call | solution.py:39
  24.8 1.3 %chip_c2.1 = (bf16[4,160,512]{2,1,0:T(8,128)(2,1)S(1)}, bf16[4,64,512]{2,1,0:T(8,128)(2,1)S(1)}, bf16[4,64,512]{2,1,0:T(8,128)(2,1)S(1)}, bf16[4,64,512]{2,1,0:T...) custom-call(bf16[1,64,512]{2,1,0:T(8,128)(2,1)S(1)} %copy-done.1, ...), custom_call_target="tpu_custom_call" | custom-call | flops 20000000 | bytes 2000000 | tf_op jit(solution)/shard_map/chip_c2/pallas_call | solution.py:39
  26.1 0.2 collective-permute-start.9
  26.3 1.1 %local_d1.1 = (f32[4,64,512]{2,1,0:T(8,128)S(1)}, f32[4,64,512]{2,1,0:T(8,128)S(1)}, f32[64,240]{1,0:T(8,128)S(1)}, f32[64,160]{1,0:T(8,128)S(1)}) custom-call(bf16[3,512,512]{2,1,0:T(8,128)(2,1)S(1)} %get-tuple-element.109.refs_0_, bf16[3,512,512]{2,1,0:T(8,128)(2,1)S(1)} %get-tuple-element.110.refs_1_, ...), custom_call_target="tpu_custom_call" | custom-call | flops 20000000 | bytes 2000000 | tf_op jit(solution)/shard_map/local_d1/pallas_call | solution.py:39
  27.4 0.6 %chip_d1.1 = (bf16[4,64,512]{2,1,0:T(8,128)(2,1)S(1)}, bf16[4,64,512]{2,1,0:T(8,128)(2,1)S(1)}, bf16[128,128]{1,0:T(8,128)(2,1)S(1)}) custom-call(bf16[128,128]{1,0:T(8,128)(2,1)S(1)} %get-tuple-element.136.refs_0_, bf16[128,128]{1,0:T(8,128)(2,1)S(1)} %collective-permute-done.9.refs_1_, ...), custom_call_target="tpu_custom_call" | custom-call | flops 20000000 | bytes 2000000 | tf_op jit(solution)/shard_map/chip_d1/pallas_call | solution.py:39
  27.9 0.4 %collective-permute-start.10 = (bf16[128,128]{1,0:T(8,128)(2,1)S(1)}, bf16[128,128]{1,0:T(8,128)(2,1)S(1)}, u32[]{:S(2)}, u32[]{:S(2)}) collective-permute-start(bf16[128,128]{1,0:T(8,128)(2,1)S(1)} %get-tuple-element.145.refs_0_), channel_id=1, source_target_pairs={{0,1},{1,0},{2,3},{3,2},{4,5},{5,4},{6,7},{7,6},{8,9},{9,8},{10,11... | collective-permute-start | bytes 98312 | tf_op jit(solution)/shard_map/ppermute | solution.py:928
  28.4 1.1 %local_d2.1 = (f32[4,64,512]{2,1,0:T(8,128)S(1)}, bf16[64,384]{1,0:T(8,128)(2,1)S(1)}) custom-call(bf16[3,512,512]{2,1,0:T(8,128)(2,1)S(1)} %get-tuple-element.109.refs_0_, bf16[3,512,512]{2,1,0:T(8,128)(2,1)S(1)} %get-tuple-element.110.refs_1_, bf16[1,512,512]{2,1,0:T(8,128)(2,1)S(1)} %get-tuple-element.111.refs_2_, ...), custom_call_target="tpu_custom_call" | custom-call | flops 20000000 | bytes 2000000 | tf_op jit(solution)/shard_map/local_d2/pallas_call | solution.py:39
  29.5 1.1 %chip_d2.1 = (bf16[4,128,512]{2,1,0:T(8,128)(2,1)S(1)}, f32[4,64,512]{2,1,0:T(8,128)S(1)}, bf16[96,384]{1,0:T(8,128)(2,1)S(1)}, bf16[96,384]{1,0:T(8,128)(2,1)S(1)}) custom-call(bf16[128,128]{1,0:T(8,128)(2,1)S(1)} %get-tuple-element.145.refs_0_, bf16[128,128]{1,0:T(8,128)(2,1)S(1)} %collective-permute-done.10.refs_1_, ...), custom_call_target="tpu_custom_call" | custom-call | flops 20000000 | bytes 2000000 | tf_op jit(solution)/shard_map/chip_d2/pallas_call | solution.py:39
  30.6 0.2 collective-permute-start.11
  30.8 0.8 %back_e.1 = (bf16[4,64,512]{2,1,0:T(8,128)(2,1)S(1)}, bf16[4,64,512]{2,1,0:T(8,128)(2,1)S(1)}, bf16[4,64,512]{2,1,0:T(8,128)(2,1)S(1)}, bf16[4,64,512]{2,1,0:T(8...) custom-call(bf16[4,32,512]{2,1,0:T(8,128)(2,1)S(1)} %get-tuple-element.103.refs_4_.refs_2_.refs_6_.refs_0_.refs_3_, ...), custom_call_target="tpu_custom_call" | custom-call | flops 20000000 | bytes 2000000 | tf_op jit(solution)/shard_map/back_e/pallas_call | solution.py:39
  31.6 0.3 collective-permute-done.11.refs_2_
  32.0 2.5 %collective-permute-start.16 = (bf16[96,384]{1,0:T(8,128)(2,1)S(1)}, bf16[96,384]{1,0:T(8,128)(2,1)S(1)}, u32[]{:S(2)}, u32[]{:S(2)}) collective-permute-start(bf16[96,384]{1,0:T(8,128)(2,1)S(1)} %get-tuple-element.176), channel_id=1, source_target_pairs={{0,24},{8,16},{16,8},{24,0},{1,25},{9,17},{17,9},{25,1},{2,26},{10... | collective-permute-start | bytes 221192 | tf_op jit(solution)/shard_map/ppermute | solution.py:928
  34.5 0.5 %collective-permute-start.15 = (bf16[96,384]{1,0:T(8,128)(2,1)S(1)}, bf16[96,384]{1,0:T(8,128)(2,1)S(1)}, u32[]{:S(2)}, u32[]{:S(2)}) collective-permute-start(bf16[96,384]{1,0:T(8,128)(2,1)S(1)} %get-tuple-element.176), channel_id=1, source_target_pairs={{0,16},{8,24},{16,0},{24,8},{1,17},{9,25},{17,1},{25,9},{2,18},{10... | collective-permute-start | bytes 221192 | tf_op jit(solution)/shard_map/ppermute | solution.py:928
  35.0 0.5 %collective-permute-start.14 = (bf16[96,384]{1,0:T(8,128)(2,1)S(1)}, bf16[96,384]{1,0:T(8,128)(2,1)S(1)}, u32[]{:S(2)}, u32[]{:S(2)}) collective-permute-start(bf16[96,384]{1,0:T(8,128)(2,1)S(1)} %get-tuple-element.176), channel_id=1, source_target_pairs={{0,8},{8,0},{16,24},{24,16},{1,9},{9,1},{17,25},{25,17},{2,10},{10... | collective-permute-start | bytes 221192 | tf_op jit(solution)/shard_map/ppermute | solution.py:928
  35.5 0.8 %local_e1.1 = (f32[4,64,512]{2,1,0:T(8,128)S(1)}, f32[4,64,512]{2,1,0:T(8,128)S(1)}) custom-call(bf16[3,512,512]{2,1,0:T(8,128)(2,1)S(1)} %get-tuple-element.109.refs_0_, bf16[3,512,512]{2,1,0:T(8,128)(2,1)S(1)} %get-tuple-element.110.refs_1_, bf16[1,512,512]{2,1,0:T(8,128)(2,1)S(1)} %get-tuple-element.111.refs_2_, ...), custom_call_target="tpu_custom_call" | custom-call | flops 20000000 | bytes 2000000 | tf_op jit(solution)/shard_map/local_e1/pallas_call | solution.py:39
  36.4 0.4 collective-permute-done.12.refs_2_
  36.8 0.6 %chip_e1.1 = (bf16[4,64,512]{2,1,0:T(8,128)(2,1)S(1)}, bf16[4,64,512]{2,1,0:T(8,128)(2,1)S(1)}, bf16[128,128]{1,0:T(8,128)(2,1)S(1)}) custom-call(bf16[96,384]{1,0:T(8,128)(2,1)S(1)} %get-tuple-element.163.refs_0_.refs_1_, bf16[128,128]{1,0:T(8,128)(2,1)S(1)} %get-tuple-element.164.refs_1_, bf16[128,128]{1,0:T(8,128)(2,1)S(1)} %collective-permute-done.12.refs_2_, ...), custom_call_target="tpu_custom_call" | custom-call | flops 20000000 | bytes 2000000 | tf_op jit(solution)/shard_map/chip_e1/pallas_call | solution.py:39
  37.3 0.2 collective-permute-start.13
  37.6 0.3 local_e2.1.refs_6_
  37.9 0.7 %collective-permute-done.13.refs_1_ = bf16[128,128]{1,0:T(8,128)(2,1)S(1)} collective-permute-done((bf16[128,128]{1,0:T(8,128)(2,1)S(1)}, bf16[128,128]{1,0:T(8,128)(2,1)S(1)}, u32[]{:S(2)}, u32[]{:S(2)}) %collective-permute-start.13) | collective-permute-done | bytes 32800 | tf_op jit(solution)/shard_map/ppermute | solution.py:928
  38.6 0.8 %chip_e2.1 = (bf16[1,64,512]{2,1,0:T(8,128)(2,1)}, f32[8,128]{1,0:T(8,128)S(1)}) custom-call(bf16[128,128]{1,0:T(8,128)(2,1)S(1)} %get-tuple-element.171.refs_0_, bf16[128,128]{1,0:T(8,128)(2,1)S(1)} %collective-permute-done.13.refs_1_, bf16[4,32,512]{2,1,0:T(8,128)(2,1)S(1)} %get-tuple-element.103.refs_4_.refs_2_.refs_6_.refs_0_.refs_3_, ...), custom_call_target="tpu_custom_call" | custom-call | flops 20000000 | bytes 2000000 | tf_op jit(solution)/shard_map/chip_e2/pallas_call | solution.py:39
  39.5 0.2 collective-permute-start.17
  39.7 1.2 %collective-permute-done.17.refs_1_ = f32[96,384]{1,0:T(8,128)S(1)} collective-permute-done((f32[96,384]{1,0:T(8,128)S(1)}, f32[96,384]{1,0:T(8,128)S(1)}, u32[]{:S(2)}, u32[]{:S(2)}) %collective-permute-start.17) | collective-permute-done | bytes 147488 | tf_op jit(solution)/shard_map/ppermute | solution.py:928
  40.9 0.9 %end.1 = (f32[330,128]{1,0:T(8,128)}, f32[1,128]{1,0:T(1,128)}, f32[64,330]{1,0:T(8,128)}, f32[1,64]{1,0:T(1,128)}) custom-call(f32[96,384]{1,0:T(8,128)S(1)} %get-tuple-element.177.refs_0_, f32[96,384]{1,0:T(8,128)S(1)} %collective-permute-done.17.refs_1_), custom_call_target="tpu_custom_call" | custom-call | flops 20000000 | bytes 2000000 | tf_op jit(solution)/shard_map/end/pallas_call | solution.py:39
  (24 shorter events, 0.3 us)
Async XLA Ops:
  2.3 9.2 %collective-permute-start = (bf16[80,512]{1,0:T(8,128)(2,1)}, bf16[80,512]{1,0:T(8,128)(2,1)S(1)}, u32[]{:S(2)}, u32[]{:S(2)}) collective-permute-start(bf16[80,512]{1,0:T(8,128)(2,1)} %get-tuple-element.94.refs_0_), channel_id=1, source_target_pairs={{0,4},{1,5},{2,6},{3,7},{4,0},{5,1},{6,2},{7,3},{8,12},{9,13},{10,... | collective-permute-start | bytes 245768 | tf_op jit(solution)/shard_map/ppermute | solution.py:928
  6.3 8.8 %collective-permute-start.2 = (bf16[144,512]{1,0:T(8,128)(2,1)}, bf16[144,512]{1,0:T(8,128)(2,1)S(1)}, u32[]{:S(2)}, u32[]{:S(2)}) collective-permute-start(bf16[144,512]{1,0:T(8,128)(2,1)} %get-tuple-element.97), channel_id=1, source_target_pairs={{0,2},{1,3},{2,0},{3,1},{4,6},{5,7},{6,4},{7,5},{8,10},{9,11},{10,... | collective-permute-start | bytes 442376 | tf_op jit(solution)/shard_map/ppermute | solution.py:928
  7.9 6.0 %collective-permute-start.3 = (bf16[1,64,512]{2,1,0:T(8,128)(2,1)}, bf16[1,64,512]{2,1,0:T(8,128)(2,1)S(1)}, u32[]{:S(2)}, u32[]{:S(2)}) collective-permute-start(bf16[1,64,512]{2,1,0:T(8,128)(2,1)} %refs_0_.3), channel_id=1, source_target_pairs={{0,4},{1,5},{2,6},{3,7},{4,0},{5,1},{6,2},{7,3},{8,12},{9,13},{10,... | collective-permute-start | bytes 196616 | tf_op jit(solution)/shard_map/ppermute | solution.py:928
  8.2 0.9 %copy-start = (bf16[80,512]{1,0:T(8,128)(2,1)S(1)}, bf16[80,512]{1,0:T(8,128)(2,1)}, u32[]{:S(2)}) copy-start(bf16[80,512]{1,0:T(8,128)(2,1)} %get-tuple-element.94.refs_0_) | copy-start | bytes 245764
  9.1 0.9 %copy-start.2 = (bf16[128,330]{0,1:T(8,128)(2,1)S(1)}, bf16[128,330]{0,1:T(8,128)(2,1)}, u32[]{:S(2)}) copy-start(bf16[128,330]{0,1:T(8,128)(2,1)} %param.13) | copy-start | bytes 253444
  10.0 0.8 %copy-start.3 = (bf16[64,330]{1,0:T(8,128)(2,1)S(1)}, bf16[64,330]{1,0:T(8,128)(2,1)}, u32[]{:S(2)}) copy-start(bf16[64,330]{1,0:T(8,128)(2,1)} %refs_2_.3) | copy-start | bytes 126724
  11.5 5.2 %collective-permute-start.1 = (bf16[80,512]{1,0:T(8,128)(2,1)S(1)}, bf16[80,512]{1,0:T(8,128)(2,1)S(1)}, u32[]{:S(2)}, u32[]{:S(2)}) collective-permute-start(bf16[80,512]{1,0:T(8,128)(2,1)S(1)} %collective-permute-done.refs_2_), channel_id=1, source_target_pairs={{0,2},{1,3},{2,0},{3,1},{4,6},{5,7},{6,4},{7,5},{8,10},{9,11},{10,... | collective-permute-start | bytes 245768 | tf_op jit(solution)/shard_map/ppermute | solution.py:928
  13.9 4.4 %collective-permute-start.4 = (bf16[1,64,512]{2,1,0:T(8,128)(2,1)S(1)}, bf16[1,64,512]{2,1,0:T(8,128)(2,1)S(1)}, u32[]{:S(2)}, u32[]{:S(2)}) collective-permute-start(bf16[1,64,512]{2,1,0:T(8,128)(2,1)S(1)} %collective-permute-done.3.refs_0_.refs_2_), channel_id=1, source_target_pairs={{0,2},{1,3},{2,0},{3,1},{4,6},{5,7},{6,4},{7,5},{8,10},{9,11},{10,... | collective-permute-start | bytes 196616 | tf_op jit(solution)/shard_map/ppermute | solution.py:928
  17.3 1.3 %collective-permute-start.5 = (bf16[160,128]{1,0:T(8,128)(2,1)S(1)}, bf16[160,128]{1,0:T(8,128)(2,1)S(1)}, u32[]{:S(2)}, u32[]{:S(2)}) collective-permute-start(bf16[160,128]{1,0:T(8,128)(2,1)S(1)} %get-tuple-element.105.refs_2_), channel_id=1, source_target_pairs={{0,1},{1,0},{2,3},{3,2},{4,5},{5,4},{6,7},{7,6},{8,9},{9,8},{10,11... | collective-permute-start | bytes 122888 | tf_op jit(solution)/shard_map/ppermute | solution.py:928
  19.2 1.3 %collective-permute-start.6 = (bf16[160,128]{1,0:T(8,128)(2,1)S(1)}, bf16[160,128]{1,0:T(8,128)(2,1)S(1)}, u32[]{:S(2)}, u32[]{:S(2)}) collective-permute-start(bf16[160,128]{1,0:T(8,128)(2,1)S(1)} %get-tuple-element.115.refs_0_), channel_id=1, source_target_pairs={{0,1},{1,0},{2,3},{3,2},{4,5},{5,4},{6,7},{7,6},{8,9},{9,8},{10,11... | collective-permute-start | bytes 122888 | tf_op jit(solution)/shard_map/ppermute | solution.py:928
  19.5 1.1 %copy-start.4 = (f32[128]{0:T(128)S(1)}, f32[128]{0:T(128)}, u32[]{:S(2)}) copy-start(f32[128]{0:T(128)} %param.14) | copy-start | bytes 1540
  21.5 1.3 %collective-permute-start.7 = (bf16[128,128]{1,0:T(8,128)(2,1)S(1)}, bf16[128,128]{1,0:T(8,128)(2,1)S(1)}, u32[]{:S(2)}, u32[]{:S(2)}) collective-permute-start(bf16[128,128]{1,0:T(8,128)(2,1)S(1)} %get-tuple-element.123.refs_0_), channel_id=1, source_target_pairs={{0,1},{1,0},{2,3},{3,2},{4,5},{5,4},{6,7},{7,6},{8,9},{9,8},{10,11... | collective-permute-start | bytes 98312 | tf_op jit(solution)/shard_map/ppermute | solution.py:928
  23.3 1.4 %collective-permute-start.8 = (bf16[128,128]{1,0:T(8,128)(2,1)S(1)}, bf16[128,128]{1,0:T(8,128)(2,1)S(1)}, u32[]{:S(2)}, u32[]{:S(2)}) collective-permute-start(bf16[128,128]{1,0:T(8,128)(2,1)S(1)} %get-tuple-element.127.refs_4_), channel_id=1, source_target_pairs={{0,1},{1,0},{2,3},{3,2},{4,5},{5,4},{6,7},{7,6},{8,9},{9,8},{10,11... | collective-permute-start | bytes 98312 | tf_op jit(solution)/shard_map/ppermute | solution.py:928
  23.7 1.0 %copy-start.1 = (bf16[1,64,512]{2,1,0:T(8,128)(2,1)S(1)}, bf16[1,64,512]{2,1,0:T(8,128)(2,1)}, u32[]{:S(2)}) copy-start(bf16[1,64,512]{2,1,0:T(8,128)(2,1)} %refs_0_.3) | copy-start | bytes 196612
  23.7 1.0 %copy-start.5 = (f32[64]{0:T(128)S(1)}, f32[64]{0:T(128)}, u32[]{:S(2)}) copy-start(f32[64]{0:T(128)} %param.16) | copy-start | bytes 772
  26.1 1.3 %collective-permute-start.9 = (bf16[128,128]{1,0:T(8,128)(2,1)S(1)}, bf16[128,128]{1,0:T(8,128)(2,1)S(1)}, u32[]{:S(2)}, u32[]{:S(2)}) collective-permute-start(bf16[128,128]{1,0:T(8,128)(2,1)S(1)} %get-tuple-element.136.refs_0_), channel_id=1, source_target_pairs={{0,1},{1,0},{2,3},{3,2},{4,5},{5,4},{6,7},{7,6},{8,9},{9,8},{10,11... | collective-permute-start | bytes 98312 | tf_op jit(solution)/shard_map/ppermute | solution.py:928
  27.9 1.6 %collective-permute-start.10 = (bf16[128,128]{1,0:T(8,128)(2,1)S(1)}, bf16[128,128]{1,0:T(8,128)(2,1)S(1)}, u32[]{:S(2)}, u32[]{:S(2)}) collective-permute-start(bf16[128,128]{1,0:T(8,128)(2,1)S(1)} %get-tuple-element.145.refs_0_), channel_id=1, source_target_pairs={{0,1},{1,0},{2,3},{3,2},{4,5},{5,4},{6,7},{7,6},{8,9},{9,8},{10,11... | collective-permute-start | bytes 98312 | tf_op jit(solution)/shard_map/ppermute | solution.py:928
  30.6 1.3 %collective-permute-start.11 = (bf16[96,384]{1,0:T(8,128)(2,1)S(1)}, bf16[96,384]{1,0:T(8,128)(2,1)S(1)}, u32[]{:S(2)}, u32[]{:S(2)}) collective-permute-start(bf16[96,384]{1,0:T(8,128)(2,1)S(1)} %get-tuple-element.162), channel_id=1, source_target_pairs={{0,1},{1,0},{2,3},{3,2},{4,5},{5,4},{6,7},{7,6},{8,9},{9,8},{10,11... | collective-permute-start | bytes 221192 | tf_op jit(solution)/shard_map/ppermute | solution.py:928
  32.0 7.4 %collective-permute-start.16 = (bf16[96,384]{1,0:T(8,128)(2,1)S(1)}, bf16[96,384]{1,0:T(8,128)(2,1)S(1)}, u32[]{:S(2)}, u32[]{:S(2)}) collective-permute-start(bf16[96,384]{1,0:T(8,128)(2,1)S(1)} %get-tuple-element.176), channel_id=1, source_target_pairs={{0,24},{8,16},{16,8},{24,0},{1,25},{9,17},{17,9},{25,1},{2,26},{10... | collective-permute-start | bytes 221192 | tf_op jit(solution)/shard_map/ppermute | solution.py:928
  34.5 4.9 %collective-permute-start.15 = (bf16[96,384]{1,0:T(8,128)(2,1)S(1)}, bf16[96,384]{1,0:T(8,128)(2,1)S(1)}, u32[]{:S(2)}, u32[]{:S(2)}) collective-permute-start(bf16[96,384]{1,0:T(8,128)(2,1)S(1)} %get-tuple-element.176), channel_id=1, source_target_pairs={{0,16},{8,24},{16,0},{24,8},{1,17},{9,25},{17,1},{25,9},{2,18},{10... | collective-permute-start | bytes 221192 | tf_op jit(solution)/shard_map/ppermute | solution.py:928
  35.0 4.4 %collective-permute-start.14 = (bf16[96,384]{1,0:T(8,128)(2,1)S(1)}, bf16[96,384]{1,0:T(8,128)(2,1)S(1)}, u32[]{:S(2)}, u32[]{:S(2)}) collective-permute-start(bf16[96,384]{1,0:T(8,128)(2,1)S(1)} %get-tuple-element.176), channel_id=1, source_target_pairs={{0,8},{8,0},{16,24},{24,16},{1,9},{9,1},{17,25},{25,17},{2,10},{10... | collective-permute-start | bytes 221192 | tf_op jit(solution)/shard_map/ppermute | solution.py:928
  35.5 1.2 %collective-permute-start.12 = (bf16[128,128]{1,0:T(8,128)(2,1)S(1)}, bf16[128,128]{1,0:T(8,128)(2,1)S(1)}, u32[]{:S(2)}, u32[]{:S(2)}) collective-permute-start(bf16[128,128]{1,0:T(8,128)(2,1)S(1)} %get-tuple-element.164.refs_1_), channel_id=1, source_target_pairs={{0,1},{1,0},{2,3},{3,2},{4,5},{5,4},{6,7},{7,6},{8,9},{9,8},{10,11... | collective-permute-start | bytes 98312 | tf_op jit(solution)/shard_map/ppermute | solution.py:928
  37.3 1.3 %collective-permute-start.13 = (bf16[128,128]{1,0:T(8,128)(2,1)S(1)}, bf16[128,128]{1,0:T(8,128)(2,1)S(1)}, u32[]{:S(2)}, u32[]{:S(2)}) collective-permute-start(bf16[128,128]{1,0:T(8,128)(2,1)S(1)} %get-tuple-element.171.refs_0_), channel_id=1, source_target_pairs={{0,1},{1,0},{2,3},{3,2},{4,5},{5,4},{6,7},{7,6},{8,9},{9,8},{10,11... | collective-permute-start | bytes 98312 | tf_op jit(solution)/shard_map/ppermute | solution.py:928
  39.5 1.4 %collective-permute-start.17 = (f32[96,384]{1,0:T(8,128)S(1)}, f32[96,384]{1,0:T(8,128)S(1)}, u32[]{:S(2)}, u32[]{:S(2)}) collective-permute-start(f32[96,384]{1,0:T(8,128)S(1)} %get-tuple-element.178), channel_id=1, source_target_pairs={{0,1},{1,0},{2,3},{3,2},{4,5},{5,4},{6,7},{7,6},{8,9},{9,8},{10,11... | collective-permute-start | bytes 442376 | tf_op jit(solution)/shard_map/ppermute | solution.py:928

commit v8 on v7

--- a/solution.py
+++ b/solution.py
@@ -550,8 +550,24 @@
     return value[:count, :], value[count:, :]
 
 
-def build_part(cap, hid, fin, degree, parts, p, block, a, at, hc, hx, sc, sx, b):
+def build_square(hid, fin, degree, block, a, at):
     n = a.shape[1]
+    row = iota((32, n), 0).astype(F32)
+    tail = block[hid : hid + 16 * (-(-(fin + 3 * degree + 2) // 16)), :].astype(F32)
+    high, low = tail[fin : fin + degree], tail[fin + degree : fin + 2 * degree]
+    w = tail[fin + 2 * degree : fin + 3 * degree]
+    low_is = [jnp.where(low[d : d + 1] == row, 1.0, 0.0).astype(BF16) for d in range(degree)]
+    for chunk in range(n // 32):
+        total = None
+        for d in range(degree):
+            term = low_is[d] * jnp.where(high[d : d + 1] == float(chunk), w[d : d + 1], 0.0).astype(BF16)
+            total = term if total is None else total + term
+        a[chunk * 32 : (chunk + 1) * 32, :] = total
+    at[...] = a[...].T
+
+
+def build_edge(cap, hid, fin, degree, parts, p, block, hc, hx, sc, sx, b):
+    n = b.shape[1]
     slots = sx.shape[0]
     nh = 2 * parts * cap
     half = parts * cap
@@ -570,22 +586,11 @@
     rest = rest - slot_rel * half
     inner = lax.div(rest, jnp.int32(cap))
     filled = iota((slots, nh), 1) == slot_rel * half + outer * cap + rest - inner * cap
-    row = iota((32, n), 0).astype(F32)
-    edges = hid + fin + 3 * degree + 2
-    tail = block[hid : hid + 16 * (-(-(edges - hid) // 16)), :].astype(F32)
-    high, low = tail[fin : fin + degree], tail[fin + degree : fin + 2 * degree]
+    tail = block[hid : hid + 16 * (-(-(fin + 3 * degree + 2) // 16)), :].astype(F32)
     w = tail[fin + 2 * degree : fin + 3 * degree]
     start = fin + 3 * degree
     sent = tail[start : start + 1] * 32.0 + tail[start + 1 : start + 2]
-    low_is = [jnp.where(low[d : d + 1] == row, 1.0, 0.0).astype(BF16) for d in range(degree)]
-    for chunk in range(n // 32):
-        total = None
-        for d in range(degree):
-            term = low_is[d] * jnp.where(high[d : d + 1] == float(chunk), w[d : d + 1], 0.0).astype(BF16)
-            total = term if total is None else total + term
-        a[chunk * 32 : (chunk + 1) * 32, :] = total
-    at[...] = a[...].T
-    names = high * 32.0 + low
+    names = tail[fin : fin + degree] * 32.0 + tail[fin + degree : fin + 2 * degree]
     total = jnp.zeros((nh, n), F32)
     for d in range(degree):
         total = total + jnp.where(names[d : d + 1] == node, w[d : d + 1], 0.0)
@@ -608,19 +613,20 @@
     z = lax.shift_right_logical(lax.axis_index("dom"), 1)
     for k in range(count):
         p = lax.bitwise_xor(z, jnp.int32(k))
-        build_part(cap, hid, fin, degree, parts, p, refs[k], *(ref.at[k] for ref in refs[count:]))
+        build_edge(cap, hid, fin, degree, parts, p, refs[k], *(ref.at[k] for ref in refs[count + 2 :]))
+        build_square(hid, fin, degree, refs[k], refs[count].at[k], refs[count + 1].at[k])
 
 
 def build_late_kernel(cap, hid, fin, degree, parts, last, *refs):
-    early, outs, pay = refs[:5], refs[5:12], refs[12]
+    early, outs, pay = refs[:5], refs[5:10], refs[10]
     z = lax.shift_right_logical(lax.axis_index("dom"), 1)
     for k in range(parts - 1):
         p = lax.bitwise_xor(z, jnp.int32(k))
-        for source, to in zip(early, outs[2:]):
+        for source, to in zip(early, outs):
             to[p] = source[k]
     p = lax.bitwise_xor(z, jnp.int32(parts - 1))
-    build_part(cap, hid, fin, degree, parts, p, last, outs[0].at[0], outs[1].at[0], *(ref.at[p] for ref in outs[2:]))
-    hc, sc, b = outs[2], outs[4], outs[6]
+    build_edge(cap, hid, fin, degree, parts, p, last, *(ref.at[p] for ref in outs))
+    hc, sc, b = outs[0], outs[2], outs[4]
     base = [b[p] for p in range(parts)]
     exchange(base, base, hc, sc, pay)
 
@@ -690,6 +696,11 @@
     exchange(ins, outs, hc, sc, pay)
 
 
+def local_a_kernel(hid, fin, degree, a0, at0, last, b, a1, at1, l1, l2):
+    build_square(hid, fin, degree, last, a1.at[0], at1.at[0])
+    local_kernel(a0, at0, a1, at1, b, b, l1, l2)
+
+
 def local_b_kernel(a0, at0, a1, at1, sa, gw, l1, l2, gp):
     chans = l1.shape[1]
     weights = gw[:, : 3 * chans]
@@ -703,24 +714,34 @@
         gp[p] = nn(weights, sa[p])
 
 
-def chip_b_kernel(mine, got, hc, hx, sc, sx, sa, l1, l2, ro, ri, gw, gb, gp, sb, reset, update, y, pay):
+def chip_b_kernel(mine, got, hc, hx, sc, sx, sa, l1, l2, ro, ri, gw, gb, gp, sb, reset, y, pay):
     hid = y.shape[1]
     chans = l1.shape[1]
-    bias = column(gb[...])
-    weights = gw[:, 3 * chans :]
+    bias = column(gb[:, :hid])
+    weights = gw[:hid, 3 * chans :]
     parts, pulled, pushed = arrive(sx, hx, mine, got, l1, l2)
     base = [sa[p, :chans, :].astype(F32) for p in parts]
     r2 = [(pulled[p] * (2.0 * ri[p]) - base[p]).astype(BF16) for p in parts]
     f2 = [(pushed[p] * (2.0 * ro[p]) - base[p]).astype(BF16) for p in parts]
     second = [jnp.concatenate([f2[p], r2[p]], axis=0) for p in parts]
-    gates = [jax.nn.sigmoid(gp[p] + nn(weights, second[p]) + bias) for p in parts]
-    now = [(gates[p][:hid] * base[p][:hid]).astype(BF16) for p in parts]
+    gates = [jax.nn.sigmoid(gp[p, :hid, :] + nn(weights, second[p]) + bias) for p in parts]
+    now = [(gates[p] * base[p][:hid]).astype(BF16) for p in parts]
     for p in parts:
         sb[p] = second[p]
-        reset[p] = gates[p][:hid]
-        update[p] = gates[p][hid:]
+        reset[p] = gates[p]
         y[p] = now[p]
     exchange(now, now, hc, sc, pay)
+
+
+def local_c1_kernel(a0, at0, a1, at1, y, sb, gw, gb, gp, l1, l2, update):
+    hid = y.shape[1]
+    local_kernel(a0, at0, a1, at1, y, y, l1, l2)
+    bias = column(gb[:, hid:])
+    weights = gw[hid:, gw.shape[1] - sb.shape[1] :]
+    parts = range(y.shape[0])
+    gates = [gp[p, hid:, :] + nn(weights, sb[p]) + bias for p in parts]
+    for p in parts:
+        update[p] = jax.nn.sigmoid(gates[p])
 
 
 def chip_c1_kernel(mine, got, hc, hx, sc, sx, y, sa, l1, l2, ro, ri, ma, pay):
@@ -954,27 +975,31 @@
         functools.partial(build_early_kernel, cap, hid, fin, degree, parts), "build_early",
         [((parts - 1, *shape), kind) for shape, kind in built], *blocks[:-1], relay,
     )
-    a, at, hc, hx, sc, sx, b, pay = run(
+    last = swap(relay, 2)
+    hc, hx, sc, sx, b, pay = run(
         functools.partial(build_late_kernel, cap, hid, fin, degree, parts), "build_late",
-        [((1 if shape == (n, n) else parts, *shape), kind) for shape, kind in built] + [wide_pay],
-        swap(relay, 2), *early[2:],
-    )
-    local = (early[0], early[1], a, at)
+        [((parts, *shape), kind) for shape, kind in built[2:]] + [wide_pay], last, *early[2:],
+    )
     edges = (hc, hx, sc, sx)
     got = swap(pay, 1)
-    l1, l2 = run(local_kernel, "local_a", [wide, wide], *local, b, b)
+    a, at, l1, l2 = run(
+        functools.partial(local_a_kernel, hid, fin, degree), "local_a", [((1, n, n), BF16)] * 2 + [wide, wide], *early[:2], last, b
+    )
+    local = (early[0], early[1], a, at)
     sa, ro, ri, pay = run(
         functools.partial(chip_a_kernel, hid + fin), "chip_a", [first, line, line, wide_pay],
         pay, got, *edges, b, l1, l2, after=ups[2:],
     )
     got = swap(pay, 1)
     l1, l2, gp = run(local_b_kernel, "local_b", [wide, wide, ((parts, 2 * hid, n), F32)], *local, sa, gw)
-    sb, reset, update, y, pay = run(
-        chip_b_kernel, "chip_b", [second, field, field, field16, pay_kind],
+    sb, reset, y, pay = run(
+        chip_b_kernel, "chip_b", [second, field, field16, pay_kind],
         pay, got, *edges, sa, l1, l2, ro, ri, gw, gate_bias[None, :], gp,
     )
     got = swap(pay, 1)
-    l1, l2 = run(local_kernel, "local_c1", [field, field], *local, y, y)
+    l1, l2, update = run(
+        local_c1_kernel, "local_c1", [field, field, field], *local, y, sb, gw, gate_bias[None, :], gp
+    )
     ma, pay = run(chip_c1_kernel, "chip_c1", [first, pay_kind], pay, got, *edges, y, sa, l1, l2, ro, ri)
     got = swap(pay, 1)
     l1, l2, cp = run(local_c2_kernel, "local_c2", [field, field, field], *local, ma, cw)

time: 42.1 us -> 42 us (level)
  transfers between devices with their start and end apart: 18 -> 18, of which waited for: 7 -> 7; matrix products, arithmetic and copies ran while one was open for 0% -> 0% of each run, Pallas kernels for 28% -> 29%
where the time goes in v8:
time: 42 us; the launch traced here: 41.7 us
  Pallas kernels  19.5 us (46%)
  starting transfers between devices  13.6 us (32%)
  waiting for transfers between devices  5.2 us (12%)
  local copies, waits for them, and re-layouts  2.58 us (6%)
  between operations  0.83 us (2%)
    pallas_call x24, Pallas kernels, run(): pl.pallas_call(lambda *refs: kernel(*refs[len(after):]), name=name, out_s...  19.5 us
    ppermute x18, starting transfers between devices, swap(): return lax.ppermute(array, axis, [(i, i ^ k) for i in range(size)])  13.6 us
    ppermute x18, waiting for transfers between devices, swap(): return lax.ppermute(array, axis, [(i, i ^ k) for i in range(size)])  5.2 us
    unnamed x12, local copies, waits for them, and re-layouts  2.58 us
  transfers between devices with their start and end apart: 18, of which 7 were waited for; matrix products, arithmetic and copies ran while one was open for 0% of the time, Pallas kernels for 29%

profile of v8, /device:TPU:0, one launch (start us, length us, event | category | flops | bytes accessed | tf_op | source)
XLA Modules:
  0.0 41.7 jit_solution(2131171240610814474)
XLA Ops:
  0.6 1.7 %pack.1 = (bf16[80,512]{1,0:T(8,128)(2,1)}, bf16[144,512]{1,0:T(8,128)(2,1)}) custom-call(s32[4,512]{1,0:T(4,128)} %refs_0_.2, f32[4,512]{1,0:T(4,128)} %refs_1_.1, s32[1,32]{1,0:T(1,128)} %refs_2_.2, bf16[1,2,512]{2,1,0:T(2,128)(2,1)} %refs_3_.1, bf16[1,64,512]{2,1,0:T(8,128)(2,1)} %refs_4_.1, bf16[1,64,512]{2,1,0:T(8,128)(2,1)} %refs_0_.3), custom_call_target="tpu_custom_call" | custom-call | flops 20000000 | bytes 2000000 | tf_op jit(solution)/shard_map/pack/pallas_call | solution.py:39
  2.3 4.0 %collective-permute-start = (bf16[80,512]{1,0:T(8,128)(2,1)}, bf16[80,512]{1,0:T(8,128)(2,1)S(1)}, u32[]{:S(2)}, u32[]{:S(2)}) collective-permute-start(bf16[80,512]{1,0:T(8,128)(2,1)} %get-tuple-element.94.refs_0_), channel_id=1, source_target_pairs={{0,4},{1,5},{2,6},{3,7},{4,0},{5,1},{6,2},{7,3},{8,12},{9,13},{10,... | collective-permute-start | bytes 245768 | tf_op jit(solution)/shard_map/ppermute | solution.py:949
  6.3 1.6 %collective-permute-start.2 = (bf16[144,512]{1,0:T(8,128)(2,1)}, bf16[144,512]{1,0:T(8,128)(2,1)S(1)}, u32[]{:S(2)}, u32[]{:S(2)}) collective-permute-start(bf16[144,512]{1,0:T(8,128)(2,1)} %get-tuple-element.97), channel_id=1, source_target_pairs={{0,2},{1,3},{2,0},{3,1},{4,6},{5,7},{6,4},{7,5},{8,10},{9,11},{10,... | collective-permute-start | bytes 442376 | tf_op jit(solution)/shard_map/ppermute | solution.py:949
  7.9 0.3 collective-permute-start.3
  8.2 0.9 %copy-done = bf16[80,512]{1,0:T(8,128)(2,1)S(1)} copy-done((bf16[80,512]{1,0:T(8,128)(2,1)S(1)}, bf16[80,512]{1,0:T(8,128)(2,1)}, u32[]{:S(2)}) %copy-start) | copy-done | bytes 81944
  9.1 0.9 %copy-done.2 = bf16[128,330]{0,1:T(8,128)(2,1)S(1)} copy-done((bf16[128,330]{0,1:T(8,128)(2,1)S(1)}, bf16[128,330]{0,1:T(8,128)(2,1)}, u32[]{:S(2)}) %copy-start.2) | copy-done | bytes 84504
  10.0 0.8 %copy-done.3 = bf16[64,330]{1,0:T(8,128)(2,1)S(1)} copy-done((bf16[64,330]{1,0:T(8,128)(2,1)S(1)}, bf16[64,330]{1,0:T(8,128)(2,1)}, u32[]{:S(2)}) %copy-start.3) | copy-done | bytes 42264
  10.8 0.6 %order.1 = (bf16[128,400]{1,0:T(8,128)(2,1)S(1)}, bf16[64,400]{1,0:T(8,128)(2,1)S(1)}, bf16[320,128]{1,0:T(8,128)(2,1)S(1)}, bf16[320,64]{1,0:T(8,128)(2,1)S(1)}, bf16[400,384]{1,0:T(8,128)(2,1)S(1)}) custom-call(bf16[80,512]{1,0:T(8,128)(2,1)S(1)} %copy-done, bf16[330,128]{1,0:T(8,128)(2,1)S(1)} %bitcast.6, bf16[64,330]{1,0:T(8,128)(2,1)S(1)} %copy-done.3), custom_call_target="tpu_custom_call" | custom-call | flops 20000000 | bytes 2000000 | tf_op jit(solution)/shard_map/order/pallas_call | solution.py:39
  11.5 0.3 collective-permute-start.1
  11.8 2.1 %collective-permute-done.3.refs_0_.refs_2_ = bf16[1,64,512]{2,1,0:T(8,128)(2,1)S(1)} collective-permute-done((bf16[1,64,512]{2,1,0:T(8,128)(2,1)}, bf16[1,64,512]{2,1,0:T(8,128)(2,1)S(1)}, u32[]{:S(2)}, u32[]{:S(2)}) %collective-permute-start.3) | collective-permute-done | bytes 65568 | tf_op jit(solution)/shard_map/ppermute | solution.py:949
  13.9 1.3 %collective-permute-start.4 = (bf16[1,64,512]{2,1,0:T(8,128)(2,1)S(1)}, bf16[1,64,512]{2,1,0:T(8,128)(2,1)S(1)}, u32[]{:S(2)}, u32[]{:S(2)}) collective-permute-start(bf16[1,64,512]{2,1,0:T(8,128)(2,1)S(1)} %collective-permute-done.3.refs_0_.refs_2_), channel_id=1, source_target_pairs={{0,2},{1,3},{2,0},{3,1},{4,6},{5,7},{6,4},{7,5},{8,10},{9,11},{10,... | collective-permute-start | bytes 196616 | tf_op jit(solution)/shard_map/ppermute | solution.py:949
  15.2 1.2 %build_early.1 = (bf16[3,512,512]{2,1,0:T(8,128)(2,1)S(1)}, bf16[3,512,512]{2,1,0:T(8,128)(2,1)S(1)}, bf16[3,32,512]{2,1,0:T(8,128)(2,1)S(1)}, bf16[3,128,512]{2...) custom-call(bf16[80,512]{1,0:T(8,128)(2,1)S(1)} %copy-done, ...), custom_call_target="tpu_custom_call" | custom-call | flops 20000000 | bytes 2000000 | tf_op jit(solution)/shard_map/build_early/pallas_call | solution.py:39
  16.3 0.3 collective-permute-done.1.refs_0_.refs_2_
  16.7 0.5 %build_late.1 = (bf16[4,32,512]{2,1,0:T(8,128)(2,1)S(1)}, bf16[4,128,512]{2,1,0:T(8,128)(2,1)S(1)}, bf16[4,32,512]{2,1,0:T(8,128)(2,1)S(1)}, bf16[4,128,512]{2,1...) custom-call(bf16[80,512]{1,0:T(8,128)(2,1)S(1)} %collective-permute-done.1.refs_0_.refs_2_, ...), custom_call_target="tpu_custom_call" | custom-call | flops 20000000 | bytes 2000000 | tf_op jit(solution)/shard_map/build_late/pallas_call | solution.py:39
  17.3 1.0 %local_a.1 = (bf16[1,512,512]{2,1,0:T(8,128)(2,1)S(1)}, bf16[1,512,512]{2,1,0:T(8,128)(2,1)S(1)}, f32[4,80,512]{2,1,0:T(8,128)S(1)}, f32[4,80,512]{2,1,0:T(8,128)S(1)}) custom-call(bf16[3,512,512]{2,1,0:T(8,128)(2,1)S(1)} %get-tuple-element.109.refs_0_, bf16[3,512,512]{2,1,0:T(8,128)(2,1)S(1)} %get-tuple-element.110.refs_1_, ...), custom_call_target="tpu_custom_call" | custom-call | flops 20000000 | bytes 2000000 | tf_op jit(solution)/shard_map/local_a/pallas_call | solution.py:39
  18.3 0.2 collective-permute-done.5.refs_3_
  18.5 0.7 %chip_a.1 = (bf16[4,240,512]{2,1,0:T(8,128)(2,1)S(1)}, f32[4,1,512]{2,1,0:T(1,128)S(1)}, f32[4,1,512]{2,1,0:T(1,128)S(1)}, bf16[160,128]{1,0:T(8,128)(2,1)S(1)}) custom-call(bf16[1,64,512]{2,1,0:T(8,128)(2,1)S(1)} %collective-permute-done.3.refs_0_.refs_2_, bf16[1,64,512]{2,1,0:T(8,128)(2,1)S(1)} %collective-permute-done.4.refs_1_.refs_3_, ...), custom_call_target="tpu_custom_call" | custom-call | flops 20000000 | bytes 2000000 | tf_op jit(solution)/shard_map/chip_a/pallas_call | solution.py:39
  19.2 0.4 collective-permute-start.6
  19.5 1.0 %local_b.1 = (f32[4,80,512]{2,1,0:T(8,128)S(1)}, f32[4,80,512]{2,1,0:T(8,128)S(1)}, f32[4,128,512]{2,1,0:T(8,128)S(1)}) custom-call(bf16[3,512,512]{2,1,0:T(8,128)(2,1)S(1)} %get-tuple-element.109.refs_0_, bf16[3,512,512]{2,1,0:T(8,128)(2,1)S(1)} %get-tuple-element.110.refs_1_, bf16[1,512,512]{2,1,0:T(8,128)(2,1)S(1)} %get-tuple-element.115.refs_2_, ...), custom_call_target="tpu_custom_call" | custom-call | flops 20000000 | bytes 2000000 | tf_op jit(solution)/shard_map/local_b/pallas_call | solution.py:39
  20.6 0.9 %chip_b.1 = (bf16[4,160,512]{2,1,0:T(8,128)(2,1)S(1)}, f32[4,64,512]{2,1,0:T(8,128)S(1)}, bf16[4,64,512]{2,1,0:T(8,128)(2,1)S(1)}, bf16[128,128]{1,0:T(8,128)(2,1)S(1)}) custom-call(bf16[160,128]{1,0:T(8,128)(2,1)S(1)} %get-tuple-element.113.refs_0_, bf16[160,128]{1,0:T(8,128)(2,1)S(1)} %collective-permute-done.6.refs_1_, ...), custom_call_target="tpu_custom_call" | custom-call | flops 20000000 | bytes 2000000 | tf_op jit(solution)/shard_map/chip_b/pallas_call | solution.py:39
  21.5 0.3 collective-permute-start.7
  21.8 1.0 %local_c1.1 = (f32[4,64,512]{2,1,0:T(8,128)S(1)}, f32[4,64,512]{2,1,0:T(8,128)S(1)}, f32[4,64,512]{2,1,0:T(8,128)S(1)}) custom-call(bf16[3,512,512]{2,1,0:T(8,128)(2,1)S(1)} %get-tuple-element.109.refs_0_, bf16[3,512,512]{2,1,0:T(8,128)(2,1)S(1)} %get-tuple-element.110.refs_1_, bf16[1,512,512]{2,1,0:T(8,128)(2,1)S(1)} %get-tuple-element.115.refs_2_, ...), custom_call_target="tpu_custom_call" | custom-call | flops 20000000 | bytes 2000000 | tf_op jit(solution)/shard_map/local_c1/pallas_call | solution.py:39
  22.8 0.5 %chip_c1.1 = (bf16[4,240,512]{2,1,0:T(8,128)(2,1)S(1)}, bf16[128,128]{1,0:T(8,128)(2,1)S(1)}) custom-call(bf16[128,128]{1,0:T(8,128)(2,1)S(1)} %get-tuple-element.123.refs_0_, bf16[128,128]{1,0:T(8,128)(2,1)S(1)} %collective-permute-done.7.refs_1_, bf16[4,32,512]{2,1,0:T(8,128)(2,1)S(1)} %get-tuple-element.103.refs_4_.refs_2_.refs_6_.refs_0_.refs_3_, ...), custom_call_target="tpu_custom_call" | custom-call | flops 20000000 | bytes 2000000 | tf_op jit(solution)/shard_map/chip_c1/pallas_call | solution.py:39
  23.3 0.4 collective-permute-start.8
  23.6 1.0 %local_c2.1 = (f32[4,64,512]{2,1,0:T(8,128)S(1)}, f32[4,64,512]{2,1,0:T(8,128)S(1)}, f32[4,64,512]{2,1,0:T(8,128)S(1)}) custom-call(bf16[3,512,512]{2,1,0:T(8,128)(2,1)S(1)} %get-tuple-element.109.refs_0_, bf16[3,512,512]{2,1,0:T(8,128)(2,1)S(1)} %get-tuple-element.110.refs_1_, bf16[1,512,512]{2,1,0:T(8,128)(2,1)S(1)} %get-tuple-element.115.refs_2_, ...), custom_call_target="tpu_custom_call" | custom-call | flops 20000000 | bytes 2000000 | tf_op jit(solution)/shard_map/local_c2/pallas_call | solution.py:39
  24.7 1.3 %chip_c2.1 = (bf16[4,160,512]{2,1,0:T(8,128)(2,1)S(1)}, bf16[4,64,512]{2,1,0:T(8,128)(2,1)S(1)}, bf16[4,64,512]{2,1,0:T(8,128)(2,1)S(1)}, bf16[4,64,512]{2,1,0:T...) custom-call(bf16[1,64,512]{2,1,0:T(8,128)(2,1)S(1)} %copy-done.1, ...), custom_call_target="tpu_custom_call" | custom-call | flops 20000000 | bytes 2000000 | tf_op jit(solution)/shard_map/chip_c2/pallas_call | solution.py:39
  26.0 0.3 collective-permute-start.9
  26.2 1.1 %local_d1.1 = (f32[4,64,512]{2,1,0:T(8,128)S(1)}, f32[4,64,512]{2,1,0:T(8,128)S(1)}, f32[64,240]{1,0:T(8,128)S(1)}, f32[64,160]{1,0:T(8,128)S(1)}) custom-call(bf16[3,512,512]{2,1,0:T(8,128)(2,1)S(1)} %get-tuple-element.109.refs_0_, bf16[3,512,512]{2,1,0:T(8,128)(2,1)S(1)} %get-tuple-element.110.refs_1_, ...), custom_call_target="tpu_custom_call" | custom-call | flops 20000000 | bytes 2000000 | tf_op jit(solution)/shard_map/local_d1/pallas_call | solution.py:39
  27.4 0.6 %chip_d1.1 = (bf16[4,64,512]{2,1,0:T(8,128)(2,1)S(1)}, bf16[4,64,512]{2,1,0:T(8,128)(2,1)S(1)}, bf16[128,128]{1,0:T(8,128)(2,1)S(1)}) custom-call(bf16[128,128]{1,0:T(8,128)(2,1)S(1)} %get-tuple-element.136.refs_0_, bf16[128,128]{1,0:T(8,128)(2,1)S(1)} %collective-permute-done.9.refs_1_, ...), custom_call_target="tpu_custom_call" | custom-call | flops 20000000 | bytes 2000000 | tf_op jit(solution)/shard_map/chip_d1/pallas_call | solution.py:39
  27.9 0.3 collective-permute-start.10
  28.3 1.1 %local_d2.1 = (f32[4,64,512]{2,1,0:T(8,128)S(1)}, bf16[64,384]{1,0:T(8,128)(2,1)S(1)}) custom-call(bf16[3,512,512]{2,1,0:T(8,128)(2,1)S(1)} %get-tuple-element.109.refs_0_, bf16[3,512,512]{2,1,0:T(8,128)(2,1)S(1)} %get-tuple-element.110.refs_1_, bf16[1,512,512]{2,1,0:T(8,128)(2,1)S(1)} %get-tuple-element.115.refs_2_, ...), custom_call_target="tpu_custom_call" | custom-call | flops 20000000 | bytes 2000000 | tf_op jit(solution)/shard_map/local_d2/pallas_call | solution.py:39
  29.4 1.1 %chip_d2.1 = (bf16[4,128,512]{2,1,0:T(8,128)(2,1)S(1)}, f32[4,64,512]{2,1,0:T(8,128)S(1)}, bf16[96,384]{1,0:T(8,128)(2,1)S(1)}, bf16[96,384]{1,0:T(8,128)(2,1)S(1)}) custom-call(bf16[128,128]{1,0:T(8,128)(2,1)S(1)} %get-tuple-element.145.refs_0_, bf16[128,128]{1,0:T(8,128)(2,1)S(1)} %collective-permute-done.10.refs_1_, ...), custom_call_target="tpu_custom_call" | custom-call | flops 20000000 | bytes 2000000 | tf_op jit(solution)/shard_map/chip_d2/pallas_call | solution.py:39
  30.5 0.3 collective-permute-start.11
  30.8 0.8 %back_e.1 = (bf16[4,64,512]{2,1,0:T(8,128)(2,1)S(1)}, bf16[4,64,512]{2,1,0:T(8,128)(2,1)S(1)}, bf16[4,64,512]{2,1,0:T(8,128)(2,1)S(1)}, bf16[4,64,512]{2,1,0:T(8...) custom-call(bf16[4,32,512]{2,1,0:T(8,128)(2,1)S(1)} %get-tuple-element.103.refs_4_.refs_2_.refs_6_.refs_0_.refs_3_, ...), custom_call_target="tpu_custom_call" | custom-call | flops 20000000 | bytes 2000000 | tf_op jit(solution)/shard_map/back_e/pallas_call | solution.py:39
  31.6 0.2 collective-permute-done.11.refs_2_
  31.9 2.5 %collective-permute-start.16 = (bf16[96,384]{1,0:T(8,128)(2,1)S(1)}, bf16[96,384]{1,0:T(8,128)(2,1)S(1)}, u32[]{:S(2)}, u32[]{:S(2)}) collective-permute-start(bf16[96,384]{1,0:T(8,128)(2,1)S(1)} %get-tuple-element.176), channel_id=1, source_target_pairs={{0,24},{8,16},{16,8},{24,0},{1,25},{9,17},{17,9},{25,1},{2,26},{10... | collective-permute-start | bytes 221192 | tf_op jit(solution)/shard_map/ppermute | solution.py:949
  34.4 0.5 %collective-permute-start.15 = (bf16[96,384]{1,0:T(8,128)(2,1)S(1)}, bf16[96,384]{1,0:T(8,128)(2,1)S(1)}, u32[]{:S(2)}, u32[]{:S(2)}) collective-permute-start(bf16[96,384]{1,0:T(8,128)(2,1)S(1)} %get-tuple-element.176), channel_id=1, source_target_pairs={{0,16},{8,24},{16,0},{24,8},{1,17},{9,25},{17,1},{25,9},{2,18},{10... | collective-permute-start | bytes 221192 | tf_op jit(solution)/shard_map/ppermute | solution.py:949
  34.9 0.5 %collective-permute-start.14 = (bf16[96,384]{1,0:T(8,128)(2,1)S(1)}, bf16[96,384]{1,0:T(8,128)(2,1)S(1)}, u32[]{:S(2)}, u32[]{:S(2)}) collective-permute-start(bf16[96,384]{1,0:T(8,128)(2,1)S(1)} %get-tuple-element.176), channel_id=1, source_target_pairs={{0,8},{8,0},{16,24},{24,16},{1,9},{9,1},{17,25},{25,17},{2,10},{10... | collective-permute-start | bytes 221192 | tf_op jit(solution)/shard_map/ppermute | solution.py:949
  35.4 0.8 %local_e1.1 = (f32[4,64,512]{2,1,0:T(8,128)S(1)}, f32[4,64,512]{2,1,0:T(8,128)S(1)}) custom-call(bf16[3,512,512]{2,1,0:T(8,128)(2,1)S(1)} %get-tuple-element.109.refs_0_, bf16[3,512,512]{2,1,0:T(8,128)(2,1)S(1)} %get-tuple-element.110.refs_1_, bf16[1,512,512]{2,1,0:T(8,128)(2,1)S(1)} %get-tuple-element.115.refs_2_, ...), custom_call_target="tpu_custom_call" | custom-call | flops 20000000 | bytes 2000000 | tf_op jit(solution)/shard_map/local_e1/pallas_call | solution.py:39
  36.3 0.4 collective-permute-done.12.refs_2_
  36.6 0.6 %chip_e1.1 = (bf16[4,64,512]{2,1,0:T(8,128)(2,1)S(1)}, bf16[4,64,512]{2,1,0:T(8,128)(2,1)S(1)}, bf16[128,128]{1,0:T(8,128)(2,1)S(1)}) custom-call(bf16[96,384]{1,0:T(8,128)(2,1)S(1)} %get-tuple-element.163.refs_0_.refs_1_, bf16[128,128]{1,0:T(8,128)(2,1)S(1)} %get-tuple-element.164.refs_1_, bf16[128,128]{1,0:T(8,128)(2,1)S(1)} %collective-permute-done.12.refs_2_, ...), custom_call_target="tpu_custom_call" | custom-call | flops 20000000 | bytes 2000000 | tf_op jit(solution)/shard_map/chip_e1/pallas_call | solution.py:39
  37.2 0.2 collective-permute-start.13
  37.5 0.3 local_e2.1.refs_6_
  37.8 0.7 %collective-permute-done.13.refs_1_ = bf16[128,128]{1,0:T(8,128)(2,1)S(1)} collective-permute-done((bf16[128,128]{1,0:T(8,128)(2,1)S(1)}, bf16[128,128]{1,0:T(8,128)(2,1)S(1)}, u32[]{:S(2)}, u32[]{:S(2)}) %collective-permute-start.13) | collective-permute-done | bytes 32800 | tf_op jit(solution)/shard_map/ppermute | solution.py:949
  38.5 0.8 %chip_e2.1 = (bf16[1,64,512]{2,1,0:T(8,128)(2,1)}, f32[8,128]{1,0:T(8,128)S(1)}) custom-call(bf16[128,128]{1,0:T(8,128)(2,1)S(1)} %get-tuple-element.171.refs_0_, bf16[128,128]{1,0:T(8,128)(2,1)S(1)} %collective-permute-done.13.refs_1_, bf16[4,32,512]{2,1,0:T(8,128)(2,1)S(1)} %get-tuple-element.103.refs_4_.refs_2_.refs_6_.refs_0_.refs_3_, ...), custom_call_target="tpu_custom_call" | custom-call | flops 20000000 | bytes 2000000 | tf_op jit(solution)/shard_map/chip_e2/pallas_call | solution.py:39
  39.4 0.2 collective-permute-start.17
  39.6 1.2 %collective-permute-done.17.refs_1_ = f32[96,384]{1,0:T(8,128)S(1)} collective-permute-done((f32[96,384]{1,0:T(8,128)S(1)}, f32[96,384]{1,0:T(8,128)S(1)}, u32[]{:S(2)}, u32[]{:S(2)}) %collective-permute-start.17) | collective-permute-done | bytes 147488 | tf_op jit(solution)/shard_map/ppermute | solution.py:949
  40.8 0.9 %end.1 = (f32[330,128]{1,0:T(8,128)}, f32[1,128]{1,0:T(1,128)}, f32[64,330]{1,0:T(8,128)}, f32[1,64]{1,0:T(1,128)}) custom-call(f32[96,384]{1,0:T(8,128)S(1)} %get-tuple-element.177.refs_0_, f32[96,384]{1,0:T(8,128)S(1)} %collective-permute-done.17.refs_1_), custom_call_target="tpu_custom_call" | custom-call | flops 20000000 | bytes 2000000 | tf_op jit(solution)/shard_map/end/pallas_call | solution.py:39
  (24 shorter events, 0.2 us)
Async XLA Ops:
  2.3 9.2 %collective-permute-start = (bf16[80,512]{1,0:T(8,128)(2,1)}, bf16[80,512]{1,0:T(8,128)(2,1)S(1)}, u32[]{:S(2)}, u32[]{:S(2)}) collective-permute-start(bf16[80,512]{1,0:T(8,128)(2,1)} %get-tuple-element.94.refs_0_), channel_id=1, source_target_pairs={{0,4},{1,5},{2,6},{3,7},{4,0},{5,1},{6,2},{7,3},{8,12},{9,13},{10,... | collective-permute-start | bytes 245768 | tf_op jit(solution)/shard_map/ppermute | solution.py:949
  6.3 8.8 %collective-permute-start.2 = (bf16[144,512]{1,0:T(8,128)(2,1)}, bf16[144,512]{1,0:T(8,128)(2,1)S(1)}, u32[]{:S(2)}, u32[]{:S(2)}) collective-permute-start(bf16[144,512]{1,0:T(8,128)(2,1)} %get-tuple-element.97), channel_id=1, source_target_pairs={{0,2},{1,3},{2,0},{3,1},{4,6},{5,7},{6,4},{7,5},{8,10},{9,11},{10,... | collective-permute-start | bytes 442376 | tf_op jit(solution)/shard_map/ppermute | solution.py:949
  7.9 6.0 %collective-permute-start.3 = (bf16[1,64,512]{2,1,0:T(8,128)(2,1)}, bf16[1,64,512]{2,1,0:T(8,128)(2,1)S(1)}, u32[]{:S(2)}, u32[]{:S(2)}) collective-permute-start(bf16[1,64,512]{2,1,0:T(8,128)(2,1)} %refs_0_.3), channel_id=1, source_target_pairs={{0,4},{1,5},{2,6},{3,7},{4,0},{5,1},{6,2},{7,3},{8,12},{9,13},{10,... | collective-permute-start | bytes 196616 | tf_op jit(solution)/shard_map/ppermute | solution.py:949
  8.2 0.9 %copy-start = (bf16[80,512]{1,0:T(8,128)(2,1)S(1)}, bf16[80,512]{1,0:T(8,128)(2,1)}, u32[]{:S(2)}) copy-start(bf16[80,512]{1,0:T(8,128)(2,1)} %get-tuple-element.94.refs_0_) | copy-start | bytes 245764
  9.1 0.9 %copy-start.2 = (bf16[128,330]{0,1:T(8,128)(2,1)S(1)}, bf16[128,330]{0,1:T(8,128)(2,1)}, u32[]{:S(2)}) copy-start(bf16[128,330]{0,1:T(8,128)(2,1)} %param.13) | copy-start | bytes 253444
  10.0 0.8 %copy-start.3 = (bf16[64,330]{1,0:T(8,128)(2,1)S(1)}, bf16[64,330]{1,0:T(8,128)(2,1)}, u32[]{:S(2)}) copy-start(bf16[64,330]{1,0:T(8,128)(2,1)} %refs_2_.3) | copy-start | bytes 126724
  11.5 5.2 %collective-permute-start.1 = (bf16[80,512]{1,0:T(8,128)(2,1)S(1)}, bf16[80,512]{1,0:T(8,128)(2,1)S(1)}, u32[]{:S(2)}, u32[]{:S(2)}) collective-permute-start(bf16[80,512]{1,0:T(8,128)(2,1)S(1)} %collective-permute-done.refs_2_), channel_id=1, source_target_pairs={{0,2},{1,3},{2,0},{3,1},{4,6},{5,7},{6,4},{7,5},{8,10},{9,11},{10,... | collective-permute-start | bytes 245768 | tf_op jit(solution)/shard_map/ppermute | solution.py:949
  13.9 4.4 %collective-permute-start.4 = (bf16[1,64,512]{2,1,0:T(8,128)(2,1)S(1)}, bf16[1,64,512]{2,1,0:T(8,128)(2,1)S(1)}, u32[]{:S(2)}, u32[]{:S(2)}) collective-permute-start(bf16[1,64,512]{2,1,0:T(8,128)(2,1)S(1)} %collective-permute-done.3.refs_0_.refs_2_), channel_id=1, source_target_pairs={{0,2},{1,3},{2,0},{3,1},{4,6},{5,7},{6,4},{7,5},{8,10},{9,11},{10,... | collective-permute-start | bytes 196616 | tf_op jit(solution)/shard_map/ppermute | solution.py:949
  17.2 1.3 %collective-permute-start.5 = (bf16[160,128]{1,0:T(8,128)(2,1)S(1)}, bf16[160,128]{1,0:T(8,128)(2,1)S(1)}, u32[]{:S(2)}, u32[]{:S(2)}) collective-permute-start(bf16[160,128]{1,0:T(8,128)(2,1)S(1)} %get-tuple-element.105.refs_2_), channel_id=1, source_target_pairs={{0,1},{1,0},{2,3},{3,2},{4,5},{5,4},{6,7},{7,6},{8,9},{9,8},{10,11... | collective-permute-start | bytes 122888 | tf_op jit(solution)/shard_map/ppermute | solution.py:949
  19.2 1.4 %collective-permute-start.6 = (bf16[160,128]{1,0:T(8,128)(2,1)S(1)}, bf16[160,128]{1,0:T(8,128)(2,1)S(1)}, u32[]{:S(2)}, u32[]{:S(2)}) collective-permute-start(bf16[160,128]{1,0:T(8,128)(2,1)S(1)} %get-tuple-element.113.refs_0_), channel_id=1, source_target_pairs={{0,1},{1,0},{2,3},{3,2},{4,5},{5,4},{6,7},{7,6},{8,9},{9,8},{10,11... | collective-permute-start | bytes 122888 | tf_op jit(solution)/shard_map/ppermute | solution.py:949
  19.5 1.0 %copy-start.4 = (f32[128]{0:T(128)S(1)}, f32[128]{0:T(128)}, u32[]{:S(2)}) copy-start(f32[128]{0:T(128)} %param.14) | copy-start | bytes 1540
  21.5 1.3 %collective-permute-start.7 = (bf16[128,128]{1,0:T(8,128)(2,1)S(1)}, bf16[128,128]{1,0:T(8,128)(2,1)S(1)}, u32[]{:S(2)}, u32[]{:S(2)}) collective-permute-start(bf16[128,128]{1,0:T(8,128)(2,1)S(1)} %get-tuple-element.123.refs_0_), channel_id=1, source_target_pairs={{0,1},{1,0},{2,3},{3,2},{4,5},{5,4},{6,7},{7,6},{8,9},{9,8},{10,11... | collective-permute-start | bytes 98312 | tf_op jit(solution)/shard_map/ppermute | solution.py:949
  23.3 1.4 %collective-permute-start.8 = (bf16[128,128]{1,0:T(8,128)(2,1)S(1)}, bf16[128,128]{1,0:T(8,128)(2,1)S(1)}, u32[]{:S(2)}, u32[]{:S(2)}) collective-permute-start(bf16[128,128]{1,0:T(8,128)(2,1)S(1)} %get-tuple-element.128.refs_4_), channel_id=1, source_target_pairs={{0,1},{1,0},{2,3},{3,2},{4,5},{5,4},{6,7},{7,6},{8,9},{9,8},{10,11... | collective-permute-start | bytes 98312 | tf_op jit(solution)/shard_map/ppermute | solution.py:949
  23.6 1.0 %copy-start.1 = (bf16[1,64,512]{2,1,0:T(8,128)(2,1)S(1)}, bf16[1,64,512]{2,1,0:T(8,128)(2,1)}, u32[]{:S(2)}) copy-start(bf16[1,64,512]{2,1,0:T(8,128)(2,1)} %refs_0_.3) | copy-start | bytes 196612
  23.6 1.0 %copy-start.5 = (f32[64]{0:T(128)S(1)}, f32[64]{0:T(128)}, u32[]{:S(2)}) copy-start(f32[64]{0:T(128)} %param.16) | copy-start | bytes 772
  26.0 1.4 %collective-permute-start.9 = (bf16[128,128]{1,0:T(8,128)(2,1)S(1)}, bf16[128,128]{1,0:T(8,128)(2,1)S(1)}, u32[]{:S(2)}, u32[]{:S(2)}) collective-permute-start(bf16[128,128]{1,0:T(8,128)(2,1)S(1)} %get-tuple-element.136.refs_0_), channel_id=1, source_target_pairs={{0,1},{1,0},{2,3},{3,2},{4,5},{5,4},{6,7},{7,6},{8,9},{9,8},{10,11... | collective-permute-start | bytes 98312 | tf_op jit(solution)/shard_map/ppermute | solution.py:949
  27.9 1.5 %collective-permute-start.10 = (bf16[128,128]{1,0:T(8,128)(2,1)S(1)}, bf16[128,128]{1,0:T(8,128)(2,1)S(1)}, u32[]{:S(2)}, u32[]{:S(2)}) collective-permute-start(bf16[128,128]{1,0:T(8,128)(2,1)S(1)} %get-tuple-element.145.refs_0_), channel_id=1, source_target_pairs={{0,1},{1,0},{2,3},{3,2},{4,5},{5,4},{6,7},{7,6},{8,9},{9,8},{10,11... | collective-permute-start | bytes 98312 | tf_op jit(solution)/shard_map/ppermute | solution.py:949
  30.5 1.3 %collective-permute-start.11 = (bf16[96,384]{1,0:T(8,128)(2,1)S(1)}, bf16[96,384]{1,0:T(8,128)(2,1)S(1)}, u32[]{:S(2)}, u32[]{:S(2)}) collective-permute-start(bf16[96,384]{1,0:T(8,128)(2,1)S(1)} %get-tuple-element.162), channel_id=1, source_target_pairs={{0,1},{1,0},{2,3},{3,2},{4,5},{5,4},{6,7},{7,6},{8,9},{9,8},{10,11... | collective-permute-start | bytes 221192 | tf_op jit(solution)/shard_map/ppermute | solution.py:949
  31.9 7.4 %collective-permute-start.16 = (bf16[96,384]{1,0:T(8,128)(2,1)S(1)}, bf16[96,384]{1,0:T(8,128)(2,1)S(1)}, u32[]{:S(2)}, u32[]{:S(2)}) collective-permute-start(bf16[96,384]{1,0:T(8,128)(2,1)S(1)} %get-tuple-element.176), channel_id=1, source_target_pairs={{0,24},{8,16},{16,8},{24,0},{1,25},{9,17},{17,9},{25,1},{2,26},{10... | collective-permute-start | bytes 221192 | tf_op jit(solution)/shard_map/ppermute | solution.py:949
  34.4 4.9 %collective-permute-start.15 = (bf16[96,384]{1,0:T(8,128)(2,1)S(1)}, bf16[96,384]{1,0:T(8,128)(2,1)S(1)}, u32[]{:S(2)}, u32[]{:S(2)}) collective-permute-start(bf16[96,384]{1,0:T(8,128)(2,1)S(1)} %get-tuple-element.176), channel_id=1, source_target_pairs={{0,16},{8,24},{16,0},{24,8},{1,17},{9,25},{17,1},{25,9},{2,18},{10... | collective-permute-start | bytes 221192 | tf_op jit(solution)/shard_map/ppermute | solution.py:949
  34.9 4.4 %collective-permute-start.14 = (bf16[96,384]{1,0:T(8,128)(2,1)S(1)}, bf16[96,384]{1,0:T(8,128)(2,1)S(1)}, u32[]{:S(2)}, u32[]{:S(2)}) collective-permute-start(bf16[96,384]{1,0:T(8,128)(2,1)S(1)} %get-tuple-element.176), channel_id=1, source_target_pairs={{0,8},{8,0},{16,24},{24,16},{1,9},{9,1},{17,25},{25,17},{2,10},{10... | collective-permute-start | bytes 221192 | tf_op jit(solution)/shard_map/ppermute | solution.py:949
  35.4 1.2 %collective-permute-start.12 = (bf16[128,128]{1,0:T(8,128)(2,1)S(1)}, bf16[128,128]{1,0:T(8,128)(2,1)S(1)}, u32[]{:S(2)}, u32[]{:S(2)}) collective-permute-start(bf16[128,128]{1,0:T(8,128)(2,1)S(1)} %get-tuple-element.164.refs_1_), channel_id=1, source_target_pairs={{0,1},{1,0},{2,3},{3,2},{4,5},{5,4},{6,7},{7,6},{8,9},{9,8},{10,11... | collective-permute-start | bytes 98312 | tf_op jit(solution)/shard_map/ppermute | solution.py:949
  37.2 1.3 %collective-permute-start.13 = (bf16[128,128]{1,0:T(8,128)(2,1)S(1)}, bf16[128,128]{1,0:T(8,128)(2,1)S(1)}, u32[]{:S(2)}, u32[]{:S(2)}) collective-permute-start(bf16[128,128]{1,0:T(8,128)(2,1)S(1)} %get-tuple-element.171.refs_0_), channel_id=1, source_target_pairs={{0,1},{1,0},{2,3},{3,2},{4,5},{5,4},{6,7},{7,6},{8,9},{9,8},{10,11... | collective-permute-start | bytes 98312 | tf_op jit(solution)/shard_map/ppermute | solution.py:949
  39.4 1.4 %collective-permute-start.17 = (f32[96,384]{1,0:T(8,128)S(1)}, f32[96,384]{1,0:T(8,128)S(1)}, u32[]{:S(2)}, u32[]{:S(2)}) collective-permute-start(f32[96,384]{1,0:T(8,128)S(1)} %get-tuple-element.178), channel_id=1, source_target_pairs={{0,1},{1,0},{2,3},{3,2},{4,5},{5,4},{6,7},{7,6},{8,9},{9,8},{10,11... | collective-permute-start | bytes 442376 | tf_op jit(solution)/shard_map/ppermute | solution.py:949
